TPU v7x, 512 devices: a whole 4x4x16 slice. The times are simulated.
512 devices in a mesh: ia: 8 (over y, core), ao: 8 (over x, z_hi), ta: 8 (over z_lo).
Axes of the slice: x: 4, y: 4, z: 16 (z_hi: 2, z_lo: 8; z = z_hi * 8 + z_lo), core: 2. Of those that a mesh axis runs over, the one named last changes fastest.
Arguments:
- inputs: bfloat16 [768, 8192], P(('ao', 'ta'), 'ia'), may hold values from -6 to 6
- out_grad: bfloat16 [768, 8192], P(('ao', 'ta'), 'ia'), may hold values from -6 to 6
- preact: bfloat16 [768, 16384], P('ia', ('ao', 'ta')), may hold values from -6 to 6
- up_weight: bfloat16 [8192, 16384], P('ia', ('ao', 'ta')), may hold values from -0.0625 to 0.0625
- down_weight: bfloat16 [16384, 8192], P(('ao', 'ta'), 'ia'), may hold values from -0.046875 to 0.046875
Outputs:
- input_grad: bfloat16 [768, 8192], P(('ao', 'ta'), 'ia')
- up_grad: float32 [8192, 16384], P('ia', ('ao', 'ta'))
- down_grad: float32 [16384, 8192], P(('ao', 'ta'), 'ia')
All inputs are finite; a program needn't handle non-finite values.
Results may differ from a plain program's by a relative error of at most 0.0049.
Values may be sent and summed in bfloat16 or wider, within the bound.
No kernel may reach another device: no remote copies, remote signals or barrier semaphores. Data moves between devices by JAX's collectives and lax.ppermute only.
A program may use at most 64 MiB of HBM per device.

v0:
```python
import math

import jax
import jax.numpy as jnp
from jax import lax
from jax.sharding import PartitionSpec as P


def gelu_parts(preact):
    value = preact.astype(jnp.float32)
    normal_cdf = 0.5 * (1.0 + jax.scipy.special.erf(value / math.sqrt(2.0)))
    density = jnp.exp(-0.5 * value * value) / math.sqrt(2.0 * math.pi)
    return (value * normal_cdf, normal_cdf + value * density)


def local(inputs, out_grad, preact, up_weight, down_weight):
    all_inputs, all_grads = (
        lax.all_gather(inputs, ("ao", "ta"), axis=0, tiled=True),
        lax.all_gather(out_grad, ("ao", "ta"), axis=0, tiled=True),
    )
    partial_hidden = jnp.einsum(
        "td,fd->tf", all_grads, down_weight, preferred_element_type=jnp.float32
    )
    hidden_grad = lax.psum(partial_hidden, "ia")
    all_preact = lax.all_gather(preact, "ia", axis=0, tiled=True)
    activ, slope = gelu_parts(all_preact)
    all_activ = activ.astype(jnp.bfloat16)
    all_pregrad = (hidden_grad * slope).astype(jnp.bfloat16)
    up_grad = jnp.einsum("td,tf->df", all_inputs, all_pregrad, preferred_element_type=jnp.float32)
    down_grad = jnp.einsum("tf,td->fd", all_activ, all_grads, preferred_element_type=jnp.float32)
    input_sum = lax.psum_scatter(
        jnp.einsum("tf,df->td", all_pregrad, up_weight, preferred_element_type=jnp.float32),
        ("ao", "ta"),
        scatter_dimension=0,
        tiled=True,
    )
    return (input_sum.astype(jnp.bfloat16), up_grad, down_grad)


def solution(mesh):
    placed = (
        P(("ao", "ta"), "ia"),
        P(("ao", "ta"), "ia"),
        P("ia", ("ao", "ta")),
        P("ia", ("ao", "ta")),
        P(("ao", "ta"), "ia"),
    )
    return jax.shard_map(
        local,
        mesh=mesh,
        in_specs=placed,
        out_specs=(P(("ao", "ta"), "ia"), P("ia", ("ao", "ta")), P(("ao", "ta"), "ia")),
        check_vma=False,
    )
```

profile of v0, /device:TPU:24, one launch (start us, length us, event | category | flops | bytes accessed | tf_op | source)
XLA Modules:
  0.0 497.3 jit_solution(17574147506039467977)
XLA Ops:
  7.2 0.0 copy-start
  7.2 0.0 all-gather.5.cloned.1.call-start
  7.2 0.7 all-gather.5.cloned.1.call-update
  7.9 0.0 all-reduce.4.cloned.1.call-start
  8.0 148.1 %all-gather.5.cloned.1.call-done = bf16[64,12,1024]{2,1,0:T(8,128)(2,1)} async-done(((bf16[1,12,1024]{2,1,0:T(8,128)(2,1)}), bf16[64,12,1024]{2,1,0:T(8,128)(2,1)}) %all-gather.5.cloned.1.call-update) | async-done | bytes 1572880 | tf_op jit(solution)/shard_map/all_gather | solution.py:19
  156.1 2.5 reshape.7
  158.6 0.0 copy-start.4
  158.6 1.5 fusion.14
  160.1 0.0 all-reduce.4.cloned.1.call-update
  160.2 0.0 all-gather.7.cloned.1.call-start
  160.2 0.7 all-gather.7.cloned.1.call-update
  160.9 13.0 %all_gather.10 = bf16[768,256]{1,0:T(8,128)(2,1)S(1)} all-gather(bf16[96,256]{1,0:T(8,128)(2,1)S(1)} %copy-done.4), channel_id=1, replica_groups=mesh['ia'=8,'ao'=8,'ta'=8] {'ia'}, dimensions={0}, use_global_device_ids=true | all-gather | bytes 442368 | tf_op jit(solution)/shard_map/all_gather | solution.py:25
  173.9 57.2 %all-reduce.4.cloned.1.call-done = f32[768,256]{1,0:T(8,128)} async-done(((f32[768,256]{1,0:T(8,128)}), f32[768,256]{1,0:T(8,128)}) %all-reduce.4.cloned.1.call-update) | async-done | bytes 786448 | tf_op jit(solution)/shard_map/psum | solution.py:24
  231.0 1.5 fusion.8
  232.5 2.2 fusion.15
  234.8 174.3 %fusion = f32[16,1024]{1,0:T(8,128)S(1)} fusion(f32[768,1024]{1,0:T(8,128)} %fusion.15), kind=kCustom, calls=%all-reduce-scatter | all-reduce-scatter fusion | flops 1048577 | bytes 3213312
  409.1 1.9 collective-permute-start.15
  411.0 0.6 convert.30
  411.7 1.3 collective-permute-start.1
  413.0 1.3 collective-permute-start.2
  414.3 1.7 collective-permute-start.3
  415.9 1.3 collective-permute-start.4
  417.2 1.8 collective-permute-start.5
  419.0 1.3 dynamic-slice.4
  421.0 1.3 collective-permute-start.6
  422.3 0.0 collective-permute-done.2
  422.3 12.0 %collective-permute-start.7 = (bf16[16,1024]{1,0:T(8,128)(2,1)}, bf16[16,1024]{1,0:T(8,128)(2,1)S(1)}, u32[]{:S(2)}, u32[]{:S(2)}) collective-permute-start(bf16[16,1024]{1,0:T(8,128)(2,1)} %convert.30), channel_id=1, source_target_pairs={{0,8},{1,9},{2,10},{3,11},{4,12},{5,13},{6,14},{7,15},{8,16},{9,17... | collective-permute-start | bytes 98312
  434.3 0.0 collective-permute-done.3
  434.3 19.8 %collective-permute-start.8 = (bf16[16,1024]{1,0:T(8,128)(2,1)}, bf16[16,1024]{1,0:T(8,128)(2,1)S(1)}, u32[]{:S(2)}, u32[]{:S(2)}) collective-permute-start(bf16[16,1024]{1,0:T(8,128)(2,1)} %convert.30), channel_id=1, source_target_pairs={{0,9},{1,10},{2,11},{3,12},{4,13},{5,14},{6,15},{7,16},{8,17},{9,1... | collective-permute-start | bytes 98312
  454.1 0.0 collective-permute-done.4
  454.1 5.3 %collective-permute-start.9 = (bf16[16,1024]{1,0:T(8,128)(2,1)}, bf16[16,1024]{1,0:T(8,128)(2,1)S(1)}, u32[]{:S(2)}, u32[]{:S(2)}) collective-permute-start(bf16[16,1024]{1,0:T(8,128)(2,1)} %convert.30), channel_id=1, source_target_pairs={{0,10},{1,11},{2,12},{3,13},{4,14},{5,15},{6,16},{7,17},{8,18},{9,... | collective-permute-start | bytes 98312
  459.5 6.4 %collective-permute-start.10 = (bf16[16,1024]{1,0:T(8,128)(2,1)}, bf16[16,1024]{1,0:T(8,128)(2,1)S(1)}, u32[]{:S(2)}, u32[]{:S(2)}) collective-permute-start(bf16[16,1024]{1,0:T(8,128)(2,1)} %convert.30), channel_id=1, source_target_pairs={{0,11},{1,12},{2,13},{3,14},{4,15},{5,16},{6,17},{7,18},{8,19},{9,... | collective-permute-start | bytes 98312
  465.8 1.6 fusion.10
  467.5 0.0 all-gather.7.cloned.1.call-done
  467.5 2.5 reshape.9
  470.0 0.0 collective-permute-done.6
  470.0 1.9 collective-permute-start.11
  471.9 1.9 collective-permute-start.12
  473.8 0.0 collective-permute-done.8
  473.8 1.9 collective-permute-start.13
  475.7 1.9 collective-permute-start.14
  477.7 0.6 copy-done.23
  478.3 3.1 collective-permute-start
  481.3 0.6 convolution_bitcast_fusion
  482.0 1.3 copy.10
  483.3 0.0 collective-permute-done.11
  483.5 6.6 %concatenate = bf16[268,1024]{1,0:T(8,128)(2,1)S(1)} concatenate(bf16[12,1024]{1,0:T(8,128)(2,1)} %collective-permute-done.15, bf16[16,1024]{1,0:T(8,128)(2,1)} %collective-permute-done.14, bf16[16,1024]{1,0:T(8,128)(2,1)} %collective-permute-done.13, bf16[16,1024]{1,0:T(8,128)(2,1)} %collective-permute-done.12, bf16[16,1024]{1,0:T(8,128)(2,1)} %collective-permute-done.11, ...), dimensions={0} | concatenate | bytes 1130496
  490.1 0.6 dynamic-slice_convert_fusion
  (58 shorter events, 0.1 us)
Async XLA Ops:
  7.2 225.4 %copy-start = (bf16[1024,256]{1,0:T(8,128)(2,1)S(1)}, bf16[1024,256]{1,0:T(8,128)(2,1)}, u32[]{:S(2)}) copy-start(bf16[1024,256]{1,0:T(8,128)(2,1)} %param.8) | copy-start | bytes 1572868
  7.2 148.9 %all-gather.5.cloned.1.call-start = ((), (), s32[]{:S(2)}) async-start(), calls=%async_computation.1 | async-start | bytes 2129920 | tf_op jit(solution)/shard_map/all_gather | solution.py:19
  7.9 150.7 %copy-start.3 = (bf16[256,1024]{1,0:T(8,128)(2,1)S(1)}, bf16[256,1024]{1,0:T(8,128)(2,1)}, u32[]{:S(2)}) copy-start(bf16[256,1024]{1,0:T(8,128)(2,1)} %param.9) | copy-start | bytes 1572868
  7.9 223.1 %all-reduce.4.cloned.1.call-start = ((), (), s32[]{:S(2)}) async-start(), calls=%async_computation | async-start | bytes 1572864 | tf_op jit(solution)/shard_map/psum | solution.py:24
  158.6 2.3 copy-start.4
  160.2 307.4 %all-gather.7.cloned.1.call-start = ((), (), s32[]{:S(2)}) async-start(), calls=%async_computation.2 | async-start | bytes 2129920 | tf_op jit(solution)/shard_map/all_gather | solution.py:18
  409.1 58.3 %copy-start.1 = (f32[16,1024]{1,0:T(8,128)}, f32[16,1024]{1,0:T(8,128)S(1)}, u32[]{:S(2)}) copy-start(f32[16,1024]{1,0:T(8,128)S(1)} %fusion) | copy-start | bytes 196612
  409.1 8.1 %collective-permute-start.15 = (bf16[12,1024]{1,0:T(8,128)(2,1)S(1)}, bf16[12,1024]{1,0:T(8,128)(2,1)}, u32[]{:S(2)}, u32[]{:S(2)}) collective-permute-start(bf16[12,1024]{1,0:T(8,128)(2,1)S(1)} %slice), channel_id=1, source_target_pairs={{0,16},{1,17},{2,18},{3,19},{4,20},{5,21},{6,22},{7,23},{8,24},{9,... | collective-permute-start | bytes 73736
  411.7 9.3 %collective-permute-start.1 = (bf16[16,1024]{1,0:T(8,128)(2,1)}, bf16[16,1024]{1,0:T(8,128)(2,1)S(1)}, u32[]{:S(2)}, u32[]{:S(2)}) collective-permute-start(bf16[16,1024]{1,0:T(8,128)(2,1)} %convert.30), channel_id=1, source_target_pairs={{0,2},{1,3},{2,4},{3,5},{4,6},{5,7},{6,8},{7,9},{8,10},{9,11},{10,... | collective-permute-start | bytes 98312
  413.0 9.3 %collective-permute-start.2 = (bf16[16,1024]{1,0:T(8,128)(2,1)}, bf16[16,1024]{1,0:T(8,128)(2,1)S(1)}, u32[]{:S(2)}, u32[]{:S(2)}) collective-permute-start(bf16[16,1024]{1,0:T(8,128)(2,1)} %convert.30), channel_id=1, source_target_pairs={{0,3},{1,4},{2,5},{3,6},{4,7},{5,8},{6,9},{7,10},{8,11},{9,12},{10... | collective-permute-start | bytes 98312
  414.3 20.0 %collective-permute-start.3 = (bf16[16,1024]{1,0:T(8,128)(2,1)}, bf16[16,1024]{1,0:T(8,128)(2,1)S(1)}, u32[]{:S(2)}, u32[]{:S(2)}) collective-permute-start(bf16[16,1024]{1,0:T(8,128)(2,1)} %convert.30), channel_id=1, source_target_pairs={{0,4},{1,5},{2,6},{3,7},{4,8},{5,9},{6,10},{7,11},{8,12},{9,13},{1... | collective-permute-start | bytes 98312
  415.9 38.2 %collective-permute-start.4 = (bf16[16,1024]{1,0:T(8,128)(2,1)}, bf16[16,1024]{1,0:T(8,128)(2,1)S(1)}, u32[]{:S(2)}, u32[]{:S(2)}) collective-permute-start(bf16[16,1024]{1,0:T(8,128)(2,1)} %convert.30), channel_id=1, source_target_pairs={{0,5},{1,6},{2,7},{3,8},{4,9},{5,10},{6,11},{7,12},{8,13},{9,14},{... | collective-permute-start | bytes 98312
  417.2 42.2 %collective-permute-start.5 = (bf16[16,1024]{1,0:T(8,128)(2,1)}, bf16[16,1024]{1,0:T(8,128)(2,1)S(1)}, u32[]{:S(2)}, u32[]{:S(2)}) collective-permute-start(bf16[16,1024]{1,0:T(8,128)(2,1)} %convert.30), channel_id=1, source_target_pairs={{0,6},{1,7},{2,8},{3,9},{4,10},{5,11},{6,12},{7,13},{8,14},{9,15},... | collective-permute-start | bytes 98312
  421.0 46.5 %copy-start.5 = (bf16[16,1024]{1,0:T(8,128)(2,1)}, bf16[16,1024]{1,0:T(8,128)(2,1)S(1)}, u32[]{:S(2)}) copy-start(bf16[16,1024]{1,0:T(8,128)(2,1)S(1)} %collective-permute-done.1) | copy-start | bytes 98308
  421.0 49.1 %collective-permute-start.6 = (bf16[16,1024]{1,0:T(8,128)(2,1)}, bf16[16,1024]{1,0:T(8,128)(2,1)S(1)}, u32[]{:S(2)}, u32[]{:S(2)}) collective-permute-start(bf16[16,1024]{1,0:T(8,128)(2,1)} %convert.30), channel_id=1, source_target_pairs={{0,7},{1,8},{2,9},{3,10},{4,11},{5,12},{6,13},{7,14},{8,15},{9,16}... | collective-permute-start | bytes 98312
  422.3 45.2 %copy-start.7 = (bf16[16,1024]{1,0:T(8,128)(2,1)}, bf16[16,1024]{1,0:T(8,128)(2,1)S(1)}, u32[]{:S(2)}) copy-start(bf16[16,1024]{1,0:T(8,128)(2,1)S(1)} %collective-permute-done.2) | copy-start | bytes 98308
  422.3 49.7 %collective-permute-start.7 = (bf16[16,1024]{1,0:T(8,128)(2,1)}, bf16[16,1024]{1,0:T(8,128)(2,1)S(1)}, u32[]{:S(2)}, u32[]{:S(2)}) collective-permute-start(bf16[16,1024]{1,0:T(8,128)(2,1)} %convert.30), channel_id=1, source_target_pairs={{0,8},{1,9},{2,10},{3,11},{4,12},{5,13},{6,14},{7,15},{8,16},{9,17... | collective-permute-start | bytes 98312
  434.3 33.2 %copy-start.9 = (bf16[16,1024]{1,0:T(8,128)(2,1)}, bf16[16,1024]{1,0:T(8,128)(2,1)S(1)}, u32[]{:S(2)}) copy-start(bf16[16,1024]{1,0:T(8,128)(2,1)S(1)} %collective-permute-done.3) | copy-start | bytes 98308
  434.3 39.5 %collective-permute-start.8 = (bf16[16,1024]{1,0:T(8,128)(2,1)}, bf16[16,1024]{1,0:T(8,128)(2,1)S(1)}, u32[]{:S(2)}, u32[]{:S(2)}) collective-permute-start(bf16[16,1024]{1,0:T(8,128)(2,1)} %convert.30), channel_id=1, source_target_pairs={{0,9},{1,10},{2,11},{3,12},{4,13},{5,14},{6,15},{7,16},{8,17},{9,1... | collective-permute-start | bytes 98312
  454.1 13.3 %copy-start.11 = (bf16[16,1024]{1,0:T(8,128)(2,1)}, bf16[16,1024]{1,0:T(8,128)(2,1)S(1)}, u32[]{:S(2)}) copy-start(bf16[16,1024]{1,0:T(8,128)(2,1)S(1)} %collective-permute-done.4) | copy-start | bytes 98308
  454.1 21.6 %collective-permute-start.9 = (bf16[16,1024]{1,0:T(8,128)(2,1)}, bf16[16,1024]{1,0:T(8,128)(2,1)S(1)}, u32[]{:S(2)}, u32[]{:S(2)}) collective-permute-start(bf16[16,1024]{1,0:T(8,128)(2,1)} %convert.30), channel_id=1, source_target_pairs={{0,10},{1,11},{2,12},{3,13},{4,14},{5,15},{6,16},{7,17},{8,18},{9,... | collective-permute-start | bytes 98312
  459.4 8.0 %copy-start.13 = (bf16[16,1024]{1,0:T(8,128)(2,1)}, bf16[16,1024]{1,0:T(8,128)(2,1)S(1)}, u32[]{:S(2)}) copy-start(bf16[16,1024]{1,0:T(8,128)(2,1)S(1)} %collective-permute-done.5) | copy-start | bytes 98308
  459.5 18.2 %collective-permute-start.10 = (bf16[16,1024]{1,0:T(8,128)(2,1)}, bf16[16,1024]{1,0:T(8,128)(2,1)S(1)}, u32[]{:S(2)}, u32[]{:S(2)}) collective-permute-start(bf16[16,1024]{1,0:T(8,128)(2,1)} %convert.30), channel_id=1, source_target_pairs={{0,11},{1,12},{2,13},{3,14},{4,15},{5,16},{6,17},{7,18},{8,19},{9,... | collective-permute-start | bytes 98312
  470.0 7.6 %copy-start.15 = (bf16[16,1024]{1,0:T(8,128)(2,1)}, bf16[16,1024]{1,0:T(8,128)(2,1)S(1)}, u32[]{:S(2)}) copy-start(bf16[16,1024]{1,0:T(8,128)(2,1)S(1)} %collective-permute-done.6) | copy-start | bytes 98308
  470.0 13.3 %collective-permute-start.11 = (bf16[16,1024]{1,0:T(8,128)(2,1)}, bf16[16,1024]{1,0:T(8,128)(2,1)}, u32[]{:S(2)}, u32[]{:S(2)}) collective-permute-start(bf16[16,1024]{1,0:T(8,128)(2,1)} %convert.30), channel_id=1, source_target_pairs={{0,12},{1,13},{2,14},{3,15},{4,16},{5,17},{6,18},{7,19},{8,20},{9,... | collective-permute-start | bytes 98312
  471.9 5.7 %copy-start.17 = (bf16[16,1024]{1,0:T(8,128)(2,1)}, bf16[16,1024]{1,0:T(8,128)(2,1)S(1)}, u32[]{:S(2)}) copy-start(bf16[16,1024]{1,0:T(8,128)(2,1)S(1)} %collective-permute-done.7) | copy-start | bytes 98308
  471.9 11.4 %collective-permute-start.12 = (bf16[16,1024]{1,0:T(8,128)(2,1)}, bf16[16,1024]{1,0:T(8,128)(2,1)}, u32[]{:S(2)}, u32[]{:S(2)}) collective-permute-start(bf16[16,1024]{1,0:T(8,128)(2,1)} %convert.30), channel_id=1, source_target_pairs={{0,13},{1,14},{2,15},{3,16},{4,17},{5,18},{6,19},{7,20},{8,21},{9,... | collective-permute-start | bytes 98312
  473.8 3.8 copy-start.19
  473.8 9.5 %collective-permute-start.13 = (bf16[16,1024]{1,0:T(8,128)(2,1)}, bf16[16,1024]{1,0:T(8,128)(2,1)}, u32[]{:S(2)}, u32[]{:S(2)}) collective-permute-start(bf16[16,1024]{1,0:T(8,128)(2,1)} %convert.30), channel_id=1, source_target_pairs={{0,14},{1,15},{2,16},{3,17},{4,18},{5,19},{6,20},{7,21},{8,22},{9,... | collective-permute-start | bytes 98312
  475.7 1.9 copy-start.21
  475.7 7.6 %collective-permute-start.14 = (bf16[16,1024]{1,0:T(8,128)(2,1)}, bf16[16,1024]{1,0:T(8,128)(2,1)}, u32[]{:S(2)}, u32[]{:S(2)}) collective-permute-start(bf16[16,1024]{1,0:T(8,128)(2,1)} %convert.30), channel_id=1, source_target_pairs={{0,15},{1,16},{2,17},{3,18},{4,19},{5,20},{6,21},{7,22},{8,23},{9,... | collective-permute-start | bytes 98312
  477.7 0.6 copy-start.23
  478.3 5.1 %collective-permute-start = (bf16[16,1024]{1,0:T(8,128)(2,1)}, bf16[16,1024]{1,0:T(8,128)(2,1)}, u32[]{:S(2)}, u32[]{:S(2)}) collective-permute-start(bf16[16,1024]{1,0:T(8,128)(2,1)} %convert.30), channel_id=1, source_target_pairs={{0,1},{1,2},{2,3},{3,4},{4,5},{5,6},{6,7},{7,8},{8,9},{9,10},{10,1... | collective-permute-start | bytes 98312
  481.9 1.5 copy-start.2
  481.9 1.5 copy-start.6
  481.9 1.5 copy-start.8
  482.0 1.5 copy-start.10
  482.0 1.5 copy-start.12
  482.0 1.5 copy-start.14
  482.0 1.5 copy-start.16
  482.0 1.5 copy-start.18
  482.0 1.5 copy-start.20
  482.0 1.5 copy-start.22
  482.0 1.5 copy-start.24
Sparse Core Ops, SparseCore 0:
  11.0 145.1 all-gather.4
  160.3 70.7 all-reduce.3
  234.4 143.4 all-gather.6
where the time goes:
time: 500 us; the launch traced here: 497 us
  waiting for transfers between devices  207 us (41%)
  blocking collectives  187 us (37%)
  starting transfers between devices  64.7 us (13%)
  local copies, waits for them, and re-layouts  15.5 us (3%)
  between operations  14.9 us (3%)
  matrix products  5.93 us (1%)
    unnamed x1, blocking collectives  174 us
    all_gather x1, waiting for transfers between devices, local(): lax.all_gather(out_grad, ('ao', 'ta'), axis=0, tiled=True)  148 us
    unnamed x16, starting transfers between devices  64.6 us
    psum x1, waiting for transfers between devices, local(): hidden_grad = lax.psum(partial_hidden, 'ia')  57.2 us
    unnamed x56, local copies, waits for them, and re-layouts  14.9 us
    all_gather x1, blocking collectives, local(): all_preact = lax.all_gather(preact, 'ia', axis=0, tiled=True)  13 us
  transfers between devices with their start and end apart: 19, of which 2 were waited for; matrix products, arithmetic and copies ran while one was open for 37% of the time, Pallas kernels for 0%

commit v1 on v0

v1 whole, which is shorter than its diff:
```python
import math

import jax
import jax.numpy as jnp
from jax import lax
from jax.sharding import Mesh, PartitionSpec as P

BF = jnp.bfloat16
F32 = jnp.float32


def gelu_parts(preact):
    value = preact.astype(F32)
    normal_cdf = 0.5 * (1.0 + jax.scipy.special.erf(value / math.sqrt(2.0)))
    density = jnp.exp(-0.5 * value * value) / math.sqrt(2.0 * math.pi)
    return (value * normal_cdf, normal_cdf + value * density)


def exchange(blocks, axis):
    return lax.all_to_all(blocks, axis, split_axis=0, concat_axis=0, tiled=False)


def spread(block, axis, n):
    return exchange(jnp.broadcast_to(block[None], (n,) + block.shape), axis)


def halves_down(block):
    lead, (rows, cols) = block.shape[:-2], block.shape[-2:]
    split = block.reshape(*lead, rows, 2, cols // 2)
    return jnp.swapaxes(split, -3, -2).reshape(*lead, rows * 2, cols // 2)


def halves_across(block):
    lead, (rows, cols) = block.shape[:-2], block.shape[-2:]
    split = block.reshape(*lead, 2, rows // 2, cols)
    return jnp.swapaxes(split, -3, -2).reshape(*lead, rows // 2, cols * 2)


def local(inputs, out_grad, preact, up_weight, down_weight):
    core = lax.axis_index("c")
    both = jnp.concatenate([halves_down(out_grad), halves_down(inputs)], axis=0)
    both = spread(both, "za", 4)
    rows = 24
    grads = halves_across(both[:, :rows]).reshape(48, 1024)
    ins = halves_across(both[:, rows:]).reshape(48, 1024)
    all_inputs = lax.all_gather(ins, ("x", "zb"), axis=0, tiled=True)
    grads = spread(grads, "zb", 4).reshape(192, 1024)
    all_grads = spread(grads, "x", 4).reshape(768, 1024)

    partial = jnp.einsum("td,fd->tf", all_grads, down_weight, preferred_element_type=F32)
    partial = partial.reshape(4, 4, 2, 24, 256)
    mine = lax.dynamic_index_in_dim(partial, core, axis=2, keepdims=False)
    theirs = lax.dynamic_index_in_dim(partial, 1 - core, axis=2, keepdims=False)
    pair = mine + lax.ppermute(theirs, "c", [(0, 1), (1, 0)])
    pair = exchange(pair.reshape(4, 96, 256), "y")
    hidden_grad = pair.sum(0)

    rows_first = preact.reshape(2, 4, 12, 256).transpose(1, 0, 2, 3).reshape(96, 256)
    activ, slope = gelu_parts(rows_first)
    own = jnp.stack([(hidden_grad * slope).astype(BF), activ.astype(BF)])
    own = spread(own, "y", 4)
    own = lax.all_gather(own, "c", axis=0, tiled=False)
    own = own.reshape(2, 4, 2, 4, 24, 256).transpose(2, 1, 3, 0, 4, 5).reshape(2, 768, 256)
    all_pregrad, all_activ = own[0], own[1]

    part = jnp.einsum("tf,df->td", all_pregrad, up_weight, preferred_element_type=F32)
    part = exchange(part.astype(BF).reshape(4, 192, 1024), "x")
    part = part.astype(F32).sum(0)
    part = exchange(part.astype(BF).reshape(4, 48, 1024), "zb")
    part = part.astype(F32).sum(0)
    part = exchange(halves_down(part.astype(BF).reshape(4, 12, 1024)), "za")
    input_grad = halves_across(part.astype(F32).sum(0)).astype(BF)

    down_grad = jnp.einsum("tf,td->fd", all_activ, all_grads, preferred_element_type=F32)
    up_grad = jnp.einsum("td,tf->df", all_inputs, all_pregrad, preferred_element_type=F32)
    return (input_grad, up_grad, down_grad)


def solution(mesh):
    fine = Mesh(mesh.devices.reshape(4, 2, 4, 4, 4), ("y", "c", "x", "za", "zb"))
    tokens, width = ("x", "za", "zb"), ("y", "c")
    return jax.shard_map(
        local,
        mesh=fine,
        in_specs=(
            P(tokens, width),
            P(tokens, width),
            P(width, tokens),
            P(width, tokens),
            P(tokens, width),
        ),
        out_specs=(P(tokens, width), P(width, tokens), P(tokens, width)),
        check_vma=False,
    )
```

time: 500 us -> 203 us (0.41)
  waiting for transfers between devices: 207 us -> 69.3 us
  blocking collectives: 187 us -> 78.9 us
  starting transfers between devices: 64.7 us -> 23.3 us
  local copies, waits for them, and re-layouts: 15.5 us -> 7.21 us
    unnamed x1 -> x0, blocking collectives: 174 us -> none
    all_gather x2 -> x1, waiting for transfers between devices: 148 us -> 24.6 us  [local(): all_inputs = lax.all_gather(ins, ('x', 'zb'), axis=0, tiled=True)]
    all_to_all x0 -> x3, blocking collectives: none -> 76.5 us  [exchange(): lax.all_to_all(blocks, axis, split_axis=0, concat_axis=0, tiled=False)]
    unnamed x16 -> x0, starting transfers between devices: 64.6 us -> none
    psum x1 -> x0, waiting for transfers between devices: 57.2 us -> none  [local(): hidden_grad = lax.psum(partial_hidden, 'ia')]
    all_to_all x0 -> x5, waiting for transfers between devices: none -> 42.7 us  [exchange(): lax.all_to_all(blocks, axis, split_axis=0, concat_axis=0, tiled=False)]
    all_to_all x0 -> x5, starting transfers between devices: none -> 21.4 us  [exchange(): lax.all_to_all(blocks, axis, split_axis=0, concat_axis=0, tiled=False)]
    unnamed x56 -> x10, local copies, waits for them, and re-layouts: 14.9 us -> 1.33 us
  transfers between devices with their start and end apart: 19 -> 7, of which waited for: 2 -> 6; matrix products, arithmetic and copies ran while one was open for 37% -> 5% of each run, Pallas kernels for 0% -> 0%
where the time goes in v1:
time: 203 us; the launch traced here: 202 us
  blocking collectives  78.9 us (39%)
  waiting for transfers between devices  69.3 us (34%)
  starting transfers between devices  23.3 us (11%)
  between operations  14.3 us (7%)
  local copies, waits for them, and re-layouts  7.21 us (4%)
  matrix products  5.81 us (3%)
  other arithmetic  3.53 us (2%)
    all_to_all x3, blocking collectives, exchange(): lax.all_to_all(blocks, axis, split_axis=0, concat_axis=0, tiled=False)  76.5 us
    all_to_all x5, waiting for transfers between devices, exchange(): lax.all_to_all(blocks, axis, split_axis=0, concat_axis=0, tiled=False)  42.7 us
    all_gather x1, waiting for transfers between devices, local(): all_inputs = lax.all_gather(ins, ('x', 'zb'), axis=0, tiled=True)  24.6 us
    all_to_all x5, starting transfers between devices, exchange(): lax.all_to_all(blocks, axis, split_axis=0, concat_axis=0, tiled=False)  21.4 us
  transfers between devices with their start and end apart: 7, of which 6 were waited for; matrix products, arithmetic and copies ran while one was open for 5% of the time, Pallas kernels for 0%

profile of v1, /device:TPU:24, one launch (start us, length us, event | category | flops | bytes accessed | tf_op | source)
XLA Modules:
  0.0 202.3 jit_solution(13033103724474525335)
XLA Ops:
  7.2 0.0 copy-start
  7.2 0.8 reshape.126
  8.0 0.8 reshape.124
  8.9 31.8 %all_to_all.40 = bf16[4,48,512]{2,1,0:T(8,128)(2,1)S(1)} all-to-all(bf16[4,48,512]{2,1,0:T(8,128)(2,1)S(1)} %broadcast_in_dim.12), channel_id=1, replica_groups=mesh['y'=4,'c'=2,'x'=4,'za'=4,'zb'=4] {'za'}, dimensions={0} | all-to-all | bytes 393216 | tf_op jit(solution)/shard_map/all_to_all | solution.py:20
  40.8 0.1 copy.35
  40.8 0.1 copy.36
  41.0 14.3 %all_to_all.41 = bf16[4,48,1024]{2,1,0:T(8,128)(2,1)S(1)} all-to-all(bf16[4,48,1024]{2,1,0:T(8,128)(2,1)S(1)} %broadcast_in_dim.28), channel_id=1, replica_groups=mesh['y'=4,'c'=2,'x'=4,'za'=4,'zb'=4] {'zb'}, dimensions={0} | all-to-all | bytes 786432 | tf_op jit(solution)/shard_map/all_to_all | solution.py:20
  55.3 1.3 broadcast_in_dim.30
  56.6 0.0 copy-start.1
  56.6 4.4 %all-to-all-start.2 = ((bf16[4,192,1024]{2,1,0:T(8,128)(2,1)}), bf16[4,192,1024]{2,1,0:T(8,128)(2,1)S(1)}, u32[]{:S(2)}, u32[]{:S(2)}) async-start(bf16[4,192,1024]{2,1,0:T(8,128)(2,1)} %broadcast_in_dim.30), calls=%async_computation.2 | async-start | bytes 3145728 | tf_op jit(solution)/shard_map/all_to_all | solution.py:20
  61.1 18.2 %all-to-all-done.2 = bf16[4,192,1024]{2,1,0:T(8,128)(2,1)S(1)} async-done(((bf16[4,192,1024]{2,1,0:T(8,128)(2,1)}), bf16[4,192,1024]{2,1,0:T(8,128)(2,1)S(1)}, u32[]{:S(2)}, u32[]{:S(2)}) %all-to-all-start.2) | async-done | bytes 1572896 | tf_op jit(solution)/shard_map/all_to_all | solution.py:20
  79.3 0.0 copy-done.1
  79.3 0.6 fusion
  79.9 0.0 copy-start.2
  79.9 0.8 dynamic-slice_bitcast_fusion
  80.7 1.9 collective-permute-start
  82.7 1.9 collective-permute-done
  84.6 0.8 bitcast_add_fusion
  85.3 4.7 %all-to-all-start.3 = ((f32[4,96,256]{2,1,0:T(8,128)}), f32[4,96,256]{2,1,0:T(8,128)S(1)}, u32[]{:S(2)}, u32[]{:S(2)}) async-start(f32[4,96,256]{2,1,0:T(8,128)} %bitcast.10), calls=%async_computation.3 | async-start | bytes 786432 | tf_op jit(solution)/shard_map/all_to_all | solution.py:20
  90.0 0.0 copy-done.2
  90.1 6.3 %all-to-all-done.3 = f32[4,96,256]{2,1,0:T(8,128)S(1)} async-done(((f32[4,96,256]{2,1,0:T(8,128)}), f32[4,96,256]{2,1,0:T(8,128)S(1)}, u32[]{:S(2)}, u32[]{:S(2)}) %all-to-all-start.3) | async-done | bytes 393248 | tf_op jit(solution)/shard_map/all_to_all | solution.py:20
  96.4 0.1 fusion.7
  96.5 0.8 broadcast_in_dim.31
  97.2 5.5 %all-to-all-start.4 = ((bf16[4,2,96,256]{3,2,1,0:T(8,128)(2,1)}), bf16[4,2,96,256]{3,2,1,0:T(8,128)(2,1)S(1)}, u32[]{:S(2)}, u32[]{:S(2)}) async-start(bf16[4,2,96,256]{3,2,1,0:T(8,128)(2,1)} %broadcast_in_dim.31), calls=%async_computation.4 | async-start | bytes 786432 | tf_op jit(solution)/shard_map/all_to_all | solution.py:20
  102.7 0.0 all-gather.3.cloned.1.call-start
  102.7 0.1 copy.42
  102.8 0.1 copy.43
  102.9 0.6 copy.48
  103.6 0.0 all-gather.3.cloned.1.call-update
  103.6 4.5 %all-to-all-done.4 = bf16[4,2,96,256]{3,2,1,0:T(8,128)(2,1)S(1)} async-done(((bf16[4,2,96,256]{3,2,1,0:T(8,128)(2,1)}), bf16[4,2,96,256]{3,2,1,0:T(8,128)(2,1)S(1)}, u32[]{:S(2)}, u32[]{:S(2)}) %all-to-all-start.4) | async-done | bytes 393248 | tf_op jit(solution)/shard_map/all_to_all | solution.py:20
  108.1 2.4 %all-gather = bf16[8,2,96,256]{3,2,1,0:T(8,128)(2,1)S(1)} all-gather(bf16[4,2,96,256]{3,2,1,0:T(8,128)(2,1)S(1)} %all-to-all-done.4), channel_id=2, replica_groups=mesh['y'=4,'c'=2,'x'=4,'za'=4,'zb'=4] {'c'}, dimensions={0}, use_global_device_ids=true | all-gather | bytes 1179648 | tf_op jit(solution)/shard_map/all_gather | solution.py:62
  110.4 0.1 fusion.8
  110.5 0.0 copy-done
  110.5 0.6 convolution_convert_fusion
  111.1 30.4 %all_to_all.42 = bf16[4,192,1024]{2,1,0:T(8,128)(2,1)} all-to-all(bf16[4,192,1024]{2,1,0:T(8,128)(2,1)S(1)} %bitcast.56), channel_id=1, replica_groups=mesh['y'=4,'c'=2,'x'=4,'za'=4,'zb'=4] {'x'}, dimensions={0} | all-to-all | bytes 3145728 | tf_op jit(solution)/shard_map/all_to_all | solution.py:20
  141.5 2.6 %reduce_sum.49 = bf16[192,1024]{1,0:T(8,128)(2,1)} reduce(bf16[4,192,1024]{2,1,0:T(8,128)(2,1)} %all_to_all.42, bf16[]{:T(256)} %constant.35.clone.1), dimensions={0}, to_apply=%region_1.2 | reduce | flops 589824 | bytes 1966082 | tf_op jit(solution)/shard_map/reduce_sum | solution.py:68
  144.1 3.5 %all-to-all-start.6 = ((bf16[4,48,1024]{2,1,0:T(8,128)(2,1)}), bf16[4,48,1024]{2,1,0:T(8,128)(2,1)S(1)}, u32[]{:S(2)}, u32[]{:S(2)}) async-start(bf16[4,48,1024]{2,1,0:T(8,128)(2,1)} %bitcast.60), calls=%async_computation.6 | async-start | bytes 786432 | tf_op jit(solution)/shard_map/all_to_all | solution.py:20
  147.6 1.6 fusion.11
  149.2 13.8 %all-to-all-done.6 = bf16[4,48,1024]{2,1,0:T(8,128)(2,1)S(1)} async-done(((bf16[4,48,1024]{2,1,0:T(8,128)(2,1)}), bf16[4,48,1024]{2,1,0:T(8,128)(2,1)S(1)}, u32[]{:S(2)}, u32[]{:S(2)}) %all-to-all-start.6) | async-done | bytes 393248 | tf_op jit(solution)/shard_map/all_to_all | solution.py:20
  162.9 0.1 reduce_sum.50
  163.1 0.1 copy.39
  163.1 0.7 copy.40
  163.8 3.4 %all-to-all-start.7 = ((bf16[4,24,512]{2,1,0:T(8,128)(2,1)}), bf16[4,24,512]{2,1,0:T(8,128)(2,1)S(1)}, u32[]{:S(2)}, u32[]{:S(2)}) async-start(bf16[4,24,512]{2,1,0:T(8,128)(2,1)} %copy.40), calls=%async_computation.7 | async-start | bytes 196608 | tf_op jit(solution)/shard_map/all_to_all | solution.py:20
  167.1 24.6 %all-gather.3.cloned.1.call-done = bf16[768,1024]{1,0:T(8,128)(2,1)} async-done(((bf16[48,1024]{1,0:T(8,128)(2,1)}), bf16[768,1024]{1,0:T(8,128)(2,1)}) %all-gather.3.cloned.1.call-update) | async-done | bytes 1572880 | tf_op jit(solution)/shard_map/all_gather | solution.py:46
  191.8 3.0 %fusion.10 = f32[1024,256]{1,0:T(8,128)} fusion(bf16[768,1024]{1,0:T(8,128)(2,1)} %all-gather.3.cloned.1.call-done, bf16[768,256]{1,0:T(8,128)(2,1)S(1)} %bitcast.59), kind=kOutput, calls=%fused_computation.20 | convolution fusion | flops 402653184 | bytes 3014656 | tf_op jit(solution)/shard_map/td,tf->df/dot_general | solution.py:75
  194.7 0.0 all-to-all-done.7
  194.9 0.6 copy.47
  (21 shorter events, 0.4 us)
Async XLA Ops:
  7.2 103.3 %copy-start = (bf16[1024,256]{1,0:T(8,128)(2,1)S(1)}, bf16[1024,256]{1,0:T(8,128)(2,1)}, u32[]{:S(2)}) copy-start(bf16[1024,256]{1,0:T(8,128)(2,1)} %param.8) | copy-start | bytes 1572868
  56.6 22.7 %copy-start.1 = (bf16[256,1024]{1,0:T(8,128)(2,1)S(1)}, bf16[256,1024]{1,0:T(8,128)(2,1)}, u32[]{:S(2)}) copy-start(bf16[256,1024]{1,0:T(8,128)(2,1)} %param.9) | copy-start | bytes 1572868
  56.6 22.6 %all-to-all-start.2 = ((bf16[4,192,1024]{2,1,0:T(8,128)(2,1)}), bf16[4,192,1024]{2,1,0:T(8,128)(2,1)S(1)}, u32[]{:S(2)}, u32[]{:S(2)}) async-start(bf16[4,192,1024]{2,1,0:T(8,128)(2,1)} %broadcast_in_dim.30), calls=%async_computation.2 | async-start | bytes 3145728 | tf_op jit(solution)/shard_map/all_to_all | solution.py:20
  79.9 10.1 %copy-start.2 = (bf16[96,256]{1,0:T(8,128)(2,1)S(1)}, bf16[96,256]{1,0:T(8,128)(2,1)}, u32[]{:S(2)}) copy-start(bf16[96,256]{1,0:T(8,128)(2,1)} %param.7) | copy-start | bytes 147460
  80.7 3.8 %collective-permute-start = (f32[4,4,24,256]{3,2,1,0:T(8,128)}, f32[4,4,24,256]{3,2,1,0:T(8,128)S(1)}, u32[]{:S(2)}, u32[]{:S(2)}) collective-permute-start(f32[4,4,24,256]{3,2,1,0:T(8,128)} %dynamic-slice_bitcast_fusion), channel_id=1, source_target_pairs={{0,64},{64,0},{1,65},{65,1},{2,66},{66,2},{3,67},{67,3},{4,68},{68... | collective-permute-start | bytes 1179656 | tf_op jit(solution)/shard_map/ppermute | solution.py:54
  85.3 11.0 %all-to-all-start.3 = ((f32[4,96,256]{2,1,0:T(8,128)}), f32[4,96,256]{2,1,0:T(8,128)S(1)}, u32[]{:S(2)}, u32[]{:S(2)}) async-start(f32[4,96,256]{2,1,0:T(8,128)} %bitcast.10), calls=%async_computation.3 | async-start | bytes 786432 | tf_op jit(solution)/shard_map/all_to_all | solution.py:20
  97.2 10.8 %all-to-all-start.4 = ((bf16[4,2,96,256]{3,2,1,0:T(8,128)(2,1)}), bf16[4,2,96,256]{3,2,1,0:T(8,128)(2,1)S(1)}, u32[]{:S(2)}, u32[]{:S(2)}) async-start(bf16[4,2,96,256]{3,2,1,0:T(8,128)(2,1)} %broadcast_in_dim.31), calls=%async_computation.4 | async-start | bytes 786432 | tf_op jit(solution)/shard_map/all_to_all | solution.py:20
  102.7 89.0 %all-gather.3.cloned.1.call-start = ((), (), s32[]{:S(2)}) async-start(), calls=%async_computation.8 | async-start | bytes 1671168 | tf_op jit(solution)/shard_map/all_gather | solution.py:46
  144.1 18.8 %all-to-all-start.6 = ((bf16[4,48,1024]{2,1,0:T(8,128)(2,1)}), bf16[4,48,1024]{2,1,0:T(8,128)(2,1)S(1)}, u32[]{:S(2)}, u32[]{:S(2)}) async-start(bf16[4,48,1024]{2,1,0:T(8,128)(2,1)} %bitcast.60), calls=%async_computation.6 | async-start | bytes 786432 | tf_op jit(solution)/shard_map/all_to_all | solution.py:20
  163.8 31.0 %all-to-all-start.7 = ((bf16[4,24,512]{2,1,0:T(8,128)(2,1)}), bf16[4,24,512]{2,1,0:T(8,128)(2,1)S(1)}, u32[]{:S(2)}, u32[]{:S(2)}) async-start(bf16[4,24,512]{2,1,0:T(8,128)(2,1)} %copy.40), calls=%async_computation.7 | async-start | bytes 196608 | tf_op jit(solution)/shard_map/all_to_all | solution.py:20
Sparse Core Ops, SparseCore 0:
  105.6 86.0 all-gather.2

commit v2 on v1

v2 whole, which is shorter than its diff:
```python
import math

import jax
import jax.numpy as jnp
from jax import lax
from jax.sharding import Mesh, PartitionSpec as P

BF = jnp.bfloat16
F32 = jnp.float32


def gelu_parts(preact):
    value = preact.astype(F32)
    normal_cdf = 0.5 * (1.0 + jax.scipy.special.erf(value / math.sqrt(2.0)))
    density = jnp.exp(-0.5 * value * value) / math.sqrt(2.0 * math.pi)
    return (value * normal_cdf, normal_cdf + value * density)


def exchange(blocks, axis):
    return lax.all_to_all(blocks, axis, split_axis=0, concat_axis=0, tiled=False)


def spread(block, axis, n=4):
    return exchange(jnp.broadcast_to(block[None], (n,) + block.shape), axis)


def halves_down(block):
    lead, (rows, cols) = block.shape[:-2], block.shape[-2:]
    split = block.reshape(*lead, rows, 2, cols // 2)
    return jnp.swapaxes(split, -3, -2).reshape(*lead, rows * 2, cols // 2)


def halves_across(block):
    lead, (rows, cols) = block.shape[:-2], block.shape[-2:]
    split = block.reshape(*lead, 2, rows // 2, cols)
    return jnp.swapaxes(split, -3, -2).reshape(*lead, rows // 2, cols * 2)


def gather_x(block):
    half = block.shape[0] // 2
    before = lax.ppermute(block, "x", shift(1))
    after = lax.ppermute(block, "x", shift(-1))
    far = jnp.concatenate(
        [lax.ppermute(before[:half], "x", shift(1)), lax.ppermute(after[half:], "x", shift(-1))]
    )
    return jnp.stack([block, after, far, before])


def shift(k):
    return [(i, (i + k) % 4) for i in range(4)]


def turn_by(blocks, start):
    twice = jnp.concatenate([blocks, blocks[:3]])
    return lax.dynamic_slice_in_dim(twice, start, 4, axis=0)


def local(inputs, out_grad, preact, up_weight, down_weight):
    core, at_x = lax.axis_index("c"), lax.axis_index("x")
    wide_down = lax.all_gather(down_weight, "x", axis=0, tiled=True).reshape(4, 256, 1024)
    both = jnp.concatenate([halves_down(out_grad), halves_down(inputs)], axis=0)
    both = spread(both, "za")
    both = halves_across(both.reshape(4, 2, 24, 512)).swapaxes(0, 1).reshape(96, 1024)
    both = spread(both, "zb").reshape(4, 2, 48, 1024).swapaxes(0, 1).reshape(2, 192, 1024)
    grads = both[0]

    rows_first = preact.reshape(2, 4, 12, 256).transpose(1, 0, 2, 3).reshape(96, 256)
    swap = [(4 * a + b, 4 * b + a) for a in range(4) for b in range(4)]
    turned = lax.ppermute(rows_first, ("y", "x"), swap)

    partial = jnp.einsum("td,xfd->xtf", grads, wide_down, preferred_element_type=F32)
    partial = partial.reshape(4, 4, 2, 24, 256)
    mine = lax.dynamic_index_in_dim(partial, core, axis=2, keepdims=False)
    theirs = lax.dynamic_index_in_dim(partial, 1 - core, axis=2, keepdims=False)
    pair = mine + lax.ppermute(theirs, "c", [(0, 1), (1, 0)])
    hidden_grad = exchange(pair.reshape(4, 96, 256), "y").sum(0)

    _, slope = gelu_parts(turned)
    activ, _ = gelu_parts(rows_first)
    own = spread(jnp.stack([(hidden_grad * slope).astype(BF), activ.astype(BF)]), "y")
    own = lax.all_gather(own, "c", axis=0, tiled=False).reshape(2, 4, 2, 4, 24, 256)
    own = own.transpose(2, 1, 3, 0, 4, 5).reshape(2, 4, 192, 256)
    pregrad, all_activ = turn_by(own[0], at_x), own[1]

    wide_up = gather_x(up_weight)
    part = jnp.einsum("xtf,xdf->td", pregrad, wide_up, preferred_element_type=F32)
    part = exchange(part.astype(BF).reshape(4, 48, 1024), "zb")
    part = part.astype(F32).sum(0)
    part = exchange(halves_down(part.astype(BF).reshape(4, 12, 1024)), "za")
    input_grad = halves_across(part.astype(F32).sum(0)).astype(BF)

    sent = [pregrad[0]] + [lax.ppermute(pregrad[k], "x", shift(k)) for k in (3, 2, 1)]
    all_pregrad = turn_by(jnp.stack(sent), (4 - at_x) % 4).reshape(768, 256)
    all_both = lax.all_gather(both.reshape(384, 1024), "x", axis=0, tiled=False)
    all_both = all_both.reshape(4, 2, 192, 1024)
    down_grad = jnp.einsum("xtf,xtd->fd", all_activ, all_both[:, 0], preferred_element_type=F32)
    up_grad = jnp.einsum(
        "xtd,xtf->df", all_both[:, 1], all_pregrad.reshape(4, 192, 256), preferred_element_type=F32
    )
    return (input_grad, up_grad, down_grad)


def solution(mesh):
    fine = Mesh(mesh.devices.reshape(4, 2, 4, 4, 4), ("y", "c", "x", "za", "zb"))
    tokens, width = ("x", "za", "zb"), ("y", "c")
    return jax.shard_map(
        local,
        mesh=fine,
        in_specs=(
            P(tokens, width),
            P(tokens, width),
            P(width, tokens),
            P(width, tokens),
            P(tokens, width),
        ),
        out_specs=(P(tokens, width), P(width, tokens), P(tokens, width)),
        check_vma=False,
    )
```

time: 203 us -> 178 us (0.88)
  blocking collectives: 78.9 us -> 34.2 us
  starting transfers between devices: 23.3 us -> 50.7 us
  waiting for transfers between devices: 69.3 us -> 59.8 us
  matrix products: 5.81 us -> 8.78 us
  other arithmetic: 3.53 us -> 1.2 us
    all_to_all x3 -> x1, blocking collectives: 76.5 us -> 31.8 us  [exchange(): lax.all_to_all(blocks, axis, split_axis=0, concat_axis=0, tiled=False)]
    ppermute x0 -> x8, starting transfers between devices: none -> 27.8 us  [the longest x3 9.82 us: local(): lax.ppermute(pregrad[k], 'x', shift(k))]
    all_gather x1 -> x2, waiting for transfers between devices: 24.6 us -> 0.02 us  [the longest x1 0.02 us: local(): lax.all_gather(down_weight, 'x', axis=0, tiled=True).reshape(4, 256, 1024)]
    ppermute x0 -> x8, waiting for transfers between devices: none -> 24.1 us  [the longest x1 14.6 us: gather_x(): after = lax.ppermute(block, 'x', shift(-1))]
    all_to_all x5, waiting for transfers between devices: 42.7 us -> 34.9 us  [exchange(): lax.all_to_all(blocks, axis, split_axis=0, concat_axis=0, tiled=False)]
    dot_general x4, matrix products: 5.81 us -> 8.78 us  [the longest x1 3.13 us: local(): jnp.einsum('xtf,xtd->fd', all_activ, all_both[:, 0], preferred_element_ty...]
    reduce_sum x2 -> x1, other arithmetic: 2.61 us -> 0.06 us  [local(): part = part.astype(F32).sum(0)]
  transfers between devices with their start and end apart: 7 -> 16, of which waited for: 6 -> 8; matrix products, arithmetic and copies ran while one was open for 5% -> 7% of each run, Pallas kernels for 0% -> 0%
where the time goes in v2:
time: 178 us; the launch traced here: 177 us
  waiting for transfers between devices  59.8 us (34%)
  starting transfers between devices  50.7 us (28%)
  blocking collectives  34.2 us (19%)
  between operations  14.6 us (8%)
  matrix products  8.78 us (5%)
  local copies, waits for them, and re-layouts  7.5 us (4%)
    all_to_all x5, waiting for transfers between devices, exchange(): lax.all_to_all(blocks, axis, split_axis=0, concat_axis=0, tiled=False)  34.9 us
    all_to_all x1, blocking collectives, exchange(): lax.all_to_all(blocks, axis, split_axis=0, concat_axis=0, tiled=False)  31.8 us
    all_to_all x5, starting transfers between devices, exchange(): lax.all_to_all(blocks, axis, split_axis=0, concat_axis=0, tiled=False)  20.9 us
    ppermute x1, waiting for transfers between devices, gather_x(): after = lax.ppermute(block, 'x', shift(-1))  14.6 us
    ppermute x3, starting transfers between devices, local(): lax.ppermute(pregrad[k], 'x', shift(k))  9.82 us
    ppermute x1, starting transfers between devices, gather_x(): lax.ppermute(after[half:], 'x', shift(-1))  5.92 us
    ppermute x3, waiting for transfers between devices, local(): lax.ppermute(pregrad[k], 'x', shift(k))  5.35 us
    ppermute x1, starting transfers between devices, gather_x(): after = lax.ppermute(block, 'x', shift(-1))  3.66 us
  transfers between devices with their start and end apart: 16, of which 8 were waited for; matrix products, arithmetic and copies ran while one was open for 7% of the time, Pallas kernels for 0%

profile of v2, /device:TPU:24, one launch (start us, length us, event | category | flops | bytes accessed | tf_op | source)
XLA Modules:
  0.0 176.7 jit_solution(6492934001374133888)
XLA Ops:
  7.2 0.0 all-gather.4.cloned.1.call-start
  7.2 0.7 all-gather.4.cloned.1.call-update
  7.9 0.8 reshape.99
  8.7 0.8 reshape.97
  9.6 31.8 %all_to_all.30 = bf16[4,48,512]{2,1,0:T(8,128)(2,1)S(1)} all-to-all(bf16[4,48,512]{2,1,0:T(8,128)(2,1)S(1)} %broadcast_in_dim.8), channel_id=1, replica_groups=mesh['y'=4,'c'=2,'x'=4,'za'=4,'zb'=4] {'za'}, dimensions={0} | all-to-all | bytes 393216 | tf_op jit(solution)/shard_map/all_to_all | solution.py:20
  41.4 0.2 copy.35
  41.6 0.2 copy.36
  41.8 0.1 reshape.101
  42.0 1.0 broadcast_in_dim.10
  43.0 4.6 %all-to-all-start.1 = ((bf16[4,96,1024]{2,1,0:T(8,128)(2,1)}), bf16[4,96,1024]{2,1,0:T(8,128)(2,1)S(1)}, u32[]{:S(2)}, u32[]{:S(2)}) async-start(bf16[4,96,1024]{2,1,0:T(8,128)(2,1)} %broadcast_in_dim.10), calls=%async_computation.1 | async-start | bytes 1572864 | tf_op jit(solution)/shard_map/all_to_all | solution.py:20
  47.6 18.3 %all-to-all-done.1 = bf16[4,96,1024]{2,1,0:T(8,128)(2,1)S(1)} async-done(((bf16[4,96,1024]{2,1,0:T(8,128)(2,1)}), bf16[4,96,1024]{2,1,0:T(8,128)(2,1)S(1)}, u32[]{:S(2)}, u32[]{:S(2)}) %all-to-all-start.1) | async-done | bytes 786464 | tf_op jit(solution)/shard_map/all_to_all | solution.py:20
  65.9 1.0 copy.45
  66.9 0.0 all-gather.4.cloned.1.call-done
  67.0 2.5 %fusion.32 = f32[192,4,256]{2,0,1:T(8,128)S(1)} fusion(bf16[192,1024,1]{1,0,2:T(8,128)(2,1)S(1)} %bitcast.99, bf16[4,256,1024]{2,1,0:T(8,128)(2,1)} %bitcast.98), kind=kOutput, calls=%fused_computation.55 | convolution fusion | flops 402653184 | bytes 3276800 | tf_op jit(solution)/shard_map/td,xfd->xtf/dot_general | solution.py:71
  69.5 1.9 %collective-permute-start = (f32[4,4,24,256]{3,2,1,0:T(8,128)S(1)}, f32[4,4,24,256]{3,2,1,0:T(8,128)S(1)}, u32[]{:S(2)}, u32[]{:S(2)}) collective-permute-start(f32[4,4,24,256]{3,2,1,0:T(8,128)S(1)} %dynamic-slice_bitcast_fusion), channel_id=1, source_target_pairs={{0,64},{64,0},{1,65},{65,1},{2,66},{66,2},{3,67},{67,3},{4,68},{68... | collective-permute-start | bytes 1179656 | tf_op jit(solution)/shard_map/ppermute | solution.py:75
  71.4 3.4 %collective-permute-start.3 = (bf16[1024,256]{1,0:T(8,128)(2,1)S(1)}, bf16[1024,256]{1,0:T(8,128)(2,1)S(1)}, u32[]{:S(2)}, u32[]{:S(2)}) collective-permute-start(bf16[1024,256]{1,0:T(8,128)(2,1)S(1)} %copy-done.2), channel_id=1, source_target_pairs={{0,16},{16,32},{32,48},{48,0},{1,17},{17,33},{33,49},{49,1},{2,18}... | collective-permute-start | bytes 1572872 | tf_op jit(solution)/shard_map/ppermute | solution.py:41
  74.8 3.7 %collective-permute-start.2 = (bf16[1024,256]{1,0:T(8,128)(2,1)S(1)}, bf16[1024,256]{1,0:T(8,128)(2,1)S(1)}, u32[]{:S(2)}, u32[]{:S(2)}) collective-permute-start(bf16[1024,256]{1,0:T(8,128)(2,1)S(1)} %copy-done.2), channel_id=1, source_target_pairs={{0,48},{16,0},{32,16},{48,32},{1,49},{17,1},{33,17},{49,33},{2,50}... | collective-permute-start | bytes 1572872 | tf_op jit(solution)/shard_map/ppermute | solution.py:42
  78.6 3.1 %collective-permute-start.1 = (bf16[96,256]{1,0:T(8,128)(2,1)S(1)}, bf16[96,256]{1,0:T(8,128)(2,1)S(1)}, u32[]{:S(2)}, u32[]{:S(2)}) collective-permute-start(bf16[96,256]{1,0:T(8,128)(2,1)S(1)} %reshape.107), channel_id=1, source_target_pairs={{0,0},{16,128},{32,256},{48,384},{128,16},{144,144},{160,272},{176... | collective-permute-start | bytes 147464 | tf_op jit(solution)/shard_map/ppermute | solution.py:69
  81.7 0.8 bitcast_add_fusion
  82.5 5.1 %all-to-all-start.2 = ((f32[4,96,256]{2,1,0:T(8,128)}), f32[4,96,256]{2,1,0:T(8,128)S(1)}, u32[]{:S(2)}, u32[]{:S(2)}) async-start(f32[4,96,256]{2,1,0:T(8,128)} %bitcast.15), calls=%async_computation.2 | async-start | bytes 786432 | tf_op jit(solution)/shard_map/all_to_all | solution.py:20
  87.7 14.6 %collective-permute-done.2 = bf16[1024,256]{1,0:T(8,128)(2,1)S(1)} collective-permute-done((bf16[1024,256]{1,0:T(8,128)(2,1)S(1)}, bf16[1024,256]{1,0:T(8,128)(2,1)S(1)}, u32[]{:S(2)}, u32[]{:S(2)}) %collective-permute-start.2) | collective-permute-done | bytes 524320 | tf_op jit(solution)/shard_map/ppermute | solution.py:42
  102.3 5.9 %collective-permute-start.5 = (bf16[512,256]{1,0:T(8,128)(2,1)S(1)}, bf16[512,256]{1,0:T(8,128)(2,1)S(1)}, u32[]{:S(2)}, u32[]{:S(2)}) collective-permute-start(bf16[512,256]{1,0:T(8,128)(2,1)S(1)} %slice.62), channel_id=1, source_target_pairs={{0,48},{16,0},{32,16},{48,32},{1,49},{17,1},{33,17},{49,33},{2,50}... | collective-permute-start | bytes 786440 | tf_op jit(solution)/shard_map/ppermute | solution.py:44
  108.2 1.9 %collective-permute-start.4 = (bf16[512,256]{1,0:T(8,128)(2,1)S(1)}, bf16[512,256]{1,0:T(8,128)(2,1)S(1)}, u32[]{:S(2)}, u32[]{:S(2)}) collective-permute-start(bf16[512,256]{1,0:T(8,128)(2,1)S(1)} %slice.61), channel_id=1, source_target_pairs={{0,16},{16,32},{32,48},{48,0},{1,17},{17,33},{33,49},{49,1},{2,18}... | collective-permute-start | bytes 786440 | tf_op jit(solution)/shard_map/ppermute | solution.py:44
  110.2 0.1 fusion.28
  110.3 0.8 broadcast_in_dim.22
  111.1 4.5 %all-to-all-start.3 = ((bf16[4,2,96,256]{3,2,1,0:T(8,128)(2,1)}), bf16[4,2,96,256]{3,2,1,0:T(8,128)(2,1)S(1)}, u32[]{:S(2)}, u32[]{:S(2)}) async-start(bf16[4,2,96,256]{3,2,1,0:T(8,128)(2,1)} %broadcast_in_dim.22), calls=%async_computation.3 | async-start | bytes 786432 | tf_op jit(solution)/shard_map/all_to_all | solution.py:20
  115.6 3.6 %collective-permute-done.5 = bf16[512,256]{1,0:T(8,128)(2,1)S(1)} collective-permute-done((bf16[512,256]{1,0:T(8,128)(2,1)S(1)}, bf16[512,256]{1,0:T(8,128)(2,1)S(1)}, u32[]{:S(2)}, u32[]{:S(2)}) %collective-permute-start.5) | collective-permute-done | bytes 262176 | tf_op jit(solution)/shard_map/ppermute | solution.py:44
  119.1 0.6 collective-permute-done.4
  119.8 1.1 all-to-all-done.3
  120.9 2.4 %all-gather = bf16[8,2,96,256]{3,2,1,0:T(8,128)(2,1)S(1)} all-gather(bf16[4,2,96,256]{3,2,1,0:T(8,128)(2,1)S(1)} %all-to-all-done.3), channel_id=2, replica_groups=mesh['y'=4,'c'=2,'x'=4,'za'=4,'zb'=4] {'c'}, dimensions={0}, use_global_device_ids=true | all-gather | bytes 1179648 | tf_op jit(solution)/shard_map/all_gather | solution.py:81
  123.3 0.1 fusion.31
  123.4 0.1 fusion.18
  123.6 0.8 copy-done.3
  124.3 1.6 fusion.15
  125.9 3.5 %all-to-all-start.4 = ((bf16[4,48,1024]{2,1,0:T(8,128)(2,1)}), bf16[4,48,1024]{2,1,0:T(8,128)(2,1)S(1)}, u32[]{:S(2)}, u32[]{:S(2)}) async-start(bf16[4,48,1024]{2,1,0:T(8,128)(2,1)} %bitcast.28), calls=%async_computation.4 | async-start | bytes 786432 | tf_op jit(solution)/shard_map/all_to_all | solution.py:20
  129.4 5.1 %collective-permute-start.6 = (bf16[192,256]{1,0:T(8,128)(2,1)S(1)}, bf16[192,256]{1,0:T(8,128)(2,1)S(1)}, u32[]{:S(2)}, u32[]{:S(2)}) collective-permute-start(bf16[192,256]{1,0:T(8,128)(2,1)S(1)} %get-tuple-element.8), channel_id=1, source_target_pairs={{0,48},{16,0},{32,16},{48,32},{1,49},{17,1},{33,17},{49,33},{2,50}... | collective-permute-start | bytes 294920 | tf_op jit(solution)/shard_map/ppermute | solution.py:92
  134.6 1.9 %collective-permute-start.7 = (bf16[192,256]{1,0:T(8,128)(2,1)S(1)}, bf16[192,256]{1,0:T(8,128)(2,1)S(1)}, u32[]{:S(2)}, u32[]{:S(2)}) collective-permute-start(bf16[192,256]{1,0:T(8,128)(2,1)S(1)} %get-tuple-element.7), channel_id=1, source_target_pairs={{0,32},{16,48},{32,0},{48,16},{1,33},{17,49},{33,1},{49,17},{2,34}... | collective-permute-start | bytes 294920 | tf_op jit(solution)/shard_map/ppermute | solution.py:92
  136.5 2.8 %collective-permute-start.8 = (bf16[192,256]{1,0:T(8,128)(2,1)S(1)}, bf16[192,256]{1,0:T(8,128)(2,1)S(1)}, u32[]{:S(2)}, u32[]{:S(2)}) collective-permute-start(bf16[192,256]{1,0:T(8,128)(2,1)S(1)} %get-tuple-element.5), channel_id=1, source_target_pairs={{0,16},{16,32},{32,48},{48,0},{1,17},{17,33},{33,49},{49,1},{2,18}... | collective-permute-start | bytes 294920 | tf_op jit(solution)/shard_map/ppermute | solution.py:92
  139.3 3.5 %collective-permute-done.7 = bf16[192,256]{1,0:T(8,128)(2,1)S(1)} collective-permute-done((bf16[192,256]{1,0:T(8,128)(2,1)S(1)}, bf16[192,256]{1,0:T(8,128)(2,1)S(1)}, u32[]{:S(2)}, u32[]{:S(2)}) %collective-permute-start.7) | collective-permute-done | bytes 98336 | tf_op jit(solution)/shard_map/ppermute | solution.py:92
  142.9 1.8 %collective-permute-done.8 = bf16[192,256]{1,0:T(8,128)(2,1)S(1)} collective-permute-done((bf16[192,256]{1,0:T(8,128)(2,1)S(1)}, bf16[192,256]{1,0:T(8,128)(2,1)S(1)}, u32[]{:S(2)}, u32[]{:S(2)}) %collective-permute-start.8) | collective-permute-done | bytes 98336 | tf_op jit(solution)/shard_map/ppermute | solution.py:92
  144.7 0.1 reduce_sum.34
  144.9 0.1 copy.42
  144.9 0.7 copy.43
  145.6 3.3 %all-to-all-start.5 = ((bf16[4,24,512]{2,1,0:T(8,128)(2,1)}), bf16[4,24,512]{2,1,0:T(8,128)(2,1)S(1)}, u32[]{:S(2)}, u32[]{:S(2)}) async-start(bf16[4,24,512]{2,1,0:T(8,128)(2,1)} %copy.43), calls=%async_computation.5 | async-start | bytes 196608 | tf_op jit(solution)/shard_map/all_to_all | solution.py:20
  148.9 15.5 %all-to-all-done.5 = bf16[4,24,512]{2,1,0:T(8,128)(2,1)S(1)} async-done(((bf16[4,24,512]{2,1,0:T(8,128)(2,1)}), bf16[4,24,512]{2,1,0:T(8,128)(2,1)S(1)}, u32[]{:S(2)}, u32[]{:S(2)}) %all-to-all-start.5) | async-done | bytes 98336 | tf_op jit(solution)/shard_map/all_to_all | solution.py:20
  164.5 0.6 copy.51
  165.2 3.1 %fusion.11 = f32[256,1024]{1,0:T(8,128)} fusion(bf16[4,192,256]{2,1,0:T(8,128)(2,1)S(1)} %bitcast.105, bf16[4,2,192,1024]{3,2,1,0:T(8,128)(2,1)} %bitcast.115), kind=kOutput, calls=%fused_computation.13 | convolution fusion | flops 402653184 | bytes 3014656 | tf_op jit(solution)/shard_map/xtf,xtd->fd/dot_general | solution.py:96
  168.3 1.6 fusion.10
  (54 shorter events, 0.8 us)
Async XLA Ops:
  7.2 59.8 %all-gather.4.cloned.1.call-start = ((), (), s32[]{:S(2)}) async-start(), calls=%async_computation.6 | async-start | bytes 2621440 | tf_op jit(solution)/shard_map/all_gather | solution.py:60
  43.0 22.9 %all-to-all-start.1 = ((bf16[4,96,1024]{2,1,0:T(8,128)(2,1)}), bf16[4,96,1024]{2,1,0:T(8,128)(2,1)S(1)}, u32[]{:S(2)}, u32[]{:S(2)}) async-start(bf16[4,96,1024]{2,1,0:T(8,128)(2,1)} %broadcast_in_dim.10), calls=%async_computation.1 | async-start | bytes 1572864 | tf_op jit(solution)/shard_map/all_to_all | solution.py:20
  47.6 117.6 %all-gather.6.cloned.1.call-start = ((), (), s32[]{:S(2)}) async-start(), calls=%async_computation.7 | async-start | bytes 3932160 | tf_op jit(solution)/shard_map/all_gather | solution.py:94
  66.9 4.5 %copy-start.2 = (bf16[1024,256]{1,0:T(8,128)(2,1)S(1)}, bf16[1024,256]{1,0:T(8,128)(2,1)}, u32[]{:S(2)}) copy-start(bf16[1024,256]{1,0:T(8,128)(2,1)} %param.8) | copy-start | bytes 1572868
  66.9 11.6 %copy-start = (bf16[96,256]{1,0:T(8,128)(2,1)S(1)}, bf16[96,256]{1,0:T(8,128)(2,1)}, u32[]{:S(2)}) copy-start(bf16[96,256]{1,0:T(8,128)(2,1)} %param.7) | copy-start | bytes 147460
  69.5 12.2 %collective-permute-start = (f32[4,4,24,256]{3,2,1,0:T(8,128)S(1)}, f32[4,4,24,256]{3,2,1,0:T(8,128)S(1)}, u32[]{:S(2)}, u32[]{:S(2)}) collective-permute-start(f32[4,4,24,256]{3,2,1,0:T(8,128)S(1)} %dynamic-slice_bitcast_fusion), channel_id=1, source_target_pairs={{0,64},{64,0},{1,65},{65,1},{2,66},{66,2},{3,67},{67,3},{4,68},{68... | collective-permute-start | bytes 1179656 | tf_op jit(solution)/shard_map/ppermute | solution.py:75
  71.4 36.8 %collective-permute-start.3 = (bf16[1024,256]{1,0:T(8,128)(2,1)S(1)}, bf16[1024,256]{1,0:T(8,128)(2,1)S(1)}, u32[]{:S(2)}, u32[]{:S(2)}) collective-permute-start(bf16[1024,256]{1,0:T(8,128)(2,1)S(1)} %copy-done.2), channel_id=1, source_target_pairs={{0,16},{16,32},{32,48},{48,0},{1,17},{17,33},{33,49},{49,1},{2,18}... | collective-permute-start | bytes 1572872 | tf_op jit(solution)/shard_map/ppermute | solution.py:41
  74.8 27.4 %collective-permute-start.2 = (bf16[1024,256]{1,0:T(8,128)(2,1)S(1)}, bf16[1024,256]{1,0:T(8,128)(2,1)S(1)}, u32[]{:S(2)}, u32[]{:S(2)}) collective-permute-start(bf16[1024,256]{1,0:T(8,128)(2,1)S(1)} %copy-done.2), channel_id=1, source_target_pairs={{0,48},{16,0},{32,16},{48,32},{1,49},{17,1},{33,17},{49,33},{2,50}... | collective-permute-start | bytes 1572872 | tf_op jit(solution)/shard_map/ppermute | solution.py:42
  78.6 31.6 %collective-permute-start.1 = (bf16[96,256]{1,0:T(8,128)(2,1)S(1)}, bf16[96,256]{1,0:T(8,128)(2,1)S(1)}, u32[]{:S(2)}, u32[]{:S(2)}) collective-permute-start(bf16[96,256]{1,0:T(8,128)(2,1)S(1)} %reshape.107), channel_id=1, source_target_pairs={{0,0},{16,128},{32,256},{48,384},{128,16},{144,144},{160,272},{176... | collective-permute-start | bytes 147464 | tf_op jit(solution)/shard_map/ppermute | solution.py:69
  82.5 27.7 %all-to-all-start.2 = ((f32[4,96,256]{2,1,0:T(8,128)}), f32[4,96,256]{2,1,0:T(8,128)S(1)}, u32[]{:S(2)}, u32[]{:S(2)}) async-start(f32[4,96,256]{2,1,0:T(8,128)} %bitcast.15), calls=%async_computation.2 | async-start | bytes 786432 | tf_op jit(solution)/shard_map/all_to_all | solution.py:20
  102.3 16.9 %collective-permute-start.5 = (bf16[512,256]{1,0:T(8,128)(2,1)S(1)}, bf16[512,256]{1,0:T(8,128)(2,1)S(1)}, u32[]{:S(2)}, u32[]{:S(2)}) collective-permute-start(bf16[512,256]{1,0:T(8,128)(2,1)S(1)} %slice.62), channel_id=1, source_target_pairs={{0,48},{16,0},{32,16},{48,32},{1,49},{17,1},{33,17},{49,33},{2,50}... | collective-permute-start | bytes 786440 | tf_op jit(solution)/shard_map/ppermute | solution.py:44
  108.2 11.5 %collective-permute-start.4 = (bf16[512,256]{1,0:T(8,128)(2,1)S(1)}, bf16[512,256]{1,0:T(8,128)(2,1)S(1)}, u32[]{:S(2)}, u32[]{:S(2)}) collective-permute-start(bf16[512,256]{1,0:T(8,128)(2,1)S(1)} %slice.61), channel_id=1, source_target_pairs={{0,16},{16,32},{32,48},{48,0},{1,17},{17,33},{33,49},{49,1},{2,18}... | collective-permute-start | bytes 786440 | tf_op jit(solution)/shard_map/ppermute | solution.py:44
  111.1 9.8 %all-to-all-start.3 = ((bf16[4,2,96,256]{3,2,1,0:T(8,128)(2,1)}), bf16[4,2,96,256]{3,2,1,0:T(8,128)(2,1)S(1)}, u32[]{:S(2)}, u32[]{:S(2)}) async-start(bf16[4,2,96,256]{3,2,1,0:T(8,128)(2,1)} %broadcast_in_dim.22), calls=%async_computation.3 | async-start | bytes 786432 | tf_op jit(solution)/shard_map/all_to_all | solution.py:20
  123.3 1.0 copy-start.3
  125.9 18.8 %all-to-all-start.4 = ((bf16[4,48,1024]{2,1,0:T(8,128)(2,1)}), bf16[4,48,1024]{2,1,0:T(8,128)(2,1)S(1)}, u32[]{:S(2)}, u32[]{:S(2)}) async-start(bf16[4,48,1024]{2,1,0:T(8,128)(2,1)} %bitcast.28), calls=%async_computation.4 | async-start | bytes 786432 | tf_op jit(solution)/shard_map/all_to_all | solution.py:20
  129.4 9.9 %collective-permute-start.6 = (bf16[192,256]{1,0:T(8,128)(2,1)S(1)}, bf16[192,256]{1,0:T(8,128)(2,1)S(1)}, u32[]{:S(2)}, u32[]{:S(2)}) collective-permute-start(bf16[192,256]{1,0:T(8,128)(2,1)S(1)} %get-tuple-element.8), channel_id=1, source_target_pairs={{0,48},{16,0},{32,16},{48,32},{1,49},{17,1},{33,17},{49,33},{2,50}... | collective-permute-start | bytes 294920 | tf_op jit(solution)/shard_map/ppermute | solution.py:92
  134.6 8.3 %collective-permute-start.7 = (bf16[192,256]{1,0:T(8,128)(2,1)S(1)}, bf16[192,256]{1,0:T(8,128)(2,1)S(1)}, u32[]{:S(2)}, u32[]{:S(2)}) collective-permute-start(bf16[192,256]{1,0:T(8,128)(2,1)S(1)} %get-tuple-element.7), channel_id=1, source_target_pairs={{0,32},{16,48},{32,0},{48,16},{1,33},{17,49},{33,1},{49,17},{2,34}... | collective-permute-start | bytes 294920 | tf_op jit(solution)/shard_map/ppermute | solution.py:92
  136.5 8.2 %collective-permute-start.8 = (bf16[192,256]{1,0:T(8,128)(2,1)S(1)}, bf16[192,256]{1,0:T(8,128)(2,1)S(1)}, u32[]{:S(2)}, u32[]{:S(2)}) collective-permute-start(bf16[192,256]{1,0:T(8,128)(2,1)S(1)} %get-tuple-element.5), channel_id=1, source_target_pairs={{0,16},{16,32},{32,48},{48,0},{1,17},{17,33},{33,49},{49,1},{2,18}... | collective-permute-start | bytes 294920 | tf_op jit(solution)/shard_map/ppermute | solution.py:92
  145.6 18.8 %all-to-all-start.5 = ((bf16[4,24,512]{2,1,0:T(8,128)(2,1)}), bf16[4,24,512]{2,1,0:T(8,128)(2,1)S(1)}, u32[]{:S(2)}, u32[]{:S(2)}) async-start(bf16[4,24,512]{2,1,0:T(8,128)(2,1)} %copy.43), calls=%async_computation.5 | async-start | bytes 196608 | tf_op jit(solution)/shard_map/all_to_all | solution.py:20
  165.2 3.1 %copy-start.1 = (bf16[4,384,1024]{2,1,0:T(8,128)(2,1)S(1)}, bf16[4,384,1024]{2,1,0:T(8,128)(2,1)}, u32[]{:S(2)}) copy-start(bf16[4,384,1024]{2,1,0:T(8,128)(2,1)} %all-gather.6.cloned.1.call-done) | copy-start | bytes 9437188
Sparse Core Ops, SparseCore 0:
  10.1 42.6 all-gather.3
  67.0 56.0 all-gather.5

commit v3 on v2

--- a/solution.py
+++ b/solution.py
@@ -36,14 +36,15 @@
     return jnp.swapaxes(split, -3, -2).reshape(*lead, rows // 2, cols * 2)
 
 
-def gather_x(block):
-    half = block.shape[0] // 2
-    before = lax.ppermute(block, "x", shift(1))
-    after = lax.ppermute(block, "x", shift(-1))
-    far = jnp.concatenate(
+def near_x(block):
+    return lax.ppermute(block, "x", shift(1)), lax.ppermute(block, "x", shift(-1))
+
+
+def far_x(before, after):
+    half = before.shape[0] // 2
+    return jnp.concatenate(
         [lax.ppermute(before[:half], "x", shift(1)), lax.ppermute(after[half:], "x", shift(-1))]
     )
-    return jnp.stack([block, after, far, before])
 
 
 def shift(k):
@@ -60,13 +61,16 @@
     wide_down = lax.all_gather(down_weight, "x", axis=0, tiled=True).reshape(4, 256, 1024)
     both = jnp.concatenate([halves_down(out_grad), halves_down(inputs)], axis=0)
     both = spread(both, "za")
-    both = halves_across(both.reshape(4, 2, 24, 512)).swapaxes(0, 1).reshape(96, 1024)
-    both = spread(both, "zb").reshape(4, 2, 48, 1024).swapaxes(0, 1).reshape(2, 192, 1024)
-    grads = both[0]
-
     rows_first = preact.reshape(2, 4, 12, 256).transpose(1, 0, 2, 3).reshape(96, 256)
     swap = [(4 * a + b, 4 * b + a) for a in range(4) for b in range(4)]
     turned = lax.ppermute(rows_first, ("y", "x"), swap)
+    before, after = near_x(up_weight)
+    both, turned, before, after = lax.optimization_barrier((both, turned, before, after))
+    both = halves_across(both.reshape(4, 2, 24, 512)).swapaxes(0, 1).reshape(2, 48, 1024)
+    grads = spread(both[0], "zb").reshape(192, 1024)
+    ins = spread(both[1], "zb").reshape(192, 1024)
+    wide_up = jnp.stack([up_weight, after, far_x(before, after), before])
+    grads, wide_up = lax.optimization_barrier((grads, wide_up))
 
     partial = jnp.einsum("td,xfd->xtf", grads, wide_down, preferred_element_type=F32)
     partial = partial.reshape(4, 4, 2, 24, 256)
@@ -82,16 +86,16 @@
     own = own.transpose(2, 1, 3, 0, 4, 5).reshape(2, 4, 192, 256)
     pregrad, all_activ = turn_by(own[0], at_x), own[1]
 
-    wide_up = gather_x(up_weight)
     part = jnp.einsum("xtf,xdf->td", pregrad, wide_up, preferred_element_type=F32)
     part = exchange(part.astype(BF).reshape(4, 48, 1024), "zb")
     part = part.astype(F32).sum(0)
+    part, pregrad = lax.optimization_barrier((part, pregrad))
     part = exchange(halves_down(part.astype(BF).reshape(4, 12, 1024)), "za")
     input_grad = halves_across(part.astype(F32).sum(0)).astype(BF)
 
     sent = [pregrad[0]] + [lax.ppermute(pregrad[k], "x", shift(k)) for k in (3, 2, 1)]
     all_pregrad = turn_by(jnp.stack(sent), (4 - at_x) % 4).reshape(768, 256)
-    all_both = lax.all_gather(both.reshape(384, 1024), "x", axis=0, tiled=False)
+    all_both = lax.all_gather(jnp.concatenate([grads, ins]), "x", axis=0, tiled=False)
     all_both = all_both.reshape(4, 2, 192, 1024)
     down_grad = jnp.einsum("xtf,xtd->fd", all_activ, all_both[:, 0], preferred_element_type=F32)
     up_grad = jnp.einsum(

time: 178 us -> 191 us (1.073); the launches traced: 177 us -> 187 us
  starting transfers between devices: 50.7 us -> 77.3 us
  blocking collectives: 34.2 us -> 19.2 us
  waiting for transfers between devices: 59.8 us -> 52.5 us
  other arithmetic: 1.2 us -> 5.56 us
  local copies, waits for them, and re-layouts: 7.5 us -> 10 us
    all_to_all x5 -> x6, starting transfers between devices: 20.9 us -> 47 us  [exchange(): lax.all_to_all(blocks, axis, split_axis=0, concat_axis=0, tiled=False)]
    ppermute x1, waiting for transfers between devices: 0.01 us -> 21.5 us  [local(): turned = lax.ppermute(rows_first, ('y', 'x'), swap)]
    all_to_all x1, blocking collectives: 31.8 us -> 16.9 us  [exchange(): lax.all_to_all(blocks, axis, split_axis=0, concat_axis=0, tiled=False)]
    ppermute x4, waiting for transfers between devices: 18.8 us -> 4.93 us  [the longest x1 2.59 us: far_x(): lax.ppermute(after[half:], 'x', shift(-1))]
    all_to_all x5 -> x6, waiting for transfers between devices: 34.9 us -> 23.4 us  [exchange(): lax.all_to_all(blocks, axis, split_axis=0, concat_axis=0, tiled=False)]
    ppermute x3, waiting for transfers between devices: 5.35 us -> 0.01 us  [local(): lax.ppermute(pregrad[k], 'x', shift(k))]
    ppermute x1, waiting for transfers between devices: 0.01 us -> 1.96 us  [local(): pair = mine + lax.ppermute(theirs, 'c', [(0, 1), (1, 0)])]
    concatenate x0 -> x1, other arithmetic: none -> 1.93 us  [local(): jnp.concatenate([grads, ins])]
  transfers between devices with their start and end apart: 16 -> 17, of which waited for: 8 -> 7; matrix products, arithmetic and copies ran while one was open for 7% -> 10% of each run, Pallas kernels for 0% -> 0%
where the time goes in v3:
time: 191 us; the launch traced here: 187 us
  starting transfers between devices  77.3 us (40%)
  waiting for transfers between devices  52.5 us (27%)
  blocking collectives  19.2 us (10%)
  between operations  14.5 us (8%)
  local copies, waits for them, and re-layouts  10 us (5%)
  matrix products  7.97 us (4%)
  other arithmetic  5.56 us (3%)
    all_to_all x6, starting transfers between devices, exchange(): lax.all_to_all(blocks, axis, split_axis=0, concat_axis=0, tiled=False)  47 us
    all_to_all x6, waiting for transfers between devices, exchange(): lax.all_to_all(blocks, axis, split_axis=0, concat_axis=0, tiled=False)  23.4 us
    ppermute x1, waiting for transfers between devices, local(): turned = lax.ppermute(rows_first, ('y', 'x'), swap)  21.5 us
    all_to_all x1, blocking collectives, exchange(): lax.all_to_all(blocks, axis, split_axis=0, concat_axis=0, tiled=False)  16.9 us
    ppermute x3, starting transfers between devices, local(): lax.ppermute(pregrad[k], 'x', shift(k))  11.1 us
  transfers between devices with their start and end apart: 17, of which 7 were waited for; matrix products, arithmetic and copies ran while one was open for 10% of the time, Pallas kernels for 0%

profile of v3, /device:TPU:24, one launch (start us, length us, event | category | flops | bytes accessed | tf_op | source)
XLA Modules:
  0.0 187.1 jit_solution(13504384755344469959)
XLA Ops:
  7.2 0.7 all-gather.5.cloned.1.call-update
  7.9 0.8 reshape.101
  8.7 0.8 reshape.103
  9.5 0.7 broadcast_in_dim.12
  10.2 15.1 %all-to-all-start = ((bf16[4,48,512]{2,1,0:T(8,128)(2,1)}), bf16[4,48,512]{2,1,0:T(8,128)(2,1)S(1)}, u32[]{:S(2)}, u32[]{:S(2)}) async-start(bf16[4,48,512]{2,1,0:T(8,128)(2,1)} %broadcast_in_dim.12), calls=%async_computation | async-start | bytes 393216 | tf_op jit(solution)/shard_map/all_to_all | solution.py:20
  25.3 3.4 %collective-permute-start.1 = (bf16[1024,256]{1,0:T(8,128)(2,1)}, bf16[1024,256]{1,0:T(8,128)(2,1)S(1)}, u32[]{:S(2)}, u32[]{:S(2)}) collective-permute-start(bf16[1024,256]{1,0:T(8,128)(2,1)} %param.8), channel_id=1, source_target_pairs={{0,16},{16,32},{32,48},{48,0},{1,17},{17,33},{33,49},{49,1},{2,18}... | collective-permute-start | bytes 1572872 | tf_op jit(solution)/shard_map/ppermute | solution.py:40
  28.7 3.7 %collective-permute-start.2 = (bf16[1024,256]{1,0:T(8,128)(2,1)}, bf16[1024,256]{1,0:T(8,128)(2,1)S(1)}, u32[]{:S(2)}, u32[]{:S(2)}) collective-permute-start(bf16[1024,256]{1,0:T(8,128)(2,1)} %param.8), channel_id=1, source_target_pairs={{0,48},{16,0},{32,16},{48,32},{1,49},{17,1},{33,17},{49,33},{2,50}... | collective-permute-start | bytes 1572872 | tf_op jit(solution)/shard_map/ppermute | solution.py:40
  32.4 0.8 reshape.105
  33.2 3.1 %collective-permute-start = (bf16[96,256]{1,0:T(8,128)(2,1)S(1)}, bf16[96,256]{1,0:T(8,128)(2,1)S(1)}, u32[]{:S(2)}, u32[]{:S(2)}) collective-permute-start(bf16[96,256]{1,0:T(8,128)(2,1)S(1)} %reshape.106), channel_id=1, source_target_pairs={{0,0},{16,128},{32,256},{48,384},{128,16},{144,144},{160,272},{176... | collective-permute-start | bytes 147464 | tf_op jit(solution)/shard_map/ppermute | solution.py:66
  36.4 21.5 %collective-permute-done = bf16[96,256]{1,0:T(8,128)(2,1)S(1)} collective-permute-done((bf16[96,256]{1,0:T(8,128)(2,1)S(1)}, bf16[96,256]{1,0:T(8,128)(2,1)S(1)}, u32[]{:S(2)}, u32[]{:S(2)}) %collective-permute-start) | collective-permute-done | bytes 49184 | tf_op jit(solution)/shard_map/ppermute | solution.py:66
  57.9 0.6 copy-done.3
  58.5 0.2 copy.33
  58.6 0.2 copy.34
  58.9 0.1 reshape.107
  59.0 0.8 slice_reduce_fusion
  59.9 0.8 broadcast_in_dim.28
  60.6 3.5 %all-to-all-start.1 = ((bf16[4,48,1024]{2,1,0:T(8,128)(2,1)}), bf16[4,48,1024]{2,1,0:T(8,128)(2,1)S(1)}, u32[]{:S(2)}, u32[]{:S(2)}) async-start(bf16[4,48,1024]{2,1,0:T(8,128)(2,1)} %broadcast_in_dim.28), calls=%async_computation.1 | async-start | bytes 786432 | tf_op jit(solution)/shard_map/all_to_all | solution.py:20
  64.1 3.8 %collective-permute-start.3 = (bf16[512,256]{1,0:T(8,128)(2,1)S(1)}, bf16[512,256]{1,0:T(8,128)(2,1)S(1)}, u32[]{:S(2)}, u32[]{:S(2)}) collective-permute-start(bf16[512,256]{1,0:T(8,128)(2,1)S(1)} %slice.50), channel_id=1, source_target_pairs={{0,16},{16,32},{32,48},{48,0},{1,17},{17,33},{33,49},{49,1},{2,18}... | collective-permute-start | bytes 786440 | tf_op jit(solution)/shard_map/ppermute | solution.py:46
  67.9 3.3 %collective-permute-start.4 = (bf16[512,256]{1,0:T(8,128)(2,1)S(1)}, bf16[512,256]{1,0:T(8,128)(2,1)S(1)}, u32[]{:S(2)}, u32[]{:S(2)}) collective-permute-start(bf16[512,256]{1,0:T(8,128)(2,1)S(1)} %slice.51), channel_id=1, source_target_pairs={{0,48},{16,0},{32,16},{48,32},{1,49},{17,1},{33,17},{49,33},{2,50}... | collective-permute-start | bytes 786440 | tf_op jit(solution)/shard_map/ppermute | solution.py:46
  71.3 2.3 %collective-permute-done.3 = bf16[512,256]{1,0:T(8,128)(2,1)S(1)} collective-permute-done((bf16[512,256]{1,0:T(8,128)(2,1)S(1)}, bf16[512,256]{1,0:T(8,128)(2,1)S(1)}, u32[]{:S(2)}, u32[]{:S(2)}) %collective-permute-start.3) | collective-permute-done | bytes 262176 | tf_op jit(solution)/shard_map/ppermute | solution.py:46
  73.6 2.6 %collective-permute-done.4 = bf16[512,256]{1,0:T(8,128)(2,1)S(1)} collective-permute-done((bf16[512,256]{1,0:T(8,128)(2,1)S(1)}, bf16[512,256]{1,0:T(8,128)(2,1)S(1)}, u32[]{:S(2)}, u32[]{:S(2)}) %collective-permute-start.4) | collective-permute-done | bytes 262176 | tf_op jit(solution)/shard_map/ppermute | solution.py:46
  76.3 0.8 broadcast_in_dim.31
  77.1 5.1 %all-to-all-start.6 = ((bf16[4,48,1024]{2,1,0:T(8,128)(2,1)}), bf16[4,48,1024]{2,1,0:T(8,128)(2,1)}, u32[]{:S(2)}, u32[]{:S(2)}) async-start(bf16[4,48,1024]{2,1,0:T(8,128)(2,1)} %broadcast_in_dim.31), calls=%async_computation.6 | async-start | bytes 786432 | tf_op jit(solution)/shard_map/all_to_all | solution.py:20
  82.1 1.5 pad_maximum_fusion
  83.6 2.4 %fusion.6 = f32[192,4,256]{2,0,1:T(8,128)S(1)} fusion(bf16[4,256,1024]{2,1,0:T(8,128)(2,1)} %bitcast.95, bf16[192,1024]{1,0:T(8,128)(2,1)S(1)} %bitcast.91), kind=kOutput, calls=%fused_computation.16 | convolution fusion | flops 402653184 | bytes 3276800 | tf_op jit(solution)/shard_map/td,xfd->xtf/dot_general | solution.py:75
  86.1 0.8 dynamic-slice_bitcast_fusion
  86.8 1.9 %collective-permute-start.5 = (f32[4,4,24,256]{3,2,1,0:T(8,128)}, f32[4,4,24,256]{3,2,1,0:T(8,128)}, u32[]{:S(2)}, u32[]{:S(2)}) collective-permute-start(f32[4,4,24,256]{3,2,1,0:T(8,128)} %dynamic-slice_bitcast_fusion), channel_id=1, source_target_pairs={{0,64},{64,0},{1,65},{65,1},{2,66},{66,2},{3,67},{67,3},{4,68},{68... | collective-permute-start | bytes 1179656 | tf_op jit(solution)/shard_map/ppermute | solution.py:79
  88.8 2.0 %collective-permute-done.5 = f32[4,4,24,256]{3,2,1,0:T(8,128)} collective-permute-done((f32[4,4,24,256]{3,2,1,0:T(8,128)}, f32[4,4,24,256]{3,2,1,0:T(8,128)}, u32[]{:S(2)}, u32[]{:S(2)}) %collective-permute-start.5) | collective-permute-done | bytes 393248 | tf_op jit(solution)/shard_map/ppermute | solution.py:79
  90.8 1.8 bitcast_add_fusion
  92.6 5.6 %all-to-all-start.2 = ((f32[4,96,256]{2,1,0:T(8,128)}), f32[4,96,256]{2,1,0:T(8,128)S(1)}, u32[]{:S(2)}, u32[]{:S(2)}) async-start(f32[4,96,256]{2,1,0:T(8,128)} %bitcast.97), calls=%async_computation.2 | async-start | bytes 786432 | tf_op jit(solution)/shard_map/all_to_all | solution.py:20
  98.2 1.9 %pad_maximum_fusion.1 = bf16[384,1024]{1,0:T(8,128)(2,1)} fusion(bf16[192,1024]{1,0:T(8,128)(2,1)} %bitcast.30, bf16[192,1024]{1,0:T(8,128)(2,1)S(1)} %bitcast.92), kind=kLoop, calls=%fused_computation.9 | loop fusion | flops 1572864 | bytes 1572864 | tf_op jit(solution)/shard_map/concatenate | solution.py:98
  100.2 4.6 %all-to-all-done.2 = f32[4,96,256]{2,1,0:T(8,128)S(1)} async-done(((f32[4,96,256]{2,1,0:T(8,128)}), f32[4,96,256]{2,1,0:T(8,128)S(1)}, u32[]{:S(2)}, u32[]{:S(2)}) %all-to-all-start.2) | async-done | bytes 393248 | tf_op jit(solution)/shard_map/all_to_all | solution.py:20
  104.9 0.8 broadcast_in_dim.29
  105.7 5.5 %all-to-all-start.3 = ((bf16[4,2,96,256]{3,2,1,0:T(8,128)(2,1)}), bf16[4,2,96,256]{3,2,1,0:T(8,128)(2,1)S(1)}, u32[]{:S(2)}, u32[]{:S(2)}) async-start(bf16[4,2,96,256]{3,2,1,0:T(8,128)(2,1)} %broadcast_in_dim.29), calls=%async_computation.3 | async-start | bytes 786432 | tf_op jit(solution)/shard_map/all_to_all | solution.py:20
  111.2 5.8 %all-to-all-done.3 = bf16[4,2,96,256]{3,2,1,0:T(8,128)(2,1)S(1)} async-done(((bf16[4,2,96,256]{3,2,1,0:T(8,128)(2,1)}), bf16[4,2,96,256]{3,2,1,0:T(8,128)(2,1)S(1)}, u32[]{:S(2)}, u32[]{:S(2)}) %all-to-all-start.3) | async-done | bytes 393248 | tf_op jit(solution)/shard_map/all_to_all | solution.py:20
  117.0 2.4 %all-gather = bf16[8,2,96,256]{3,2,1,0:T(8,128)(2,1)S(1)} all-gather(bf16[4,2,96,256]{3,2,1,0:T(8,128)(2,1)S(1)} %all-to-all-done.3), channel_id=2, replica_groups=mesh['y'=4,'c'=2,'x'=4,'za'=4,'zb'=4] {'c'}, dimensions={0}, use_global_device_ids=true | all-gather | bytes 1179648 | tf_op jit(solution)/shard_map/all_gather | solution.py:85
  119.5 0.1 fusion.5
  119.6 0.8 fusion.4
  120.5 16.9 %all_to_all.35 = bf16[4,48,1024]{2,1,0:T(8,128)(2,1)S(1)} all-to-all(bf16[4,48,1024]{2,1,0:T(8,128)(2,1)S(1)} %bitcast.99), channel_id=1, replica_groups=mesh['y'=4,'c'=2,'x'=4,'za'=4,'zb'=4] {'zb'}, dimensions={0} | all-to-all | bytes 786432 | tf_op jit(solution)/shard_map/all_to_all | solution.py:20
  137.4 5.6 %collective-permute-start.6 = (bf16[192,256]{1,0:T(8,128)(2,1)S(1)}, bf16[192,256]{1,0:T(8,128)(2,1)S(1)}, u32[]{:S(2)}, u32[]{:S(2)}) collective-permute-start(bf16[192,256]{1,0:T(8,128)(2,1)S(1)} %get-tuple-element.26), channel_id=1, source_target_pairs={{0,48},{16,0},{32,16},{48,32},{1,49},{17,1},{33,17},{49,33},{2,50}... | collective-permute-start | bytes 294920 | tf_op jit(solution)/shard_map/ppermute | solution.py:96
  143.1 2.2 %collective-permute-start.7 = (bf16[192,256]{1,0:T(8,128)(2,1)S(1)}, bf16[192,256]{1,0:T(8,128)(2,1)S(1)}, u32[]{:S(2)}, u32[]{:S(2)}) collective-permute-start(bf16[192,256]{1,0:T(8,128)(2,1)S(1)} %get-tuple-element.25), channel_id=1, source_target_pairs={{0,32},{16,48},{32,0},{48,16},{1,33},{17,49},{33,1},{49,17},{2,34}... | collective-permute-start | bytes 294920 | tf_op jit(solution)/shard_map/ppermute | solution.py:96
  145.3 3.3 %collective-permute-start.8 = (bf16[192,256]{1,0:T(8,128)(2,1)S(1)}, bf16[192,256]{1,0:T(8,128)(2,1)S(1)}, u32[]{:S(2)}, u32[]{:S(2)}) collective-permute-start(bf16[192,256]{1,0:T(8,128)(2,1)S(1)} %get-tuple-element.23), channel_id=1, source_target_pairs={{0,16},{16,32},{32,48},{48,0},{1,17},{17,33},{33,49},{49,1},{2,18}... | collective-permute-start | bytes 294920 | tf_op jit(solution)/shard_map/ppermute | solution.py:96
  148.7 0.7 copy.39
  149.4 12.3 %all-to-all-start.5 = ((bf16[4,24,512]{2,1,0:T(8,128)(2,1)}), bf16[4,24,512]{2,1,0:T(8,128)(2,1)S(1)}, u32[]{:S(2)}, u32[]{:S(2)}) async-start(bf16[4,24,512]{2,1,0:T(8,128)(2,1)} %copy.39), calls=%async_computation.5 | async-start | bytes 196608 | tf_op jit(solution)/shard_map/all_to_all | solution.py:20
  161.8 13.0 %all-to-all-done.5 = bf16[4,24,512]{2,1,0:T(8,128)(2,1)S(1)} async-done(((bf16[4,24,512]{2,1,0:T(8,128)(2,1)}), bf16[4,24,512]{2,1,0:T(8,128)(2,1)S(1)}, u32[]{:S(2)}, u32[]{:S(2)}) %all-to-all-start.5) | async-done | bytes 98336 | tf_op jit(solution)/shard_map/all_to_all | solution.py:20
  174.9 0.6 copy.48
  175.5 3.1 %fusion.3 = f32[256,1024]{1,0:T(8,128)} fusion(bf16[4,192,256]{2,1,0:T(8,128)(2,1)S(1)} %bitcast.106, bf16[4,2,192,1024]{3,2,1,0:T(8,128)(2,1)} %bitcast.114), kind=kOutput, calls=%fused_computation.6 | convolution fusion | flops 402653184 | bytes 3014656 | tf_op jit(solution)/shard_map/xtf,xtd->fd/dot_general | solution.py:100
  178.7 1.6 fusion.2
  (62 shorter events, 0.9 us)
Async XLA Ops:
  7.2 76.4 %all-gather.5.cloned.1.call-start = ((), (), s32[]{:S(2)}) async-start(), calls=%async_computation.7 | async-start | bytes 2621440 | tf_op jit(solution)/shard_map/all_gather | solution.py:61
  10.2 48.3 %all-to-all-start = ((bf16[4,48,512]{2,1,0:T(8,128)(2,1)}), bf16[4,48,512]{2,1,0:T(8,128)(2,1)S(1)}, u32[]{:S(2)}, u32[]{:S(2)}) async-start(bf16[4,48,512]{2,1,0:T(8,128)(2,1)} %broadcast_in_dim.12), calls=%async_computation | async-start | bytes 393216 | tf_op jit(solution)/shard_map/all_to_all | solution.py:20
  25.3 32.6 %collective-permute-start.1 = (bf16[1024,256]{1,0:T(8,128)(2,1)}, bf16[1024,256]{1,0:T(8,128)(2,1)S(1)}, u32[]{:S(2)}, u32[]{:S(2)}) collective-permute-start(bf16[1024,256]{1,0:T(8,128)(2,1)} %param.8), channel_id=1, source_target_pairs={{0,16},{16,32},{32,48},{48,0},{1,17},{17,33},{33,49},{49,1},{2,18}... | collective-permute-start | bytes 1572872 | tf_op jit(solution)/shard_map/ppermute | solution.py:40
  28.7 29.2 %collective-permute-start.2 = (bf16[1024,256]{1,0:T(8,128)(2,1)}, bf16[1024,256]{1,0:T(8,128)(2,1)S(1)}, u32[]{:S(2)}, u32[]{:S(2)}) collective-permute-start(bf16[1024,256]{1,0:T(8,128)(2,1)} %param.8), channel_id=1, source_target_pairs={{0,48},{16,0},{32,16},{48,32},{1,49},{17,1},{33,17},{49,33},{2,50}... | collective-permute-start | bytes 1572872 | tf_op jit(solution)/shard_map/ppermute | solution.py:40
  33.2 24.7 %copy-start.1 = (bf16[2,4,12,256]{3,2,1,0:T(8,128)(2,1)}, bf16[2,4,12,256]{3,2,1,0:T(8,128)(2,1)S(1)}, u32[]{:S(2)}) copy-start(bf16[2,4,12,256]{3,2,1,0:T(8,128)(2,1)S(1)} %reshape.105) | copy-start | bytes 147460
  33.2 24.6 %collective-permute-start = (bf16[96,256]{1,0:T(8,128)(2,1)S(1)}, bf16[96,256]{1,0:T(8,128)(2,1)S(1)}, u32[]{:S(2)}, u32[]{:S(2)}) collective-permute-start(bf16[96,256]{1,0:T(8,128)(2,1)S(1)} %reshape.106), channel_id=1, source_target_pairs={{0,0},{16,128},{32,256},{48,384},{128,16},{144,144},{160,272},{176... | collective-permute-start | bytes 147464 | tf_op jit(solution)/shard_map/ppermute | solution.py:66
  57.9 0.6 copy-start.3
  58.5 9.5 %copy-start = (bf16[1024,256]{1,0:T(8,128)(2,1)}, bf16[1024,256]{1,0:T(8,128)(2,1)S(1)}, u32[]{:S(2)}) copy-start(bf16[1024,256]{1,0:T(8,128)(2,1)S(1)} %collective-permute-done.2) | copy-start | bytes 1572868
  60.6 15.6 %all-to-all-start.1 = ((bf16[4,48,1024]{2,1,0:T(8,128)(2,1)}), bf16[4,48,1024]{2,1,0:T(8,128)(2,1)S(1)}, u32[]{:S(2)}, u32[]{:S(2)}) async-start(bf16[4,48,1024]{2,1,0:T(8,128)(2,1)} %broadcast_in_dim.28), calls=%async_computation.1 | async-start | bytes 786432 | tf_op jit(solution)/shard_map/all_to_all | solution.py:20
  64.1 9.5 %collective-permute-start.3 = (bf16[512,256]{1,0:T(8,128)(2,1)S(1)}, bf16[512,256]{1,0:T(8,128)(2,1)S(1)}, u32[]{:S(2)}, u32[]{:S(2)}) collective-permute-start(bf16[512,256]{1,0:T(8,128)(2,1)S(1)} %slice.50), channel_id=1, source_target_pairs={{0,16},{16,32},{32,48},{48,0},{1,17},{17,33},{33,49},{49,1},{2,18}... | collective-permute-start | bytes 786440 | tf_op jit(solution)/shard_map/ppermute | solution.py:46
  67.9 8.3 %collective-permute-start.4 = (bf16[512,256]{1,0:T(8,128)(2,1)S(1)}, bf16[512,256]{1,0:T(8,128)(2,1)S(1)}, u32[]{:S(2)}, u32[]{:S(2)}) collective-permute-start(bf16[512,256]{1,0:T(8,128)(2,1)S(1)} %slice.51), channel_id=1, source_target_pairs={{0,48},{16,0},{32,16},{48,32},{1,49},{17,1},{33,17},{49,33},{2,50}... | collective-permute-start | bytes 786440 | tf_op jit(solution)/shard_map/ppermute | solution.py:46
  77.1 15.5 %all-to-all-start.6 = ((bf16[4,48,1024]{2,1,0:T(8,128)(2,1)}), bf16[4,48,1024]{2,1,0:T(8,128)(2,1)}, u32[]{:S(2)}, u32[]{:S(2)}) async-start(bf16[4,48,1024]{2,1,0:T(8,128)(2,1)} %broadcast_in_dim.31), calls=%async_computation.6 | async-start | bytes 786432 | tf_op jit(solution)/shard_map/all_to_all | solution.py:20
  83.6 5.2 %copy-start.2 = (bf16[2,4,12,256]{3,2,1,0:T(8,128)(2,1)S(1)}, bf16[2,4,12,256]{3,2,1,0:T(8,128)(2,1)}, u32[]{:S(2)}) copy-start(bf16[2,4,12,256]{3,2,1,0:T(8,128)(2,1)} %copy-done.1) | copy-start | bytes 147460
  86.8 3.9 %collective-permute-start.5 = (f32[4,4,24,256]{3,2,1,0:T(8,128)}, f32[4,4,24,256]{3,2,1,0:T(8,128)}, u32[]{:S(2)}, u32[]{:S(2)}) collective-permute-start(f32[4,4,24,256]{3,2,1,0:T(8,128)} %dynamic-slice_bitcast_fusion), channel_id=1, source_target_pairs={{0,64},{64,0},{1,65},{65,1},{2,66},{66,2},{3,67},{67,3},{4,68},{68... | collective-permute-start | bytes 1179656 | tf_op jit(solution)/shard_map/ppermute | solution.py:79
  92.6 12.2 %copy-start.4 = (bf16[96,256]{1,0:T(8,128)(2,1)S(1)}, bf16[96,256]{1,0:T(8,128)(2,1)}, u32[]{:S(2)}) copy-start(bf16[96,256]{1,0:T(8,128)(2,1)} %copy-done.3) | copy-start | bytes 147460
  92.6 12.2 %all-to-all-start.2 = ((f32[4,96,256]{2,1,0:T(8,128)}), f32[4,96,256]{2,1,0:T(8,128)S(1)}, u32[]{:S(2)}, u32[]{:S(2)}) async-start(f32[4,96,256]{2,1,0:T(8,128)} %bitcast.97), calls=%async_computation.2 | async-start | bytes 786432 | tf_op jit(solution)/shard_map/all_to_all | solution.py:20
  98.2 77.3 %all-gather.7.cloned.1.call-start = ((), (), s32[]{:S(2)}) async-start(), calls=%async_computation.8 | async-start | bytes 3932160 | tf_op jit(solution)/shard_map/all_gather | solution.py:98
  105.7 11.3 %all-to-all-start.3 = ((bf16[4,2,96,256]{3,2,1,0:T(8,128)(2,1)}), bf16[4,2,96,256]{3,2,1,0:T(8,128)(2,1)S(1)}, u32[]{:S(2)}, u32[]{:S(2)}) async-start(bf16[4,2,96,256]{3,2,1,0:T(8,128)(2,1)} %broadcast_in_dim.29), calls=%async_computation.3 | async-start | bytes 786432 | tf_op jit(solution)/shard_map/all_to_all | solution.py:20
  137.4 24.3 %collective-permute-start.6 = (bf16[192,256]{1,0:T(8,128)(2,1)S(1)}, bf16[192,256]{1,0:T(8,128)(2,1)S(1)}, u32[]{:S(2)}, u32[]{:S(2)}) collective-permute-start(bf16[192,256]{1,0:T(8,128)(2,1)S(1)} %get-tuple-element.26), channel_id=1, source_target_pairs={{0,48},{16,0},{32,16},{48,32},{1,49},{17,1},{33,17},{49,33},{2,50}... | collective-permute-start | bytes 294920 | tf_op jit(solution)/shard_map/ppermute | solution.py:96
  143.1 18.6 %collective-permute-start.7 = (bf16[192,256]{1,0:T(8,128)(2,1)S(1)}, bf16[192,256]{1,0:T(8,128)(2,1)S(1)}, u32[]{:S(2)}, u32[]{:S(2)}) collective-permute-start(bf16[192,256]{1,0:T(8,128)(2,1)S(1)} %get-tuple-element.25), channel_id=1, source_target_pairs={{0,32},{16,48},{32,0},{48,16},{1,33},{17,49},{33,1},{49,17},{2,34}... | collective-permute-start | bytes 294920 | tf_op jit(solution)/shard_map/ppermute | solution.py:96
  145.3 16.5 %collective-permute-start.8 = (bf16[192,256]{1,0:T(8,128)(2,1)S(1)}, bf16[192,256]{1,0:T(8,128)(2,1)S(1)}, u32[]{:S(2)}, u32[]{:S(2)}) collective-permute-start(bf16[192,256]{1,0:T(8,128)(2,1)S(1)} %get-tuple-element.23), channel_id=1, source_target_pairs={{0,16},{16,32},{32,48},{48,0},{1,17},{17,33},{33,49},{49,1},{2,18}... | collective-permute-start | bytes 294920 | tf_op jit(solution)/shard_map/ppermute | solution.py:96
  149.4 25.4 %all-to-all-start.5 = ((bf16[4,24,512]{2,1,0:T(8,128)(2,1)}), bf16[4,24,512]{2,1,0:T(8,128)(2,1)S(1)}, u32[]{:S(2)}, u32[]{:S(2)}) async-start(bf16[4,24,512]{2,1,0:T(8,128)(2,1)} %copy.39), calls=%async_computation.5 | async-start | bytes 196608 | tf_op jit(solution)/shard_map/all_to_all | solution.py:20
  175.5 3.1 %copy-start.5 = (bf16[1536,1024]{1,0:T(8,128)(2,1)S(1)}, bf16[1536,1024]{1,0:T(8,128)(2,1)}, u32[]{:S(2)}) copy-start(bf16[1536,1024]{1,0:T(8,128)(2,1)} %all-gather.7.cloned.1.call-done) | copy-start | bytes 9437188
Sparse Core Ops, SparseCore 0:
  10.1 52.1 all-gather.4
  101.7 54.2 all-gather.6

commit v4 on v2

--- a/solution.py
+++ b/solution.py
@@ -36,16 +36,6 @@
     return jnp.swapaxes(split, -3, -2).reshape(*lead, rows // 2, cols * 2)
 
 
-def gather_x(block):
-    half = block.shape[0] // 2
-    before = lax.ppermute(block, "x", shift(1))
-    after = lax.ppermute(block, "x", shift(-1))
-    far = jnp.concatenate(
-        [lax.ppermute(before[:half], "x", shift(1)), lax.ppermute(after[half:], "x", shift(-1))]
-    )
-    return jnp.stack([block, after, far, before])
-
-
 def shift(k):
     return [(i, (i + k) % 4) for i in range(4)]
 
@@ -57,16 +47,19 @@
 
 def local(inputs, out_grad, preact, up_weight, down_weight):
     core, at_x = lax.axis_index("c"), lax.axis_index("x")
-    wide_down = lax.all_gather(down_weight, "x", axis=0, tiled=True).reshape(4, 256, 1024)
+    up_rows = up_weight.reshape(4, 256, 256).swapaxes(0, 1).reshape(256, 1024)
+    wide = lax.all_gather(jnp.concatenate([down_weight, up_rows]), "x", axis=0, tiled=False)
+    wide_down, wide_up = wide[:, :256], wide[:, 256:].reshape(4, 256, 4, 256)
+
     both = jnp.concatenate([halves_down(out_grad), halves_down(inputs)], axis=0)
     both = spread(both, "za")
-    both = halves_across(both.reshape(4, 2, 24, 512)).swapaxes(0, 1).reshape(96, 1024)
-    both = spread(both, "zb").reshape(4, 2, 48, 1024).swapaxes(0, 1).reshape(2, 192, 1024)
-    grads = both[0]
-
     rows_first = preact.reshape(2, 4, 12, 256).transpose(1, 0, 2, 3).reshape(96, 256)
     swap = [(4 * a + b, 4 * b + a) for a in range(4) for b in range(4)]
     turned = lax.ppermute(rows_first, ("y", "x"), swap)
+    both, turned = lax.optimization_barrier((both, turned))
+    both = halves_across(both.reshape(4, 2, 24, 512)).swapaxes(0, 1).reshape(96, 1024)
+    both = spread(both, "zb").reshape(4, 2, 48, 1024).swapaxes(0, 1).reshape(2, 192, 1024)
+    grads, ins = both[0], both[1]
 
     partial = jnp.einsum("td,xfd->xtf", grads, wide_down, preferred_element_type=F32)
     partial = partial.reshape(4, 4, 2, 24, 256)
@@ -80,22 +73,24 @@
     own = spread(jnp.stack([(hidden_grad * slope).astype(BF), activ.astype(BF)]), "y")
     own = lax.all_gather(own, "c", axis=0, tiled=False).reshape(2, 4, 2, 4, 24, 256)
     own = own.transpose(2, 1, 3, 0, 4, 5).reshape(2, 4, 192, 256)
-    pregrad, all_activ = turn_by(own[0], at_x), own[1]
+    pregrad, all_activ = own[0], own[1]
 
-    wide_up = gather_x(up_weight)
-    part = jnp.einsum("xtf,xdf->td", pregrad, wide_up, preferred_element_type=F32)
+    part = jnp.einsum("xtf,xrkf->tkr", pregrad, wide_up, preferred_element_type=F32)
     part = exchange(part.astype(BF).reshape(4, 48, 1024), "zb")
     part = part.astype(F32).sum(0)
+    part, pregrad = lax.optimization_barrier((part, pregrad))
     part = exchange(halves_down(part.astype(BF).reshape(4, 12, 1024)), "za")
     input_grad = halves_across(part.astype(F32).sum(0)).astype(BF)
 
+    pregrad = turn_by(pregrad, at_x)
     sent = [pregrad[0]] + [lax.ppermute(pregrad[k], "x", shift(k)) for k in (3, 2, 1)]
-    all_pregrad = turn_by(jnp.stack(sent), (4 - at_x) % 4).reshape(768, 256)
+    all_pregrad = turn_by(jnp.stack(sent), (4 - at_x) % 4)
+    all_pregrad, all_activ = lax.optimization_barrier((all_pregrad, all_activ))
     all_both = lax.all_gather(both.reshape(384, 1024), "x", axis=0, tiled=False)
     all_both = all_both.reshape(4, 2, 192, 1024)
     down_grad = jnp.einsum("xtf,xtd->fd", all_activ, all_both[:, 0], preferred_element_type=F32)
     up_grad = jnp.einsum(
-        "xtd,xtf->df", all_both[:, 1], all_pregrad.reshape(4, 192, 256), preferred_element_type=F32
+        "xtd,xtf->df", all_both[:, 1], all_pregrad, preferred_element_type=F32
     )
     return (input_grad, up_grad, down_grad)
 

time: 178 us -> 167 us (0.938)
  blocking collectives: 34.2 us -> 2.36 us
  starting transfers between devices: 50.7 us -> 61.5 us
  waiting for transfers between devices: 59.8 us -> 65.1 us
  local copies, waits for them, and re-layouts: 7.5 us -> 10.6 us
    all_to_all x1 -> x0, blocking collectives: 31.8 us -> none  [exchange(): lax.all_to_all(blocks, axis, split_axis=0, concat_axis=0, tiled=False)]
    all_to_all x5 -> x6, starting transfers between devices: 20.9 us -> 46 us  [exchange(): lax.all_to_all(blocks, axis, split_axis=0, concat_axis=0, tiled=False)]
    all_to_all x5 -> x6, waiting for transfers between devices: 34.9 us -> 54.2 us  [exchange(): lax.all_to_all(blocks, axis, split_axis=0, concat_axis=0, tiled=False)]
    ppermute x4 -> x0, waiting for transfers between devices: 18.8 us -> none  [the longest x1 14.6 us: gather_x(): after = lax.ppermute(block, 'x', shift(-1))]
    ppermute x4 -> x0, starting transfers between devices: 14.9 us -> none  [the longest x1 5.92 us: gather_x(): lax.ppermute(after[half:], 'x', shift(-1))]
    ppermute x1, waiting for transfers between devices: 0.01 us -> 5.5 us  [local(): turned = lax.ppermute(rows_first, ('y', 'x'), swap)]
    ppermute x3, waiting for transfers between devices: 5.35 us -> 0.01 us  [local(): lax.ppermute(pregrad[k], 'x', shift(k))]
    all_gather x1, waiting for transfers between devices: 0.02 us -> 3.63 us  [local(): lax.all_gather(jnp.concatenate([down_weight, up_rows]), 'x', axis=0, tile...]
  transfers between devices with their start and end apart: 16 -> 13, of which waited for: 8 -> 9; matrix products, arithmetic and copies ran while one was open for 7% -> 9% of each run, Pallas kernels for 0% -> 0%
where the time goes in v4:
time: 167 us; the launch traced here: 164 us
  waiting for transfers between devices  65.1 us (39%)
  starting transfers between devices  61.5 us (37%)
  between operations  14.5 us (9%)
  local copies, waits for them, and re-layouts  10.6 us (6%)
  matrix products  7.99 us (5%)
  blocking collectives  2.36 us (1%)
  other arithmetic  2.18 us (1%)
    all_to_all x6, waiting for transfers between devices, exchange(): lax.all_to_all(blocks, axis, split_axis=0, concat_axis=0, tiled=False)  54.2 us
    all_to_all x6, starting transfers between devices, exchange(): lax.all_to_all(blocks, axis, split_axis=0, concat_axis=0, tiled=False)  46 us
    ppermute x3, starting transfers between devices, local(): lax.ppermute(pregrad[k], 'x', shift(k))  9.21 us
    ppermute x1, waiting for transfers between devices, local(): turned = lax.ppermute(rows_first, ('y', 'x'), swap)  5.5 us
    ppermute x1, starting transfers between devices, local(): turned = lax.ppermute(rows_first, ('y', 'x'), swap)  4.33 us
    all_gather x1, waiting for transfers between devices, local(): lax.all_gather(jnp.concatenate([down_weight, up_rows]), 'x', axis=0, tile...  3.63 us
  transfers between devices with their start and end apart: 13, of which 9 were waited for; matrix products, arithmetic and copies ran while one was open for 9% of the time, Pallas kernels for 0%

profile of v4, /device:TPU:24, one launch (start us, length us, event | category | flops | bytes accessed | tf_op | source)
XLA Modules:
  0.0 164.2 jit_solution(10283797338526698128)
XLA Ops:
  7.2 0.0 all-gather.7.cloned.1.call-start
  7.2 1.5 copy.38
  8.7 0.1 copy.60
  8.9 1.0 pad_maximum_fusion
  10.1 0.7 broadcast_in_dim.8
  10.8 15.1 %all-to-all-start = ((bf16[4,48,512]{2,1,0:T(8,128)(2,1)}), bf16[4,48,512]{2,1,0:T(8,128)(2,1)S(1)}, u32[]{:S(2)}, u32[]{:S(2)}) async-start(bf16[4,48,512]{2,1,0:T(8,128)(2,1)} %broadcast_in_dim.8), calls=%async_computation | async-start | bytes 393216 | tf_op jit(solution)/shard_map/all_to_all | solution.py:20
  25.9 4.3 %collective-permute-start = (bf16[96,256]{1,0:T(8,128)(2,1)S(1)}, bf16[96,256]{1,0:T(8,128)(2,1)S(1)}, u32[]{:S(2)}, u32[]{:S(2)}) collective-permute-start(bf16[96,256]{1,0:T(8,128)(2,1)S(1)} %reshape.110), channel_id=1, source_target_pairs={{0,0},{16,128},{32,256},{48,384},{128,16},{144,144},{160,272},{176... | collective-permute-start | bytes 147464 | tf_op jit(solution)/shard_map/ppermute | solution.py:58
  30.2 5.5 %collective-permute-done = bf16[96,256]{1,0:T(8,128)(2,1)S(1)} collective-permute-done((bf16[96,256]{1,0:T(8,128)(2,1)S(1)}, bf16[96,256]{1,0:T(8,128)(2,1)S(1)}, u32[]{:S(2)}, u32[]{:S(2)}) %collective-permute-start) | collective-permute-done | bytes 49184 | tf_op jit(solution)/shard_map/ppermute | solution.py:58
  35.7 6.5 %all-to-all-done = bf16[4,48,512]{2,1,0:T(8,128)(2,1)S(1)} async-done(((bf16[4,48,512]{2,1,0:T(8,128)(2,1)}), bf16[4,48,512]{2,1,0:T(8,128)(2,1)S(1)}, u32[]{:S(2)}, u32[]{:S(2)}) %all-to-all-start) | async-done | bytes 196640 | tf_op jit(solution)/shard_map/all_to_all | solution.py:20
  42.3 0.2 copy.42
  42.4 0.2 copy.43
  42.7 0.1 reshape.111
  42.9 1.0 broadcast_in_dim.10
  43.9 4.7 %all-to-all-start.1 = ((bf16[4,96,1024]{2,1,0:T(8,128)(2,1)}), bf16[4,96,1024]{2,1,0:T(8,128)(2,1)S(1)}, u32[]{:S(2)}, u32[]{:S(2)}) async-start(bf16[4,96,1024]{2,1,0:T(8,128)(2,1)} %broadcast_in_dim.10), calls=%async_computation.1 | async-start | bytes 1572864 | tf_op jit(solution)/shard_map/all_to_all | solution.py:20
  48.6 18.6 %all-to-all-done.1 = bf16[4,96,1024]{2,1,0:T(8,128)(2,1)S(1)} async-done(((bf16[4,96,1024]{2,1,0:T(8,128)(2,1)}), bf16[4,96,1024]{2,1,0:T(8,128)(2,1)S(1)}, u32[]{:S(2)}, u32[]{:S(2)}) %all-to-all-start.1) | async-done | bytes 786464 | tf_op jit(solution)/shard_map/all_to_all | solution.py:20
  67.2 3.6 %all-gather.7.cloned.1.call-done = bf16[2048,1024]{1,0:T(8,128)(2,1)} async-done(((bf16[512,1024]{1,0:T(8,128)(2,1)}), bf16[2048,1024]{1,0:T(8,128)(2,1)}) %all-gather.7.cloned.1.call-update) | async-done | bytes 4194320 | tf_op jit(solution)/shard_map/all_gather | solution.py:51
  70.8 2.4 %fusion.3 = f32[4,256,192]{1,2,0:T(8,128)S(1)} fusion(bf16[192,1024,1]{1,0,2:T(8,128)(2,1)S(1)} %bitcast.124, bf16[4,512,1024]{2,1,0:T(8,128)(2,1)} %bitcast.115), kind=kOutput, calls=%fused_computation.3 | convolution fusion | flops 402653184 | bytes 3276800 | tf_op jit(solution)/shard_map/td,xfd->xtf/dot_general | solution.py:64
  73.3 1.9 %collective-permute-start.1 = (f32[4,4,24,256]{3,2,1,0:T(8,128)S(1)}, f32[4,4,24,256]{3,2,1,0:T(8,128)S(1)}, u32[]{:S(2)}, u32[]{:S(2)}) collective-permute-start(f32[4,4,24,256]{3,2,1,0:T(8,128)S(1)} %dynamic-slice_bitcast_fusion), channel_id=1, source_target_pairs={{0,64},{64,0},{1,65},{65,1},{2,66},{66,2},{3,67},{67,3},{4,68},{68... | collective-permute-start | bytes 1179656 | tf_op jit(solution)/shard_map/ppermute | solution.py:68
  75.2 1.7 %collective-permute-done.1 = f32[4,4,24,256]{3,2,1,0:T(8,128)S(1)} collective-permute-done((f32[4,4,24,256]{3,2,1,0:T(8,128)S(1)}, f32[4,4,24,256]{3,2,1,0:T(8,128)S(1)}, u32[]{:S(2)}, u32[]{:S(2)}) %collective-permute-start.1) | collective-permute-done | bytes 393248 | tf_op jit(solution)/shard_map/ppermute | solution.py:68
  76.9 0.8 bitcast_add_fusion
  77.7 4.8 %all-to-all-start.2 = ((f32[4,96,256]{2,1,0:T(8,128)}), f32[4,96,256]{2,1,0:T(8,128)S(1)}, u32[]{:S(2)}, u32[]{:S(2)}) async-start(f32[4,96,256]{2,1,0:T(8,128)} %bitcast.18), calls=%async_computation.2 | async-start | bytes 786432 | tf_op jit(solution)/shard_map/all_to_all | solution.py:20
  82.6 1.0 copy.52
  83.6 5.2 %all-to-all-done.2 = f32[4,96,256]{2,1,0:T(8,128)S(1)} async-done(((f32[4,96,256]{2,1,0:T(8,128)}), f32[4,96,256]{2,1,0:T(8,128)S(1)}, u32[]{:S(2)}, u32[]{:S(2)}) %all-to-all-start.2) | async-done | bytes 393248 | tf_op jit(solution)/shard_map/all_to_all | solution.py:20
  88.9 0.1 fusion.27
  88.9 0.8 broadcast_in_dim.22
  89.7 5.5 %all-to-all-start.3 = ((bf16[4,2,96,256]{3,2,1,0:T(8,128)(2,1)}), bf16[4,2,96,256]{3,2,1,0:T(8,128)(2,1)S(1)}, u32[]{:S(2)}, u32[]{:S(2)}) async-start(bf16[4,2,96,256]{3,2,1,0:T(8,128)(2,1)} %broadcast_in_dim.22), calls=%async_computation.3 | async-start | bytes 786432 | tf_op jit(solution)/shard_map/all_to_all | solution.py:20
  95.2 1.8 %slice.53 = bf16[4,256,1024]{2,1,0:T(8,128)(2,1)S(1)} slice(bf16[4,512,1024]{2,1,0:T(8,128)(2,1)} %bitcast.116), slice={[0:4], [256:512], [0:1024]} | slice | bytes 4194304 | tf_op jit(solution)/shard_map/slice | solution.py:52
  97.0 3.5 %all-to-all-done.3 = bf16[4,2,96,256]{3,2,1,0:T(8,128)(2,1)S(1)} async-done(((bf16[4,2,96,256]{3,2,1,0:T(8,128)(2,1)}), bf16[4,2,96,256]{3,2,1,0:T(8,128)(2,1)S(1)}, u32[]{:S(2)}, u32[]{:S(2)}) %all-to-all-start.3) | async-done | bytes 393248 | tf_op jit(solution)/shard_map/all_to_all | solution.py:20
  100.5 2.4 %all-gather.1 = bf16[8,2,96,256]{3,2,1,0:T(8,128)(2,1)S(1)} all-gather(bf16[4,2,96,256]{3,2,1,0:T(8,128)(2,1)S(1)} %all-to-all-done.3), channel_id=3, replica_groups=mesh['y'=4,'c'=2,'x'=4,'za'=4,'zb'=4] {'c'}, dimensions={0}, use_global_device_ids=true | all-gather | bytes 1179648 | tf_op jit(solution)/shard_map/all_gather | solution.py:74
  102.9 0.1 fusion.28
  103.0 0.8 fusion.15
  103.8 0.3 copy.48
  104.1 1.0 reshape.116
  105.1 4.8 %all-to-all-start.4 = ((bf16[4,48,1024]{2,1,0:T(8,128)(2,1)}), bf16[4,48,1024]{2,1,0:T(8,128)(2,1)S(1)}, u32[]{:S(2)}, u32[]{:S(2)}) async-start(bf16[4,48,1024]{2,1,0:T(8,128)(2,1)} %reshape.116), calls=%async_computation.4 | async-start | bytes 786432 | tf_op jit(solution)/shard_map/all_to_all | solution.py:20
  110.0 12.0 %all-to-all-done.4 = bf16[4,48,1024]{2,1,0:T(8,128)(2,1)S(1)} async-done(((bf16[4,48,1024]{2,1,0:T(8,128)(2,1)}), bf16[4,48,1024]{2,1,0:T(8,128)(2,1)S(1)}, u32[]{:S(2)}, u32[]{:S(2)}) %all-to-all-start.4) | async-done | bytes 393248 | tf_op jit(solution)/shard_map/all_to_all | solution.py:20
  121.9 0.1 convert_reduce_fusion
  122.0 0.1 fusion.18
  122.2 3.1 %collective-permute-start.2 = (bf16[192,256]{1,0:T(8,128)(2,1)S(1)}, bf16[192,256]{1,0:T(8,128)(2,1)S(1)}, u32[]{:S(2)}, u32[]{:S(2)}) collective-permute-start(bf16[192,256]{1,0:T(8,128)(2,1)S(1)} %get-tuple-element.20), channel_id=1, source_target_pairs={{0,48},{16,0},{32,16},{48,32},{1,49},{17,1},{33,17},{49,33},{2,50}... | collective-permute-start | bytes 294920 | tf_op jit(solution)/shard_map/ppermute | solution.py:86
  125.3 3.7 %collective-permute-start.3 = (bf16[192,256]{1,0:T(8,128)(2,1)S(1)}, bf16[192,256]{1,0:T(8,128)(2,1)S(1)}, u32[]{:S(2)}, u32[]{:S(2)}) collective-permute-start(bf16[192,256]{1,0:T(8,128)(2,1)S(1)} %get-tuple-element.19), channel_id=1, source_target_pairs={{0,32},{16,48},{32,0},{48,16},{1,33},{17,49},{33,1},{49,17},{2,34}... | collective-permute-start | bytes 294920 | tf_op jit(solution)/shard_map/ppermute | solution.py:86
  129.0 2.5 %collective-permute-start.4 = (bf16[192,256]{1,0:T(8,128)(2,1)S(1)}, bf16[192,256]{1,0:T(8,128)(2,1)S(1)}, u32[]{:S(2)}, u32[]{:S(2)}) collective-permute-start(bf16[192,256]{1,0:T(8,128)(2,1)S(1)} %get-tuple-element.17), channel_id=1, source_target_pairs={{0,16},{16,32},{32,48},{48,0},{1,17},{17,33},{33,49},{49,1},{2,18}... | collective-permute-start | bytes 294920 | tf_op jit(solution)/shard_map/ppermute | solution.py:86
  131.6 0.1 copy.49
  131.6 0.7 copy.50
  132.3 11.1 %all-to-all-start.5 = ((bf16[4,24,512]{2,1,0:T(8,128)(2,1)}), bf16[4,24,512]{2,1,0:T(8,128)(2,1)S(1)}, u32[]{:S(2)}, u32[]{:S(2)}) async-start(bf16[4,24,512]{2,1,0:T(8,128)(2,1)} %copy.50), calls=%async_computation.5 | async-start | bytes 196608 | tf_op jit(solution)/shard_map/all_to_all | solution.py:20
  143.5 0.0 all-gather.5.cloned.1.call-done
  143.6 3.1 %fusion.8 = f32[256,1024]{1,0:T(8,128)} fusion(bf16[4,192,256]{2,1,0:T(8,128)(2,1)S(1)} %bitcast.123, bf16[4,2,192,1024]{3,2,1,0:T(8,128)(2,1)} %bitcast.132), kind=kOutput, calls=%fused_computation.10 | convolution fusion | flops 402653184 | bytes 3014656 | tf_op jit(solution)/shard_map/xtf,xtd->fd/dot_general | solution.py:91
  146.7 1.6 fusion.7
  148.3 8.3 %all-to-all-done.5 = bf16[4,24,512]{2,1,0:T(8,128)(2,1)S(1)} async-done(((bf16[4,24,512]{2,1,0:T(8,128)(2,1)}), bf16[4,24,512]{2,1,0:T(8,128)(2,1)S(1)}, u32[]{:S(2)}, u32[]{:S(2)}) %all-to-all-start.5) | async-done | bytes 98336 | tf_op jit(solution)/shard_map/all_to_all | solution.py:20
  156.7 0.6 copy.61
  (52 shorter events, 0.8 us)
Async XLA Ops:
  7.2 1.7 %copy-start = (bf16[256,1024]{1,0:T(8,128)(2,1)S(1)}, bf16[256,1024]{1,0:T(8,128)(2,1)}, u32[]{:S(2)}) copy-start(bf16[256,1024]{1,0:T(8,128)(2,1)} %param.9) | copy-start | bytes 1572868
  7.2 63.7 %all-gather.7.cloned.1.call-start = ((), (), s32[]{:S(2)}) async-start(), calls=%async_computation.7 | async-start | bytes 5242880 | tf_op jit(solution)/shard_map/all_gather | solution.py:51
  8.7 1.2 copy-start.2
  8.7 1.3 copy-start.3
  8.9 17.0 %copy-start.1 = (bf16[96,256]{1,0:T(8,128)(2,1)S(1)}, bf16[96,256]{1,0:T(8,128)(2,1)}, u32[]{:S(2)}) copy-start(bf16[96,256]{1,0:T(8,128)(2,1)} %param.7) | copy-start | bytes 147460
  10.8 31.5 %all-to-all-start = ((bf16[4,48,512]{2,1,0:T(8,128)(2,1)}), bf16[4,48,512]{2,1,0:T(8,128)(2,1)S(1)}, u32[]{:S(2)}, u32[]{:S(2)}) async-start(bf16[4,48,512]{2,1,0:T(8,128)(2,1)} %broadcast_in_dim.8), calls=%async_computation | async-start | bytes 393216 | tf_op jit(solution)/shard_map/all_to_all | solution.py:20
  25.9 9.8 %collective-permute-start = (bf16[96,256]{1,0:T(8,128)(2,1)S(1)}, bf16[96,256]{1,0:T(8,128)(2,1)S(1)}, u32[]{:S(2)}, u32[]{:S(2)}) collective-permute-start(bf16[96,256]{1,0:T(8,128)(2,1)S(1)} %reshape.110), channel_id=1, source_target_pairs={{0,0},{16,128},{32,256},{48,384},{128,16},{144,144},{160,272},{176... | collective-permute-start | bytes 147464 | tf_op jit(solution)/shard_map/ppermute | solution.py:58
  43.9 23.3 %all-to-all-start.1 = ((bf16[4,96,1024]{2,1,0:T(8,128)(2,1)}), bf16[4,96,1024]{2,1,0:T(8,128)(2,1)S(1)}, u32[]{:S(2)}, u32[]{:S(2)}) async-start(bf16[4,96,1024]{2,1,0:T(8,128)(2,1)} %broadcast_in_dim.10), calls=%async_computation.1 | async-start | bytes 1572864 | tf_op jit(solution)/shard_map/all_to_all | solution.py:20
  73.3 3.6 %collective-permute-start.1 = (f32[4,4,24,256]{3,2,1,0:T(8,128)S(1)}, f32[4,4,24,256]{3,2,1,0:T(8,128)S(1)}, u32[]{:S(2)}, u32[]{:S(2)}) collective-permute-start(f32[4,4,24,256]{3,2,1,0:T(8,128)S(1)} %dynamic-slice_bitcast_fusion), channel_id=1, source_target_pairs={{0,64},{64,0},{1,65},{65,1},{2,66},{66,2},{3,67},{67,3},{4,68},{68... | collective-permute-start | bytes 1179656 | tf_op jit(solution)/shard_map/ppermute | solution.py:68
  77.7 11.1 %all-to-all-start.2 = ((f32[4,96,256]{2,1,0:T(8,128)}), f32[4,96,256]{2,1,0:T(8,128)S(1)}, u32[]{:S(2)}, u32[]{:S(2)}) async-start(f32[4,96,256]{2,1,0:T(8,128)} %bitcast.18), calls=%async_computation.2 | async-start | bytes 786432 | tf_op jit(solution)/shard_map/all_to_all | solution.py:20
  82.5 61.0 %all-gather.5.cloned.1.call-start = ((), (), s32[]{:S(2)}) async-start(), calls=%async_computation.6 | async-start | bytes 3932160 | tf_op jit(solution)/shard_map/all_gather | solution.py:89
  89.7 10.8 %all-to-all-start.3 = ((bf16[4,2,96,256]{3,2,1,0:T(8,128)(2,1)}), bf16[4,2,96,256]{3,2,1,0:T(8,128)(2,1)S(1)}, u32[]{:S(2)}, u32[]{:S(2)}) async-start(bf16[4,2,96,256]{3,2,1,0:T(8,128)(2,1)} %broadcast_in_dim.22), calls=%async_computation.3 | async-start | bytes 786432 | tf_op jit(solution)/shard_map/all_to_all | solution.py:20
  105.1 16.8 %all-to-all-start.4 = ((bf16[4,48,1024]{2,1,0:T(8,128)(2,1)}), bf16[4,48,1024]{2,1,0:T(8,128)(2,1)S(1)}, u32[]{:S(2)}, u32[]{:S(2)}) async-start(bf16[4,48,1024]{2,1,0:T(8,128)(2,1)} %reshape.116), calls=%async_computation.4 | async-start | bytes 786432 | tf_op jit(solution)/shard_map/all_to_all | solution.py:20
  122.2 21.2 %collective-permute-start.2 = (bf16[192,256]{1,0:T(8,128)(2,1)S(1)}, bf16[192,256]{1,0:T(8,128)(2,1)S(1)}, u32[]{:S(2)}, u32[]{:S(2)}) collective-permute-start(bf16[192,256]{1,0:T(8,128)(2,1)S(1)} %get-tuple-element.20), channel_id=1, source_target_pairs={{0,48},{16,0},{32,16},{48,32},{1,49},{17,1},{33,17},{49,33},{2,50}... | collective-permute-start | bytes 294920 | tf_op jit(solution)/shard_map/ppermute | solution.py:86
  125.3 18.0 %collective-permute-start.3 = (bf16[192,256]{1,0:T(8,128)(2,1)S(1)}, bf16[192,256]{1,0:T(8,128)(2,1)S(1)}, u32[]{:S(2)}, u32[]{:S(2)}) collective-permute-start(bf16[192,256]{1,0:T(8,128)(2,1)S(1)} %get-tuple-element.19), channel_id=1, source_target_pairs={{0,32},{16,48},{32,0},{48,16},{1,33},{17,49},{33,1},{49,17},{2,34}... | collective-permute-start | bytes 294920 | tf_op jit(solution)/shard_map/ppermute | solution.py:86
  129.0 14.4 %collective-permute-start.4 = (bf16[192,256]{1,0:T(8,128)(2,1)S(1)}, bf16[192,256]{1,0:T(8,128)(2,1)S(1)}, u32[]{:S(2)}, u32[]{:S(2)}) collective-permute-start(bf16[192,256]{1,0:T(8,128)(2,1)S(1)} %get-tuple-element.17), channel_id=1, source_target_pairs={{0,16},{16,32},{32,48},{48,0},{1,17},{17,33},{33,49},{49,1},{2,18}... | collective-permute-start | bytes 294920 | tf_op jit(solution)/shard_map/ppermute | solution.py:86
  132.3 24.4 %all-to-all-start.5 = ((bf16[4,24,512]{2,1,0:T(8,128)(2,1)}), bf16[4,24,512]{2,1,0:T(8,128)(2,1)S(1)}, u32[]{:S(2)}, u32[]{:S(2)}) async-start(bf16[4,24,512]{2,1,0:T(8,128)(2,1)} %copy.50), calls=%async_computation.5 | async-start | bytes 196608 | tf_op jit(solution)/shard_map/all_to_all | solution.py:20
  143.6 3.2 %copy-start.4 = (bf16[4,384,1024]{2,1,0:T(8,128)(2,1)S(1)}, bf16[4,384,1024]{2,1,0:T(8,128)(2,1)}, u32[]{:S(2)}) copy-start(bf16[4,384,1024]{2,1,0:T(8,128)(2,1)} %all-gather.5.cloned.1.call-done) | copy-start | bytes 9437188
Sparse Core Ops, SparseCore 0:
  10.7 60.1 all-gather.6
  86.0 51.0 all-gather.4

commit v5 on v4

--- a/solution.py
+++ b/solution.py
@@ -46,40 +46,45 @@
 
 
 def local(inputs, out_grad, preact, up_weight, down_weight):
-    core, at_x = lax.axis_index("c"), lax.axis_index("x")
-    up_rows = up_weight.reshape(4, 256, 256).swapaxes(0, 1).reshape(256, 1024)
+    core, at_x, at_y = lax.axis_index("c"), lax.axis_index("x"), lax.axis_index("y")
+    up_rows = jnp.concatenate([up_weight[256 * k : 256 * (k + 1)] for k in range(4)], axis=1)
     wide = lax.all_gather(jnp.concatenate([down_weight, up_rows]), "x", axis=0, tiled=False)
     wide_down, wide_up = wide[:, :256], wide[:, 256:].reshape(4, 256, 4, 256)
 
     both = jnp.concatenate([halves_down(out_grad), halves_down(inputs)], axis=0)
     both = spread(both, "za")
     rows_first = preact.reshape(2, 4, 12, 256).transpose(1, 0, 2, 3).reshape(96, 256)
-    swap = [(4 * a + b, 4 * b + a) for a in range(4) for b in range(4)]
-    turned = lax.ppermute(rows_first, ("y", "x"), swap)
+    turned = [
+        lax.ppermute(
+            rows_first,
+            ("y", "x"),
+            [(4 * a + b, 4 * ((b - k) % 4) + a) for a in range(4) for b in range(4)],
+        )
+        for k in range(4)
+    ]
     both, turned = lax.optimization_barrier((both, turned))
+    turned = turn_by(jnp.stack(turned), (4 - at_y) % 4)
     both = halves_across(both.reshape(4, 2, 24, 512)).swapaxes(0, 1).reshape(96, 1024)
     both = spread(both, "zb").reshape(4, 2, 48, 1024).swapaxes(0, 1).reshape(2, 192, 1024)
-    grads, ins = both[0], both[1]
+    grads = both[0]
 
     partial = jnp.einsum("td,xfd->xtf", grads, wide_down, preferred_element_type=F32)
     partial = partial.reshape(4, 4, 2, 24, 256)
     mine = lax.dynamic_index_in_dim(partial, core, axis=2, keepdims=False)
     theirs = lax.dynamic_index_in_dim(partial, 1 - core, axis=2, keepdims=False)
-    pair = mine + lax.ppermute(theirs, "c", [(0, 1), (1, 0)])
-    hidden_grad = exchange(pair.reshape(4, 96, 256), "y").sum(0)
-
+    pair = (mine + lax.ppermute(theirs, "c", [(0, 1), (1, 0)])).astype(BF).reshape(4, 96, 256)
+    activ, _ = gelu_parts(rows_first)
+    own = spread(jnp.concatenate([pair, activ.astype(BF)[None]]), "y")
+    hidden_grad = own[:, :4].astype(F32).sum(0)
     _, slope = gelu_parts(turned)
-    activ, _ = gelu_parts(rows_first)
-    own = spread(jnp.stack([(hidden_grad * slope).astype(BF), activ.astype(BF)]), "y")
-    own = lax.all_gather(own, "c", axis=0, tiled=False).reshape(2, 4, 2, 4, 24, 256)
-    own = own.transpose(2, 1, 3, 0, 4, 5).reshape(2, 4, 192, 256)
+    own = jnp.concatenate([(hidden_grad * slope).astype(BF), own[:, 4]])
+    own = lax.all_gather(own, "c", axis=0, tiled=False).reshape(2, 2, 4, 4, 24, 256)
+    own = own.transpose(1, 2, 3, 0, 4, 5).reshape(2, 4, 192, 256)
     pregrad, all_activ = own[0], own[1]
 
     part = jnp.einsum("xtf,xrkf->tkr", pregrad, wide_up, preferred_element_type=F32)
-    part = exchange(part.astype(BF).reshape(4, 48, 1024), "zb")
-    part = part.astype(F32).sum(0)
-    part, pregrad = lax.optimization_barrier((part, pregrad))
-    part = exchange(halves_down(part.astype(BF).reshape(4, 12, 1024)), "za")
+    part = part.astype(BF).reshape(4, 4, 12, 1024).swapaxes(0, 1)
+    part = exchange(halves_down(part.reshape(16, 12, 1024)), ("za", "zb"))
     input_grad = halves_across(part.astype(F32).sum(0)).astype(BF)
 
     pregrad = turn_by(pregrad, at_x)
@@ -89,9 +94,7 @@
     all_both = lax.all_gather(both.reshape(384, 1024), "x", axis=0, tiled=False)
     all_both = all_both.reshape(4, 2, 192, 1024)
     down_grad = jnp.einsum("xtf,xtd->fd", all_activ, all_both[:, 0], preferred_element_type=F32)
-    up_grad = jnp.einsum(
-        "xtd,xtf->df", all_both[:, 1], all_pregrad, preferred_element_type=F32
-    )
+    up_grad = jnp.einsum("xtd,xtf->df", all_both[:, 1], all_pregrad, preferred_element_type=F32)
     return (input_grad, up_grad, down_grad)
 
 

time: 167 us -> 156 us (0.934)
  waiting for transfers between devices: 65.1 us -> 49.4 us
  local copies, waits for them, and re-layouts: 10.6 us -> 12.9 us
  starting transfers between devices: 61.5 us -> 63.8 us
    all_to_all x6 -> x4, waiting for transfers between devices: 54.2 us -> 36.6 us  [exchange(): lax.all_to_all(blocks, axis, split_axis=0, concat_axis=0, tiled=False)]
    ppermute x2 -> x5, starting transfers between devices: 6.25 us -> 16.8 us  [the longest x4 14.9 us: local(): lax.ppermute(rows_first, ('y', 'x'), [(4 * a + b, 4 * ((b - k) % 4) + a)...]
    all_to_all x6 -> x4, starting transfers between devices: 46 us -> 37.9 us  [exchange(): lax.all_to_all(blocks, axis, split_axis=0, concat_axis=0, tiled=False)]
    ppermute x3, waiting for transfers between devices: 0.01 us -> 3.51 us  [local(): lax.ppermute(pregrad[k], 'x', shift(k))]
    reshape x2 -> x1, local copies, waits for them, and re-layouts: 2.51 us -> 0.25 us  [local(): part = part.astype(BF).reshape(4, 4, 12, 1024).swapaxes(0, 1)]
    unnamed x18 -> x27, local copies, waits for them, and re-layouts: 0.81 us -> 2.54 us
    ppermute x2 -> x5, waiting for transfers between devices: 7.19 us -> 6.6 us  [the longest x4 5.95 us: local(): lax.ppermute(rows_first, ('y', 'x'), [(4 * a + b, 4 * ((b - k) % 4) + a)...]
  transfers between devices with their start and end apart: 13 -> 14, of which waited for: 9 -> 9; matrix products, arithmetic and copies ran while one was open for 9% -> 11% of each run, Pallas kernels for 0% -> 0%
where the time goes in v5:
time: 156 us; the launch traced here: 154 us
  starting transfers between devices  63.8 us (41%)
  waiting for transfers between devices  49.4 us (32%)
  between operations  14.7 us (9%)
  local copies, waits for them, and re-layouts  12.9 us (8%)
  matrix products  7.99 us (5%)
  other arithmetic  2.83 us (2%)
  blocking collectives  2.37 us (2%)
    all_to_all x4, starting transfers between devices, exchange(): lax.all_to_all(blocks, axis, split_axis=0, concat_axis=0, tiled=False)  37.9 us
    all_to_all x4, waiting for transfers between devices, exchange(): lax.all_to_all(blocks, axis, split_axis=0, concat_axis=0, tiled=False)  36.6 us
    ppermute x4, starting transfers between devices, local(): lax.ppermute(rows_first, ('y', 'x'), [(4 * a + b, 4 * ((b - k) % 4) + a)...  14.9 us
    ppermute x3, starting transfers between devices, local(): lax.ppermute(pregrad[k], 'x', shift(k))  9.02 us
    ppermute x4, waiting for transfers between devices, local(): lax.ppermute(rows_first, ('y', 'x'), [(4 * a + b, 4 * ((b - k) % 4) + a)...  5.95 us
    ppermute x3, waiting for transfers between devices, local(): lax.ppermute(pregrad[k], 'x', shift(k))  3.51 us
    dot_general x1, matrix products, local(): jnp.einsum('xtf,xtd->fd', all_activ, all_both[:, 0], preferred_element_ty...  3.14 us
  transfers between devices with their start and end apart: 14, of which 9 were waited for; matrix products, arithmetic and copies ran while one was open for 11% of the time, Pallas kernels for 0%

profile of v5, /device:TPU:24, one launch (start us, length us, event | category | flops | bytes accessed | tf_op | source)
XLA Modules:
  0.0 154.0 jit_solution(937148891203567658)
XLA Ops:
  7.2 1.1 fusion.29
  8.4 2.2 %maximum_maximum_fusion = bf16[512,1024]{1,0:T(8,128)(2,1)} fusion(bf16[256,256]{1,0:T(8,128)(2,1)S(1)} %get-tuple-element.21, bf16[256,256]{1,0:T(8,128)(2,1)S(1)} %get-tuple-element.22, bf16[256,256]{1,0:T(8,128)(2,1)S(1)} %get-tuple-element.20, bf16[256,256]{1,0:T(8,128)(2,1)S(1)} %get-tuple-element.19, bf16[256,1024]{1,0:T(8,128)(2,1)} %param.9), kind=kLoop, calls=%fused_computation.15 | loop fusion | flops 5242880 | bytes 2097152 | tf_op jit(solution)/shard_map/concatenate | solution.py:51
  10.7 0.7 broadcast_in_dim.8
  11.4 15.1 %all-to-all-start = ((bf16[4,48,512]{2,1,0:T(8,128)(2,1)}), bf16[4,48,512]{2,1,0:T(8,128)(2,1)S(1)}, u32[]{:S(2)}, u32[]{:S(2)}) async-start(bf16[4,48,512]{2,1,0:T(8,128)(2,1)} %broadcast_in_dim.8), calls=%async_computation | async-start | bytes 393216 | tf_op jit(solution)/shard_map/all_to_all | solution.py:20
  26.6 4.3 %collective-permute-start = (bf16[96,256]{1,0:T(8,128)(2,1)S(1)}, bf16[96,256]{1,0:T(8,128)(2,1)S(1)}, u32[]{:S(2)}, u32[]{:S(2)}) collective-permute-start(bf16[96,256]{1,0:T(8,128)(2,1)S(1)} %reshape.103), channel_id=1, source_target_pairs={{0,0},{16,128},{32,256},{48,384},{128,16},{144,144},{160,272},{176... | collective-permute-start | bytes 147464 | tf_op jit(solution)/shard_map/ppermute | solution.py:58
  30.9 1.9 %collective-permute-start.1 = (bf16[96,256]{1,0:T(8,128)(2,1)S(1)}, bf16[96,256]{1,0:T(8,128)(2,1)S(1)}, u32[]{:S(2)}, u32[]{:S(2)}) collective-permute-start(bf16[96,256]{1,0:T(8,128)(2,1)S(1)} %reshape.103), channel_id=1, source_target_pairs={{0,384},{16,0},{32,128},{48,256},{128,400},{144,16},{160,144},{176... | collective-permute-start | bytes 147464 | tf_op jit(solution)/shard_map/ppermute | solution.py:58
  32.8 4.0 %collective-permute-start.2 = (bf16[96,256]{1,0:T(8,128)(2,1)S(1)}, bf16[96,256]{1,0:T(8,128)(2,1)S(1)}, u32[]{:S(2)}, u32[]{:S(2)}) collective-permute-start(bf16[96,256]{1,0:T(8,128)(2,1)S(1)} %reshape.103), channel_id=1, source_target_pairs={{0,256},{16,384},{32,0},{48,128},{128,272},{144,400},{160,16},{176... | collective-permute-start | bytes 147464 | tf_op jit(solution)/shard_map/ppermute | solution.py:58
  36.8 4.6 %collective-permute-start.3 = (bf16[96,256]{1,0:T(8,128)(2,1)S(1)}, bf16[96,256]{1,0:T(8,128)(2,1)S(1)}, u32[]{:S(2)}, u32[]{:S(2)}) collective-permute-start(bf16[96,256]{1,0:T(8,128)(2,1)S(1)} %reshape.103), channel_id=1, source_target_pairs={{0,128},{16,256},{32,384},{48,0},{128,144},{144,272},{160,400},{17... | collective-permute-start | bytes 147464 | tf_op jit(solution)/shard_map/ppermute | solution.py:58
  41.5 0.5 collective-permute-done.2
  41.9 5.5 %collective-permute-done.3 = bf16[96,256]{1,0:T(8,128)(2,1)S(1)} collective-permute-done((bf16[96,256]{1,0:T(8,128)(2,1)S(1)}, bf16[96,256]{1,0:T(8,128)(2,1)S(1)}, u32[]{:S(2)}, u32[]{:S(2)}) %collective-permute-start.3) | collective-permute-done | bytes 49184 | tf_op jit(solution)/shard_map/ppermute | solution.py:58
  47.4 0.2 copy.43
  47.6 0.2 copy.44
  47.8 0.1 reshape.104
  48.0 1.0 broadcast_in_dim.10
  49.0 3.5 %all-to-all-start.1 = ((bf16[4,96,1024]{2,1,0:T(8,128)(2,1)}), bf16[4,96,1024]{2,1,0:T(8,128)(2,1)S(1)}, u32[]{:S(2)}, u32[]{:S(2)}) async-start(bf16[4,96,1024]{2,1,0:T(8,128)(2,1)} %broadcast_in_dim.10), calls=%async_computation.1 | async-start | bytes 1572864 | tf_op jit(solution)/shard_map/all_to_all | solution.py:20
  52.7 18.2 %all-to-all-done.1 = bf16[4,96,1024]{2,1,0:T(8,128)(2,1)S(1)} async-done(((bf16[4,96,1024]{2,1,0:T(8,128)(2,1)}), bf16[4,96,1024]{2,1,0:T(8,128)(2,1)S(1)}, u32[]{:S(2)}, u32[]{:S(2)}) %all-to-all-start.1) | async-done | bytes 786464 | tf_op jit(solution)/shard_map/all_to_all | solution.py:20
  70.9 2.6 %all-gather.7.cloned.1.call-done = bf16[2048,1024]{1,0:T(8,128)(2,1)} async-done(((bf16[512,1024]{1,0:T(8,128)(2,1)}), bf16[2048,1024]{1,0:T(8,128)(2,1)}) %all-gather.7.cloned.1.call-update) | async-done | bytes 4194320 | tf_op jit(solution)/shard_map/all_gather | solution.py:51
  73.6 2.4 %fusion.3 = f32[4,256,192]{1,2,0:T(8,128)S(1)} fusion(bf16[192,1024,1]{1,0,2:T(8,128)(2,1)S(1)} %bitcast.141, bf16[4,512,1024]{2,1,0:T(8,128)(2,1)} %bitcast.132), kind=kOutput, calls=%fused_computation.3 | convolution fusion | flops 402653184 | bytes 3276800 | tf_op jit(solution)/shard_map/td,xfd->xtf/dot_general | solution.py:71
  76.1 1.9 %collective-permute-start.4 = (f32[4,4,24,256]{3,2,1,0:T(8,128)S(1)}, f32[4,4,24,256]{3,2,1,0:T(8,128)S(1)}, u32[]{:S(2)}, u32[]{:S(2)}) collective-permute-start(f32[4,4,24,256]{3,2,1,0:T(8,128)S(1)} %dynamic-slice_bitcast_fusion), channel_id=1, source_target_pairs={{0,64},{64,0},{1,65},{65,1},{2,66},{66,2},{3,67},{67,3},{4,68},{68... | collective-permute-start | bytes 1179656 | tf_op jit(solution)/shard_map/ppermute | solution.py:75
  78.0 1.0 copy.55
  79.0 0.6 collective-permute-done.4
  79.8 1.0 broadcast_in_dim.11
  80.8 7.3 %all-to-all-start.2 = ((bf16[4,5,96,256]{3,2,1,0:T(8,128)(2,1)}), bf16[4,5,96,256]{3,2,1,0:T(8,128)(2,1)S(1)}, u32[]{:S(2)}, u32[]{:S(2)}) async-start(bf16[4,5,96,256]{3,2,1,0:T(8,128)(2,1)} %broadcast_in_dim.11), calls=%async_computation.2 | async-start | bytes 1966080 | tf_op jit(solution)/shard_map/all_to_all | solution.py:20
  88.1 1.8 %slice.84 = bf16[4,256,1024]{2,1,0:T(8,128)(2,1)S(1)} slice(bf16[4,512,1024]{2,1,0:T(8,128)(2,1)} %bitcast.133), slice={[0:4], [256:512], [0:1024]} | slice | bytes 4194304 | tf_op jit(solution)/shard_map/slice | solution.py:52
  89.9 11.1 %all-to-all-done.2 = bf16[4,5,96,256]{3,2,1,0:T(8,128)(2,1)S(1)} async-done(((bf16[4,5,96,256]{3,2,1,0:T(8,128)(2,1)}), bf16[4,5,96,256]{3,2,1,0:T(8,128)(2,1)S(1)}, u32[]{:S(2)}, u32[]{:S(2)}) %all-to-all-start.2) | async-done | bytes 983072 | tf_op jit(solution)/shard_map/all_to_all | solution.py:20
  101.0 0.1 convert_reduce_fusion
  101.2 0.2 fusion.27
  101.4 2.4 %all-gather.1 = bf16[16,96,256]{2,1,0:T(8,128)(2,1)S(1)} all-gather(bf16[8,96,256]{2,1,0:T(8,128)(2,1)S(1)} %pad_maximum_fusion), channel_id=3, replica_groups=mesh['y'=4,'c'=2,'x'=4,'za'=4,'zb'=4] {'c'}, dimensions={0}, use_global_device_ids=true | all-gather | bytes 1179648 | tf_op jit(solution)/shard_map/all_gather | solution.py:81
  103.9 0.1 fusion.25
  104.1 0.8 slice_bitcast_fusion.9
  104.8 2.8 %collective-permute-start.5 = (bf16[192,256]{1,0:T(8,128)(2,1)}, bf16[192,256]{1,0:T(8,128)(2,1)}, u32[]{:S(2)}, u32[]{:S(2)}) collective-permute-start(bf16[192,256]{1,0:T(8,128)(2,1)} %get-tuple-element.26), channel_id=1, source_target_pairs={{0,48},{16,0},{32,16},{48,32},{1,49},{17,1},{33,17},{49,33},{2,50}... | collective-permute-start | bytes 294920 | tf_op jit(solution)/shard_map/ppermute | solution.py:91
  107.6 0.8 fusion.15
  108.5 0.3 copy.50
  108.8 0.2 reshape.109
  109.1 0.3 copy.51
  109.4 0.2 reshape_reshape.7
  109.6 1.0 copy.53
  110.6 12.0 %all-to-all-start.3 = ((bf16[16,24,512]{2,1,0:T(8,128)(2,1)}), bf16[16,24,512]{2,1,0:T(8,128)(2,1)S(1)}, u32[]{:S(2)}, u32[]{:S(2)}) async-start(bf16[16,24,512]{2,1,0:T(8,128)(2,1)} %copy.53), calls=%async_computation.3 | async-start | bytes 786432 | tf_op jit(solution)/shard_map/all_to_all | solution.py:20
  122.6 2.9 %collective-permute-start.6 = (bf16[192,256]{1,0:T(8,128)(2,1)S(1)}, bf16[192,256]{1,0:T(8,128)(2,1)S(1)}, u32[]{:S(2)}, u32[]{:S(2)}) collective-permute-start(bf16[192,256]{1,0:T(8,128)(2,1)S(1)} %copy-done.2), channel_id=1, source_target_pairs={{0,32},{16,48},{32,0},{48,16},{1,33},{17,49},{33,1},{49,17},{2,34}... | collective-permute-start | bytes 294920 | tf_op jit(solution)/shard_map/ppermute | solution.py:91
  125.6 3.3 %collective-permute-start.7 = (bf16[192,256]{1,0:T(8,128)(2,1)S(1)}, bf16[192,256]{1,0:T(8,128)(2,1)S(1)}, u32[]{:S(2)}, u32[]{:S(2)}) collective-permute-start(bf16[192,256]{1,0:T(8,128)(2,1)S(1)} %copy-done.1), channel_id=1, source_target_pairs={{0,16},{16,32},{32,48},{48,0},{1,17},{17,33},{33,49},{49,1},{2,18}... | collective-permute-start | bytes 294920 | tf_op jit(solution)/shard_map/ppermute | solution.py:91
  129.0 0.9 bitcast_dynamic-update-slice_fusion.3
  129.9 1.5 collective-permute-done.6
  131.3 2.1 %collective-permute-done.7 = bf16[192,256]{1,0:T(8,128)(2,1)S(1)} collective-permute-done((bf16[192,256]{1,0:T(8,128)(2,1)S(1)}, bf16[192,256]{1,0:T(8,128)(2,1)S(1)}, u32[]{:S(2)}, u32[]{:S(2)}) %collective-permute-start.7) | collective-permute-done | bytes 98336 | tf_op jit(solution)/shard_map/ppermute | solution.py:91
  133.4 0.9 bitcast_dynamic-update-slice_fusion.4
  134.4 3.1 %fusion.8 = f32[256,1024]{1,0:T(8,128)} fusion(bf16[4,192,256]{2,1,0:T(8,128)(2,1)S(1)} %bitcast.140, bf16[4,2,192,1024]{3,2,1,0:T(8,128)(2,1)} %bitcast.147), kind=kOutput, calls=%fused_computation.11 | convolution fusion | flops 402653184 | bytes 3014656 | tf_op jit(solution)/shard_map/xtf,xtd->fd/dot_general | solution.py:96
  137.5 1.6 %fusion.7 = f32[1024,256]{1,0:T(8,128)} fusion(bf16[4,192,256]{2,1,0:T(8,128)(2,1)S(1)} %constant_dynamic-slice_fusion, bf16[4,2,192,1024]{3,2,1,0:T(8,128)(2,1)S(1)} %bitcast.148), kind=kOutput, calls=%fused_computation.10 | convolution fusion | flops 402653184 | bytes 3014656 | tf_op jit(solution)/shard_map/xtd,xtf->df/dot_general | solution.py:97
  139.1 7.3 %all-to-all-done.3 = bf16[16,24,512]{2,1,0:T(8,128)(2,1)S(1)} async-done(((bf16[16,24,512]{2,1,0:T(8,128)(2,1)}), bf16[16,24,512]{2,1,0:T(8,128)(2,1)S(1)}, u32[]{:S(2)}, u32[]{:S(2)}) %all-to-all-start.3) | async-done | bytes 393248 | tf_op jit(solution)/shard_map/all_to_all | solution.py:20
  146.6 0.6 copy.65
  (67 shorter events, 1.1 us)
Async XLA Ops:
  7.2 3.4 %copy-start.4 = (bf16[12,1024]{1,0:T(8,128)(2,1)S(1)}, bf16[12,1024]{1,0:T(8,128)(2,1)}, u32[]{:S(2)}) copy-start(bf16[12,1024]{1,0:T(8,128)(2,1)} %param.5) | copy-start | bytes 73732
  7.2 3.5 %copy-start.5 = (bf16[12,1024]{1,0:T(8,128)(2,1)S(1)}, bf16[12,1024]{1,0:T(8,128)(2,1)}, u32[]{:S(2)}) copy-start(bf16[12,1024]{1,0:T(8,128)(2,1)} %param.6) | copy-start | bytes 73732
  7.2 66.4 %all-gather.7.cloned.1.call-start = ((), (), s32[]{:S(2)}) async-start(), calls=%async_computation.5 | async-start | bytes 5242880 | tf_op jit(solution)/shard_map/all_gather | solution.py:51
  8.4 18.1 %copy-start.3 = (bf16[96,256]{1,0:T(8,128)(2,1)S(1)}, bf16[96,256]{1,0:T(8,128)(2,1)}, u32[]{:S(2)}) copy-start(bf16[96,256]{1,0:T(8,128)(2,1)} %param.7) | copy-start | bytes 147460
  11.4 36.0 %all-to-all-start = ((bf16[4,48,512]{2,1,0:T(8,128)(2,1)}), bf16[4,48,512]{2,1,0:T(8,128)(2,1)S(1)}, u32[]{:S(2)}, u32[]{:S(2)}) async-start(bf16[4,48,512]{2,1,0:T(8,128)(2,1)} %broadcast_in_dim.8), calls=%async_computation | async-start | bytes 393216 | tf_op jit(solution)/shard_map/all_to_all | solution.py:20
  26.6 14.9 %collective-permute-start = (bf16[96,256]{1,0:T(8,128)(2,1)S(1)}, bf16[96,256]{1,0:T(8,128)(2,1)S(1)}, u32[]{:S(2)}, u32[]{:S(2)}) collective-permute-start(bf16[96,256]{1,0:T(8,128)(2,1)S(1)} %reshape.103), channel_id=1, source_target_pairs={{0,0},{16,128},{32,256},{48,384},{128,16},{144,144},{160,272},{176... | collective-permute-start | bytes 147464 | tf_op jit(solution)/shard_map/ppermute | solution.py:58
  30.9 10.6 %collective-permute-start.1 = (bf16[96,256]{1,0:T(8,128)(2,1)S(1)}, bf16[96,256]{1,0:T(8,128)(2,1)S(1)}, u32[]{:S(2)}, u32[]{:S(2)}) collective-permute-start(bf16[96,256]{1,0:T(8,128)(2,1)S(1)} %reshape.103), channel_id=1, source_target_pairs={{0,384},{16,0},{32,128},{48,256},{128,400},{144,16},{160,144},{176... | collective-permute-start | bytes 147464 | tf_op jit(solution)/shard_map/ppermute | solution.py:58
  32.8 9.1 %collective-permute-start.2 = (bf16[96,256]{1,0:T(8,128)(2,1)S(1)}, bf16[96,256]{1,0:T(8,128)(2,1)S(1)}, u32[]{:S(2)}, u32[]{:S(2)}) collective-permute-start(bf16[96,256]{1,0:T(8,128)(2,1)S(1)} %reshape.103), channel_id=1, source_target_pairs={{0,256},{16,384},{32,0},{48,128},{128,272},{144,400},{160,16},{176... | collective-permute-start | bytes 147464 | tf_op jit(solution)/shard_map/ppermute | solution.py:58
  36.8 10.6 %collective-permute-start.3 = (bf16[96,256]{1,0:T(8,128)(2,1)S(1)}, bf16[96,256]{1,0:T(8,128)(2,1)S(1)}, u32[]{:S(2)}, u32[]{:S(2)}) collective-permute-start(bf16[96,256]{1,0:T(8,128)(2,1)S(1)} %reshape.103), channel_id=1, source_target_pairs={{0,128},{16,256},{32,384},{48,0},{128,144},{144,272},{160,400},{17... | collective-permute-start | bytes 147464 | tf_op jit(solution)/shard_map/ppermute | solution.py:58
  49.0 21.9 %all-to-all-start.1 = ((bf16[4,96,1024]{2,1,0:T(8,128)(2,1)}), bf16[4,96,1024]{2,1,0:T(8,128)(2,1)S(1)}, u32[]{:S(2)}, u32[]{:S(2)}) async-start(bf16[4,96,1024]{2,1,0:T(8,128)(2,1)} %broadcast_in_dim.10), calls=%async_computation.1 | async-start | bytes 1572864 | tf_op jit(solution)/shard_map/all_to_all | solution.py:20
  52.5 81.9 %all-gather.5.cloned.1.call-start = ((), (), s32[]{:S(2)}) async-start(), calls=%async_computation.4 | async-start | bytes 3932160 | tf_op jit(solution)/shard_map/all_gather | solution.py:94
  76.1 3.6 %collective-permute-start.4 = (f32[4,4,24,256]{3,2,1,0:T(8,128)S(1)}, f32[4,4,24,256]{3,2,1,0:T(8,128)S(1)}, u32[]{:S(2)}, u32[]{:S(2)}) collective-permute-start(f32[4,4,24,256]{3,2,1,0:T(8,128)S(1)} %dynamic-slice_bitcast_fusion), channel_id=1, source_target_pairs={{0,64},{64,0},{1,65},{65,1},{2,66},{66,2},{3,67},{67,3},{4,68},{68... | collective-permute-start | bytes 1179656 | tf_op jit(solution)/shard_map/ppermute | solution.py:75
  80.8 20.2 %all-to-all-start.2 = ((bf16[4,5,96,256]{3,2,1,0:T(8,128)(2,1)}), bf16[4,5,96,256]{3,2,1,0:T(8,128)(2,1)S(1)}, u32[]{:S(2)}, u32[]{:S(2)}) async-start(bf16[4,5,96,256]{3,2,1,0:T(8,128)(2,1)} %broadcast_in_dim.11), calls=%async_computation.2 | async-start | bytes 1966080 | tf_op jit(solution)/shard_map/all_to_all | solution.py:20
  104.8 24.1 %collective-permute-start.5 = (bf16[192,256]{1,0:T(8,128)(2,1)}, bf16[192,256]{1,0:T(8,128)(2,1)}, u32[]{:S(2)}, u32[]{:S(2)}) collective-permute-start(bf16[192,256]{1,0:T(8,128)(2,1)} %get-tuple-element.26), channel_id=1, source_target_pairs={{0,48},{16,0},{32,16},{48,32},{1,49},{17,1},{33,17},{49,33},{2,50}... | collective-permute-start | bytes 294920 | tf_op jit(solution)/shard_map/ppermute | solution.py:91
  109.0 13.6 %copy-start.2 = (bf16[192,256]{1,0:T(8,128)(2,1)S(1)}, bf16[192,256]{1,0:T(8,128)(2,1)}, u32[]{:S(2)}) copy-start(bf16[192,256]{1,0:T(8,128)(2,1)} %get-tuple-element.25) | copy-start | bytes 294916
  109.0 16.5 %copy-start.1 = (bf16[192,256]{1,0:T(8,128)(2,1)S(1)}, bf16[192,256]{1,0:T(8,128)(2,1)}, u32[]{:S(2)}) copy-start(bf16[192,256]{1,0:T(8,128)(2,1)} %get-tuple-element.23) | copy-start | bytes 294916
  109.4 19.6 %copy-start = (bf16[7,192,256]{2,1,0:T(8,128)(2,1)S(1)}, bf16[7,192,256]{2,1,0:T(8,128)(2,1)}, u32[]{:S(2)}) copy-start(bf16[7,192,256]{2,1,0:T(8,128)(2,1)} %get-tuple-element.24) | copy-start | bytes 2064388
  110.6 35.9 %all-to-all-start.3 = ((bf16[16,24,512]{2,1,0:T(8,128)(2,1)}), bf16[16,24,512]{2,1,0:T(8,128)(2,1)S(1)}, u32[]{:S(2)}, u32[]{:S(2)}) async-start(bf16[16,24,512]{2,1,0:T(8,128)(2,1)} %copy.53), calls=%async_computation.3 | async-start | bytes 786432 | tf_op jit(solution)/shard_map/all_to_all | solution.py:20
  122.6 8.7 %collective-permute-start.6 = (bf16[192,256]{1,0:T(8,128)(2,1)S(1)}, bf16[192,256]{1,0:T(8,128)(2,1)S(1)}, u32[]{:S(2)}, u32[]{:S(2)}) collective-permute-start(bf16[192,256]{1,0:T(8,128)(2,1)S(1)} %copy-done.2), channel_id=1, source_target_pairs={{0,32},{16,48},{32,0},{48,16},{1,33},{17,49},{33,1},{49,17},{2,34}... | collective-permute-start | bytes 294920 | tf_op jit(solution)/shard_map/ppermute | solution.py:91
  125.6 7.8 %collective-permute-start.7 = (bf16[192,256]{1,0:T(8,128)(2,1)S(1)}, bf16[192,256]{1,0:T(8,128)(2,1)S(1)}, u32[]{:S(2)}, u32[]{:S(2)}) collective-permute-start(bf16[192,256]{1,0:T(8,128)(2,1)S(1)} %copy-done.1), channel_id=1, source_target_pairs={{0,16},{16,32},{32,48},{48,0},{1,17},{17,33},{33,49},{49,1},{2,18}... | collective-permute-start | bytes 294920 | tf_op jit(solution)/shard_map/ppermute | solution.py:91
  134.4 3.1 %copy-start.6 = (bf16[4,384,1024]{2,1,0:T(8,128)(2,1)S(1)}, bf16[4,384,1024]{2,1,0:T(8,128)(2,1)}, u32[]{:S(2)}) copy-start(bf16[4,384,1024]{2,1,0:T(8,128)(2,1)} %all-gather.5.cloned.1.call-done) | copy-start | bytes 9437188
Sparse Core Ops, SparseCore 0:
  10.7 62.8 all-gather.6
  79.1 53.5 all-gather.4

commit v6 on v5

--- a/solution.py
+++ b/solution.py
@@ -40,54 +40,65 @@
     return [(i, (i + k) % 4) for i in range(4)]
 
 
+def near_x(block):
+    return lax.ppermute(block, "x", shift(1)), lax.ppermute(block, "x", shift(-1))
+
+
+def far_x(before, after):
+    half = before.shape[0] // 2
+    return jnp.concatenate(
+        [lax.ppermute(before[:half], "x", shift(1)), lax.ppermute(after[half:], "x", shift(-1))]
+    )
+
+
 def turn_by(blocks, start):
     twice = jnp.concatenate([blocks, blocks[:3]])
     return lax.dynamic_slice_in_dim(twice, start, 4, axis=0)
 
 
+def half_tokens(partial, at_x, half):
+    blocks = [
+        lax.dynamic_slice(partial, ((at_x + d) % 4, 0, half, 0, 0), (1, 4, 1, 24, 256)) for d in range(4)
+    ]
+    return jnp.concatenate(blocks).reshape(4, 96, 256)
+
+
 def local(inputs, out_grad, preact, up_weight, down_weight):
-    core, at_x, at_y = lax.axis_index("c"), lax.axis_index("x"), lax.axis_index("y")
-    up_rows = jnp.concatenate([up_weight[256 * k : 256 * (k + 1)] for k in range(4)], axis=1)
-    wide = lax.all_gather(jnp.concatenate([down_weight, up_rows]), "x", axis=0, tiled=False)
-    wide_down, wide_up = wide[:, :256], wide[:, 256:].reshape(4, 256, 4, 256)
+    core, at_x = lax.axis_index("c"), lax.axis_index("x")
+    wide_down = lax.all_gather(down_weight, "x", axis=0, tiled=False)
 
     both = jnp.concatenate([halves_down(out_grad), halves_down(inputs)], axis=0)
     both = spread(both, "za")
     rows_first = preact.reshape(2, 4, 12, 256).transpose(1, 0, 2, 3).reshape(96, 256)
-    turned = [
-        lax.ppermute(
-            rows_first,
-            ("y", "x"),
-            [(4 * a + b, 4 * ((b - k) % 4) + a) for a in range(4) for b in range(4)],
-        )
-        for k in range(4)
-    ]
+    swap = [(4 * a + b, 4 * ((b - a) % 4) + a) for a in range(4) for b in range(4)]
+    turned = lax.ppermute(rows_first, ("y", "x"), swap)
     both, turned = lax.optimization_barrier((both, turned))
-    turned = turn_by(jnp.stack(turned), (4 - at_y) % 4)
     both = halves_across(both.reshape(4, 2, 24, 512)).swapaxes(0, 1).reshape(96, 1024)
     both = spread(both, "zb").reshape(4, 2, 48, 1024).swapaxes(0, 1).reshape(2, 192, 1024)
     grads = both[0]
+    before, after = near_x(up_weight)
+    grads, before, after = lax.optimization_barrier((grads, before, after))
 
     partial = jnp.einsum("td,xfd->xtf", grads, wide_down, preferred_element_type=F32)
     partial = partial.reshape(4, 4, 2, 24, 256)
-    mine = lax.dynamic_index_in_dim(partial, core, axis=2, keepdims=False)
-    theirs = lax.dynamic_index_in_dim(partial, 1 - core, axis=2, keepdims=False)
-    pair = (mine + lax.ppermute(theirs, "c", [(0, 1), (1, 0)])).astype(BF).reshape(4, 96, 256)
+    theirs = lax.ppermute(half_tokens(partial, at_x, 1 - core), "c", [(0, 1), (1, 0)])
+    pair = (half_tokens(partial, at_x, core) + theirs).astype(BF)
     activ, _ = gelu_parts(rows_first)
-    own = spread(jnp.concatenate([pair, activ.astype(BF)[None]]), "y")
+    own = spread(jnp.concatenate([pair, activ.astype(BF)[None], turned[None]]), "y")
+    own, far = lax.optimization_barrier((own, far_x(before, after)))
     hidden_grad = own[:, :4].astype(F32).sum(0)
-    _, slope = gelu_parts(turned)
+    _, slope = gelu_parts(own[:, 5])
     own = jnp.concatenate([(hidden_grad * slope).astype(BF), own[:, 4]])
     own = lax.all_gather(own, "c", axis=0, tiled=False).reshape(2, 2, 4, 4, 24, 256)
     own = own.transpose(1, 2, 3, 0, 4, 5).reshape(2, 4, 192, 256)
     pregrad, all_activ = own[0], own[1]
 
-    part = jnp.einsum("xtf,xrkf->tkr", pregrad, wide_up, preferred_element_type=F32)
+    wide_up = jnp.stack([up_weight, after, far, before])
+    part = jnp.einsum("xtf,xdf->td", pregrad, wide_up, preferred_element_type=F32)
     part = part.astype(BF).reshape(4, 4, 12, 1024).swapaxes(0, 1)
     part = exchange(halves_down(part.reshape(16, 12, 1024)), ("za", "zb"))
     input_grad = halves_across(part.astype(F32).sum(0)).astype(BF)
 
-    pregrad = turn_by(pregrad, at_x)
     sent = [pregrad[0]] + [lax.ppermute(pregrad[k], "x", shift(k)) for k in (3, 2, 1)]
     all_pregrad = turn_by(jnp.stack(sent), (4 - at_x) % 4)
     all_pregrad, all_activ = lax.optimization_barrier((all_pregrad, all_activ))

time: 156 us -> 147 us (0.942)
  starting transfers between devices: 63.8 us -> 58.2 us
  local copies, waits for them, and re-layouts: 12.9 us -> 9.47 us
  other arithmetic: 2.83 us -> 0.61 us
  waiting for transfers between devices: 49.4 us -> 51.5 us
    ppermute x5 -> x6, waiting for transfers between devices: 6.6 us -> 18.8 us  [the longest x1 9.58 us: far_x(): lax.ppermute(before[:half], 'x', shift(1))]
    all_to_all x4, waiting for transfers between devices: 36.6 us -> 25.8 us  [exchange(): lax.all_to_all(blocks, axis, split_axis=0, concat_axis=0, tiled=False)]
    all_to_all x4, starting transfers between devices: 37.9 us -> 28.4 us  [exchange(): lax.all_to_all(blocks, axis, split_axis=0, concat_axis=0, tiled=False)]
    ppermute x5 -> x6, starting transfers between devices: 16.8 us -> 20.9 us  [the longest x1 5.34 us: local(): turned = lax.ppermute(rows_first, ('y', 'x'), swap)]
    slice x4 -> x7, local copies, waits for them, and re-layouts: 2.94 us -> 0.1 us  [the longest x4 0.05 us: local(): pregrad[k]]
    ppermute x3, waiting for transfers between devices: 3.51 us -> 6.21 us  [local(): lax.ppermute(pregrad[k], 'x', shift(k))]
    all_gather x1, waiting for transfers between devices: 2.64 us -> 0.02 us  [local(): wide_down = lax.all_gather(down_weight, 'x', axis=0, tiled=False)]
    concatenate x3 -> x4, other arithmetic: 2.34 us -> 0.13 us  [the longest x2 0.06 us: half_tokens(): return jnp.concatenate(blocks).reshape(4, 96, 256)]
  transfers between devices with their start and end apart: 14 -> 15, of which waited for: 9 -> 10; matrix products, arithmetic and copies ran while one was open for 11% -> 7% of each run, Pallas kernels for 0% -> 0%
where the time goes in v6:
time: 147 us; the launch traced here: 145 us
  starting transfers between devices  58.2 us (40%)
  waiting for transfers between devices  51.5 us (35%)
  between operations  14.6 us (10%)
  local copies, waits for them, and re-layouts  9.47 us (6%)
  matrix products  7.99 us (5%)
  blocking collectives  2.5 us (2%)
    all_to_all x4, starting transfers between devices, exchange(): lax.all_to_all(blocks, axis, split_axis=0, concat_axis=0, tiled=False)  28.4 us
    all_to_all x4, waiting for transfers between devices, exchange(): lax.all_to_all(blocks, axis, split_axis=0, concat_axis=0, tiled=False)  25.8 us
    ppermute x1, waiting for transfers between devices, far_x(): lax.ppermute(before[:half], 'x', shift(1))  9.58 us
    ppermute x3, starting transfers between devices, local(): lax.ppermute(pregrad[k], 'x', shift(k))  8.91 us
    ppermute x3, waiting for transfers between devices, local(): lax.ppermute(pregrad[k], 'x', shift(k))  6.21 us
    ppermute x1, starting transfers between devices, local(): turned = lax.ppermute(rows_first, ('y', 'x'), swap)  5.34 us
    ppermute x1, waiting for transfers between devices, local(): turned = lax.ppermute(rows_first, ('y', 'x'), swap)  4.72 us
    ppermute x1, starting transfers between devices, far_x(): lax.ppermute(after[half:], 'x', shift(-1))  4.66 us
  transfers between devices with their start and end apart: 15, of which 10 were waited for; matrix products, arithmetic and copies ran while one was open for 7% of the time, Pallas kernels for 0%

profile of v6, /device:TPU:24, one launch (start us, length us, event | category | flops | bytes accessed | tf_op | source)
XLA Modules:
  0.0 144.9 jit_solution(18085220060733374707)
XLA Ops:
  7.2 0.7 all-gather.7.cloned.1.call-update
  7.9 0.8 reshape.107
  8.7 0.8 reshape.105
  9.5 0.7 broadcast_in_dim.10
  10.2 15.1 %all-to-all-start = ((bf16[4,48,512]{2,1,0:T(8,128)(2,1)}), bf16[4,48,512]{2,1,0:T(8,128)(2,1)S(1)}, u32[]{:S(2)}, u32[]{:S(2)}) async-start(bf16[4,48,512]{2,1,0:T(8,128)(2,1)} %broadcast_in_dim.10), calls=%async_computation | async-start | bytes 393216 | tf_op jit(solution)/shard_map/all_to_all | solution.py:20
  25.3 0.8 reshape.109
  26.2 5.3 %collective-permute-start = (bf16[96,256]{1,0:T(8,128)(2,1)S(1)}, bf16[96,256]{1,0:T(8,128)(2,1)S(1)}, u32[]{:S(2)}, u32[]{:S(2)}) collective-permute-start(bf16[96,256]{1,0:T(8,128)(2,1)S(1)} %reshape.110), channel_id=1, source_target_pairs={{0,0},{16,128},{32,256},{48,384},{128,400},{144,16},{160,144},{176... | collective-permute-start | bytes 147464 | tf_op jit(solution)/shard_map/ppermute | solution.py:74
  31.5 4.7 %collective-permute-done = bf16[96,256]{1,0:T(8,128)(2,1)S(1)} collective-permute-done((bf16[96,256]{1,0:T(8,128)(2,1)S(1)}, bf16[96,256]{1,0:T(8,128)(2,1)S(1)}, u32[]{:S(2)}, u32[]{:S(2)}) %collective-permute-start) | collective-permute-done | bytes 49184 | tf_op jit(solution)/shard_map/ppermute | solution.py:74
  36.2 5.5 %all-to-all-done = bf16[4,48,512]{2,1,0:T(8,128)(2,1)S(1)} async-done(((bf16[4,48,512]{2,1,0:T(8,128)(2,1)}), bf16[4,48,512]{2,1,0:T(8,128)(2,1)S(1)}, u32[]{:S(2)}, u32[]{:S(2)}) %all-to-all-start) | async-done | bytes 196640 | tf_op jit(solution)/shard_map/all_to_all | solution.py:20
  41.7 0.2 copy.41
  41.9 0.2 copy.42
  42.1 0.1 reshape.111
  42.4 1.0 broadcast_in_dim.12
  43.3 4.7 %all-to-all-start.1 = ((bf16[4,96,1024]{2,1,0:T(8,128)(2,1)}), bf16[4,96,1024]{2,1,0:T(8,128)(2,1)S(1)}, u32[]{:S(2)}, u32[]{:S(2)}) async-start(bf16[4,96,1024]{2,1,0:T(8,128)(2,1)} %broadcast_in_dim.12), calls=%async_computation.1 | async-start | bytes 1572864 | tf_op jit(solution)/shard_map/all_to_all | solution.py:20
  48.1 3.4 %collective-permute-start.1 = (bf16[1024,256]{1,0:T(8,128)(2,1)S(1)}, bf16[1024,256]{1,0:T(8,128)(2,1)S(1)}, u32[]{:S(2)}, u32[]{:S(2)}) collective-permute-start(bf16[1024,256]{1,0:T(8,128)(2,1)S(1)} %copy-done.1), channel_id=1, source_target_pairs={{0,16},{16,32},{32,48},{48,0},{1,17},{17,33},{33,49},{49,1},{2,18}... | collective-permute-start | bytes 1572872 | tf_op jit(solution)/shard_map/ppermute | solution.py:44
  51.5 3.7 %collective-permute-start.2 = (bf16[1024,256]{1,0:T(8,128)(2,1)S(1)}, bf16[1024,256]{1,0:T(8,128)(2,1)S(1)}, u32[]{:S(2)}, u32[]{:S(2)}) collective-permute-start(bf16[1024,256]{1,0:T(8,128)(2,1)S(1)} %copy-done.1), channel_id=1, source_target_pairs={{0,48},{16,0},{32,16},{48,32},{1,49},{17,1},{33,17},{49,33},{2,50}... | collective-permute-start | bytes 1572872 | tf_op jit(solution)/shard_map/ppermute | solution.py:44
  55.2 11.4 %all-to-all-done.1 = bf16[4,96,1024]{2,1,0:T(8,128)(2,1)S(1)} async-done(((bf16[4,96,1024]{2,1,0:T(8,128)(2,1)}), bf16[4,96,1024]{2,1,0:T(8,128)(2,1)S(1)}, u32[]{:S(2)}, u32[]{:S(2)}) %all-to-all-start.1) | async-done | bytes 786464 | tf_op jit(solution)/shard_map/all_to_all | solution.py:20
  66.7 2.4 %fusion.26 = f32[192,4,256]{2,0,1:T(8,128)S(1)} fusion(bf16[4,256,1024]{2,1,0:T(8,128)(2,1)} %bitcast.103, bf16[192,1024]{1,0:T(8,128)(2,1)S(1)} %bitcast.104), kind=kOutput, calls=%fused_computation.34 | convolution fusion | flops 402653184 | bytes 3276800 | tf_op jit(solution)/shard_map/td,xfd->xtf/dot_general | solution.py:82
  69.2 0.1 constant_dynamic-slice_fusion.8
  69.3 1.9 %collective-permute-start.3 = (f32[4,96,256]{2,1,0:T(8,128)S(1)}, f32[4,96,256]{2,1,0:T(8,128)S(1)}, u32[]{:S(2)}, u32[]{:S(2)}) collective-permute-start(f32[4,96,256]{2,1,0:T(8,128)S(1)} %bitcast.114), channel_id=1, source_target_pairs={{0,64},{64,0},{1,65},{65,1},{2,66},{66,2},{3,67},{67,3},{4,68},{68... | collective-permute-start | bytes 1179656 | tf_op jit(solution)/shard_map/ppermute | solution.py:84
  71.3 0.9 copy.51
  72.3 0.6 collective-permute-done.3
  73.0 1.1 broadcast_in_dim.27
  74.1 4.7 %all-to-all-start.2 = ((bf16[4,6,96,256]{3,2,1,0:T(8,128)(2,1)}), bf16[4,6,96,256]{3,2,1,0:T(8,128)(2,1)S(1)}, u32[]{:S(2)}, u32[]{:S(2)}) async-start(bf16[4,6,96,256]{3,2,1,0:T(8,128)(2,1)} %broadcast_in_dim.27), calls=%async_computation.2 | async-start | bytes 2359296 | tf_op jit(solution)/shard_map/all_to_all | solution.py:20
  78.8 4.7 %collective-permute-start.5 = (bf16[512,256]{1,0:T(8,128)(2,1)S(1)}, bf16[512,256]{1,0:T(8,128)(2,1)S(1)}, u32[]{:S(2)}, u32[]{:S(2)}) collective-permute-start(bf16[512,256]{1,0:T(8,128)(2,1)S(1)} %slice.59), channel_id=1, source_target_pairs={{0,48},{16,0},{32,16},{48,32},{1,49},{17,1},{33,17},{49,33},{2,50}... | collective-permute-start | bytes 786440 | tf_op jit(solution)/shard_map/ppermute | solution.py:50
  83.5 1.9 %collective-permute-start.4 = (bf16[512,256]{1,0:T(8,128)(2,1)S(1)}, bf16[512,256]{1,0:T(8,128)(2,1)S(1)}, u32[]{:S(2)}, u32[]{:S(2)}) collective-permute-start(bf16[512,256]{1,0:T(8,128)(2,1)S(1)} %slice.58), channel_id=1, source_target_pairs={{0,16},{16,32},{32,48},{48,0},{1,17},{17,33},{33,49},{49,1},{2,18}... | collective-permute-start | bytes 786440 | tf_op jit(solution)/shard_map/ppermute | solution.py:50
  85.5 3.9 %collective-permute-done.5 = bf16[512,256]{1,0:T(8,128)(2,1)S(1)} collective-permute-done((bf16[512,256]{1,0:T(8,128)(2,1)S(1)}, bf16[512,256]{1,0:T(8,128)(2,1)S(1)}, u32[]{:S(2)}, u32[]{:S(2)}) %collective-permute-start.5) | collective-permute-done | bytes 262176 | tf_op jit(solution)/shard_map/ppermute | solution.py:50
  89.4 9.6 %collective-permute-done.4 = bf16[512,256]{1,0:T(8,128)(2,1)S(1)} collective-permute-done((bf16[512,256]{1,0:T(8,128)(2,1)S(1)}, bf16[512,256]{1,0:T(8,128)(2,1)S(1)}, u32[]{:S(2)}, u32[]{:S(2)}) %collective-permute-start.4) | collective-permute-done | bytes 262176 | tf_op jit(solution)/shard_map/ppermute | solution.py:50
  99.0 0.1 convert_reduce_fusion
  99.1 0.2 fusion.28
  99.4 2.5 %all-gather.1 = bf16[16,96,256]{2,1,0:T(8,128)(2,1)S(1)} all-gather(bf16[8,96,256]{2,1,0:T(8,128)(2,1)S(1)} %pad_maximum_fusion.3), channel_id=3, replica_groups=mesh['y'=4,'c'=2,'x'=4,'za'=4,'zb'=4] {'c'}, dimensions={0}, use_global_device_ids=true | all-gather | bytes 1179648 | tf_op jit(solution)/shard_map/all_gather | solution.py:92
  101.9 0.1 fusion.30
  102.0 0.8 fusion.15
  102.9 0.1 reshape.117
  103.0 0.3 copy.47
  103.3 0.2 reshape_reshape.7
  103.5 1.0 copy.49
  104.5 3.9 %all-to-all-start.3 = ((bf16[16,24,512]{2,1,0:T(8,128)(2,1)}), bf16[16,24,512]{2,1,0:T(8,128)(2,1)S(1)}, u32[]{:S(2)}, u32[]{:S(2)}) async-start(bf16[16,24,512]{2,1,0:T(8,128)(2,1)} %copy.49), calls=%async_computation.3 | async-start | bytes 786432 | tf_op jit(solution)/shard_map/all_to_all | solution.py:20
  108.4 3.0 %collective-permute-start.6 = (bf16[192,256]{1,0:T(8,128)(2,1)S(1)}, bf16[192,256]{1,0:T(8,128)(2,1)S(1)}, u32[]{:S(2)}, u32[]{:S(2)}) collective-permute-start(bf16[192,256]{1,0:T(8,128)(2,1)S(1)} %bitcast.122), channel_id=1, source_target_pairs={{0,48},{16,0},{32,16},{48,32},{1,49},{17,1},{33,17},{49,33},{2,50}... | collective-permute-start | bytes 294920 | tf_op jit(solution)/shard_map/ppermute | solution.py:102
  111.4 3.4 %collective-permute-start.7 = (bf16[192,256]{1,0:T(8,128)(2,1)S(1)}, bf16[192,256]{1,0:T(8,128)(2,1)S(1)}, u32[]{:S(2)}, u32[]{:S(2)}) collective-permute-start(bf16[192,256]{1,0:T(8,128)(2,1)S(1)} %bitcast.123), channel_id=1, source_target_pairs={{0,32},{16,48},{32,0},{48,16},{1,33},{17,49},{33,1},{49,17},{2,34}... | collective-permute-start | bytes 294920 | tf_op jit(solution)/shard_map/ppermute | solution.py:102
  114.9 2.5 %collective-permute-start.8 = (bf16[192,256]{1,0:T(8,128)(2,1)S(1)}, bf16[192,256]{1,0:T(8,128)(2,1)S(1)}, u32[]{:S(2)}, u32[]{:S(2)}) collective-permute-start(bf16[192,256]{1,0:T(8,128)(2,1)S(1)} %bitcast.124), channel_id=1, source_target_pairs={{0,16},{16,32},{32,48},{48,0},{1,17},{17,33},{33,49},{49,1},{2,18}... | collective-permute-start | bytes 294920 | tf_op jit(solution)/shard_map/ppermute | solution.py:102
  117.4 0.5 collective-permute-done.6
  118.0 3.0 %collective-permute-done.7 = bf16[192,256]{1,0:T(8,128)(2,1)S(1)} collective-permute-done((bf16[192,256]{1,0:T(8,128)(2,1)S(1)}, bf16[192,256]{1,0:T(8,128)(2,1)S(1)}, u32[]{:S(2)}, u32[]{:S(2)}) %collective-permute-start.7) | collective-permute-done | bytes 98336 | tf_op jit(solution)/shard_map/ppermute | solution.py:102
  121.0 2.7 %collective-permute-done.8 = bf16[192,256]{1,0:T(8,128)(2,1)S(1)} collective-permute-done((bf16[192,256]{1,0:T(8,128)(2,1)S(1)}, bf16[192,256]{1,0:T(8,128)(2,1)S(1)}, u32[]{:S(2)}, u32[]{:S(2)}) %collective-permute-start.8) | collective-permute-done | bytes 98336 | tf_op jit(solution)/shard_map/ppermute | solution.py:102
  123.8 8.9 %all-to-all-done.3 = bf16[16,24,512]{2,1,0:T(8,128)(2,1)S(1)} async-done(((bf16[16,24,512]{2,1,0:T(8,128)(2,1)}), bf16[16,24,512]{2,1,0:T(8,128)(2,1)S(1)}, u32[]{:S(2)}, u32[]{:S(2)}) %all-to-all-start.3) | async-done | bytes 393248 | tf_op jit(solution)/shard_map/all_to_all | solution.py:20
  132.8 0.6 copy.61
  133.4 3.1 %fusion.10 = f32[1024,256]{1,0:T(8,128)} fusion(bf16[4,192,256]{2,1,0:T(8,128)(2,1)S(1)} %constant_dynamic-slice_fusion, bf16[4,2,192,1024]{3,2,1,0:T(8,128)(2,1)} %bitcast.127), kind=kOutput, calls=%fused_computation.13 | convolution fusion | flops 402653184 | bytes 3014656 | tf_op jit(solution)/shard_map/xtd,xtf->df/dot_general | solution.py:108
  136.5 1.6 %fusion.11 = f32[256,1024]{1,0:T(8,128)} fusion(bf16[4,192,256]{2,1,0:T(8,128)(2,1)S(1)} %bitcast.113, bf16[4,2,192,1024]{3,2,1,0:T(8,128)(2,1)S(1)} %bitcast.128), kind=kOutput, calls=%fused_computation.14 | convolution fusion | flops 402653184 | bytes 3014656 | tf_op jit(solution)/shard_map/xtf,xtd->fd/dot_general | solution.py:107
  (57 shorter events, 1.0 us)
Async XLA Ops:
  7.2 59.6 %all-gather.7.cloned.1.call-start = ((), (), s32[]{:S(2)}) async-start(), calls=%async_computation.5 | async-start | bytes 2621440 | tf_op jit(solution)/shard_map/all_gather | solution.py:68
  10.2 31.5 %all-to-all-start = ((bf16[4,48,512]{2,1,0:T(8,128)(2,1)}), bf16[4,48,512]{2,1,0:T(8,128)(2,1)S(1)}, u32[]{:S(2)}, u32[]{:S(2)}) async-start(bf16[4,48,512]{2,1,0:T(8,128)(2,1)} %broadcast_in_dim.10), calls=%async_computation | async-start | bytes 393216 | tf_op jit(solution)/shard_map/all_to_all | solution.py:20
  26.2 10.1 %collective-permute-start = (bf16[96,256]{1,0:T(8,128)(2,1)S(1)}, bf16[96,256]{1,0:T(8,128)(2,1)S(1)}, u32[]{:S(2)}, u32[]{:S(2)}) collective-permute-start(bf16[96,256]{1,0:T(8,128)(2,1)S(1)} %reshape.110), channel_id=1, source_target_pairs={{0,0},{16,128},{32,256},{48,384},{128,400},{144,16},{160,144},{176... | collective-permute-start | bytes 147464 | tf_op jit(solution)/shard_map/ppermute | solution.py:74
  41.9 6.2 %copy-start.1 = (bf16[1024,256]{1,0:T(8,128)(2,1)S(1)}, bf16[1024,256]{1,0:T(8,128)(2,1)}, u32[]{:S(2)}) copy-start(bf16[1024,256]{1,0:T(8,128)(2,1)} %param.8) | copy-start | bytes 1572868
  43.3 23.3 %all-to-all-start.1 = ((bf16[4,96,1024]{2,1,0:T(8,128)(2,1)}), bf16[4,96,1024]{2,1,0:T(8,128)(2,1)S(1)}, u32[]{:S(2)}, u32[]{:S(2)}) async-start(bf16[4,96,1024]{2,1,0:T(8,128)(2,1)} %broadcast_in_dim.12), calls=%async_computation.1 | async-start | bytes 1572864 | tf_op jit(solution)/shard_map/all_to_all | solution.py:20
  48.1 85.3 %all-gather.5.cloned.1.call-start = ((), (), s32[]{:S(2)}) async-start(), calls=%async_computation.4 | async-start | bytes 3932160 | tf_op jit(solution)/shard_map/all_gather | solution.py:105
  48.1 18.6 %collective-permute-start.1 = (bf16[1024,256]{1,0:T(8,128)(2,1)S(1)}, bf16[1024,256]{1,0:T(8,128)(2,1)S(1)}, u32[]{:S(2)}, u32[]{:S(2)}) collective-permute-start(bf16[1024,256]{1,0:T(8,128)(2,1)S(1)} %copy-done.1), channel_id=1, source_target_pairs={{0,16},{16,32},{32,48},{48,0},{1,17},{17,33},{33,49},{49,1},{2,18}... | collective-permute-start | bytes 1572872 | tf_op jit(solution)/shard_map/ppermute | solution.py:44
  51.5 15.2 %collective-permute-start.2 = (bf16[1024,256]{1,0:T(8,128)(2,1)S(1)}, bf16[1024,256]{1,0:T(8,128)(2,1)S(1)}, u32[]{:S(2)}, u32[]{:S(2)}) collective-permute-start(bf16[1024,256]{1,0:T(8,128)(2,1)S(1)} %copy-done.1), channel_id=1, source_target_pairs={{0,48},{16,0},{32,16},{48,32},{1,49},{17,1},{33,17},{49,33},{2,50}... | collective-permute-start | bytes 1572872 | tf_op jit(solution)/shard_map/ppermute | solution.py:44
  69.3 3.6 %collective-permute-start.3 = (f32[4,96,256]{2,1,0:T(8,128)S(1)}, f32[4,96,256]{2,1,0:T(8,128)S(1)}, u32[]{:S(2)}, u32[]{:S(2)}) collective-permute-start(f32[4,96,256]{2,1,0:T(8,128)S(1)} %bitcast.114), channel_id=1, source_target_pairs={{0,64},{64,0},{1,65},{65,1},{2,66},{66,2},{3,67},{67,3},{4,68},{68... | collective-permute-start | bytes 1179656 | tf_op jit(solution)/shard_map/ppermute | solution.py:84
  74.1 24.9 %all-to-all-start.2 = ((bf16[4,6,96,256]{3,2,1,0:T(8,128)(2,1)}), bf16[4,6,96,256]{3,2,1,0:T(8,128)(2,1)S(1)}, u32[]{:S(2)}, u32[]{:S(2)}) async-start(bf16[4,6,96,256]{3,2,1,0:T(8,128)(2,1)} %broadcast_in_dim.27), calls=%async_computation.2 | async-start | bytes 2359296 | tf_op jit(solution)/shard_map/all_to_all | solution.py:20
  78.8 10.5 %collective-permute-start.5 = (bf16[512,256]{1,0:T(8,128)(2,1)S(1)}, bf16[512,256]{1,0:T(8,128)(2,1)S(1)}, u32[]{:S(2)}, u32[]{:S(2)}) collective-permute-start(bf16[512,256]{1,0:T(8,128)(2,1)S(1)} %slice.59), channel_id=1, source_target_pairs={{0,48},{16,0},{32,16},{48,32},{1,49},{17,1},{33,17},{49,33},{2,50}... | collective-permute-start | bytes 786440 | tf_op jit(solution)/shard_map/ppermute | solution.py:50
  83.5 15.4 %collective-permute-start.4 = (bf16[512,256]{1,0:T(8,128)(2,1)S(1)}, bf16[512,256]{1,0:T(8,128)(2,1)S(1)}, u32[]{:S(2)}, u32[]{:S(2)}) collective-permute-start(bf16[512,256]{1,0:T(8,128)(2,1)S(1)} %slice.58), channel_id=1, source_target_pairs={{0,16},{16,32},{32,48},{48,0},{1,17},{17,33},{33,49},{49,1},{2,18}... | collective-permute-start | bytes 786440 | tf_op jit(solution)/shard_map/ppermute | solution.py:50
  99.3 2.7 %copy-start.2 = (bf16[1024,256]{1,0:T(8,128)(2,1)S(1)}, bf16[1024,256]{1,0:T(8,128)(2,1)}, u32[]{:S(2)}) copy-start(bf16[1024,256]{1,0:T(8,128)(2,1)} %param.8) | copy-start | bytes 1572868
  104.5 28.2 %all-to-all-start.3 = ((bf16[16,24,512]{2,1,0:T(8,128)(2,1)}), bf16[16,24,512]{2,1,0:T(8,128)(2,1)S(1)}, u32[]{:S(2)}, u32[]{:S(2)}) async-start(bf16[16,24,512]{2,1,0:T(8,128)(2,1)} %copy.49), calls=%async_computation.3 | async-start | bytes 786432 | tf_op jit(solution)/shard_map/all_to_all | solution.py:20
  108.4 9.6 %collective-permute-start.6 = (bf16[192,256]{1,0:T(8,128)(2,1)S(1)}, bf16[192,256]{1,0:T(8,128)(2,1)S(1)}, u32[]{:S(2)}, u32[]{:S(2)}) collective-permute-start(bf16[192,256]{1,0:T(8,128)(2,1)S(1)} %bitcast.122), channel_id=1, source_target_pairs={{0,48},{16,0},{32,16},{48,32},{1,49},{17,1},{33,17},{49,33},{2,50}... | collective-permute-start | bytes 294920 | tf_op jit(solution)/shard_map/ppermute | solution.py:102
  111.4 9.5 %collective-permute-start.7 = (bf16[192,256]{1,0:T(8,128)(2,1)S(1)}, bf16[192,256]{1,0:T(8,128)(2,1)S(1)}, u32[]{:S(2)}, u32[]{:S(2)}) collective-permute-start(bf16[192,256]{1,0:T(8,128)(2,1)S(1)} %bitcast.123), channel_id=1, source_target_pairs={{0,32},{16,48},{32,0},{48,16},{1,33},{17,49},{33,1},{49,17},{2,34}... | collective-permute-start | bytes 294920 | tf_op jit(solution)/shard_map/ppermute | solution.py:102
  114.9 8.8 %collective-permute-start.8 = (bf16[192,256]{1,0:T(8,128)(2,1)S(1)}, bf16[192,256]{1,0:T(8,128)(2,1)S(1)}, u32[]{:S(2)}, u32[]{:S(2)}) collective-permute-start(bf16[192,256]{1,0:T(8,128)(2,1)S(1)} %bitcast.124), channel_id=1, source_target_pairs={{0,16},{16,32},{32,48},{48,0},{1,17},{17,33},{33,49},{49,1},{2,18}... | collective-permute-start | bytes 294920 | tf_op jit(solution)/shard_map/ppermute | solution.py:102
  133.4 3.1 %copy-start = (bf16[4,384,1024]{2,1,0:T(8,128)(2,1)S(1)}, bf16[4,384,1024]{2,1,0:T(8,128)(2,1)}, u32[]{:S(2)}) copy-start(bf16[4,384,1024]{2,1,0:T(8,128)(2,1)} %all-gather.5.cloned.1.call-done) | copy-start | bytes 9437188
Sparse Core Ops, SparseCore 0:
  10.1 43.1 all-gather.6
  72.4 50.1 all-gather.4

commit v7 on v6

--- a/solution.py
+++ b/solution.py
@@ -57,55 +57,56 @@
 
 
 def half_tokens(partial, at_x, half):
-    blocks = [
-        lax.dynamic_slice(partial, ((at_x + d) % 4, 0, half, 0, 0), (1, 4, 1, 24, 256)) for d in range(4)
-    ]
+    blocks = [lax.dynamic_slice(partial, ((at_x + d) % 4, half, 0, 0), (1, 1, 96, 256)) for d in range(4)]
     return jnp.concatenate(blocks).reshape(4, 96, 256)
 
 
+def others_y(block):
+    return [lax.ppermute(block, "y", shift(k)) for k in (3, 2, 1)]
+
+
 def local(inputs, out_grad, preact, up_weight, down_weight):
-    core, at_x = lax.axis_index("c"), lax.axis_index("x")
+    core, at_x, at_y = lax.axis_index("c"), lax.axis_index("x"), lax.axis_index("y")
     wide_down = lax.all_gather(down_weight, "x", axis=0, tiled=False)
 
-    both = jnp.concatenate([halves_down(out_grad), halves_down(inputs)], axis=0)
-    both = spread(both, "za")
-    rows_first = preact.reshape(2, 4, 12, 256).transpose(1, 0, 2, 3).reshape(96, 256)
+    grads = spread(halves_down(out_grad), ("za", "zb"), 16)
     swap = [(4 * a + b, 4 * ((b - a) % 4) + a) for a in range(4) for b in range(4)]
-    turned = lax.ppermute(rows_first, ("y", "x"), swap)
-    both, turned = lax.optimization_barrier((both, turned))
-    both = halves_across(both.reshape(4, 2, 24, 512)).swapaxes(0, 1).reshape(96, 1024)
-    both = spread(both, "zb").reshape(4, 2, 48, 1024).swapaxes(0, 1).reshape(2, 192, 1024)
-    grads = both[0]
+    turned = lax.ppermute(preact, ("y", "x"), swap)
+    turned = jnp.stack([turned, preact])
+    turned = jnp.stack([turned] + others_y(turned))
     before, after = near_x(up_weight)
-    grads, before, after = lax.optimization_barrier((grads, before, after))
+    grads, turned, before, after = lax.optimization_barrier((grads, turned, before, after))
+    grads = halves_across(grads).reshape(192, 1024)
+    inputs, grads = lax.optimization_barrier((inputs, grads))
+    ins = halves_across(spread(halves_down(inputs), ("za", "zb"), 16)).reshape(192, 1024)
+    turned = turn_by(turned, (4 - at_y) % 4)
+    _, slope = gelu_parts(turned[:, 0])
+    activ, _ = gelu_parts(turned[:, 1])
 
     partial = jnp.einsum("td,xfd->xtf", grads, wide_down, preferred_element_type=F32)
-    partial = partial.reshape(4, 4, 2, 24, 256)
+    partial = partial.reshape(4, 2, 96, 256)
     theirs = lax.ppermute(half_tokens(partial, at_x, 1 - core), "c", [(0, 1), (1, 0)])
     pair = (half_tokens(partial, at_x, core) + theirs).astype(BF)
-    activ, _ = gelu_parts(rows_first)
-    own = spread(jnp.concatenate([pair, activ.astype(BF)[None], turned[None]]), "y")
-    own, far = lax.optimization_barrier((own, far_x(before, after)))
-    hidden_grad = own[:, :4].astype(F32).sum(0)
-    _, slope = gelu_parts(own[:, 5])
-    own = jnp.concatenate([(hidden_grad * slope).astype(BF), own[:, 4]])
-    own = lax.all_gather(own, "c", axis=0, tiled=False).reshape(2, 2, 4, 4, 24, 256)
-    own = own.transpose(1, 2, 3, 0, 4, 5).reshape(2, 4, 192, 256)
-    pregrad, all_activ = own[0], own[1]
+    sums = others_y(pair)
+    far = far_x(before, after)
+    pair, sums, far = lax.optimization_barrier((pair, sums, far))
+    hidden_grad = sum((s.astype(F32) for s in sums), pair.astype(F32))
+    pregrad = lax.all_gather((hidden_grad * slope).astype(BF), "c", axis=1, tiled=False)
+    pregrad = pregrad.reshape(4, 192, 256)
 
     wide_up = jnp.stack([up_weight, after, far, before])
     part = jnp.einsum("xtf,xdf->td", pregrad, wide_up, preferred_element_type=F32)
-    part = part.astype(BF).reshape(4, 4, 12, 1024).swapaxes(0, 1)
-    part = exchange(halves_down(part.reshape(16, 12, 1024)), ("za", "zb"))
+    part = exchange(halves_down(part.astype(BF).reshape(16, 12, 1024)), ("za", "zb"))
     input_grad = halves_across(part.astype(F32).sum(0)).astype(BF)
 
     sent = [pregrad[0]] + [lax.ppermute(pregrad[k], "x", shift(k)) for k in (3, 2, 1)]
     all_pregrad = turn_by(jnp.stack(sent), (4 - at_x) % 4)
+    all_activ = lax.all_gather(activ.astype(BF), "c", axis=1, tiled=False).reshape(4, 192, 256)
     all_pregrad, all_activ = lax.optimization_barrier((all_pregrad, all_activ))
-    all_both = lax.all_gather(both.reshape(384, 1024), "x", axis=0, tiled=False)
-    all_both = all_both.reshape(4, 2, 192, 1024)
-    down_grad = jnp.einsum("xtf,xtd->fd", all_activ, all_both[:, 0], preferred_element_type=F32)
-    up_grad = jnp.einsum("xtd,xtf->df", all_both[:, 1], all_pregrad, preferred_element_type=F32)
+    all_grads = lax.all_gather(grads, "x", axis=0, tiled=False)
+    all_inputs = lax.all_gather(ins, "x", axis=0, tiled=False)
+    down_grad = jnp.einsum("xtf,xtd->fd", all_activ, all_grads, preferred_element_type=F32)
+    up_grad = jnp.einsum("xtd,xtf->df", all_inputs, all_pregrad, preferred_element_type=F32)
     return (input_grad, up_grad, down_grad)
 
 

time: 147 us -> 176 us (1.20)
  starting transfers between devices: 58.2 us -> 87.2 us
  waiting for transfers between devices: 51.5 us -> 47.3 us
  matrix products: 7.99 us -> 10.4 us
    ppermute x1 -> x7, waiting for transfers between devices: 4.72 us -> 26.4 us  [the longest x1 21.2 us: local(): turned = lax.ppermute(preact, ('y', 'x'), swap)]
    all_to_all x4 -> x3, waiting for transfers between devices: 25.8 us -> 7.33 us  [exchange(): lax.all_to_all(blocks, axis, split_axis=0, concat_axis=0, tiled=False)]
    ppermute x1 -> x7, starting transfers between devices: 5.34 us -> 20.9 us  [the longest x6 16.7 us: others_y(): return [lax.ppermute(block, 'y', shift(k)) for k in (3, 2, 1)]]
    all_to_all x4 -> x3, starting transfers between devices: 28.4 us -> 39 us  [exchange(): lax.all_to_all(blocks, axis, split_axis=0, concat_axis=0, tiled=False)]
    ppermute x1, waiting for transfers between devices: 9.58 us -> 4.2 us  [far_x(): lax.ppermute(before[:half], 'x', shift(1))]
    ppermute x1, waiting for transfers between devices: 3.89 us -> 0.01 us  [far_x(): lax.ppermute(after[half:], 'x', shift(-1))]
    ppermute x3, waiting for transfers between devices: 6.21 us -> 8.62 us  [local(): lax.ppermute(pregrad[k], 'x', shift(k))]
    ppermute x1, starting transfers between devices: 4.66 us -> 7 us  [far_x(): lax.ppermute(after[half:], 'x', shift(-1))]
  transfers between devices with their start and end apart: 15 -> 21, of which waited for: 10 -> 7; matrix products, arithmetic and copies ran while one was open for 7% -> 10% of each run, Pallas kernels for 0% -> 0%
where the time goes in v7:
time: 176 us; the launch traced here: 173 us
  starting transfers between devices  87.2 us (50%)
  waiting for transfers between devices  47.3 us (27%)
  between operations  14.4 us (8%)
  matrix products  10.4 us (6%)
  local copies, waits for them, and re-layouts  8.26 us (5%)
  blocking collectives  4.18 us (2%)
    all_to_all x3, starting transfers between devices, exchange(): lax.all_to_all(blocks, axis, split_axis=0, concat_axis=0, tiled=False)  39 us
    ppermute x1, waiting for transfers between devices, local(): turned = lax.ppermute(preact, ('y', 'x'), swap)  21.2 us
    ppermute x6, starting transfers between devices, others_y(): return [lax.ppermute(block, 'y', shift(k)) for k in (3, 2, 1)]  16.7 us
    ppermute x3, starting transfers between devices, local(): lax.ppermute(pregrad[k], 'x', shift(k))  9.34 us
    ppermute x3, waiting for transfers between devices, local(): lax.ppermute(pregrad[k], 'x', shift(k))  8.62 us
    all_to_all x3, waiting for transfers between devices, exchange(): lax.all_to_all(blocks, axis, split_axis=0, concat_axis=0, tiled=False)  7.33 us
    ppermute x1, starting transfers between devices, far_x(): lax.ppermute(after[half:], 'x', shift(-1))  7 us
    ppermute x6, waiting for transfers between devices, others_y(): return [lax.ppermute(block, 'y', shift(k)) for k in (3, 2, 1)]  5.24 us
  transfers between devices with their start and end apart: 21, of which 7 were waited for; matrix products, arithmetic and copies ran while one was open for 10% of the time, Pallas kernels for 0%

profile of v7, /device:TPU:24, one launch (start us, length us, event | category | flops | bytes accessed | tf_op | source)
XLA Modules:
  0.0 173.3 jit_solution(13608221694434544275)
XLA Ops:
  7.2 0.7 all-gather.9.cloned.1.call-update
  7.9 0.8 reshape.51
  8.7 0.8 broadcast_in_dim.15
  9.5 15.2 %all-to-all-start = ((bf16[16,24,512]{2,1,0:T(8,128)(2,1)}), bf16[16,24,512]{2,1,0:T(8,128)(2,1)S(1)}, u32[]{:S(2)}, u32[]{:S(2)}) async-start(bf16[16,24,512]{2,1,0:T(8,128)(2,1)} %broadcast_in_dim.15), calls=%async_computation | async-start | bytes 786432 | tf_op jit(solution)/shard_map/all_to_all | solution.py:20
  24.7 3.4 %collective-permute-start.4 = (bf16[1024,256]{1,0:T(8,128)(2,1)}, bf16[1024,256]{1,0:T(8,128)(2,1)S(1)}, u32[]{:S(2)}, u32[]{:S(2)}) collective-permute-start(bf16[1024,256]{1,0:T(8,128)(2,1)} %param.8), channel_id=1, source_target_pairs={{0,16},{16,32},{32,48},{48,0},{1,17},{17,33},{33,49},{49,1},{2,18}... | collective-permute-start | bytes 1572872 | tf_op jit(solution)/shard_map/ppermute | solution.py:44
  28.2 3.7 %collective-permute-start.5 = (bf16[1024,256]{1,0:T(8,128)(2,1)}, bf16[1024,256]{1,0:T(8,128)(2,1)S(1)}, u32[]{:S(2)}, u32[]{:S(2)}) collective-permute-start(bf16[1024,256]{1,0:T(8,128)(2,1)} %param.8), channel_id=1, source_target_pairs={{0,48},{16,0},{32,16},{48,32},{1,49},{17,1},{33,17},{49,33},{2,50}... | collective-permute-start | bytes 1572872 | tf_op jit(solution)/shard_map/ppermute | solution.py:44
  31.8 4.1 %collective-permute-start = (bf16[96,256]{1,0:T(8,128)(2,1)}, bf16[96,256]{1,0:T(8,128)(2,1)S(1)}, u32[]{:S(2)}, u32[]{:S(2)}) collective-permute-start(bf16[96,256]{1,0:T(8,128)(2,1)} %param.7), channel_id=1, source_target_pairs={{0,0},{16,128},{32,256},{48,384},{128,400},{144,16},{160,144},{176... | collective-permute-start | bytes 147464 | tf_op jit(solution)/shard_map/ppermute | solution.py:74
  36.0 21.2 %collective-permute-done = bf16[96,256]{1,0:T(8,128)(2,1)S(1)} collective-permute-done((bf16[96,256]{1,0:T(8,128)(2,1)}, bf16[96,256]{1,0:T(8,128)(2,1)S(1)}, u32[]{:S(2)}, u32[]{:S(2)}) %collective-permute-start) | collective-permute-done | bytes 49184 | tf_op jit(solution)/shard_map/ppermute | solution.py:74
  57.1 0.8 fusion.32
  57.9 1.9 %collective-permute-start.3 = (bf16[2,96,256]{2,1,0:T(8,128)(2,1)S(1)}, bf16[2,96,256]{2,1,0:T(8,128)(2,1)S(1)}, u32[]{:S(2)}, u32[]{:S(2)}) collective-permute-start(bf16[2,96,256]{2,1,0:T(8,128)(2,1)S(1)} %get-tuple-element.42), channel_id=1, source_target_pairs={{0,128},{128,256},{256,384},{384,0},{1,129},{129,257},{257,385},{3... | collective-permute-start | bytes 294920 | tf_op jit(solution)/shard_map/ppermute | solution.py:65
  59.9 1.9 %collective-permute-start.2 = (bf16[2,96,256]{2,1,0:T(8,128)(2,1)S(1)}, bf16[2,96,256]{2,1,0:T(8,128)(2,1)S(1)}, u32[]{:S(2)}, u32[]{:S(2)}) collective-permute-start(bf16[2,96,256]{2,1,0:T(8,128)(2,1)S(1)} %get-tuple-element.42), channel_id=1, source_target_pairs={{0,256},{128,384},{256,0},{384,128},{1,257},{129,385},{257,1},{385... | collective-permute-start | bytes 294920 | tf_op jit(solution)/shard_map/ppermute | solution.py:65
  61.8 3.9 %collective-permute-start.1 = (bf16[2,96,256]{2,1,0:T(8,128)(2,1)S(1)}, bf16[2,96,256]{2,1,0:T(8,128)(2,1)S(1)}, u32[]{:S(2)}, u32[]{:S(2)}) collective-permute-start(bf16[2,96,256]{2,1,0:T(8,128)(2,1)S(1)} %get-tuple-element.42), channel_id=1, source_target_pairs={{0,384},{128,0},{256,128},{384,256},{1,385},{129,1},{257,129},{385... | collective-permute-start | bytes 294920 | tf_op jit(solution)/shard_map/ppermute | solution.py:65
  65.7 2.1 %collective-permute-done.2 = bf16[2,96,256]{2,1,0:T(8,128)(2,1)S(1)} collective-permute-done((bf16[2,96,256]{2,1,0:T(8,128)(2,1)S(1)}, bf16[2,96,256]{2,1,0:T(8,128)(2,1)S(1)}, u32[]{:S(2)}, u32[]{:S(2)}) %collective-permute-start.2) | collective-permute-done | bytes 98336 | tf_op jit(solution)/shard_map/ppermute | solution.py:65
  67.9 3.1 %collective-permute-done.1 = bf16[2,96,256]{2,1,0:T(8,128)(2,1)S(1)} collective-permute-done((bf16[2,96,256]{2,1,0:T(8,128)(2,1)S(1)}, bf16[2,96,256]{2,1,0:T(8,128)(2,1)S(1)}, u32[]{:S(2)}, u32[]{:S(2)}) %collective-permute-start.1) | collective-permute-done | bytes 98336 | tf_op jit(solution)/shard_map/ppermute | solution.py:65
  71.1 0.1 copy.77
  71.2 0.4 copy.78
  71.6 0.8 copy.102
  72.5 0.8 broadcast_in_dim.17
  73.3 11.7 %all-to-all-start.2 = ((bf16[16,24,512]{2,1,0:T(8,128)(2,1)}), bf16[16,24,512]{2,1,0:T(8,128)(2,1)S(1)}, u32[]{:S(2)}, u32[]{:S(2)}) async-start(bf16[16,24,512]{2,1,0:T(8,128)(2,1)} %broadcast_in_dim.17), calls=%async_computation.2 | async-start | bytes 786432 | tf_op jit(solution)/shard_map/all_to_all | solution.py:20
  85.2 2.4 %fusion.28 = f32[192,4,256]{2,0,1:T(8,128)S(1)} fusion(bf16[4,256,1024]{2,1,0:T(8,128)(2,1)} %bitcast.108, bf16[192,1024]{1,0:T(8,128)(2,1)S(1)} %bitcast.106), kind=kOutput, calls=%fused_computation.38 | convolution fusion | flops 402653184 | bytes 3276800 | tf_op jit(solution)/shard_map/td,xfd->xtf/dot_general | solution.py:86
  87.7 1.9 %collective-permute-start.6 = (f32[4,96,256]{2,1,0:T(8,128)S(1)}, f32[4,96,256]{2,1,0:T(8,128)S(1)}, u32[]{:S(2)}, u32[]{:S(2)}) collective-permute-start(f32[4,96,256]{2,1,0:T(8,128)S(1)} %maximum_bitcast_fusion.1), channel_id=1, source_target_pairs={{0,64},{64,0},{1,65},{65,1},{2,66},{66,2},{3,67},{67,3},{4,68},{68... | collective-permute-start | bytes 1179656 | tf_op jit(solution)/shard_map/ppermute | solution.py:88
  89.7 7.0 %collective-permute-start.11 = (bf16[512,256]{1,0:T(8,128)(2,1)S(1)}, bf16[512,256]{1,0:T(8,128)(2,1)S(1)}, u32[]{:S(2)}, u32[]{:S(2)}) collective-permute-start(bf16[512,256]{1,0:T(8,128)(2,1)S(1)} %slice.36), channel_id=1, source_target_pairs={{0,48},{16,0},{32,16},{48,32},{1,49},{17,1},{33,17},{49,33},{2,50}... | collective-permute-start | bytes 786440 | tf_op jit(solution)/shard_map/ppermute | solution.py:50
  96.7 1.9 %collective-permute-start.10 = (bf16[512,256]{1,0:T(8,128)(2,1)S(1)}, bf16[512,256]{1,0:T(8,128)(2,1)S(1)}, u32[]{:S(2)}, u32[]{:S(2)}) collective-permute-start(bf16[512,256]{1,0:T(8,128)(2,1)S(1)} %slice.35), channel_id=1, source_target_pairs={{0,16},{16,32},{32,48},{48,0},{1,17},{17,33},{33,49},{49,1},{2,18}... | collective-permute-start | bytes 786440 | tf_op jit(solution)/shard_map/ppermute | solution.py:50
  98.7 0.1 fusion.25
  99.0 2.1 %collective-permute-start.7 = (bf16[4,96,256]{2,1,0:T(8,128)(2,1)S(1)}, bf16[4,96,256]{2,1,0:T(8,128)(2,1)S(1)}, u32[]{:S(2)}, u32[]{:S(2)}) collective-permute-start(bf16[4,96,256]{2,1,0:T(8,128)(2,1)S(1)} %fusion.27), channel_id=1, source_target_pairs={{0,384},{128,0},{256,128},{384,256},{1,385},{129,1},{257,129},{385... | collective-permute-start | bytes 589832 | tf_op jit(solution)/shard_map/ppermute | solution.py:65
  101.1 2.8 %collective-permute-start.8 = (bf16[4,96,256]{2,1,0:T(8,128)(2,1)S(1)}, bf16[4,96,256]{2,1,0:T(8,128)(2,1)S(1)}, u32[]{:S(2)}, u32[]{:S(2)}) collective-permute-start(bf16[4,96,256]{2,1,0:T(8,128)(2,1)S(1)} %fusion.27), channel_id=1, source_target_pairs={{0,256},{128,384},{256,0},{384,128},{1,257},{129,385},{257,1},{385... | collective-permute-start | bytes 589832 | tf_op jit(solution)/shard_map/ppermute | solution.py:65
  103.9 4.1 %collective-permute-start.9 = (bf16[4,96,256]{2,1,0:T(8,128)(2,1)S(1)}, bf16[4,96,256]{2,1,0:T(8,128)(2,1)S(1)}, u32[]{:S(2)}, u32[]{:S(2)}) collective-permute-start(bf16[4,96,256]{2,1,0:T(8,128)(2,1)S(1)} %fusion.27), channel_id=1, source_target_pairs={{0,128},{128,256},{256,384},{384,0},{1,129},{129,257},{257,385},{3... | collective-permute-start | bytes 589832 | tf_op jit(solution)/shard_map/ppermute | solution.py:65
  108.0 2.1 %all_gather.30 = bf16[4,2,96,256]{3,2,0,1:T(8,128)(2,1)S(1)} all-gather(bf16[4,1,96,256]{3,2,0,1:T(8,128)(2,1)S(1)} %fusion.17), channel_id=1, replica_groups=mesh['y'=4,'c'=2,'x'=4,'za'=4,'zb'=4] {'c'}, dimensions={1}, use_global_device_ids=true | all-gather | bytes 589824 | tf_op jit(solution)/shard_map/all_gather | solution.py:104
  110.2 4.2 %collective-permute-done.10 = bf16[512,256]{1,0:T(8,128)(2,1)S(1)} collective-permute-done((bf16[512,256]{1,0:T(8,128)(2,1)S(1)}, bf16[512,256]{1,0:T(8,128)(2,1)S(1)}, u32[]{:S(2)}, u32[]{:S(2)}) %collective-permute-start.10) | collective-permute-done | bytes 262176 | tf_op jit(solution)/shard_map/ppermute | solution.py:50
  114.4 0.1 copy.91
  114.5 0.4 copy.92
  114.9 1.0 all_gather_reshape_reshape.3
  116.0 0.3 fusion.30
  116.3 2.1 %all-gather.1 = bf16[4,192,256]{2,1,0:T(8,128)(2,1)S(1)} all-gather(bf16[4,96,256]{2,1,0:T(8,128)(2,1)S(1)} %fusion.30), channel_id=3, replica_groups=mesh['y'=4,'c'=2,'x'=4,'za'=4,'zb'=4] {'c'}, dimensions={1}, use_global_device_ids=true | all-gather | bytes 589824 | tf_op jit(solution)/shard_map/all_gather | solution.py:94
  118.4 0.7 slice_bitcast_fusion.1
  119.1 4.7 %collective-permute-start.12 = (bf16[192,256]{1,0:T(8,128)(2,1)}, bf16[192,256]{1,0:T(8,128)(2,1)S(1)}, u32[]{:S(2)}, u32[]{:S(2)}) collective-permute-start(bf16[192,256]{1,0:T(8,128)(2,1)} %get-tuple-element.40), channel_id=1, source_target_pairs={{0,48},{16,0},{32,16},{48,32},{1,49},{17,1},{33,17},{49,33},{2,50}... | collective-permute-start | bytes 294920 | tf_op jit(solution)/shard_map/ppermute | solution.py:102
  123.8 2.0 %fusion.11 = bf16[192,1024]{1,0:T(8,128)(2,1)S(1)} fusion(bf16[4,192,256]{2,1,0:T(8,128)(2,1)S(1)} %all-gather.1, bf16[1,1024,256]{2,1,0:T(8,128)(2,1)S(1)} %bitcast.119, bf16[1,1024,256]{2,1,0:T(8,128)(2,1)S(1)} %bitcast.113, bf16[1,1024,256]{2,1,0:T(8,128)(2,1)} %bitcast.120, bf16[1,1024,256]{2,1,0:T(8,128)(2,1)} %bitcast.128), kind=kOutput, calls=%fused_computation.11 | convolution fusion | flops 405995520 | bytes 2883584 | tf_op jit(solution)/shard_map/xtf,xdf->td/dot_general | solution.py:98
  125.8 0.3 reshape_reshape.7
  126.2 1.0 copy.88
  127.2 12.0 %all-to-all-start.1 = ((bf16[16,24,512]{2,1,0:T(8,128)(2,1)}), bf16[16,24,512]{2,1,0:T(8,128)(2,1)S(1)}, u32[]{:S(2)}, u32[]{:S(2)}) async-start(bf16[16,24,512]{2,1,0:T(8,128)(2,1)} %copy.88), calls=%async_computation.1 | async-start | bytes 786432 | tf_op jit(solution)/shard_map/all_to_all | solution.py:20
  139.2 1.9 %collective-permute-start.13 = (bf16[192,256]{1,0:T(8,128)(2,1)S(1)}, bf16[192,256]{1,0:T(8,128)(2,1)S(1)}, u32[]{:S(2)}, u32[]{:S(2)}) collective-permute-start(bf16[192,256]{1,0:T(8,128)(2,1)S(1)} %copy-done.2), channel_id=1, source_target_pairs={{0,32},{16,48},{32,0},{48,16},{1,33},{17,49},{33,1},{49,17},{2,34}... | collective-permute-start | bytes 294920 | tf_op jit(solution)/shard_map/ppermute | solution.py:102
  141.2 2.8 %collective-permute-start.14 = (bf16[192,256]{1,0:T(8,128)(2,1)S(1)}, bf16[192,256]{1,0:T(8,128)(2,1)S(1)}, u32[]{:S(2)}, u32[]{:S(2)}) collective-permute-start(bf16[192,256]{1,0:T(8,128)(2,1)S(1)} %get-tuple-element.37), channel_id=1, source_target_pairs={{0,16},{16,32},{32,48},{48,0},{1,17},{17,33},{33,49},{49,1},{2,18}... | collective-permute-start | bytes 294920 | tf_op jit(solution)/shard_map/ppermute | solution.py:102
  144.0 6.4 %collective-permute-done.13 = bf16[192,256]{1,0:T(8,128)(2,1)S(1)} collective-permute-done((bf16[192,256]{1,0:T(8,128)(2,1)S(1)}, bf16[192,256]{1,0:T(8,128)(2,1)S(1)}, u32[]{:S(2)}, u32[]{:S(2)}) %collective-permute-start.13) | collective-permute-done | bytes 98336 | tf_op jit(solution)/shard_map/ppermute | solution.py:102
  150.4 2.2 %collective-permute-done.14 = bf16[192,256]{1,0:T(8,128)(2,1)S(1)} collective-permute-done((bf16[192,256]{1,0:T(8,128)(2,1)S(1)}, bf16[192,256]{1,0:T(8,128)(2,1)S(1)}, u32[]{:S(2)}, u32[]{:S(2)}) %collective-permute-start.14) | collective-permute-done | bytes 98336 | tf_op jit(solution)/shard_map/ppermute | solution.py:102
  152.7 3.0 %convolution_bitcast_fusion = f32[256,1024]{1,0:T(8,128)} fusion(bf16[4,192,256]{2,1,0:T(8,128)(2,1)S(1)} %bitcast.114, bf16[4,192,1024]{2,1,0:T(8,128)(2,1)} %bitcast.127), kind=kOutput, calls=%fused_computation.8 | convolution fusion | flops 402653184 | bytes 3014656 | tf_op jit(solution)/shard_map/xtf,xtd->fd/dot_general | solution.py:108
  155.7 7.3 %all-to-all-done.1 = bf16[16,24,512]{2,1,0:T(8,128)(2,1)S(1)} async-done(((bf16[16,24,512]{2,1,0:T(8,128)(2,1)}), bf16[16,24,512]{2,1,0:T(8,128)(2,1)S(1)}, u32[]{:S(2)}, u32[]{:S(2)}) %all-to-all-start.1) | async-done | bytes 393248 | tf_op jit(solution)/shard_map/all_to_all | solution.py:20
  163.2 0.6 copy.103
  163.8 3.0 %convolution_bitcast_fusion.1 = f32[1024,256]{1,0:T(8,128)} fusion(bf16[4,192,1024]{2,1,0:T(8,128)(2,1)} %all-gather.7.cloned.1.call-done, bf16[4,192,256]{2,1,0:T(8,128)(2,1)S(1)} %constant_dynamic-slice_fusion), kind=kOutput, calls=%fused_computation.9 | convolution fusion | flops 402653184 | bytes 3014656 | tf_op jit(solution)/shard_map/xtd,xtf->df/dot_general | solution.py:109
  (54 shorter events, 1.0 us)
Async XLA Ops:
  7.2 78.0 %all-gather.9.cloned.1.call-start = ((), (), s32[]{:S(2)}) async-start(), calls=%async_computation.4 | async-start | bytes 2621440 | tf_op jit(solution)/shard_map/all_gather | solution.py:70
  9.5 61.6 %all-to-all-start = ((bf16[16,24,512]{2,1,0:T(8,128)(2,1)}), bf16[16,24,512]{2,1,0:T(8,128)(2,1)S(1)}, u32[]{:S(2)}, u32[]{:S(2)}) async-start(bf16[16,24,512]{2,1,0:T(8,128)(2,1)} %broadcast_in_dim.15), calls=%async_computation | async-start | bytes 786432 | tf_op jit(solution)/shard_map/all_to_all | solution.py:20
  24.7 47.7 %copy-start.3 = (bf16[12,1024]{1,0:T(8,128)(2,1)S(1)}, bf16[12,1024]{1,0:T(8,128)(2,1)}, u32[]{:S(2)}) copy-start(bf16[12,1024]{1,0:T(8,128)(2,1)} %param.5) | copy-start | bytes 73732
  24.7 128.0 %all-gather.11.cloned.1.call-start = ((), (), s32[]{:S(2)}) async-start(), calls=%async_computation.5 | async-start | bytes 1966080 | tf_op jit(solution)/shard_map/all_gather | solution.py:106
  24.7 46.3 %collective-permute-start.4 = (bf16[1024,256]{1,0:T(8,128)(2,1)}, bf16[1024,256]{1,0:T(8,128)(2,1)S(1)}, u32[]{:S(2)}, u32[]{:S(2)}) collective-permute-start(bf16[1024,256]{1,0:T(8,128)(2,1)} %param.8), channel_id=1, source_target_pairs={{0,16},{16,32},{32,48},{48,0},{1,17},{17,33},{33,49},{49,1},{2,18}... | collective-permute-start | bytes 1572872 | tf_op jit(solution)/shard_map/ppermute | solution.py:44
  28.2 42.9 %collective-permute-start.5 = (bf16[1024,256]{1,0:T(8,128)(2,1)}, bf16[1024,256]{1,0:T(8,128)(2,1)S(1)}, u32[]{:S(2)}, u32[]{:S(2)}) collective-permute-start(bf16[1024,256]{1,0:T(8,128)(2,1)} %param.8), channel_id=1, source_target_pairs={{0,48},{16,0},{32,16},{48,32},{1,49},{17,1},{33,17},{49,33},{2,50}... | collective-permute-start | bytes 1572872 | tf_op jit(solution)/shard_map/ppermute | solution.py:44
  31.8 25.3 %collective-permute-start = (bf16[96,256]{1,0:T(8,128)(2,1)}, bf16[96,256]{1,0:T(8,128)(2,1)S(1)}, u32[]{:S(2)}, u32[]{:S(2)}) collective-permute-start(bf16[96,256]{1,0:T(8,128)(2,1)} %param.7), channel_id=1, source_target_pairs={{0,0},{16,128},{32,256},{48,384},{128,400},{144,16},{160,144},{176... | collective-permute-start | bytes 147464 | tf_op jit(solution)/shard_map/ppermute | solution.py:74
  57.9 7.8 %collective-permute-start.3 = (bf16[2,96,256]{2,1,0:T(8,128)(2,1)S(1)}, bf16[2,96,256]{2,1,0:T(8,128)(2,1)S(1)}, u32[]{:S(2)}, u32[]{:S(2)}) collective-permute-start(bf16[2,96,256]{2,1,0:T(8,128)(2,1)S(1)} %get-tuple-element.42), channel_id=1, source_target_pairs={{0,128},{128,256},{256,384},{384,0},{1,129},{129,257},{257,385},{3... | collective-permute-start | bytes 294920 | tf_op jit(solution)/shard_map/ppermute | solution.py:65
  59.9 8.0 %collective-permute-start.2 = (bf16[2,96,256]{2,1,0:T(8,128)(2,1)S(1)}, bf16[2,96,256]{2,1,0:T(8,128)(2,1)S(1)}, u32[]{:S(2)}, u32[]{:S(2)}) collective-permute-start(bf16[2,96,256]{2,1,0:T(8,128)(2,1)S(1)} %get-tuple-element.42), channel_id=1, source_target_pairs={{0,256},{128,384},{256,0},{384,128},{1,257},{129,385},{257,1},{385... | collective-permute-start | bytes 294920 | tf_op jit(solution)/shard_map/ppermute | solution.py:65
  61.8 9.2 %collective-permute-start.1 = (bf16[2,96,256]{2,1,0:T(8,128)(2,1)S(1)}, bf16[2,96,256]{2,1,0:T(8,128)(2,1)S(1)}, u32[]{:S(2)}, u32[]{:S(2)}) collective-permute-start(bf16[2,96,256]{2,1,0:T(8,128)(2,1)S(1)} %get-tuple-element.42), channel_id=1, source_target_pairs={{0,384},{128,0},{256,128},{384,256},{1,385},{129,1},{257,129},{385... | collective-permute-start | bytes 294920 | tf_op jit(solution)/shard_map/ppermute | solution.py:65
  71.0 18.6 %copy-start.1 = (bf16[1024,256]{1,0:T(8,128)(2,1)}, bf16[1024,256]{1,0:T(8,128)(2,1)S(1)}, u32[]{:S(2)}) copy-start(bf16[1024,256]{1,0:T(8,128)(2,1)S(1)} %collective-permute-done.5) | copy-start | bytes 1572868
  72.4 12.7 %copy-start = (bf16[24,8,2,512]{3,1,2,0:T(8,128)(2,1)S(1)}, bf16[24,8,2,512]{3,1,2,0:T(8,128)(2,1)}, u32[]{:S(2)}) copy-start(bf16[24,8,2,512]{3,1,2,0:T(8,128)(2,1)} %copy.102) | copy-start | bytes 1179652
  73.3 41.1 %all-to-all-start.2 = ((bf16[16,24,512]{2,1,0:T(8,128)(2,1)}), bf16[16,24,512]{2,1,0:T(8,128)(2,1)S(1)}, u32[]{:S(2)}, u32[]{:S(2)}) async-start(bf16[16,24,512]{2,1,0:T(8,128)(2,1)} %broadcast_in_dim.17), calls=%async_computation.2 | async-start | bytes 786432 | tf_op jit(solution)/shard_map/all_to_all | solution.py:20
  85.0 78.8 %all-gather.7.cloned.1.call-start = ((), (), s32[]{:S(2)}) async-start(), calls=%async_computation.3 | async-start | bytes 1966080 | tf_op jit(solution)/shard_map/all_gather | solution.py:107
  87.7 11.2 %collective-permute-start.6 = (f32[4,96,256]{2,1,0:T(8,128)S(1)}, f32[4,96,256]{2,1,0:T(8,128)S(1)}, u32[]{:S(2)}, u32[]{:S(2)}) collective-permute-start(f32[4,96,256]{2,1,0:T(8,128)S(1)} %maximum_bitcast_fusion.1), channel_id=1, source_target_pairs={{0,64},{64,0},{1,65},{65,1},{2,66},{66,2},{3,67},{67,3},{4,68},{68... | collective-permute-start | bytes 1179656 | tf_op jit(solution)/shard_map/ppermute | solution.py:88
  89.7 20.4 %collective-permute-start.11 = (bf16[512,256]{1,0:T(8,128)(2,1)S(1)}, bf16[512,256]{1,0:T(8,128)(2,1)S(1)}, u32[]{:S(2)}, u32[]{:S(2)}) collective-permute-start(bf16[512,256]{1,0:T(8,128)(2,1)S(1)} %slice.36), channel_id=1, source_target_pairs={{0,48},{16,0},{32,16},{48,32},{1,49},{17,1},{33,17},{49,33},{2,50}... | collective-permute-start | bytes 786440 | tf_op jit(solution)/shard_map/ppermute | solution.py:50
  96.7 17.6 %collective-permute-start.10 = (bf16[512,256]{1,0:T(8,128)(2,1)S(1)}, bf16[512,256]{1,0:T(8,128)(2,1)S(1)}, u32[]{:S(2)}, u32[]{:S(2)}) collective-permute-start(bf16[512,256]{1,0:T(8,128)(2,1)S(1)} %slice.35), channel_id=1, source_target_pairs={{0,16},{16,32},{32,48},{48,0},{1,17},{17,33},{33,49},{49,1},{2,18}... | collective-permute-start | bytes 786440 | tf_op jit(solution)/shard_map/ppermute | solution.py:50
  99.0 17.0 %collective-permute-start.7 = (bf16[4,96,256]{2,1,0:T(8,128)(2,1)S(1)}, bf16[4,96,256]{2,1,0:T(8,128)(2,1)S(1)}, u32[]{:S(2)}, u32[]{:S(2)}) collective-permute-start(bf16[4,96,256]{2,1,0:T(8,128)(2,1)S(1)} %fusion.27), channel_id=1, source_target_pairs={{0,384},{128,0},{256,128},{384,256},{1,385},{129,1},{257,129},{385... | collective-permute-start | bytes 589832 | tf_op jit(solution)/shard_map/ppermute | solution.py:65
  101.1 14.9 %collective-permute-start.8 = (bf16[4,96,256]{2,1,0:T(8,128)(2,1)S(1)}, bf16[4,96,256]{2,1,0:T(8,128)(2,1)S(1)}, u32[]{:S(2)}, u32[]{:S(2)}) collective-permute-start(bf16[4,96,256]{2,1,0:T(8,128)(2,1)S(1)} %fusion.27), channel_id=1, source_target_pairs={{0,256},{128,384},{256,0},{384,128},{1,257},{129,385},{257,1},{385... | collective-permute-start | bytes 589832 | tf_op jit(solution)/shard_map/ppermute | solution.py:65
  103.9 12.1 %collective-permute-start.9 = (bf16[4,96,256]{2,1,0:T(8,128)(2,1)S(1)}, bf16[4,96,256]{2,1,0:T(8,128)(2,1)S(1)}, u32[]{:S(2)}, u32[]{:S(2)}) collective-permute-start(bf16[4,96,256]{2,1,0:T(8,128)(2,1)S(1)} %fusion.27), channel_id=1, source_target_pairs={{0,128},{128,256},{256,384},{384,0},{1,129},{129,257},{257,385},{3... | collective-permute-start | bytes 589832 | tf_op jit(solution)/shard_map/ppermute | solution.py:65
  119.1 24.8 %collective-permute-start.12 = (bf16[192,256]{1,0:T(8,128)(2,1)}, bf16[192,256]{1,0:T(8,128)(2,1)S(1)}, u32[]{:S(2)}, u32[]{:S(2)}) collective-permute-start(bf16[192,256]{1,0:T(8,128)(2,1)} %get-tuple-element.40), channel_id=1, source_target_pairs={{0,48},{16,0},{32,16},{48,32},{1,49},{17,1},{33,17},{49,33},{2,50}... | collective-permute-start | bytes 294920 | tf_op jit(solution)/shard_map/ppermute | solution.py:102
  125.8 13.4 %copy-start.2 = (bf16[192,256]{1,0:T(8,128)(2,1)S(1)}, bf16[192,256]{1,0:T(8,128)(2,1)}, u32[]{:S(2)}) copy-start(bf16[192,256]{1,0:T(8,128)(2,1)} %get-tuple-element.39) | copy-start | bytes 294916
  127.2 35.8 %all-to-all-start.1 = ((bf16[16,24,512]{2,1,0:T(8,128)(2,1)}), bf16[16,24,512]{2,1,0:T(8,128)(2,1)S(1)}, u32[]{:S(2)}, u32[]{:S(2)}) async-start(bf16[16,24,512]{2,1,0:T(8,128)(2,1)} %copy.88), calls=%async_computation.1 | async-start | bytes 786432 | tf_op jit(solution)/shard_map/all_to_all | solution.py:20
  139.2 11.1 %collective-permute-start.13 = (bf16[192,256]{1,0:T(8,128)(2,1)S(1)}, bf16[192,256]{1,0:T(8,128)(2,1)S(1)}, u32[]{:S(2)}, u32[]{:S(2)}) collective-permute-start(bf16[192,256]{1,0:T(8,128)(2,1)S(1)} %copy-done.2), channel_id=1, source_target_pairs={{0,32},{16,48},{32,0},{48,16},{1,33},{17,49},{33,1},{49,17},{2,34}... | collective-permute-start | bytes 294920 | tf_op jit(solution)/shard_map/ppermute | solution.py:102
  141.2 11.4 %collective-permute-start.14 = (bf16[192,256]{1,0:T(8,128)(2,1)S(1)}, bf16[192,256]{1,0:T(8,128)(2,1)S(1)}, u32[]{:S(2)}, u32[]{:S(2)}) collective-permute-start(bf16[192,256]{1,0:T(8,128)(2,1)S(1)} %get-tuple-element.37), channel_id=1, source_target_pairs={{0,16},{16,32},{32,48},{48,0},{1,17},{17,33},{33,49},{49,1},{2,18}... | collective-permute-start | bytes 294920 | tf_op jit(solution)/shard_map/ppermute | solution.py:102
Sparse Core Ops, SparseCore 0:
  10.1 51.5 all-gather.8
  72.6 42.4 all-gather.10
  117.1 38.3 all-gather.6

commit v8 on v6

v8 whole, which is shorter than its diff:
```python
import math

import jax
import jax.numpy as jnp
from jax import lax
from jax.sharding import Mesh, PartitionSpec as P

BF = jnp.bfloat16
F32 = jnp.float32


def gelu_parts(preact):
    value = preact.astype(F32)
    normal_cdf = 0.5 * (1.0 + jax.scipy.special.erf(value / math.sqrt(2.0)))
    density = jnp.exp(-0.5 * value * value) / math.sqrt(2.0 * math.pi)
    return (value * normal_cdf, normal_cdf + value * density)


def exchange(blocks, axis):
    return lax.all_to_all(blocks, axis, split_axis=0, concat_axis=0, tiled=False)


def spread(block, axis, n=4):
    return exchange(jnp.broadcast_to(block[None], (n,) + block.shape), axis)


def halves_down(block):
    lead, (rows, cols) = block.shape[:-2], block.shape[-2:]
    split = block.reshape(*lead, rows, 2, cols // 2)
    return jnp.swapaxes(split, -3, -2).reshape(*lead, rows * 2, cols // 2)


def halves_across(block):
    lead, (rows, cols) = block.shape[:-2], block.shape[-2:]
    split = block.reshape(*lead, 2, rows // 2, cols)
    return jnp.swapaxes(split, -3, -2).reshape(*lead, rows // 2, cols * 2)


def shift(k):
    return [(i, (i + k) % 4) for i in range(4)]


def near_x(block):
    return lax.ppermute(block, "x", shift(1)), lax.ppermute(block, "x", shift(-1))


def far_x(before, after):
    half = before.shape[0] // 2
    return jnp.concatenate(
        [lax.ppermute(before[:half], "x", shift(1)), lax.ppermute(after[half:], "x", shift(-1))]
    )


def turn_by(blocks, start):
    turned = [lax.dynamic_index_in_dim(blocks, (start + i) % 4, keepdims=True) for i in range(4)]
    return jnp.concatenate(turned)


def local(inputs, out_grad, preact, up_weight, down_weight):
    core, at_x = lax.axis_index("c"), lax.axis_index("x")

    both = jnp.concatenate([halves_down(out_grad), halves_down(inputs)], axis=0)
    both = spread(both, ("za", "zb"), 16)
    swap = [(4 * a + b, 4 * ((b - a) % 4) + a) for a in range(4) for b in range(4)]
    turned = lax.ppermute(preact, ("y", "x"), swap)
    before, after = near_x(down_weight)
    far = far_x(before, after)
    both, turned, before, after, far = lax.optimization_barrier((both, turned, before, after, far))
    wide_down = jnp.stack([down_weight, after, far, before])
    wide_up = lax.all_gather(up_weight, "x", axis=0, tiled=False)
    grads = halves_across(both[:, :24]).reshape(192, 1024)
    ins = halves_across(both[:, 24:]).reshape(192, 1024)

    partial = jnp.einsum("td,xfd->xtf", grads, wide_down, preferred_element_type=F32)
    partial = partial.reshape(4, 2, 96, 256)
    mine = lax.dynamic_index_in_dim(partial, core, axis=1, keepdims=False)
    theirs = lax.dynamic_index_in_dim(partial, 1 - core, axis=1, keepdims=False)
    pair = (mine + lax.ppermute(theirs, "c", [(0, 1), (1, 0)])).astype(BF)
    activ, _ = gelu_parts(preact)
    own = spread(jnp.concatenate([pair, activ.astype(BF)[None], turned[None]]), "y")
    wide_up = turn_by(wide_up, at_x)
    own, wide_up = lax.optimization_barrier((own, wide_up))
    hidden_grad = own[:, :4].astype(F32).sum(0)
    _, slope = gelu_parts(own[:, 5])
    own = jnp.concatenate([(hidden_grad * slope).astype(BF), own[:, 4]])
    own = lax.all_gather(own, "c", axis=1, tiled=False).reshape(2, 4, 192, 256)
    pregrad, all_activ = own[0], own[1]

    part = jnp.einsum("xtf,xdf->td", pregrad, wide_up, preferred_element_type=F32)
    part = exchange(halves_down(part.astype(BF).reshape(16, 12, 1024)), ("za", "zb"))

    sent = [pregrad[0]] + [lax.ppermute(pregrad[k], "x", shift(k)) for k in (3, 2, 1)]
    all_pregrad = turn_by(jnp.stack(sent), 4 - at_x)
    all_pregrad, all_activ = lax.optimization_barrier((all_pregrad, all_activ))
    all_both = lax.all_gather(jnp.concatenate([grads, ins]), "x", axis=0, tiled=False)
    all_both = all_both.reshape(4, 2, 192, 1024)
    down_grad = jnp.einsum("xtf,xtd->fd", all_activ, all_both[:, 0], preferred_element_type=F32)
    up_grad = jnp.einsum("xtd,xtf->df", all_both[:, 1], all_pregrad, preferred_element_type=F32)
    part, up_grad, down_grad = lax.optimization_barrier((part, up_grad, down_grad))
    input_grad = halves_across(part.astype(F32).sum(0)).astype(BF)
    return (input_grad, up_grad, down_grad)


def solution(mesh):
    fine = Mesh(mesh.devices.reshape(4, 2, 4, 4, 4), ("y", "c", "x", "za", "zb"))
    tokens, width = ("x", "za", "zb"), ("y", "c")
    return jax.shard_map(
        local,
        mesh=fine,
        in_specs=(
            P(tokens, width),
            P(tokens, width),
            P(width, tokens),
            P(width, tokens),
            P(tokens, width),
        ),
        out_specs=(P(tokens, width), P(width, tokens), P(tokens, width)),
        check_vma=False,
    )
```

time: 147 us -> 144 us (0.980)
  waiting for transfers between devices: 51.5 us -> 46.3 us
  starting transfers between devices: 58.2 us -> 62.2 us
  matrix products: 7.99 us -> 6.38 us
    ppermute x1, waiting for transfers between devices: 0.01 us -> 8.95 us  [near_x(): lax.ppermute(block, 'x', shift(-1))]
    all_to_all x4 -> x3, waiting for transfers between devices: 25.8 us -> 17.3 us  [exchange(): lax.all_to_all(blocks, axis, split_axis=0, concat_axis=0, tiled=False)]
    ppermute x1, waiting for transfers between devices: 9.58 us -> 5.37 us  [far_x(): lax.ppermute(before[:half], 'x', shift(1))]
    all_to_all x4 -> x3, starting transfers between devices: 28.4 us -> 31.3 us  [exchange(): lax.all_to_all(blocks, axis, split_axis=0, concat_axis=0, tiled=False)]
    dot_general x1, matrix products: 2.43 us -> 0.84 us  [local(): jnp.einsum('td,xfd->xtf', grads, wide_down, preferred_element_type=F32)]
    dynamic_slice x2, local copies, waits for them, and re-layouts: 0.13 us -> 1.69 us  [turn_by(): lax.dynamic_index_in_dim(blocks, (start + i) % 4, keepdims=True)]
    dot_general x1, matrix products: 3.14 us -> 1.58 us  [local(): jnp.einsum('xtd,xtf->df', all_both[:, 1], all_pregrad, preferred_element_...]
    dot_general x1, matrix products: 1.57 us -> 3.13 us  [local(): jnp.einsum('xtf,xtd->fd', all_activ, all_both[:, 0], preferred_element_ty...]
  transfers between devices with their start and end apart: 15 -> 14, of which waited for: 10 -> 11; matrix products, arithmetic and copies ran while one was open for 7% -> 10% of each run, Pallas kernels for 0% -> 0%
where the time goes in v8:
time: 144 us; the launch traced here: 143 us
  starting transfers between devices  62.2 us (43%)
  waiting for transfers between devices  46.3 us (32%)
  between operations  14.5 us (10%)
  local copies, waits for them, and re-layouts  9.31 us (6%)
  matrix products  6.38 us (4%)
  blocking collectives  2.37 us (2%)
  other arithmetic  1.85 us (1%)
    all_to_all x3, starting transfers between devices, exchange(): lax.all_to_all(blocks, axis, split_axis=0, concat_axis=0, tiled=False)  31.3 us
    all_to_all x3, waiting for transfers between devices, exchange(): lax.all_to_all(blocks, axis, split_axis=0, concat_axis=0, tiled=False)  17.3 us
    ppermute x3, starting transfers between devices, local(): lax.ppermute(pregrad[k], 'x', shift(k))  8.97 us
    ppermute x1, waiting for transfers between devices, near_x(): lax.ppermute(block, 'x', shift(-1))  8.95 us
    ppermute x1, starting transfers between devices, local(): turned = lax.ppermute(preact, ('y', 'x'), swap)  5.8 us
    ppermute x1, starting transfers between devices, far_x(): lax.ppermute(after[half:], 'x', shift(-1))  5.6 us
    ppermute x1, waiting for transfers between devices, far_x(): lax.ppermute(before[:half], 'x', shift(1))  5.37 us
    ppermute x3, waiting for transfers between devices, local(): lax.ppermute(pregrad[k], 'x', shift(k))  4.85 us
  transfers between devices with their start and end apart: 14, of which 11 were waited for; matrix products, arithmetic and copies ran while one was open for 10% of the time, Pallas kernels for 0%

profile of v8, /device:TPU:24, one launch (start us, length us, event | category | flops | bytes accessed | tf_op | source)
XLA Modules:
  0.0 142.9 jit_solution(16919197695779541272)
XLA Ops:
  7.2 0.8 reshape.55
  8.0 0.8 reshape.53
  8.9 1.0 broadcast_in_dim.8
  9.8 15.2 %all-to-all-start = ((bf16[16,48,512]{2,1,0:T(8,128)(2,1)}), bf16[16,48,512]{2,1,0:T(8,128)(2,1)S(1)}, u32[]{:S(2)}, u32[]{:S(2)}) async-start(bf16[16,48,512]{2,1,0:T(8,128)(2,1)} %broadcast_in_dim.8), calls=%async_computation | async-start | bytes 1572864 | tf_op jit(solution)/shard_map/all_to_all | solution.py:20
  25.1 0.7 all-gather.6.cloned.1.call-update
  25.8 4.7 %collective-permute-start.2 = (bf16[256,1024]{1,0:T(8,128)(2,1)S(1)}, bf16[256,1024]{1,0:T(8,128)(2,1)S(1)}, u32[]{:S(2)}, u32[]{:S(2)}) collective-permute-start(bf16[256,1024]{1,0:T(8,128)(2,1)S(1)} %copy-done.3), channel_id=1, source_target_pairs={{0,48},{16,0},{32,16},{48,32},{1,49},{17,1},{33,17},{49,33},{2,50}... | collective-permute-start | bytes 1572872 | tf_op jit(solution)/shard_map/ppermute | solution.py:44
  30.5 1.9 %collective-permute-start.1 = (bf16[256,1024]{1,0:T(8,128)(2,1)S(1)}, bf16[256,1024]{1,0:T(8,128)(2,1)S(1)}, u32[]{:S(2)}, u32[]{:S(2)}) collective-permute-start(bf16[256,1024]{1,0:T(8,128)(2,1)S(1)} %copy-done.3), channel_id=1, source_target_pairs={{0,16},{16,32},{32,48},{48,0},{1,17},{17,33},{33,49},{49,1},{2,18}... | collective-permute-start | bytes 1572872 | tf_op jit(solution)/shard_map/ppermute | solution.py:44
  32.4 9.0 %collective-permute-done.2 = bf16[256,1024]{1,0:T(8,128)(2,1)S(1)} collective-permute-done((bf16[256,1024]{1,0:T(8,128)(2,1)S(1)}, bf16[256,1024]{1,0:T(8,128)(2,1)S(1)}, u32[]{:S(2)}, u32[]{:S(2)}) %collective-permute-start.2) | collective-permute-done | bytes 524320 | tf_op jit(solution)/shard_map/ppermute | solution.py:44
  41.4 5.6 %collective-permute-start.4 = (bf16[128,1024]{1,0:T(8,128)(2,1)S(1)}, bf16[128,1024]{1,0:T(8,128)(2,1)S(1)}, u32[]{:S(2)}, u32[]{:S(2)}) collective-permute-start(bf16[128,1024]{1,0:T(8,128)(2,1)S(1)} %slice.80), channel_id=1, source_target_pairs={{0,48},{16,0},{32,16},{48,32},{1,49},{17,1},{33,17},{49,33},{2,50}... | collective-permute-start | bytes 786440 | tf_op jit(solution)/shard_map/ppermute | solution.py:50
  47.1 1.9 %collective-permute-start.3 = (bf16[128,1024]{1,0:T(8,128)(2,1)S(1)}, bf16[128,1024]{1,0:T(8,128)(2,1)S(1)}, u32[]{:S(2)}, u32[]{:S(2)}) collective-permute-start(bf16[128,1024]{1,0:T(8,128)(2,1)S(1)} %slice.79), channel_id=1, source_target_pairs={{0,16},{16,32},{32,48},{48,0},{1,17},{17,33},{33,49},{49,1},{2,18}... | collective-permute-start | bytes 786440 | tf_op jit(solution)/shard_map/ppermute | solution.py:50
  49.0 5.8 %collective-permute-start = (bf16[96,256]{1,0:T(8,128)(2,1)S(1)}, bf16[96,256]{1,0:T(8,128)(2,1)S(1)}, u32[]{:S(2)}, u32[]{:S(2)}) collective-permute-start(bf16[96,256]{1,0:T(8,128)(2,1)S(1)} %copy-done.1), channel_id=1, source_target_pairs={{0,0},{16,128},{32,256},{48,384},{128,400},{144,16},{160,144},{176... | collective-permute-start | bytes 147464 | tf_op jit(solution)/shard_map/ppermute | solution.py:65
  54.8 3.8 %collective-permute-done.4 = bf16[128,1024]{1,0:T(8,128)(2,1)S(1)} collective-permute-done((bf16[128,1024]{1,0:T(8,128)(2,1)S(1)}, bf16[128,1024]{1,0:T(8,128)(2,1)S(1)}, u32[]{:S(2)}, u32[]{:S(2)}) %collective-permute-start.4) | collective-permute-done | bytes 262176 | tf_op jit(solution)/shard_map/ppermute | solution.py:50
  58.6 5.4 %collective-permute-done.3 = bf16[128,1024]{1,0:T(8,128)(2,1)S(1)} collective-permute-done((bf16[128,1024]{1,0:T(8,128)(2,1)S(1)}, bf16[128,1024]{1,0:T(8,128)(2,1)S(1)}, u32[]{:S(2)}, u32[]{:S(2)}) %collective-permute-start.3) | collective-permute-done | bytes 262176 | tf_op jit(solution)/shard_map/ppermute | solution.py:50
  64.0 2.8 %collective-permute-done = bf16[96,256]{1,0:T(8,128)(2,1)S(1)} collective-permute-done((bf16[96,256]{1,0:T(8,128)(2,1)S(1)}, bf16[96,256]{1,0:T(8,128)(2,1)S(1)}, u32[]{:S(2)}, u32[]{:S(2)}) %collective-permute-start) | collective-permute-done | bytes 49184 | tf_op jit(solution)/shard_map/ppermute | solution.py:65
  66.8 0.4 copy.27
  67.3 0.4 copy.28
  67.7 0.4 copy.34
  68.2 0.9 pad_maximum_fusion.1
  69.2 0.3 reshape.79
  69.4 0.8 fusion
  70.3 1.9 %collective-permute-start.5 = (f32[4,96,256]{2,1,0:T(8,128)S(1)}, f32[4,96,256]{2,1,0:T(8,128)S(1)}, u32[]{:S(2)}, u32[]{:S(2)}) collective-permute-start(f32[4,96,256]{2,1,0:T(8,128)S(1)} %dynamic-slice_bitcast_fusion), channel_id=1, source_target_pairs={{0,64},{64,0},{1,65},{65,1},{2,66},{66,2},{3,67},{67,3},{4,68},{68... | collective-permute-start | bytes 1179656 | tf_op jit(solution)/shard_map/ppermute | solution.py:78
  72.3 1.7 %collective-permute-done.5 = f32[4,96,256]{2,1,0:T(8,128)S(1)} collective-permute-done((f32[4,96,256]{2,1,0:T(8,128)S(1)}, f32[4,96,256]{2,1,0:T(8,128)S(1)}, u32[]{:S(2)}, u32[]{:S(2)}) %collective-permute-start.5) | collective-permute-done | bytes 393248 | tf_op jit(solution)/shard_map/ppermute | solution.py:78
  73.9 0.1 fusion.20
  74.0 1.2 broadcast_in_dim.21
  75.2 4.5 %all-to-all-start.1 = ((bf16[4,6,96,256]{3,2,1,0:T(8,128)(2,1)}), bf16[4,6,96,256]{3,2,1,0:T(8,128)(2,1)S(1)}, u32[]{:S(2)}, u32[]{:S(2)}) async-start(bf16[4,6,96,256]{3,2,1,0:T(8,128)(2,1)} %broadcast_in_dim.21), calls=%async_computation.1 | async-start | bytes 2359296 | tf_op jit(solution)/shard_map/all_to_all | solution.py:20
  79.7 1.7 %constant_dynamic-slice_fusion.7 = (bf16[1,1024,256]{2,1,0:T(8,128)(2,1)S(1)}, bf16[1,1024,256]{2,1,0:T(8,128)(2,1)S(1)}, bf16[1,1024,256]{2,1,0:T(8,128)(2,1)S(1)}, bf16[1,1024,256]{2,1,0:T(8,128)(2,1)S(1)}) fusion(bf16[4,1024,256]{2,1,0:T(8,128)(2,1)} %bitcast.87, s32[]{:T(128)S(6)} %select_n.71, s32[]{:T(128)S(6)} %select_n.77, s32[]{:T(128)S(6)} %select_n.75, ...), kind=kLoop, calls=%fused_computation.61 | loop fusion | bytes 4194320 | tf_op jit(solution)/shard_map/jit(dynamic_index_in_dim)/dynamic_slice | solution.py:55
  81.4 0.3 pad_maximum_fusion
  81.7 12.8 %all-to-all-done.1 = bf16[4,6,96,256]{3,2,1,0:T(8,128)(2,1)S(1)} async-done(((bf16[4,6,96,256]{3,2,1,0:T(8,128)(2,1)}), bf16[4,6,96,256]{3,2,1,0:T(8,128)(2,1)S(1)}, u32[]{:S(2)}, u32[]{:S(2)}) %all-to-all-start.1) | async-done | bytes 1179680 | tf_op jit(solution)/shard_map/all_to_all | solution.py:20
  94.5 0.1 convert_reduce_fusion
  94.6 0.2 fusion.21
  94.8 2.4 %all-gather.1 = bf16[8,192,256]{2,1,0:T(8,128)(2,1)S(1)} all-gather(bf16[8,96,256]{2,1,0:T(8,128)(2,1)S(1)} %pad_maximum_fusion.3), channel_id=3, replica_groups=mesh['y'=4,'c'=2,'x'=4,'za'=4,'zb'=4] {'c'}, dimensions={1}, use_global_device_ids=true | all-gather | bytes 1179648 | tf_op jit(solution)/shard_map/all_gather | solution.py:86
  97.2 0.8 fusion.12
  98.0 0.3 reshape_reshape.10
  98.3 0.1 copy.31
  98.5 1.0 copy.32
  99.4 11.6 %all-to-all-start.2 = ((bf16[16,24,512]{2,1,0:T(8,128)(2,1)}), bf16[16,24,512]{2,1,0:T(8,128)(2,1)S(1)}, u32[]{:S(2)}, u32[]{:S(2)}) async-start(bf16[16,24,512]{2,1,0:T(8,128)(2,1)} %copy.32), calls=%async_computation.2 | async-start | bytes 786432 | tf_op jit(solution)/shard_map/all_to_all | solution.py:20
  111.0 1.9 %collective-permute-start.8 = (bf16[192,256]{1,0:T(8,128)(2,1)S(1)}, bf16[192,256]{1,0:T(8,128)(2,1)S(1)}, u32[]{:S(2)}, u32[]{:S(2)}) collective-permute-start(bf16[192,256]{1,0:T(8,128)(2,1)S(1)} %get-tuple-element.34), channel_id=1, source_target_pairs={{0,16},{16,32},{32,48},{48,0},{1,17},{17,33},{33,49},{49,1},{2,18}... | collective-permute-start | bytes 294920 | tf_op jit(solution)/shard_map/ppermute | solution.py:92
  112.9 2.7 %collective-permute-start.7 = (bf16[192,256]{1,0:T(8,128)(2,1)S(1)}, bf16[192,256]{1,0:T(8,128)(2,1)S(1)}, u32[]{:S(2)}, u32[]{:S(2)}) collective-permute-start(bf16[192,256]{1,0:T(8,128)(2,1)S(1)} %get-tuple-element.35), channel_id=1, source_target_pairs={{0,32},{16,48},{32,0},{48,16},{1,33},{17,49},{33,1},{49,17},{2,34}... | collective-permute-start | bytes 294920 | tf_op jit(solution)/shard_map/ppermute | solution.py:92
  115.7 4.3 %collective-permute-start.6 = (bf16[192,256]{1,0:T(8,128)(2,1)S(1)}, bf16[192,256]{1,0:T(8,128)(2,1)S(1)}, u32[]{:S(2)}, u32[]{:S(2)}) collective-permute-start(bf16[192,256]{1,0:T(8,128)(2,1)S(1)} %get-tuple-element.36), channel_id=1, source_target_pairs={{0,48},{16,0},{32,16},{48,32},{1,49},{17,1},{33,17},{49,33},{2,50}... | collective-permute-start | bytes 294920 | tf_op jit(solution)/shard_map/ppermute | solution.py:92
  120.1 3.4 %collective-permute-done.8 = bf16[192,256]{1,0:T(8,128)(2,1)S(1)} collective-permute-done((bf16[192,256]{1,0:T(8,128)(2,1)S(1)}, bf16[192,256]{1,0:T(8,128)(2,1)S(1)}, u32[]{:S(2)}, u32[]{:S(2)}) %collective-permute-start.8) | collective-permute-done | bytes 98336 | tf_op jit(solution)/shard_map/ppermute | solution.py:92
  123.5 0.2 collective-permute-done.7
  123.7 1.2 collective-permute-done.6
  125.1 1.0 all-gather.8.cloned.1.call-done
  126.1 3.1 %fusion.11 = f32[256,1024]{1,0:T(8,128)} fusion(bf16[4,192,256]{2,1,0:T(8,128)(2,1)S(1)} %slice-done, bf16[4,2,192,1024]{3,2,1,0:T(8,128)(2,1)} %bitcast.108), kind=kOutput, calls=%fused_computation.15 | convolution fusion | flops 402653184 | bytes 3014656 | tf_op jit(solution)/shard_map/xtf,xtd->fd/dot_general | solution.py:97
  129.2 1.6 %fusion.10 = f32[1024,256]{1,0:T(8,128)} fusion(bf16[4,192,256]{2,1,0:T(8,128)(2,1)S(1)} %pad_maximum_fusion.5, bf16[4,2,192,1024]{3,2,1,0:T(8,128)(2,1)S(1)} %bitcast.109), kind=kOutput, calls=%fused_computation.14 | convolution fusion | flops 402653184 | bytes 3014656 | tf_op jit(solution)/shard_map/xtd,xtf->df/dot_general | solution.py:98
  130.8 4.5 %all-to-all-done.2 = bf16[16,24,512]{2,1,0:T(8,128)(2,1)S(1)} async-done(((bf16[16,24,512]{2,1,0:T(8,128)(2,1)}), bf16[16,24,512]{2,1,0:T(8,128)(2,1)S(1)}, u32[]{:S(2)}, u32[]{:S(2)}) %all-to-all-start.2) | async-done | bytes 393248 | tf_op jit(solution)/shard_map/all_to_all | solution.py:20
  135.3 0.1 reduce_sum.22
  135.4 0.6 copy.42
  (39 shorter events, 0.8 us)
Async XLA Ops:
  7.2 18.7 %copy-start.3 = (bf16[256,1024]{1,0:T(8,128)(2,1)S(1)}, bf16[256,1024]{1,0:T(8,128)(2,1)}, u32[]{:S(2)}) copy-start(bf16[256,1024]{1,0:T(8,128)(2,1)} %param.9) | copy-start | bytes 1572868
  8.8 40.2 %copy-start.1 = (bf16[96,256]{1,0:T(8,128)(2,1)S(1)}, bf16[96,256]{1,0:T(8,128)(2,1)}, u32[]{:S(2)}) copy-start(bf16[96,256]{1,0:T(8,128)(2,1)} %param.7) | copy-start | bytes 147460
  9.8 56.9 %all-to-all-start = ((bf16[16,48,512]{2,1,0:T(8,128)(2,1)}), bf16[16,48,512]{2,1,0:T(8,128)(2,1)S(1)}, u32[]{:S(2)}, u32[]{:S(2)}) async-start(bf16[16,48,512]{2,1,0:T(8,128)(2,1)} %broadcast_in_dim.8), calls=%async_computation | async-start | bytes 1572864 | tf_op jit(solution)/shard_map/all_to_all | solution.py:20
  25.0 54.7 %all-gather.6.cloned.1.call-start = ((), (), s32[]{:S(2)}) async-start(), calls=%async_computation.3 | async-start | bytes 2621440 | tf_op jit(solution)/shard_map/all_gather | solution.py:70
  25.8 100.3 %all-gather.8.cloned.1.call-start = ((), (), s32[]{:S(2)}) async-start(), calls=%async_computation.4 | async-start | bytes 3932160 | tf_op jit(solution)/shard_map/all_gather | solution.py:95
  25.8 15.6 %collective-permute-start.2 = (bf16[256,1024]{1,0:T(8,128)(2,1)S(1)}, bf16[256,1024]{1,0:T(8,128)(2,1)S(1)}, u32[]{:S(2)}, u32[]{:S(2)}) collective-permute-start(bf16[256,1024]{1,0:T(8,128)(2,1)S(1)} %copy-done.3), channel_id=1, source_target_pairs={{0,48},{16,0},{32,16},{48,32},{1,49},{17,1},{33,17},{49,33},{2,50}... | collective-permute-start | bytes 1572872 | tf_op jit(solution)/shard_map/ppermute | solution.py:44
  30.5 16.5 %collective-permute-start.1 = (bf16[256,1024]{1,0:T(8,128)(2,1)S(1)}, bf16[256,1024]{1,0:T(8,128)(2,1)S(1)}, u32[]{:S(2)}, u32[]{:S(2)}) collective-permute-start(bf16[256,1024]{1,0:T(8,128)(2,1)S(1)} %copy-done.3), channel_id=1, source_target_pairs={{0,16},{16,32},{32,48},{48,0},{1,17},{17,33},{33,49},{49,1},{2,18}... | collective-permute-start | bytes 1572872 | tf_op jit(solution)/shard_map/ppermute | solution.py:44
  41.4 17.2 %collective-permute-start.4 = (bf16[128,1024]{1,0:T(8,128)(2,1)S(1)}, bf16[128,1024]{1,0:T(8,128)(2,1)S(1)}, u32[]{:S(2)}, u32[]{:S(2)}) collective-permute-start(bf16[128,1024]{1,0:T(8,128)(2,1)S(1)} %slice.80), channel_id=1, source_target_pairs={{0,48},{16,0},{32,16},{48,32},{1,49},{17,1},{33,17},{49,33},{2,50}... | collective-permute-start | bytes 786440 | tf_op jit(solution)/shard_map/ppermute | solution.py:50
  47.1 16.9 %collective-permute-start.3 = (bf16[128,1024]{1,0:T(8,128)(2,1)S(1)}, bf16[128,1024]{1,0:T(8,128)(2,1)S(1)}, u32[]{:S(2)}, u32[]{:S(2)}) collective-permute-start(bf16[128,1024]{1,0:T(8,128)(2,1)S(1)} %slice.79), channel_id=1, source_target_pairs={{0,16},{16,32},{32,48},{48,0},{1,17},{17,33},{33,49},{49,1},{2,18}... | collective-permute-start | bytes 786440 | tf_op jit(solution)/shard_map/ppermute | solution.py:50
  49.0 17.8 %collective-permute-start = (bf16[96,256]{1,0:T(8,128)(2,1)S(1)}, bf16[96,256]{1,0:T(8,128)(2,1)S(1)}, u32[]{:S(2)}, u32[]{:S(2)}) collective-permute-start(bf16[96,256]{1,0:T(8,128)(2,1)S(1)} %copy-done.1), channel_id=1, source_target_pairs={{0,0},{16,128},{32,256},{48,384},{128,400},{144,16},{160,144},{176... | collective-permute-start | bytes 147464 | tf_op jit(solution)/shard_map/ppermute | solution.py:65
  70.3 3.6 %collective-permute-start.5 = (f32[4,96,256]{2,1,0:T(8,128)S(1)}, f32[4,96,256]{2,1,0:T(8,128)S(1)}, u32[]{:S(2)}, u32[]{:S(2)}) collective-permute-start(f32[4,96,256]{2,1,0:T(8,128)S(1)} %dynamic-slice_bitcast_fusion), channel_id=1, source_target_pairs={{0,64},{64,0},{1,65},{65,1},{2,66},{66,2},{3,67},{67,3},{4,68},{68... | collective-permute-start | bytes 1179656 | tf_op jit(solution)/shard_map/ppermute | solution.py:78
  75.2 19.2 %all-to-all-start.1 = ((bf16[4,6,96,256]{3,2,1,0:T(8,128)(2,1)}), bf16[4,6,96,256]{3,2,1,0:T(8,128)(2,1)S(1)}, u32[]{:S(2)}, u32[]{:S(2)}) async-start(bf16[4,6,96,256]{3,2,1,0:T(8,128)(2,1)} %broadcast_in_dim.21), calls=%async_computation.1 | async-start | bytes 2359296 | tf_op jit(solution)/shard_map/all_to_all | solution.py:20
  97.2 22.9 %copy-start = (bf16[8,192,256]{2,1,0:T(8,128)(2,1)}, bf16[8,192,256]{2,1,0:T(8,128)(2,1)S(1)}, u32[]{:S(2)}) copy-start(bf16[8,192,256]{2,1,0:T(8,128)(2,1)S(1)} %all-gather.1) | copy-start | bytes 2359300
  99.4 35.9 %all-to-all-start.2 = ((bf16[16,24,512]{2,1,0:T(8,128)(2,1)}), bf16[16,24,512]{2,1,0:T(8,128)(2,1)S(1)}, u32[]{:S(2)}, u32[]{:S(2)}) async-start(bf16[16,24,512]{2,1,0:T(8,128)(2,1)} %copy.32), calls=%async_computation.2 | async-start | bytes 786432 | tf_op jit(solution)/shard_map/all_to_all | solution.py:20
  111.0 12.5 %collective-permute-start.8 = (bf16[192,256]{1,0:T(8,128)(2,1)S(1)}, bf16[192,256]{1,0:T(8,128)(2,1)S(1)}, u32[]{:S(2)}, u32[]{:S(2)}) collective-permute-start(bf16[192,256]{1,0:T(8,128)(2,1)S(1)} %get-tuple-element.34), channel_id=1, source_target_pairs={{0,16},{16,32},{32,48},{48,0},{1,17},{17,33},{33,49},{49,1},{2,18}... | collective-permute-start | bytes 294920 | tf_op jit(solution)/shard_map/ppermute | solution.py:92
  112.9 10.8 %collective-permute-start.7 = (bf16[192,256]{1,0:T(8,128)(2,1)S(1)}, bf16[192,256]{1,0:T(8,128)(2,1)S(1)}, u32[]{:S(2)}, u32[]{:S(2)}) collective-permute-start(bf16[192,256]{1,0:T(8,128)(2,1)S(1)} %get-tuple-element.35), channel_id=1, source_target_pairs={{0,32},{16,48},{32,0},{48,16},{1,33},{17,49},{33,1},{49,17},{2,34}... | collective-permute-start | bytes 294920 | tf_op jit(solution)/shard_map/ppermute | solution.py:92
  115.7 9.3 %collective-permute-start.6 = (bf16[192,256]{1,0:T(8,128)(2,1)S(1)}, bf16[192,256]{1,0:T(8,128)(2,1)S(1)}, u32[]{:S(2)}, u32[]{:S(2)}) collective-permute-start(bf16[192,256]{1,0:T(8,128)(2,1)S(1)} %get-tuple-element.36), channel_id=1, source_target_pairs={{0,48},{16,0},{32,16},{48,32},{1,49},{17,1},{33,17},{49,33},{2,50}... | collective-permute-start | bytes 294920 | tf_op jit(solution)/shard_map/ppermute | solution.py:92
  120.1 6.0 %slice-start = ((bf16[8,192,256]{2,1,0:T(8,128)(2,1)}), bf16[4,192,256]{2,1,0:T(8,128)(2,1)S(1)}, s32[]{:S(2)}) async-start(bf16[8,192,256]{2,1,0:T(8,128)(2,1)} %copy-done), calls=%async_computation.5 | async-start | bytes 786432 | tf_op jit(solution)/shard_map/slice | solution.py:87
  126.1 3.1 %copy-start.2 = (bf16[1536,1024]{1,0:T(8,128)(2,1)S(1)}, bf16[1536,1024]{1,0:T(8,128)(2,1)}, u32[]{:S(2)}) copy-start(bf16[1536,1024]{1,0:T(8,128)(2,1)} %all-gather.8.cloned.1.call-done) | copy-start | bytes 9437188
Sparse Core Ops, SparseCore 0:
  28.0 45.1 all-gather.5
  75.8 50.2 all-gather.7

commit v9 on v8

v9 whole, which is shorter than its diff:
```python
import math

import jax
import jax.numpy as jnp
from jax import lax
from jax.experimental import pallas as pl
from jax.experimental.pallas import tpu as pltpu
from jax.sharding import Mesh, PartitionSpec as P

BF = jnp.bfloat16
F32 = jnp.float32


def gelu_parts(preact):
    value = preact.astype(F32)
    normal_cdf = 0.5 * (1.0 + jax.scipy.special.erf(value / math.sqrt(2.0)))
    density = jnp.exp(-0.5 * value * value) / math.sqrt(2.0 * math.pi)
    return (value * normal_cdf, normal_cdf + value * density)


def exchange(blocks, axis):
    return lax.all_to_all(blocks, axis, split_axis=0, concat_axis=0, tiled=False)


def spread(block, axis, n=4):
    return exchange(jnp.broadcast_to(block[None], (n,) + block.shape), axis)


def call(body, outs, scratch, flops, operands, smem=0):
    moved = sum(a.size * a.dtype.itemsize for a in (*operands, *outs))
    spaces = [pltpu.SMEM] * smem + [pltpu.VMEM] * (len(operands) - smem)
    return pl.pallas_call(
        body,
        out_shape=outs,
        in_specs=[pl.BlockSpec(memory_space=space) for space in spaces],
        out_specs=[pl.BlockSpec(memory_space=pltpu.VMEM)] * len(outs),
        scratch_shapes=[pltpu.VMEM(shape, F32) for shape in scratch],
        cost_estimate=pl.CostEstimate(flops=flops, bytes_accessed=moved, transcendentals=0),
        compiler_params=pltpu.CompilerParams(vmem_limit_bytes=40 * 2**20),
    )(*operands)


def times_transposed(a, b):
    return lax.dot_general(a, b, (((1,), (1,)), ((), ())), preferred_element_type=F32)


def lay_out_kernel(grad_ref, in_ref, out_ref, rows):
    for k, ref in enumerate((grad_ref, in_ref)):
        block = ref[...].astype(F32)
        rows[24 * k : 24 * k + 12] = block[:, :512]
        rows[24 * k + 12 : 24 * k + 24] = block[:, 512:]
    block = rows[...].astype(BF)
    for z in range(16):
        out_ref[z] = block


def hidden_kernel(core_ref, both_ref, own_ref, after_ref, far0_ref, far1_ref, before_ref, *refs):
    mine_ref, theirs_ref, tokens_ref, rows, grads, ins = refs
    for z in range(16):
        rows[z] = both_ref[z].astype(F32)
        here = slice(12 * z, 12 * z + 12)
        grads[here, :512] = rows[z, 0:12]
        grads[here, 512:] = rows[z, 12:24]
        ins[here, :512] = rows[z, 24:36]
        ins[here, 512:] = rows[z, 36:48]
    tokens_ref[0] = grads[...].astype(BF)
    tokens_ref[1] = ins[...].astype(BF)
    first = pl.multiple_of(core_ref[0] * 96, 96)
    second = pl.multiple_of(96 - core_ref[0] * 96, 96)
    for start, out_ref in ((second, theirs_ref), (first, mine_ref)):
        half = grads[pl.ds(start, 96)].astype(BF)
        out_ref[0] = times_transposed(half, own_ref[...])
        out_ref[1] = times_transposed(half, after_ref[...])
        out_ref[2, :, :128] = times_transposed(half, far0_ref[...])
        out_ref[2, :, 128:] = times_transposed(half, far1_ref[...])
        out_ref[3] = times_transposed(half, before_ref[...])


def part_kernel(x_ref, pregrad_ref, up_ref, out_ref, total, rows):
    for d in range(4):
        product = times_transposed(pregrad_ref[d], up_ref[lax.rem(x_ref[0] + d, 4)])
        total[...] = product if d == 0 else total[...] + product
    for z in range(16):
        here = slice(12 * z, 12 * z + 12)
        rows[z, 0:12] = total[here, :512]
        rows[z, 12:24] = total[here, 512:]
        out_ref[z] = rows[z].astype(BF)


def sum_kernel(part_ref, out_ref, rows):
    total = part_ref[0].astype(F32)
    for z in range(1, 16):
        total = total + part_ref[z].astype(F32)
    rows[...] = total
    out_ref[:, :512] = rows[0:12].astype(BF)
    out_ref[:, 512:] = rows[12:24].astype(BF)


def shift(k):
    return [(i, (i + k) % 4) for i in range(4)]


def near_x(block):
    return lax.ppermute(block, "x", shift(1)), lax.ppermute(block, "x", shift(-1))


def far_x(before, after):
    half = before.shape[0] // 2
    return lax.ppermute(before[:half], "x", shift(1)), lax.ppermute(after[half:], "x", shift(-1))


def turn_by(blocks, start):
    turned = [lax.dynamic_index_in_dim(blocks, (start + i) % 4, keepdims=True) for i in range(4)]
    return jnp.concatenate(turned)


def local(inputs, out_grad, preact, up_weight, down_weight):
    core, at_x = lax.axis_index("c"), lax.axis_index("x")

    sixteen = jax.ShapeDtypeStruct((16, 48, 512), BF)
    (both,) = call(lay_out_kernel, [sixteen], [(48, 512)], 0, (out_grad, inputs))
    both = exchange(both, ("za", "zb"))
    swap = [(4 * a + b, 4 * ((b - a) % 4) + a) for a in range(4) for b in range(4)]
    turned = lax.ppermute(preact, ("y", "x"), swap)
    before, after = near_x(down_weight)
    far = far_x(before, after)
    both, turned, before, after, far = lax.optimization_barrier((both, turned, before, after, far))
    wide_up = lax.all_gather(up_weight, "x", axis=0, tiled=False)

    half = jax.ShapeDtypeStruct((4, 96, 256), F32)
    mine, theirs, tokens = call(
        hidden_kernel,
        [half, half, jax.ShapeDtypeStruct((2, 192, 1024), BF)],
        [(16, 48, 512), (192, 1024), (192, 1024)],
        2 * 192 * 1024 * 1024,
        (core[None], both, down_weight, after, *far, before),
        smem=1,
    )
    pair = (mine + lax.ppermute(theirs, "c", [(0, 1), (1, 0)])).astype(BF)
    activ, _ = gelu_parts(preact)
    own = spread(jnp.concatenate([pair, activ.astype(BF)[None], turned[None]]), "y")
    own, wide_up = lax.optimization_barrier((own, wide_up))
    hidden_grad = own[:, :4].astype(F32).sum(0)
    _, slope = gelu_parts(own[:, 5])
    own = jnp.concatenate([(hidden_grad * slope).astype(BF), own[:, 4]])
    own = lax.all_gather(own, "c", axis=1, tiled=False).reshape(8, 192, 256)
    pregrad, all_activ = own[:4], own[4:]

    (part,) = call(
        part_kernel,
        [jax.ShapeDtypeStruct((16, 24, 512), BF)],
        [(192, 1024), (16, 24, 512)],
        2 * 192 * 1024 * 1024,
        (at_x[None], own, wide_up),
        smem=1,
    )
    part = exchange(part, ("za", "zb"))

    sent = [pregrad[0]] + [lax.ppermute(pregrad[k], "x", shift(k)) for k in (3, 2, 1)]
    all_pregrad = turn_by(jnp.stack(sent), 4 - at_x)
    all_pregrad, all_activ = lax.optimization_barrier((all_pregrad, all_activ))
    all_both = lax.all_gather(tokens, "x", axis=0, tiled=False)
    down_grad = jnp.einsum("xtf,xtd->fd", all_activ, all_both[:, 0], preferred_element_type=F32)
    up_grad = jnp.einsum("xtd,xtf->df", all_both[:, 1], all_pregrad, preferred_element_type=F32)
    part, up_grad, down_grad = lax.optimization_barrier((part, up_grad, down_grad))
    (input_grad,) = call(sum_kernel, [jax.ShapeDtypeStruct((12, 1024), BF)], [(24, 512)], 0, (part,))
    return (input_grad, up_grad, down_grad)


def solution(mesh):
    fine = Mesh(mesh.devices.reshape(4, 2, 4, 4, 4), ("y", "c", "x", "za", "zb"))
    tokens, width = ("x", "za", "zb"), ("y", "c")
    return jax.shard_map(
        local,
        mesh=fine,
        in_specs=(
            P(tokens, width),
            P(tokens, width),
            P(width, tokens),
            P(width, tokens),
            P(tokens, width),
        ),
        out_specs=(P(tokens, width), P(width, tokens), P(tokens, width)),
        check_vma=False,
    )
```

time: 144 us -> 148 us (1.028)
  waiting for transfers between devices: 46.3 us -> 53.7 us
  Pallas kernels: 0 us -> 5.61 us
  local copies, waits for them, and re-layouts: 9.31 us -> 4.17 us
  matrix products: 6.38 us -> 4.72 us
    ppermute x1, waiting for transfers between devices: 0.01 us -> 17.3 us  [near_x(): lax.ppermute(block, 'x', shift(1))]
    ppermute x1, waiting for transfers between devices: 8.95 us -> 2 us  [near_x(): lax.ppermute(block, 'x', shift(-1))]
    pallas_call x0 -> x4, Pallas kernels: none -> 5.61 us  [call(): pl.pallas_call(body, out_shape=outs, in_specs=[pl.BlockSpec(memory_space=...]
    ppermute x1, waiting for transfers between devices: 5.37 us -> 0.01 us  [far_x(): lax.ppermute(before[:half], 'x', shift(1))]
    ppermute x1, waiting for transfers between devices: 2.78 us -> 7.41 us  [local(): turned = lax.ppermute(preact, ('y', 'x'), swap)]
    ppermute x1, waiting for transfers between devices: 3.76 us -> 0.01 us  [far_x(): lax.ppermute(after[half:], 'x', shift(-1))]
    ppermute x1, starting transfers between devices: 5.8 us -> 2.41 us  [local(): turned = lax.ppermute(preact, ('y', 'x'), swap)]
    all_to_all x3, waiting for transfers between devices: 17.3 us -> 20 us  [exchange(): lax.all_to_all(blocks, axis, split_axis=0, concat_axis=0, tiled=False)]
  transfers between devices with their start and end apart: 14 -> 14, of which waited for: 11 -> 8; matrix products, arithmetic and copies ran while one was open for 10% -> 4% of each run, Pallas kernels for 0% -> 3%
where the time goes in v9:
time: 148 us; the launch traced here: 147 us
  starting transfers between devices  60.8 us (41%)
  waiting for transfers between devices  53.7 us (36%)
  between operations  14.4 us (10%)
  Pallas kernels  5.61 us (4%)
  matrix products  4.72 us (3%)
  local copies, waits for them, and re-layouts  4.17 us (3%)
  blocking collectives  2.5 us (2%)
    all_to_all x3, starting transfers between devices, exchange(): lax.all_to_all(blocks, axis, split_axis=0, concat_axis=0, tiled=False)  31.4 us
    all_to_all x3, waiting for transfers between devices, exchange(): lax.all_to_all(blocks, axis, split_axis=0, concat_axis=0, tiled=False)  20 us
    ppermute x1, waiting for transfers between devices, near_x(): lax.ppermute(block, 'x', shift(1))  17.3 us
    ppermute x3, starting transfers between devices, local(): lax.ppermute(pregrad[k], 'x', shift(k))  9.5 us
    ppermute x1, waiting for transfers between devices, local(): turned = lax.ppermute(preact, ('y', 'x'), swap)  7.41 us
    pallas_call x4, Pallas kernels, call(): pl.pallas_call(body, out_shape=outs, in_specs=[pl.BlockSpec(memory_space=...  5.61 us
    ppermute x1, starting transfers between devices, far_x(): lax.ppermute(after[half:], 'x', shift(-1))  5.36 us
    ppermute x3, waiting for transfers between devices, local(): lax.ppermute(pregrad[k], 'x', shift(k))  4.5 us
  transfers between devices with their start and end apart: 14, of which 8 were waited for; matrix products, arithmetic and copies ran while one was open for 4% of the time, Pallas kernels for 3%

profile of v9, /device:TPU:24, one launch (start us, length us, event | category | flops | bytes accessed | tf_op | source)
XLA Modules:
  0.0 146.5 jit_solution(6953492947665404269)
XLA Ops:
  7.2 0.0 all-gather.6.cloned.1.call-start
  7.2 0.7 all-gather.6.cloned.1.call-update
  7.9 0.7 copy-done.3
  8.7 0.8 copy-done.4
  9.4 0.9 shard_map.76
  10.4 15.2 %all-to-all-start = ((bf16[16,48,512]{2,1,0:T(8,128)(2,1)}), bf16[16,48,512]{2,1,0:T(8,128)(2,1)S(1)}, u32[]{:S(2)}, u32[]{:S(2)}) async-start(bf16[16,48,512]{2,1,0:T(8,128)(2,1)} %shard_map.76), calls=%async_computation | async-start | bytes 1572864 | tf_op jit(solution)/shard_map/all_to_all | solution.py:22
  25.6 0.0 all-gather.8.cloned.1.call-start
  25.6 3.4 %collective-permute-start.1 = (bf16[256,1024]{1,0:T(8,128)(2,1)S(1)}, bf16[256,1024]{1,0:T(8,128)(2,1)S(1)}, u32[]{:S(2)}, u32[]{:S(2)}) collective-permute-start(bf16[256,1024]{1,0:T(8,128)(2,1)S(1)} %copy-done.2), channel_id=1, source_target_pairs={{0,16},{16,32},{32,48},{48,0},{1,17},{17,33},{33,49},{49,1},{2,18}... | collective-permute-start | bytes 1572872 | tf_op jit(solution)/shard_map/ppermute | solution.py:104
  29.0 3.7 %collective-permute-start.2 = (bf16[256,1024]{1,0:T(8,128)(2,1)S(1)}, bf16[256,1024]{1,0:T(8,128)(2,1)S(1)}, u32[]{:S(2)}, u32[]{:S(2)}) collective-permute-start(bf16[256,1024]{1,0:T(8,128)(2,1)S(1)} %copy-done.2), channel_id=1, source_target_pairs={{0,48},{16,0},{32,16},{48,32},{1,49},{17,1},{33,17},{49,33},{2,50}... | collective-permute-start | bytes 1572872 | tf_op jit(solution)/shard_map/ppermute | solution.py:104
  32.7 17.3 %collective-permute-done.1.before_ref = bf16[256,1024]{1,0:T(8,128)(2,1)S(1)} collective-permute-done((bf16[256,1024]{1,0:T(8,128)(2,1)S(1)}, bf16[256,1024]{1,0:T(8,128)(2,1)S(1)}, u32[]{:S(2)}, u32[]{:S(2)}) %collective-permute-start.1) | collective-permute-done | bytes 524320 | tf_op jit(solution)/shard_map/ppermute | solution.py:104
  50.0 3.1 %collective-permute-start.3 = (bf16[128,1024]{1,0:T(8,128)(2,1)S(1)}, bf16[128,1024]{1,0:T(8,128)(2,1)S(1)}, u32[]{:S(2)}, u32[]{:S(2)}) collective-permute-start(bf16[128,1024]{1,0:T(8,128)(2,1)S(1)} %slice.70), channel_id=1, source_target_pairs={{0,16},{16,32},{32,48},{48,0},{1,17},{17,33},{33,49},{49,1},{2,18}... | collective-permute-start | bytes 786440 | tf_op jit(solution)/shard_map/ppermute | solution.py:109
  53.2 2.0 %collective-permute-done.2.after_ref = bf16[256,1024]{1,0:T(8,128)(2,1)S(1)} collective-permute-done((bf16[256,1024]{1,0:T(8,128)(2,1)S(1)}, bf16[256,1024]{1,0:T(8,128)(2,1)S(1)}, u32[]{:S(2)}, u32[]{:S(2)}) %collective-permute-start.2) | collective-permute-done | bytes 524320 | tf_op jit(solution)/shard_map/ppermute | solution.py:104
  55.2 5.4 %collective-permute-start.4 = (bf16[128,1024]{1,0:T(8,128)(2,1)S(1)}, bf16[128,1024]{1,0:T(8,128)(2,1)S(1)}, u32[]{:S(2)}, u32[]{:S(2)}) collective-permute-start(bf16[128,1024]{1,0:T(8,128)(2,1)S(1)} %slice.71), channel_id=1, source_target_pairs={{0,48},{16,0},{32,16},{48,32},{1,49},{17,1},{33,17},{49,33},{2,50}... | collective-permute-start | bytes 786440 | tf_op jit(solution)/shard_map/ppermute | solution.py:109
  60.6 2.4 %collective-permute-start = (bf16[96,256]{1,0:T(8,128)(2,1)S(1)}, bf16[96,256]{1,0:T(8,128)(2,1)S(1)}, u32[]{:S(2)}, u32[]{:S(2)}) collective-permute-start(bf16[96,256]{1,0:T(8,128)(2,1)S(1)} %copy-done.8), channel_id=1, source_target_pairs={{0,0},{16,128},{32,256},{48,384},{128,400},{144,16},{160,144},{176... | collective-permute-start | bytes 147464 | tf_op jit(solution)/shard_map/ppermute | solution.py:124
  63.0 7.4 %collective-permute-done = bf16[96,256]{1,0:T(8,128)(2,1)S(1)} collective-permute-done((bf16[96,256]{1,0:T(8,128)(2,1)S(1)}, bf16[96,256]{1,0:T(8,128)(2,1)S(1)}, u32[]{:S(2)}, u32[]{:S(2)}) %collective-permute-start) | collective-permute-done | bytes 49184 | tf_op jit(solution)/shard_map/ppermute | solution.py:124
  70.4 0.0 collective-permute-done.3.far0_ref
  70.4 0.0 collective-permute-done.4.far1_ref
  70.4 0.0 all-to-all-done.both_ref
  70.4 0.6 copy-done.6
  71.0 2.4 %shard_map.77 = (f32[4,96,256]{2,1,0:T(8,128)S(1)}, f32[4,96,256]{2,1,0:T(8,128)S(1)}, bf16[2,192,1024]{2,1,0:T(8,128)(2,1)}) custom-call(s32[1]{0:T(128)} %bitcast.1.core_ref, bf16[16,48,512]{2,1,0:T(8,128)(2,1)S(1)} %all-to-all-done.both_ref, bf16[256,1024]{1,0:T(8,128)(2,1)S(1)} %copy-done.2, bf16[256,1024]{1,0:T(8,128)(2,1)S(1)} %collective-permute-done.2.after_ref, ...), custom_call_target="tpu_custom_call" | custom-call | flops 402653184 | bytes 4456452 | tf_op jit(solution)/shard_map/pallas_call | solution.py:32
  73.4 0.7 copy-done.5
  74.1 0.0 all-gather.8.cloned.1.call-update
  74.1 1.9 %collective-permute-start.5 = (f32[4,96,256]{2,1,0:T(8,128)}, f32[4,96,256]{2,1,0:T(8,128)S(1)}, u32[]{:S(2)}, u32[]{:S(2)}) collective-permute-start(f32[4,96,256]{2,1,0:T(8,128)} %copy-done.5), channel_id=1, source_target_pairs={{0,64},{64,0},{1,65},{65,1},{2,66},{66,2},{3,67},{67,3},{4,68},{68... | collective-permute-start | bytes 1179656 | tf_op jit(solution)/shard_map/ppermute | solution.py:139
  76.1 0.0 copy-done.9
  76.1 1.9 %collective-permute-done.5 = f32[4,96,256]{2,1,0:T(8,128)S(1)} collective-permute-done((f32[4,96,256]{2,1,0:T(8,128)}, f32[4,96,256]{2,1,0:T(8,128)S(1)}, u32[]{:S(2)}, u32[]{:S(2)}) %collective-permute-start.5) | collective-permute-done | bytes 393248 | tf_op jit(solution)/shard_map/ppermute | solution.py:139
  78.0 0.1 add_convert_fusion
  78.1 1.2 broadcast_in_dim.22
  79.3 4.8 %all-to-all-start.1 = ((bf16[4,6,96,256]{3,2,1,0:T(8,128)(2,1)}), bf16[4,6,96,256]{3,2,1,0:T(8,128)(2,1)S(1)}, u32[]{:S(2)}, u32[]{:S(2)}) async-start(bf16[4,6,96,256]{3,2,1,0:T(8,128)(2,1)} %broadcast_in_dim.22), calls=%async_computation.1 | async-start | bytes 2359296 | tf_op jit(solution)/shard_map/all_to_all | solution.py:22
  84.0 14.7 %all-to-all-done.1 = bf16[4,6,96,256]{3,2,1,0:T(8,128)(2,1)S(1)} async-done(((bf16[4,6,96,256]{3,2,1,0:T(8,128)(2,1)}), bf16[4,6,96,256]{3,2,1,0:T(8,128)(2,1)S(1)}, u32[]{:S(2)}, u32[]{:S(2)}) %all-to-all-start.1) | async-done | bytes 1179680 | tf_op jit(solution)/shard_map/all_to_all | solution.py:22
  98.7 0.1 convert_reduce_fusion
  98.9 0.2 fusion.11
  99.1 2.5 %all-gather.1.pregrad_ref = bf16[8,192,256]{2,1,0:T(8,128)(2,1)S(1)} all-gather(bf16[8,96,256]{2,1,0:T(8,128)(2,1)S(1)} %pad_maximum_fusion), channel_id=3, replica_groups=mesh['y'=4,'c'=2,'x'=4,'za'=4,'zb'=4] {'c'}, dimensions={1}, use_global_device_ids=true | all-gather | bytes 1179648 | tf_op jit(solution)/shard_map/all_gather | solution.py:146
  101.6 1.6 %shard_map.78 = bf16[16,24,512]{2,1,0:T(8,128)(2,1)} custom-call(s32[1]{0:T(128)} %bitcast.x_ref, bf16[8,192,256]{2,1,0:T(8,128)(2,1)S(1)} %all-gather.1.pregrad_ref, bf16[4,1024,256]{2,1,0:T(8,128)(2,1)S(1)} %bitcast.43), custom_call_target="tpu_custom_call" | custom-call | flops 402653184 | bytes 3276804 | tf_op jit(solution)/shard_map/pallas_call | solution.py:32
  103.3 11.4 %all-to-all-start.2 = ((bf16[16,24,512]{2,1,0:T(8,128)(2,1)}), bf16[16,24,512]{2,1,0:T(8,128)(2,1)S(1)}, u32[]{:S(2)}, u32[]{:S(2)}) async-start(bf16[16,24,512]{2,1,0:T(8,128)(2,1)} %shard_map.78), calls=%async_computation.2 | async-start | bytes 786432 | tf_op jit(solution)/shard_map/all_to_all | solution.py:22
  114.7 1.9 %collective-permute-start.8 = (bf16[192,256]{1,0:T(8,128)(2,1)S(1)}, bf16[192,256]{1,0:T(8,128)(2,1)S(1)}, u32[]{:S(2)}, u32[]{:S(2)}) collective-permute-start(bf16[192,256]{1,0:T(8,128)(2,1)S(1)} %get-tuple-element.36), channel_id=1, source_target_pairs={{0,16},{16,32},{32,48},{48,0},{1,17},{17,33},{33,49},{49,1},{2,18}... | collective-permute-start | bytes 294920 | tf_op jit(solution)/shard_map/ppermute | solution.py:159
  116.7 5.7 %collective-permute-start.7 = (bf16[192,256]{1,0:T(8,128)(2,1)S(1)}, bf16[192,256]{1,0:T(8,128)(2,1)S(1)}, u32[]{:S(2)}, u32[]{:S(2)}) collective-permute-start(bf16[192,256]{1,0:T(8,128)(2,1)S(1)} %get-tuple-element.37), channel_id=1, source_target_pairs={{0,32},{16,48},{32,0},{48,16},{1,33},{17,49},{33,1},{49,17},{2,34}... | collective-permute-start | bytes 294920 | tf_op jit(solution)/shard_map/ppermute | solution.py:159
  122.3 1.9 %collective-permute-start.6 = (bf16[192,256]{1,0:T(8,128)(2,1)S(1)}, bf16[192,256]{1,0:T(8,128)(2,1)S(1)}, u32[]{:S(2)}, u32[]{:S(2)}) collective-permute-start(bf16[192,256]{1,0:T(8,128)(2,1)S(1)} %get-tuple-element.38), channel_id=1, source_target_pairs={{0,48},{16,0},{32,16},{48,32},{1,49},{17,1},{33,17},{49,33},{2,50}... | collective-permute-start | bytes 294920 | tf_op jit(solution)/shard_map/ppermute | solution.py:159
  124.3 0.0 slice-start
  124.3 0.0 collective-permute-done.8
  124.4 0.7 collective-permute-done.7
  125.1 3.8 %collective-permute-done.6 = bf16[192,256]{1,0:T(8,128)(2,1)S(1)} collective-permute-done((bf16[192,256]{1,0:T(8,128)(2,1)S(1)}, bf16[192,256]{1,0:T(8,128)(2,1)S(1)}, u32[]{:S(2)}, u32[]{:S(2)}) %collective-permute-start.6) | collective-permute-done | bytes 98336 | tf_op jit(solution)/shard_map/ppermute | solution.py:159
  128.8 0.1 pad_maximum_fusion.1
  128.9 0.1 pad_maximum_fusion.2
  129.0 0.0 all-gather.8.cloned.1.call-done
  129.1 3.1 %fusion.3 = f32[256,1024]{1,0:T(8,128)} fusion(bf16[4,192,256]{2,1,0:T(8,128)(2,1)S(1)} %slice-done, bf16[4,2,192,1024]{3,2,1,0:T(8,128)(2,1)} %bitcast.48), kind=kOutput, calls=%fused_computation.6 | convolution fusion | flops 402653184 | bytes 3014656 | tf_op jit(solution)/shard_map/xtf,xtd->fd/dot_general | solution.py:163
  132.2 1.6 %fusion.2 = f32[1024,256]{1,0:T(8,128)} fusion(bf16[4,192,256]{2,1,0:T(8,128)(2,1)S(1)} %pad_maximum_fusion.2, bf16[4,2,192,1024]{3,2,1,0:T(8,128)(2,1)S(1)} %bitcast.49), kind=kOutput, calls=%fused_computation.5 | convolution fusion | flops 402653184 | bytes 3014656 | tf_op jit(solution)/shard_map/xtd,xtf->df/dot_general | solution.py:164
  133.8 5.2 %all-to-all-done.2.part_ref = bf16[16,24,512]{2,1,0:T(8,128)(2,1)S(1)} async-done(((bf16[16,24,512]{2,1,0:T(8,128)(2,1)}), bf16[16,24,512]{2,1,0:T(8,128)(2,1)S(1)}, u32[]{:S(2)}, u32[]{:S(2)}) %all-to-all-start.2) | async-done | bytes 393248 | tf_op jit(solution)/shard_map/all_to_all | solution.py:22
  139.0 0.7 shard_map.79
  (27 shorter events, 0.3 us)
Async XLA Ops:
  7.2 18.5 %copy-start.2 = (bf16[256,1024]{1,0:T(8,128)(2,1)S(1)}, bf16[256,1024]{1,0:T(8,128)(2,1)}, u32[]{:S(2)}) copy-start(bf16[256,1024]{1,0:T(8,128)(2,1)} %own_ref.1) | copy-start | bytes 1572868
  7.2 76.8 %all-gather.6.cloned.1.call-start = ((), (), s32[]{:S(2)}) async-start(), calls=%async_computation.3 | async-start | bytes 2621440 | tf_op jit(solution)/shard_map/all_gather | solution.py:128
  7.9 0.8 copy-start.3
  8.7 0.8 copy-start.4
  9.4 51.1 %copy-start.8 = (bf16[96,256]{1,0:T(8,128)(2,1)S(1)}, bf16[96,256]{1,0:T(8,128)(2,1)}, u32[]{:S(2)}) copy-start(bf16[96,256]{1,0:T(8,128)(2,1)} %param.7) | copy-start | bytes 147460
  10.4 60.0 %all-to-all-start = ((bf16[16,48,512]{2,1,0:T(8,128)(2,1)}), bf16[16,48,512]{2,1,0:T(8,128)(2,1)S(1)}, u32[]{:S(2)}, u32[]{:S(2)}) async-start(bf16[16,48,512]{2,1,0:T(8,128)(2,1)} %shard_map.76), calls=%async_computation | async-start | bytes 1572864 | tf_op jit(solution)/shard_map/all_to_all | solution.py:22
  25.6 103.5 %all-gather.8.cloned.1.call-start = ((), (), s32[]{:S(2)}) async-start(), calls=%async_computation.4 | async-start | bytes 3932160 | tf_op jit(solution)/shard_map/all_gather | solution.py:162
  25.6 24.4 %collective-permute-start.1 = (bf16[256,1024]{1,0:T(8,128)(2,1)S(1)}, bf16[256,1024]{1,0:T(8,128)(2,1)S(1)}, u32[]{:S(2)}, u32[]{:S(2)}) collective-permute-start(bf16[256,1024]{1,0:T(8,128)(2,1)S(1)} %copy-done.2), channel_id=1, source_target_pairs={{0,16},{16,32},{32,48},{48,0},{1,17},{17,33},{33,49},{49,1},{2,18}... | collective-permute-start | bytes 1572872 | tf_op jit(solution)/shard_map/ppermute | solution.py:104
  29.0 26.1 %collective-permute-start.2 = (bf16[256,1024]{1,0:T(8,128)(2,1)S(1)}, bf16[256,1024]{1,0:T(8,128)(2,1)S(1)}, u32[]{:S(2)}, u32[]{:S(2)}) collective-permute-start(bf16[256,1024]{1,0:T(8,128)(2,1)S(1)} %copy-done.2), channel_id=1, source_target_pairs={{0,48},{16,0},{32,16},{48,32},{1,49},{17,1},{33,17},{49,33},{2,50}... | collective-permute-start | bytes 1572872 | tf_op jit(solution)/shard_map/ppermute | solution.py:104
  50.0 20.4 %collective-permute-start.3 = (bf16[128,1024]{1,0:T(8,128)(2,1)S(1)}, bf16[128,1024]{1,0:T(8,128)(2,1)S(1)}, u32[]{:S(2)}, u32[]{:S(2)}) collective-permute-start(bf16[128,1024]{1,0:T(8,128)(2,1)S(1)} %slice.70), channel_id=1, source_target_pairs={{0,16},{16,32},{32,48},{48,0},{1,17},{17,33},{33,49},{49,1},{2,18}... | collective-permute-start | bytes 786440 | tf_op jit(solution)/shard_map/ppermute | solution.py:109
  55.2 15.2 %collective-permute-start.4 = (bf16[128,1024]{1,0:T(8,128)(2,1)S(1)}, bf16[128,1024]{1,0:T(8,128)(2,1)S(1)}, u32[]{:S(2)}, u32[]{:S(2)}) collective-permute-start(bf16[128,1024]{1,0:T(8,128)(2,1)S(1)} %slice.71), channel_id=1, source_target_pairs={{0,48},{16,0},{32,16},{48,32},{1,49},{17,1},{33,17},{49,33},{2,50}... | collective-permute-start | bytes 786440 | tf_op jit(solution)/shard_map/ppermute | solution.py:109
  60.6 9.8 %collective-permute-start = (bf16[96,256]{1,0:T(8,128)(2,1)S(1)}, bf16[96,256]{1,0:T(8,128)(2,1)S(1)}, u32[]{:S(2)}, u32[]{:S(2)}) collective-permute-start(bf16[96,256]{1,0:T(8,128)(2,1)S(1)} %copy-done.8), channel_id=1, source_target_pairs={{0,0},{16,128},{32,256},{48,384},{128,400},{144,16},{160,144},{176... | collective-permute-start | bytes 147464 | tf_op jit(solution)/shard_map/ppermute | solution.py:124
  70.4 0.6 copy-start.6
  71.0 5.1 %copy-start.9 = (bf16[96,256]{1,0:T(8,128)(2,1)S(1)}, bf16[96,256]{1,0:T(8,128)(2,1)}, u32[]{:S(2)}) copy-start(bf16[96,256]{1,0:T(8,128)(2,1)} %param.7) | copy-start | bytes 147460
  73.4 0.7 copy-start.5
  74.1 3.9 %copy-start.7 = (bf16[96,256]{1,0:T(8,128)(2,1)S(1)}, bf16[96,256]{1,0:T(8,128)(2,1)}, u32[]{:S(2)}) copy-start(bf16[96,256]{1,0:T(8,128)(2,1)} %copy-done.6) | copy-start | bytes 147460
  74.1 3.8 %collective-permute-start.5 = (f32[4,96,256]{2,1,0:T(8,128)}, f32[4,96,256]{2,1,0:T(8,128)S(1)}, u32[]{:S(2)}, u32[]{:S(2)}) collective-permute-start(f32[4,96,256]{2,1,0:T(8,128)} %copy-done.5), channel_id=1, source_target_pairs={{0,64},{64,0},{1,65},{65,1},{2,66},{66,2},{3,67},{67,3},{4,68},{68... | collective-permute-start | bytes 1179656 | tf_op jit(solution)/shard_map/ppermute | solution.py:139
  79.3 19.5 %all-to-all-start.1 = ((bf16[4,6,96,256]{3,2,1,0:T(8,128)(2,1)}), bf16[4,6,96,256]{3,2,1,0:T(8,128)(2,1)S(1)}, u32[]{:S(2)}, u32[]{:S(2)}) async-start(bf16[4,6,96,256]{3,2,1,0:T(8,128)(2,1)} %broadcast_in_dim.22), calls=%async_computation.1 | async-start | bytes 2359296 | tf_op jit(solution)/shard_map/all_to_all | solution.py:22
  98.8 2.8 %copy-start.1 = (bf16[4096,256]{1,0:T(8,128)(2,1)S(1)}, bf16[4096,256]{1,0:T(8,128)(2,1)}, u32[]{:S(2)}) copy-start(bf16[4096,256]{1,0:T(8,128)(2,1)} %all-gather.6.cloned.1.call-done) | copy-start | bytes 6291460
  101.6 22.7 %copy-start = (bf16[8,192,256]{2,1,0:T(8,128)(2,1)}, bf16[8,192,256]{2,1,0:T(8,128)(2,1)S(1)}, u32[]{:S(2)}) copy-start(bf16[8,192,256]{2,1,0:T(8,128)(2,1)S(1)} %all-gather.1.pregrad_ref) | copy-start | bytes 2359300
  103.3 35.8 %all-to-all-start.2 = ((bf16[16,24,512]{2,1,0:T(8,128)(2,1)}), bf16[16,24,512]{2,1,0:T(8,128)(2,1)S(1)}, u32[]{:S(2)}, u32[]{:S(2)}) async-start(bf16[16,24,512]{2,1,0:T(8,128)(2,1)} %shard_map.78), calls=%async_computation.2 | async-start | bytes 786432 | tf_op jit(solution)/shard_map/all_to_all | solution.py:22
  114.7 9.6 %collective-permute-start.8 = (bf16[192,256]{1,0:T(8,128)(2,1)S(1)}, bf16[192,256]{1,0:T(8,128)(2,1)S(1)}, u32[]{:S(2)}, u32[]{:S(2)}) collective-permute-start(bf16[192,256]{1,0:T(8,128)(2,1)S(1)} %get-tuple-element.36), channel_id=1, source_target_pairs={{0,16},{16,32},{32,48},{48,0},{1,17},{17,33},{33,49},{49,1},{2,18}... | collective-permute-start | bytes 294920 | tf_op jit(solution)/shard_map/ppermute | solution.py:159
  116.7 8.4 %collective-permute-start.7 = (bf16[192,256]{1,0:T(8,128)(2,1)S(1)}, bf16[192,256]{1,0:T(8,128)(2,1)S(1)}, u32[]{:S(2)}, u32[]{:S(2)}) collective-permute-start(bf16[192,256]{1,0:T(8,128)(2,1)S(1)} %get-tuple-element.37), channel_id=1, source_target_pairs={{0,32},{16,48},{32,0},{48,16},{1,33},{17,49},{33,1},{49,17},{2,34}... | collective-permute-start | bytes 294920 | tf_op jit(solution)/shard_map/ppermute | solution.py:159
  122.3 6.5 %collective-permute-start.6 = (bf16[192,256]{1,0:T(8,128)(2,1)S(1)}, bf16[192,256]{1,0:T(8,128)(2,1)S(1)}, u32[]{:S(2)}, u32[]{:S(2)}) collective-permute-start(bf16[192,256]{1,0:T(8,128)(2,1)S(1)} %get-tuple-element.38), channel_id=1, source_target_pairs={{0,48},{16,0},{32,16},{48,32},{1,49},{17,1},{33,17},{49,33},{2,50}... | collective-permute-start | bytes 294920 | tf_op jit(solution)/shard_map/ppermute | solution.py:159
  124.3 4.7 %slice-start = ((bf16[8,192,256]{2,1,0:T(8,128)(2,1)}), bf16[4,192,256]{2,1,0:T(8,128)(2,1)S(1)}, s32[]{:S(2)}) async-start(bf16[8,192,256]{2,1,0:T(8,128)(2,1)} %copy-done), calls=%async_computation.5 | async-start | bytes 786432 | tf_op jit(solution)/shard_map/slice | solution.py:147
  129.1 3.2 %copy-start.10 = (bf16[8,192,1024]{2,1,0:T(8,128)(2,1)S(1)}, bf16[8,192,1024]{2,1,0:T(8,128)(2,1)}, u32[]{:S(2)}) copy-start(bf16[8,192,1024]{2,1,0:T(8,128)(2,1)} %all-gather.8.cloned.1.call-done) | copy-start | bytes 9437188
Sparse Core Ops, SparseCore 0:
  10.1 54.0 all-gather.5
  74.3 46.1 all-gather.7

commit v10 on v9

--- a/solution.py
+++ b/solution.py
@@ -76,10 +76,12 @@
         out_ref[3] = times_transposed(half, before_ref[...])
 
 
-def part_kernel(x_ref, pregrad_ref, up_ref, out_ref, total, rows):
-    for d in range(4):
-        product = times_transposed(pregrad_ref[d], up_ref[lax.rem(x_ref[0] + d, 4)])
-        total[...] = product if d == 0 else total[...] + product
+def part_kernel(pregrad_ref, own_ref, after_ref, far0_ref, far1_ref, before_ref, out_ref, total, rows):
+    total[...] = times_transposed(pregrad_ref[0], own_ref[...])
+    total[...] += times_transposed(pregrad_ref[1], after_ref[...])
+    total[:, :512] += times_transposed(pregrad_ref[2], far0_ref[...])
+    total[:, 512:] += times_transposed(pregrad_ref[2], far1_ref[...])
+    total[...] += times_transposed(pregrad_ref[3], before_ref[...])
     for z in range(16):
         here = slice(12 * z, 12 * z + 12)
         rows[z, 0:12] = total[here, :512]
@@ -124,8 +126,10 @@
     turned = lax.ppermute(preact, ("y", "x"), swap)
     before, after = near_x(down_weight)
     far = far_x(before, after)
-    both, turned, before, after, far = lax.optimization_barrier((both, turned, before, after, far))
-    wide_up = lax.all_gather(up_weight, "x", axis=0, tiled=False)
+    up_before, up_after = near_x(up_weight)
+    both, turned, before, after, far, up_before, up_after = lax.optimization_barrier(
+        (both, turned, before, after, far, up_before, up_after)
+    )
 
     half = jax.ShapeDtypeStruct((4, 96, 256), F32)
     mine, theirs, tokens = call(
@@ -139,7 +143,9 @@
     pair = (mine + lax.ppermute(theirs, "c", [(0, 1), (1, 0)])).astype(BF)
     activ, _ = gelu_parts(preact)
     own = spread(jnp.concatenate([pair, activ.astype(BF)[None], turned[None]]), "y")
-    own, wide_up = lax.optimization_barrier((own, wide_up))
+    up_far = far_x(up_before, up_after)
+    tok_before, tok_after = near_x(tokens)
+    own, up_far = lax.optimization_barrier((own, up_far))
     hidden_grad = own[:, :4].astype(F32).sum(0)
     _, slope = gelu_parts(own[:, 5])
     own = jnp.concatenate([(hidden_grad * slope).astype(BF), own[:, 4]])
@@ -151,17 +157,18 @@
         [jax.ShapeDtypeStruct((16, 24, 512), BF)],
         [(192, 1024), (16, 24, 512)],
         2 * 192 * 1024 * 1024,
-        (at_x[None], own, wide_up),
-        smem=1,
+        (own, up_weight, up_after, *up_far, up_before),
     )
     part = exchange(part, ("za", "zb"))
 
-    sent = [pregrad[0]] + [lax.ppermute(pregrad[k], "x", shift(k)) for k in (3, 2, 1)]
-    all_pregrad = turn_by(jnp.stack(sent), 4 - at_x)
+    all_pregrad = jnp.stack([pregrad[0]] + [lax.ppermute(pregrad[k], "x", shift(k)) for k in (3, 2, 1)])
+    all_pregrad, tok_before, tok_after = lax.optimization_barrier((all_pregrad, tok_before, tok_after))
+    tok_far = jnp.concatenate(far_x(tok_before.reshape(384, 1024), tok_after.reshape(384, 1024)))
+    all_tokens = jnp.stack([tokens, tok_after, tok_far.reshape(2, 192, 1024), tok_before])
+    all_activ = turn_by(all_activ, at_x)
     all_pregrad, all_activ = lax.optimization_barrier((all_pregrad, all_activ))
-    all_both = lax.all_gather(tokens, "x", axis=0, tiled=False)
-    down_grad = jnp.einsum("xtf,xtd->fd", all_activ, all_both[:, 0], preferred_element_type=F32)
-    up_grad = jnp.einsum("xtd,xtf->df", all_both[:, 1], all_pregrad, preferred_element_type=F32)
+    down_grad = jnp.einsum("xtf,xtd->fd", all_activ, all_tokens[:, 0], preferred_element_type=F32)
+    up_grad = jnp.einsum("xtd,xtf->df", all_tokens[:, 1], all_pregrad, preferred_element_type=F32)
     part, up_grad, down_grad = lax.optimization_barrier((part, up_grad, down_grad))
     (input_grad,) = call(sum_kernel, [jax.ShapeDtypeStruct((12, 1024), BF)], [(24, 512)], 0, (part,))
     return (input_grad, up_grad, down_grad)

time: 148 us -> 143 us (0.966)
  waiting for transfers between devices: 53.7 us -> 25.5 us
  starting transfers between devices: 60.8 us -> 87.1 us
  between operations: 14.4 us -> 1.08 us
  other arithmetic: 0.56 us -> 6.32 us
  local copies, waits for them, and re-layouts: 4.17 us -> 9.65 us
  matrix products: 4.72 us -> 3.17 us
    all_to_all x3, waiting for transfers between devices: 20 us -> 2.45 us  [exchange(): lax.all_to_all(blocks, axis, split_axis=0, concat_axis=0, tiled=False)]
    ppermute x1 -> x3, waiting for transfers between devices: 17.3 us -> 4.02 us  [near_x(): lax.ppermute(block, 'x', shift(1))]
    ppermute x1 -> x3, starting transfers between devices: 3.65 us -> 13.7 us  [near_x(): lax.ppermute(block, 'x', shift(-1))]
    ppermute x1 -> x3, waiting for transfers between devices: 0.01 us -> 7.89 us  [far_x(): lax.ppermute(before[:half], 'x', shift(1))]
    ppermute x1 -> x3, starting transfers between devices: 5.36 us -> 12.7 us  [far_x(): lax.ppermute(after[half:], 'x', shift(-1))]
    ppermute x1 -> x3, starting transfers between devices: 3.14 us -> 8.02 us  [far_x(): lax.ppermute(before[:half], 'x', shift(1))]
    ppermute x3, waiting for transfers between devices: 4.5 us -> 0.01 us  [local(): lax.ppermute(pregrad[k], 'x', shift(k))]
    ppermute x1 -> x3, starting transfers between devices: 3.4 us -> 7.51 us  [near_x(): lax.ppermute(block, 'x', shift(1))]
  transfers between devices with their start and end apart: 14 -> 20, of which waited for: 8 -> 7; matrix products, arithmetic and copies ran while one was open for 4% -> 10% of each run, Pallas kernels for 3% -> 1%
where the time goes in v10:
time: 143 us; the launch traced here: 141 us
  starting transfers between devices  87.1 us (61%)
  waiting for transfers between devices  25.5 us (18%)
  local copies, waits for them, and re-layouts  9.65 us (7%)
  other arithmetic  6.32 us (4%)
  Pallas kernels  6.09 us (4%)
  matrix products  3.17 us (2%)
  blocking collectives  2.37 us (2%)
    all_to_all x3, starting transfers between devices, exchange(): lax.all_to_all(blocks, axis, split_axis=0, concat_axis=0, tiled=False)  30.4 us
    ppermute x3, starting transfers between devices, near_x(): lax.ppermute(block, 'x', shift(-1))  13.7 us
    ppermute x3, starting transfers between devices, far_x(): lax.ppermute(after[half:], 'x', shift(-1))  12.7 us
    ppermute x3, starting transfers between devices, local(): lax.ppermute(pregrad[k], 'x', shift(k))  10.1 us
    ppermute x3, starting transfers between devices, far_x(): lax.ppermute(before[:half], 'x', shift(1))  8.02 us
    ppermute x3, waiting for transfers between devices, far_x(): lax.ppermute(before[:half], 'x', shift(1))  7.89 us
    ppermute x3, starting transfers between devices, near_x(): lax.ppermute(block, 'x', shift(1))  7.51 us
    ppermute x1, waiting for transfers between devices, local(): turned = lax.ppermute(preact, ('y', 'x'), swap)  7.22 us
  transfers between devices with their start and end apart: 20, of which 7 were waited for; matrix products, arithmetic and copies ran while one was open for 10% of the time, Pallas kernels for 1%

profile of v10, /device:TPU:24, one launch (start us, length us, event | category | flops | bytes accessed | tf_op | source)
XLA Modules:
  0.0 141.3 jit_solution(17964749217179620019)
XLA Ops:
  0.7 0.8 copy-done.5
  1.5 0.8 copy-done.6
  2.2 0.9 shard_map.76
  3.2 15.2 %all-to-all-start = ((bf16[16,48,512]{2,1,0:T(8,128)(2,1)}), bf16[16,48,512]{2,1,0:T(8,128)(2,1)S(1)}, u32[]{:S(2)}, u32[]{:S(2)}) async-start(bf16[16,48,512]{2,1,0:T(8,128)(2,1)} %shard_map.76), calls=%async_computation | async-start | bytes 1572864 | tf_op jit(solution)/shard_map/all_to_all | solution.py:22
  18.4 3.4 %collective-permute-start.1 = (bf16[256,1024]{1,0:T(8,128)(2,1)}, bf16[256,1024]{1,0:T(8,128)(2,1)S(1)}, u32[]{:S(2)}, u32[]{:S(2)}) collective-permute-start(bf16[256,1024]{1,0:T(8,128)(2,1)} %own_ref.2), channel_id=1, source_target_pairs={{0,16},{16,32},{32,48},{48,0},{1,17},{17,33},{33,49},{49,1},{2,18}... | collective-permute-start | bytes 1572872 | tf_op jit(solution)/shard_map/ppermute | solution.py:106
  21.8 3.7 %collective-permute-start.2 = (bf16[256,1024]{1,0:T(8,128)(2,1)}, bf16[256,1024]{1,0:T(8,128)(2,1)S(1)}, u32[]{:S(2)}, u32[]{:S(2)}) collective-permute-start(bf16[256,1024]{1,0:T(8,128)(2,1)} %own_ref.2), channel_id=1, source_target_pairs={{0,48},{16,0},{32,16},{48,32},{1,49},{17,1},{33,17},{49,33},{2,50}... | collective-permute-start | bytes 1572872 | tf_op jit(solution)/shard_map/ppermute | solution.py:106
  25.4 2.2 %collective-permute-start.5 = (bf16[1024,256]{1,0:T(8,128)(2,1)S(1)}, bf16[1024,256]{1,0:T(8,128)(2,1)S(1)}, u32[]{:S(2)}, u32[]{:S(2)}) collective-permute-start(bf16[1024,256]{1,0:T(8,128)(2,1)S(1)} %copy-done.2), channel_id=1, source_target_pairs={{0,16},{16,32},{32,48},{48,0},{1,17},{17,33},{33,49},{49,1},{2,18}... | collective-permute-start | bytes 1572872 | tf_op jit(solution)/shard_map/ppermute | solution.py:106
  27.6 4.9 %collective-permute-start.6 = (bf16[1024,256]{1,0:T(8,128)(2,1)S(1)}, bf16[1024,256]{1,0:T(8,128)(2,1)S(1)}, u32[]{:S(2)}, u32[]{:S(2)}) collective-permute-start(bf16[1024,256]{1,0:T(8,128)(2,1)S(1)} %copy-done.2), channel_id=1, source_target_pairs={{0,48},{16,0},{32,16},{48,32},{1,49},{17,1},{33,17},{49,33},{2,50}... | collective-permute-start | bytes 1572872 | tf_op jit(solution)/shard_map/ppermute | solution.py:106
  32.5 4.0 %collective-permute-done.1.before_ref = bf16[256,1024]{1,0:T(8,128)(2,1)S(1)} collective-permute-done((bf16[256,1024]{1,0:T(8,128)(2,1)}, bf16[256,1024]{1,0:T(8,128)(2,1)S(1)}, u32[]{:S(2)}, u32[]{:S(2)}) %collective-permute-start.1) | collective-permute-done | bytes 524320 | tf_op jit(solution)/shard_map/ppermute | solution.py:106
  36.5 0.7 slice.94
  37.3 2.2 %collective-permute-start.3 = (bf16[128,1024]{1,0:T(8,128)(2,1)}, bf16[128,1024]{1,0:T(8,128)(2,1)}, u32[]{:S(2)}, u32[]{:S(2)}) collective-permute-start(bf16[128,1024]{1,0:T(8,128)(2,1)} %slice.94), channel_id=1, source_target_pairs={{0,16},{16,32},{32,48},{48,0},{1,17},{17,33},{33,49},{49,1},{2,18}... | collective-permute-start | bytes 786440 | tf_op jit(solution)/shard_map/ppermute | solution.py:111
  39.5 0.7 slice.95
  40.2 4.9 %collective-permute-start.4 = (bf16[128,1024]{1,0:T(8,128)(2,1)}, bf16[128,1024]{1,0:T(8,128)(2,1)}, u32[]{:S(2)}, u32[]{:S(2)}) collective-permute-start(bf16[128,1024]{1,0:T(8,128)(2,1)} %slice.95), channel_id=1, source_target_pairs={{0,48},{16,0},{32,16},{48,32},{1,49},{17,1},{33,17},{49,33},{2,50}... | collective-permute-start | bytes 786440 | tf_op jit(solution)/shard_map/ppermute | solution.py:111
  45.1 2.9 %collective-permute-start = (bf16[96,256]{1,0:T(8,128)(2,1)S(1)}, bf16[96,256]{1,0:T(8,128)(2,1)S(1)}, u32[]{:S(2)}, u32[]{:S(2)}) collective-permute-start(bf16[96,256]{1,0:T(8,128)(2,1)S(1)} %copy-done.7), channel_id=1, source_target_pairs={{0,0},{16,128},{32,256},{48,384},{128,400},{144,16},{160,144},{176... | collective-permute-start | bytes 147464 | tf_op jit(solution)/shard_map/ppermute | solution.py:126
  48.0 7.2 %collective-permute-done = bf16[96,256]{1,0:T(8,128)(2,1)S(1)} collective-permute-done((bf16[96,256]{1,0:T(8,128)(2,1)S(1)}, bf16[96,256]{1,0:T(8,128)(2,1)S(1)}, u32[]{:S(2)}, u32[]{:S(2)}) %collective-permute-start) | collective-permute-done | bytes 49184 | tf_op jit(solution)/shard_map/ppermute | solution.py:126
  55.2 2.4 %all-to-all-done.both_ref = bf16[16,48,512]{2,1,0:T(8,128)(2,1)S(1)} async-done(((bf16[16,48,512]{2,1,0:T(8,128)(2,1)}), bf16[16,48,512]{2,1,0:T(8,128)(2,1)S(1)}, u32[]{:S(2)}, u32[]{:S(2)}) %all-to-all-start) | async-done | bytes 786464 | tf_op jit(solution)/shard_map/all_to_all | solution.py:22
  57.7 2.8 %shard_map.77 = (f32[4,96,256]{2,1,0:T(8,128)S(1)}, f32[4,96,256]{2,1,0:T(8,128)S(1)}, bf16[2,192,1024]{2,1,0:T(8,128)(2,1)S(1)}) custom-call(s32[1]{0:T(128)} %bitcast.core_ref, bf16[16,48,512]{2,1,0:T(8,128)(2,1)S(1)} %all-to-all-done.both_ref, bf16[256,1024]{1,0:T(8,128)(2,1)} %own_ref.2, bf16[256,1024]{1,0:T(8,128)(2,1)S(1)} %collective-permute-done.2.after_ref, ...), custom_call_target="tpu_custom_call" | custom-call | flops 402653184 | bytes 4456452 | tf_op jit(solution)/shard_map/pallas_call | solution.py:32
  60.5 0.9 copy-done
  61.4 1.9 %collective-permute-start.7 = (f32[4,96,256]{2,1,0:T(8,128)S(1)}, f32[4,96,256]{2,1,0:T(8,128)S(1)}, u32[]{:S(2)}, u32[]{:S(2)}) collective-permute-start(f32[4,96,256]{2,1,0:T(8,128)S(1)} %get-tuple-element.31), channel_id=1, source_target_pairs={{0,64},{64,0},{1,65},{65,1},{2,66},{66,2},{3,67},{67,3},{4,68},{68... | collective-permute-start | bytes 1179656 | tf_op jit(solution)/shard_map/ppermute | solution.py:143
  63.4 1.7 %collective-permute-done.7 = f32[4,96,256]{2,1,0:T(8,128)S(1)} collective-permute-done((f32[4,96,256]{2,1,0:T(8,128)S(1)}, f32[4,96,256]{2,1,0:T(8,128)S(1)}, u32[]{:S(2)}, u32[]{:S(2)}) %collective-permute-start.7) | collective-permute-done | bytes 393248 | tf_op jit(solution)/shard_map/ppermute | solution.py:143
  65.1 1.2 broadcast_in_dim.18
  66.3 4.8 %all-to-all-start.1 = ((bf16[4,6,96,256]{3,2,1,0:T(8,128)(2,1)}), bf16[4,6,96,256]{3,2,1,0:T(8,128)(2,1)}, u32[]{:S(2)}, u32[]{:S(2)}) async-start(bf16[4,6,96,256]{3,2,1,0:T(8,128)(2,1)} %broadcast_in_dim.18), calls=%async_computation.1 | async-start | bytes 2359296 | tf_op jit(solution)/shard_map/all_to_all | solution.py:22
  71.1 4.7 %collective-permute-start.9 = (bf16[512,256]{1,0:T(8,128)(2,1)S(1)}, bf16[512,256]{1,0:T(8,128)(2,1)S(1)}, u32[]{:S(2)}, u32[]{:S(2)}) collective-permute-start(bf16[512,256]{1,0:T(8,128)(2,1)S(1)} %slice.72), channel_id=1, source_target_pairs={{0,48},{16,0},{32,16},{48,32},{1,49},{17,1},{33,17},{49,33},{2,50}... | collective-permute-start | bytes 786440 | tf_op jit(solution)/shard_map/ppermute | solution.py:111
  75.8 1.9 %collective-permute-start.8 = (bf16[512,256]{1,0:T(8,128)(2,1)S(1)}, bf16[512,256]{1,0:T(8,128)(2,1)S(1)}, u32[]{:S(2)}, u32[]{:S(2)}) collective-permute-start(bf16[512,256]{1,0:T(8,128)(2,1)S(1)} %slice.71), channel_id=1, source_target_pairs={{0,16},{16,32},{32,48},{48,0},{1,17},{17,33},{33,49},{49,1},{2,18}... | collective-permute-start | bytes 786440 | tf_op jit(solution)/shard_map/ppermute | solution.py:111
  77.8 5.1 %collective-permute-start.14 = (bf16[2,192,1024]{2,1,0:T(8,128)(2,1)S(1)}, bf16[2,192,1024]{2,1,0:T(8,128)(2,1)}, u32[]{:S(2)}, u32[]{:S(2)}) collective-permute-start(bf16[2,192,1024]{2,1,0:T(8,128)(2,1)S(1)} %copy-done.1), channel_id=1, source_target_pairs={{0,48},{16,0},{32,16},{48,32},{1,49},{17,1},{33,17},{49,33},{2,50}... | collective-permute-start | bytes 2359304 | tf_op jit(solution)/shard_map/ppermute | solution.py:106
  82.9 1.9 %collective-permute-start.13 = (bf16[2,192,1024]{2,1,0:T(8,128)(2,1)S(1)}, bf16[2,192,1024]{2,1,0:T(8,128)(2,1)}, u32[]{:S(2)}, u32[]{:S(2)}) collective-permute-start(bf16[2,192,1024]{2,1,0:T(8,128)(2,1)S(1)} %copy-done.1), channel_id=1, source_target_pairs={{0,16},{16,32},{32,48},{48,0},{1,17},{17,33},{33,49},{49,1},{2,18}... | collective-permute-start | bytes 2359304 | tf_op jit(solution)/shard_map/ppermute | solution.py:106
  84.8 1.7 %collective-permute-done.8.far0_ref = bf16[512,256]{1,0:T(8,128)(2,1)S(1)} collective-permute-done((bf16[512,256]{1,0:T(8,128)(2,1)S(1)}, bf16[512,256]{1,0:T(8,128)(2,1)S(1)}, u32[]{:S(2)}, u32[]{:S(2)}) %collective-permute-start.8) | collective-permute-done | bytes 262176 | tf_op jit(solution)/shard_map/ppermute | solution.py:111
  87.3 1.3 convert_reduce_fusion
  88.6 1.1 fusion.11
  89.7 1.0 slice_bitcast_fusion.10
  90.7 2.4 %all-gather.pregrad_ref = bf16[8,192,256]{2,1,0:T(8,128)(2,1)S(1)} all-gather(bf16[8,96,256]{2,1,0:T(8,128)(2,1)S(1)} %pad_maximum_fusion.2), channel_id=2, replica_groups=mesh['y'=4,'c'=2,'x'=4,'za'=4,'zb'=4] {'c'}, dimensions={1}, use_global_device_ids=true | all-gather | bytes 1179648 | tf_op jit(solution)/shard_map/all_gather | solution.py:152
  93.1 0.7 fusion.17
  93.8 2.1 %collective-permute-start.12 = (bf16[192,256]{1,0:T(8,128)(2,1)}, bf16[192,256]{1,0:T(8,128)(2,1)}, u32[]{:S(2)}, u32[]{:S(2)}) collective-permute-start(bf16[192,256]{1,0:T(8,128)(2,1)} %get-tuple-element.48), channel_id=1, source_target_pairs={{0,16},{16,32},{32,48},{48,0},{1,17},{17,33},{33,49},{49,1},{2,18}... | collective-permute-start | bytes 294920 | tf_op jit(solution)/shard_map/ppermute | solution.py:164
  95.9 4.7 %collective-permute-start.11 = (bf16[192,256]{1,0:T(8,128)(2,1)}, bf16[192,256]{1,0:T(8,128)(2,1)}, u32[]{:S(2)}, u32[]{:S(2)}) collective-permute-start(bf16[192,256]{1,0:T(8,128)(2,1)} %get-tuple-element.49), channel_id=1, source_target_pairs={{0,32},{16,48},{32,0},{48,16},{1,33},{17,49},{33,1},{49,17},{2,34}... | collective-permute-start | bytes 294920 | tf_op jit(solution)/shard_map/ppermute | solution.py:164
  100.6 3.3 %collective-permute-start.10 = (bf16[192,256]{1,0:T(8,128)(2,1)}, bf16[192,256]{1,0:T(8,128)(2,1)}, u32[]{:S(2)}, u32[]{:S(2)}) collective-permute-start(bf16[192,256]{1,0:T(8,128)(2,1)} %get-tuple-element.50), channel_id=1, source_target_pairs={{0,48},{16,0},{32,16},{48,32},{1,49},{17,1},{33,17},{49,33},{2,50}... | collective-permute-start | bytes 294920 | tf_op jit(solution)/shard_map/ppermute | solution.py:164
  103.9 1.6 %shard_map.78 = bf16[16,24,512]{2,1,0:T(8,128)(2,1)} custom-call(bf16[8,192,256]{2,1,0:T(8,128)(2,1)S(1)} %all-gather.pregrad_ref, bf16[1024,256]{1,0:T(8,128)(2,1)S(1)} %copy-done.2, bf16[1024,256]{1,0:T(8,128)(2,1)S(1)} %collective-permute-done.6.after_ref, bf16[512,256]{1,0:T(8,128)(2,1)S(1)} %copy-done.4, ...), custom_call_target="tpu_custom_call" | custom-call | flops 402653184 | bytes 3276800 | tf_op jit(solution)/shard_map/pallas_call | solution.py:32
  105.6 10.4 %all-to-all-start.2 = ((bf16[16,24,512]{2,1,0:T(8,128)(2,1)}), bf16[16,24,512]{2,1,0:T(8,128)(2,1)S(1)}, u32[]{:S(2)}, u32[]{:S(2)}) async-start(bf16[16,24,512]{2,1,0:T(8,128)(2,1)} %shard_map.78), calls=%async_computation.2 | async-start | bytes 786432 | tf_op jit(solution)/shard_map/all_to_all | solution.py:22
  116.0 1.1 pad_maximum_fusion.3
  117.1 1.0 slice_bitcast_fusion.8
  118.1 1.0 slice_bitcast_fusion.9
  119.2 3.9 %collective-permute-start.15 = (bf16[192,1024]{1,0:T(8,128)(2,1)S(1)}, bf16[192,1024]{1,0:T(8,128)(2,1)S(1)}, u32[]{:S(2)}, u32[]{:S(2)}) collective-permute-start(bf16[192,1024]{1,0:T(8,128)(2,1)S(1)} %slice_bitcast_fusion.9), channel_id=1, source_target_pairs={{0,16},{16,32},{32,48},{48,0},{1,17},{17,33},{33,49},{49,1},{2,18}... | collective-permute-start | bytes 1179656 | tf_op jit(solution)/shard_map/ppermute | solution.py:111
  123.1 3.1 %collective-permute-start.16 = (bf16[192,1024]{1,0:T(8,128)(2,1)S(1)}, bf16[192,1024]{1,0:T(8,128)(2,1)}, u32[]{:S(2)}, u32[]{:S(2)}) collective-permute-start(bf16[192,1024]{1,0:T(8,128)(2,1)S(1)} %slice_bitcast_fusion.8), channel_id=1, source_target_pairs={{0,48},{16,0},{32,16},{48,32},{1,49},{17,1},{33,17},{49,33},{2,50}... | collective-permute-start | bytes 1179656 | tf_op jit(solution)/shard_map/ppermute | solution.py:111
  126.4 6.2 %collective-permute-done.15 = bf16[192,1024]{1,0:T(8,128)(2,1)S(1)} collective-permute-done((bf16[192,1024]{1,0:T(8,128)(2,1)S(1)}, bf16[192,1024]{1,0:T(8,128)(2,1)S(1)}, u32[]{:S(2)}, u32[]{:S(2)}) %collective-permute-start.15) | collective-permute-done | bytes 393248 | tf_op jit(solution)/shard_map/ppermute | solution.py:111
  132.6 2.3 %collective-permute-done.16 = bf16[192,1024]{1,0:T(8,128)(2,1)} collective-permute-done((bf16[192,1024]{1,0:T(8,128)(2,1)S(1)}, bf16[192,1024]{1,0:T(8,128)(2,1)}, u32[]{:S(2)}, u32[]{:S(2)}) %collective-permute-start.16) | collective-permute-done | bytes 393248 | tf_op jit(solution)/shard_map/ppermute | solution.py:111
  134.8 1.0 pad_maximum_fusion.1
  135.9 1.6 %pad_maximum_fusion = bf16[4,2,192,1024]{3,2,1,0:T(8,128)(2,1)S(1)} fusion(bf16[1,2,192,1024]{3,2,1,0:T(8,128)(2,1)} %bitcast.17, bf16[1,2,192,1024]{3,2,1,0:T(8,128)(2,1)S(1)} %bitcast.45, bf16[1,2,192,1024]{3,2,1,0:T(8,128)(2,1)} %bitcast.13, bf16[1,2,192,1024]{3,2,1,0:T(8,128)(2,1)S(1)} %bitcast.44), kind=kLoop, calls=%fused_computation | loop fusion | flops 4718592 | bytes 6291456 | tf_op jit(solution)/shard_map/stack | solution.py:167
  137.5 1.6 %fusion.3 = f32[256,1024]{1,0:T(8,128)} fusion(bf16[4,192,256]{2,1,0:T(8,128)(2,1)S(1)} %pad_maximum_fusion.4, bf16[4,2,192,1024]{3,2,1,0:T(8,128)(2,1)S(1)} %pad_maximum_fusion), kind=kOutput, calls=%fused_computation.7 | convolution fusion | flops 402653184 | bytes 3014656 | tf_op jit(solution)/shard_map/xtf,xtd->fd/dot_general | solution.py:170
  139.1 1.6 %fusion.2 = f32[1024,256]{1,0:T(8,128)} fusion(bf16[4,192,256]{2,1,0:T(8,128)(2,1)S(1)} %pad_maximum_fusion.3, bf16[4,2,192,1024]{3,2,1,0:T(8,128)(2,1)S(1)} %pad_maximum_fusion), kind=kOutput, calls=%fused_computation.6 | convolution fusion | flops 402653184 | bytes 3014656 | tf_op jit(solution)/shard_map/xtd,xtf->df/dot_general | solution.py:171
  (36 shorter events, 1.8 us)
Async XLA Ops:
  0.6 24.8 %copy-start.2 = (bf16[1024,256]{1,0:T(8,128)(2,1)S(1)}, bf16[1024,256]{1,0:T(8,128)(2,1)}, u32[]{:S(2)}) copy-start(bf16[1024,256]{1,0:T(8,128)(2,1)} %own_ref.3) | copy-start | bytes 1572868
  0.6 0.8 copy-start.5
  1.5 0.8 copy-start.6
  2.2 42.8 %copy-start.7 = (bf16[96,256]{1,0:T(8,128)(2,1)S(1)}, bf16[96,256]{1,0:T(8,128)(2,1)}, u32[]{:S(2)}) copy-start(bf16[96,256]{1,0:T(8,128)(2,1)} %param.7) | copy-start | bytes 147460
  3.2 54.5 %all-to-all-start = ((bf16[16,48,512]{2,1,0:T(8,128)(2,1)}), bf16[16,48,512]{2,1,0:T(8,128)(2,1)S(1)}, u32[]{:S(2)}, u32[]{:S(2)}) async-start(bf16[16,48,512]{2,1,0:T(8,128)(2,1)} %shard_map.76), calls=%async_computation | async-start | bytes 1572864 | tf_op jit(solution)/shard_map/all_to_all | solution.py:22
  18.4 18.2 %collective-permute-start.1 = (bf16[256,1024]{1,0:T(8,128)(2,1)}, bf16[256,1024]{1,0:T(8,128)(2,1)S(1)}, u32[]{:S(2)}, u32[]{:S(2)}) collective-permute-start(bf16[256,1024]{1,0:T(8,128)(2,1)} %own_ref.2), channel_id=1, source_target_pairs={{0,16},{16,32},{32,48},{48,0},{1,17},{17,33},{33,49},{49,1},{2,18}... | collective-permute-start | bytes 1572872 | tf_op jit(solution)/shard_map/ppermute | solution.py:106
  21.8 17.7 %collective-permute-start.2 = (bf16[256,1024]{1,0:T(8,128)(2,1)}, bf16[256,1024]{1,0:T(8,128)(2,1)S(1)}, u32[]{:S(2)}, u32[]{:S(2)}) collective-permute-start(bf16[256,1024]{1,0:T(8,128)(2,1)} %own_ref.2), channel_id=1, source_target_pairs={{0,48},{16,0},{32,16},{48,32},{1,49},{17,1},{33,17},{49,33},{2,50}... | collective-permute-start | bytes 1572872 | tf_op jit(solution)/shard_map/ppermute | solution.py:106
  25.4 29.8 %collective-permute-start.5 = (bf16[1024,256]{1,0:T(8,128)(2,1)S(1)}, bf16[1024,256]{1,0:T(8,128)(2,1)S(1)}, u32[]{:S(2)}, u32[]{:S(2)}) collective-permute-start(bf16[1024,256]{1,0:T(8,128)(2,1)S(1)} %copy-done.2), channel_id=1, source_target_pairs={{0,16},{16,32},{32,48},{48,0},{1,17},{17,33},{33,49},{49,1},{2,18}... | collective-permute-start | bytes 1572872 | tf_op jit(solution)/shard_map/ppermute | solution.py:106
  27.6 27.6 %collective-permute-start.6 = (bf16[1024,256]{1,0:T(8,128)(2,1)S(1)}, bf16[1024,256]{1,0:T(8,128)(2,1)S(1)}, u32[]{:S(2)}, u32[]{:S(2)}) collective-permute-start(bf16[1024,256]{1,0:T(8,128)(2,1)S(1)} %copy-done.2), channel_id=1, source_target_pairs={{0,48},{16,0},{32,16},{48,32},{1,49},{17,1},{33,17},{49,33},{2,50}... | collective-permute-start | bytes 1572872 | tf_op jit(solution)/shard_map/ppermute | solution.py:106
  37.3 18.0 %collective-permute-start.3 = (bf16[128,1024]{1,0:T(8,128)(2,1)}, bf16[128,1024]{1,0:T(8,128)(2,1)}, u32[]{:S(2)}, u32[]{:S(2)}) collective-permute-start(bf16[128,1024]{1,0:T(8,128)(2,1)} %slice.94), channel_id=1, source_target_pairs={{0,16},{16,32},{32,48},{48,0},{1,17},{17,33},{33,49},{49,1},{2,18}... | collective-permute-start | bytes 786440 | tf_op jit(solution)/shard_map/ppermute | solution.py:111
  40.2 15.0 %collective-permute-start.4 = (bf16[128,1024]{1,0:T(8,128)(2,1)}, bf16[128,1024]{1,0:T(8,128)(2,1)}, u32[]{:S(2)}, u32[]{:S(2)}) collective-permute-start(bf16[128,1024]{1,0:T(8,128)(2,1)} %slice.95), channel_id=1, source_target_pairs={{0,48},{16,0},{32,16},{48,32},{1,49},{17,1},{33,17},{49,33},{2,50}... | collective-permute-start | bytes 786440 | tf_op jit(solution)/shard_map/ppermute | solution.py:111
  45.1 10.2 %collective-permute-start = (bf16[96,256]{1,0:T(8,128)(2,1)S(1)}, bf16[96,256]{1,0:T(8,128)(2,1)S(1)}, u32[]{:S(2)}, u32[]{:S(2)}) collective-permute-start(bf16[96,256]{1,0:T(8,128)(2,1)S(1)} %copy-done.7), channel_id=1, source_target_pairs={{0,0},{16,128},{32,256},{48,384},{128,400},{144,16},{160,144},{176... | collective-permute-start | bytes 147464 | tf_op jit(solution)/shard_map/ppermute | solution.py:126
  60.5 0.9 copy-start
  61.4 3.6 %collective-permute-start.7 = (f32[4,96,256]{2,1,0:T(8,128)S(1)}, f32[4,96,256]{2,1,0:T(8,128)S(1)}, u32[]{:S(2)}, u32[]{:S(2)}) collective-permute-start(f32[4,96,256]{2,1,0:T(8,128)S(1)} %get-tuple-element.31), channel_id=1, source_target_pairs={{0,64},{64,0},{1,65},{65,1},{2,66},{66,2},{3,67},{67,3},{4,68},{68... | collective-permute-start | bytes 1179656 | tf_op jit(solution)/shard_map/ppermute | solution.py:143
  66.3 11.5 %copy-start.1 = (bf16[2,192,1024]{2,1,0:T(8,128)(2,1)S(1)}, bf16[2,192,1024]{2,1,0:T(8,128)(2,1)}, u32[]{:S(2)}) copy-start(bf16[2,192,1024]{2,1,0:T(8,128)(2,1)} %copy-done) | copy-start | bytes 2359300
  66.3 21.0 %all-to-all-start.1 = ((bf16[4,6,96,256]{3,2,1,0:T(8,128)(2,1)}), bf16[4,6,96,256]{3,2,1,0:T(8,128)(2,1)}, u32[]{:S(2)}, u32[]{:S(2)}) async-start(bf16[4,6,96,256]{3,2,1,0:T(8,128)(2,1)} %broadcast_in_dim.18), calls=%async_computation.1 | async-start | bytes 2359296 | tf_op jit(solution)/shard_map/all_to_all | solution.py:22
  71.1 13.7 %collective-permute-start.9 = (bf16[512,256]{1,0:T(8,128)(2,1)S(1)}, bf16[512,256]{1,0:T(8,128)(2,1)S(1)}, u32[]{:S(2)}, u32[]{:S(2)}) collective-permute-start(bf16[512,256]{1,0:T(8,128)(2,1)S(1)} %slice.72), channel_id=1, source_target_pairs={{0,48},{16,0},{32,16},{48,32},{1,49},{17,1},{33,17},{49,33},{2,50}... | collective-permute-start | bytes 786440 | tf_op jit(solution)/shard_map/ppermute | solution.py:111
  75.8 10.8 %collective-permute-start.8 = (bf16[512,256]{1,0:T(8,128)(2,1)S(1)}, bf16[512,256]{1,0:T(8,128)(2,1)S(1)}, u32[]{:S(2)}, u32[]{:S(2)}) collective-permute-start(bf16[512,256]{1,0:T(8,128)(2,1)S(1)} %slice.71), channel_id=1, source_target_pairs={{0,16},{16,32},{32,48},{48,0},{1,17},{17,33},{33,49},{49,1},{2,18}... | collective-permute-start | bytes 786440 | tf_op jit(solution)/shard_map/ppermute | solution.py:111
  77.8 39.3 %collective-permute-start.14 = (bf16[2,192,1024]{2,1,0:T(8,128)(2,1)S(1)}, bf16[2,192,1024]{2,1,0:T(8,128)(2,1)}, u32[]{:S(2)}, u32[]{:S(2)}) collective-permute-start(bf16[2,192,1024]{2,1,0:T(8,128)(2,1)S(1)} %copy-done.1), channel_id=1, source_target_pairs={{0,48},{16,0},{32,16},{48,32},{1,49},{17,1},{33,17},{49,33},{2,50}... | collective-permute-start | bytes 2359304 | tf_op jit(solution)/shard_map/ppermute | solution.py:106
  82.9 34.2 %collective-permute-start.13 = (bf16[2,192,1024]{2,1,0:T(8,128)(2,1)S(1)}, bf16[2,192,1024]{2,1,0:T(8,128)(2,1)}, u32[]{:S(2)}, u32[]{:S(2)}) collective-permute-start(bf16[2,192,1024]{2,1,0:T(8,128)(2,1)S(1)} %copy-done.1), channel_id=1, source_target_pairs={{0,16},{16,32},{32,48},{48,0},{1,17},{17,33},{33,49},{49,1},{2,18}... | collective-permute-start | bytes 2359304 | tf_op jit(solution)/shard_map/ppermute | solution.py:106
  86.6 0.7 copy-start.3
  89.7 14.2 %copy-start.4 = (bf16[512,256]{1,0:T(8,128)(2,1)S(1)}, bf16[512,256]{1,0:T(8,128)(2,1)}, u32[]{:S(2)}) copy-start(bf16[512,256]{1,0:T(8,128)(2,1)} %copy-done.3) | copy-start | bytes 786436
  93.8 22.1 %collective-permute-start.12 = (bf16[192,256]{1,0:T(8,128)(2,1)}, bf16[192,256]{1,0:T(8,128)(2,1)}, u32[]{:S(2)}, u32[]{:S(2)}) collective-permute-start(bf16[192,256]{1,0:T(8,128)(2,1)} %get-tuple-element.48), channel_id=1, source_target_pairs={{0,16},{16,32},{32,48},{48,0},{1,17},{17,33},{33,49},{49,1},{2,18}... | collective-permute-start | bytes 294920 | tf_op jit(solution)/shard_map/ppermute | solution.py:164
  95.9 20.1 %collective-permute-start.11 = (bf16[192,256]{1,0:T(8,128)(2,1)}, bf16[192,256]{1,0:T(8,128)(2,1)}, u32[]{:S(2)}, u32[]{:S(2)}) collective-permute-start(bf16[192,256]{1,0:T(8,128)(2,1)} %get-tuple-element.49), channel_id=1, source_target_pairs={{0,32},{16,48},{32,0},{48,16},{1,33},{17,49},{33,1},{49,17},{2,34}... | collective-permute-start | bytes 294920 | tf_op jit(solution)/shard_map/ppermute | solution.py:164
  100.6 15.3 %collective-permute-start.10 = (bf16[192,256]{1,0:T(8,128)(2,1)}, bf16[192,256]{1,0:T(8,128)(2,1)}, u32[]{:S(2)}, u32[]{:S(2)}) collective-permute-start(bf16[192,256]{1,0:T(8,128)(2,1)} %get-tuple-element.50), channel_id=1, source_target_pairs={{0,48},{16,0},{32,16},{48,32},{1,49},{17,1},{33,17},{49,33},{2,50}... | collective-permute-start | bytes 294920 | tf_op jit(solution)/shard_map/ppermute | solution.py:164
  105.6 35.1 %all-to-all-start.2 = ((bf16[16,24,512]{2,1,0:T(8,128)(2,1)}), bf16[16,24,512]{2,1,0:T(8,128)(2,1)S(1)}, u32[]{:S(2)}, u32[]{:S(2)}) async-start(bf16[16,24,512]{2,1,0:T(8,128)(2,1)} %shard_map.78), calls=%async_computation.2 | async-start | bytes 786432 | tf_op jit(solution)/shard_map/all_to_all | solution.py:22
  119.2 13.4 %collective-permute-start.15 = (bf16[192,1024]{1,0:T(8,128)(2,1)S(1)}, bf16[192,1024]{1,0:T(8,128)(2,1)S(1)}, u32[]{:S(2)}, u32[]{:S(2)}) collective-permute-start(bf16[192,1024]{1,0:T(8,128)(2,1)S(1)} %slice_bitcast_fusion.9), channel_id=1, source_target_pairs={{0,16},{16,32},{32,48},{48,0},{1,17},{17,33},{33,49},{49,1},{2,18}... | collective-permute-start | bytes 1179656 | tf_op jit(solution)/shard_map/ppermute | solution.py:111
  123.1 11.8 %collective-permute-start.16 = (bf16[192,1024]{1,0:T(8,128)(2,1)S(1)}, bf16[192,1024]{1,0:T(8,128)(2,1)}, u32[]{:S(2)}, u32[]{:S(2)}) collective-permute-start(bf16[192,1024]{1,0:T(8,128)(2,1)S(1)} %slice_bitcast_fusion.8), channel_id=1, source_target_pairs={{0,48},{16,0},{32,16},{48,32},{1,49},{17,1},{33,17},{49,33},{2,50}... | collective-permute-start | bytes 1179656 | tf_op jit(solution)/shard_map/ppermute | solution.py:111

commit v11 on v10

--- a/solution.py
+++ b/solution.py
@@ -89,6 +89,33 @@
         out_ref[z] = rows[z].astype(BF)
 
 
+def pack_kernel(before_ref, after_ref, own_ref, plus_ref, minus_ref):
+    plus_ref[:, :1024] = before_ref[0]
+    plus_ref[:, 1024:] = own_ref[1]
+    minus_ref[:, :1024] = after_ref[1]
+    minus_ref[:, 1024:] = own_ref[3]
+
+
+def times_tokens(a, b):
+    return lax.dot_general(a, b, (((0,), (0,)), ((), ())), preferred_element_type=F32)
+
+
+def weights_kernel(x_ref, tokens_ref, after_ref, plus_ref, minus_ref, before_ref, own_ref, two_ref, *outs):
+    up_ref, down_ref = outs
+    up_ref[...] = times_tokens(tokens_ref[1], own_ref[0])
+    up_ref[...] += times_tokens(after_ref[1], minus_ref[:, 1024:])
+    up_ref[...] += times_tokens(minus_ref[:, :1024], two_ref[...])
+    up_ref[...] += times_tokens(before_ref[1], plus_ref[:, 1024:])
+
+    def activ(d):
+        return own_ref[4 + lax.rem(x_ref[0] + d, 4)]
+
+    down_ref[...] = times_tokens(activ(0), tokens_ref[0])
+    down_ref[...] += times_tokens(activ(1), after_ref[0])
+    down_ref[...] += times_tokens(activ(2), plus_ref[:, :1024])
+    down_ref[...] += times_tokens(activ(3), before_ref[0])
+
+
 def sum_kernel(part_ref, out_ref, rows):
     total = part_ref[0].astype(F32)
     for z in range(1, 16):
@@ -109,11 +136,6 @@
 def far_x(before, after):
     half = before.shape[0] // 2
     return lax.ppermute(before[:half], "x", shift(1)), lax.ppermute(after[half:], "x", shift(-1))
-
-
-def turn_by(blocks, start):
-    turned = [lax.dynamic_index_in_dim(blocks, (start + i) % 4, keepdims=True) for i in range(4)]
-    return jnp.concatenate(turned)
 
 
 def local(inputs, out_grad, preact, up_weight, down_weight):
@@ -146,11 +168,10 @@
     up_far = far_x(up_before, up_after)
     tok_before, tok_after = near_x(tokens)
     own, up_far = lax.optimization_barrier((own, up_far))
-    hidden_grad = own[:, :4].astype(F32).sum(0)
+    hidden_grad = sum((own[k, :4].astype(F32) for k in range(1, 4)), own[0, :4].astype(F32))
     _, slope = gelu_parts(own[:, 5])
     own = jnp.concatenate([(hidden_grad * slope).astype(BF), own[:, 4]])
     own = lax.all_gather(own, "c", axis=1, tiled=False).reshape(8, 192, 256)
-    pregrad, all_activ = own[:4], own[4:]
 
     (part,) = call(
         part_kernel,
@@ -159,16 +180,21 @@
         2 * 192 * 1024 * 1024,
         (own, up_weight, up_after, *up_far, up_before),
     )
+    part, tok_before, tok_after = lax.optimization_barrier((part, tok_before, tok_after))
     part = exchange(part, ("za", "zb"))
 
-    all_pregrad = jnp.stack([pregrad[0]] + [lax.ppermute(pregrad[k], "x", shift(k)) for k in (3, 2, 1)])
-    all_pregrad, tok_before, tok_after = lax.optimization_barrier((all_pregrad, tok_before, tok_after))
-    tok_far = jnp.concatenate(far_x(tok_before.reshape(384, 1024), tok_after.reshape(384, 1024)))
-    all_tokens = jnp.stack([tokens, tok_after, tok_far.reshape(2, 192, 1024), tok_before])
-    all_activ = turn_by(all_activ, at_x)
-    all_pregrad, all_activ = lax.optimization_barrier((all_pregrad, all_activ))
-    down_grad = jnp.einsum("xtf,xtd->fd", all_activ, all_tokens[:, 0], preferred_element_type=F32)
-    up_grad = jnp.einsum("xtd,xtf->df", all_tokens[:, 1], all_pregrad, preferred_element_type=F32)
+    packed = jax.ShapeDtypeStruct((192, 1280), BF)
+    plus, minus = call(pack_kernel, [packed, packed], [], 0, (tok_before, tok_after, own))
+    plus, minus = lax.ppermute(plus, "x", shift(1)), lax.ppermute(minus, "x", shift(-1))
+    two = lax.ppermute(own[2], "x", shift(2))
+    up_grad, down_grad = call(
+        weights_kernel,
+        [jax.ShapeDtypeStruct((1024, 256), F32), jax.ShapeDtypeStruct((256, 1024), F32)],
+        [],
+        4 * 768 * 1024 * 256,
+        (at_x[None], tokens, tok_after, plus, minus, tok_before, own, two),
+        smem=1,
+    )
     part, up_grad, down_grad = lax.optimization_barrier((part, up_grad, down_grad))
     (input_grad,) = call(sum_kernel, [jax.ShapeDtypeStruct((12, 1024), BF)], [(24, 512)], 0, (part,))
     return (input_grad, up_grad, down_grad)

time: 143 us -> 142 us (level)
  the two profiles are of different devices: /device:TPU:24 before, /device:TPU:14 now
where the time goes in v11:
time: 142 us; the launch traced here: 141 us
  starting transfers between devices  80.4 us (57%)
  waiting for transfers between devices  37 us (26%)
  Pallas kernels  11.7 us (8%)
  local copies, waits for them, and re-layouts  6.6 us (5%)
  blocking collectives  2.5 us (2%)
  other arithmetic  1.7 us (1%)
    all_to_all x3, starting transfers between devices, exchange(): lax.all_to_all(blocks, axis, split_axis=0, concat_axis=0, tiled=False)  31.7 us
    pallas_call x6, Pallas kernels, call(): pl.pallas_call(body, out_shape=outs, in_specs=[pl.BlockSpec(memory_space=...  11.7 us
    ppermute x3, starting transfers between devices, near_x(): lax.ppermute(block, 'x', shift(1))  11.1 us
    ppermute x1, waiting for transfers between devices, local(): turned = lax.ppermute(preact, ('y', 'x'), swap)  10.9 us
    ppermute x1, waiting for transfers between devices, local(): two = lax.ppermute(own[2], 'x', shift(2))  9.65 us
    ppermute x2, starting transfers between devices, far_x(): lax.ppermute(before[:half], 'x', shift(1))  7.9 us
    ppermute x3, starting transfers between devices, near_x(): lax.ppermute(block, 'x', shift(-1))  7.62 us
    ppermute x3, waiting for transfers between devices, near_x(): lax.ppermute(block, 'x', shift(-1))  6.73 us
  transfers between devices with their start and end apart: 18, of which 7 were waited for; matrix products, arithmetic and copies ran while one was open for 3% of the time, Pallas kernels for 5%

profile of v11, /device:TPU:14, one launch (start us, length us, event | category | flops | bytes accessed | tf_op | source)
XLA Modules:
  0.0 140.8 jit_solution(13818743273971044929)
XLA Ops:
  0.6 0.0 copy-start
  0.7 0.8 copy-done.6
  1.5 0.8 copy-done.7
  2.2 0.9 shard_map.76
  3.2 15.3 %all-to-all-start = ((bf16[16,48,512]{2,1,0:T(8,128)(2,1)}), bf16[16,48,512]{2,1,0:T(8,128)(2,1)S(1)}, u32[]{:S(2)}, u32[]{:S(2)}) async-start(bf16[16,48,512]{2,1,0:T(8,128)(2,1)} %shard_map.76), calls=%async_computation | async-start | bytes 1572864 | tf_op jit(solution)/shard_map/all_to_all | solution.py:22
  18.5 2.4 %collective-permute-start.1 = (bf16[256,1024]{1,0:T(8,128)(2,1)}, bf16[256,1024]{1,0:T(8,128)(2,1)S(1)}, u32[]{:S(2)}, u32[]{:S(2)}) collective-permute-start(bf16[256,1024]{1,0:T(8,128)(2,1)} %own_ref.2), channel_id=1, source_target_pairs={{0,16},{16,32},{32,48},{48,0},{1,17},{17,33},{33,49},{49,1},{2,18}... | collective-permute-start | bytes 1572872 | tf_op jit(solution)/shard_map/ppermute | solution.py:133
  20.9 3.5 %collective-permute-start.2 = (bf16[256,1024]{1,0:T(8,128)(2,1)}, bf16[256,1024]{1,0:T(8,128)(2,1)S(1)}, u32[]{:S(2)}, u32[]{:S(2)}) collective-permute-start(bf16[256,1024]{1,0:T(8,128)(2,1)} %own_ref.2), channel_id=1, source_target_pairs={{0,48},{16,0},{32,16},{48,32},{1,49},{17,1},{33,17},{49,33},{2,50}... | collective-permute-start | bytes 1572872 | tf_op jit(solution)/shard_map/ppermute | solution.py:133
  24.4 3.6 %collective-permute-start.5 = (bf16[1024,256]{1,0:T(8,128)(2,1)S(1)}, bf16[1024,256]{1,0:T(8,128)(2,1)S(1)}, u32[]{:S(2)}, u32[]{:S(2)}) collective-permute-start(bf16[1024,256]{1,0:T(8,128)(2,1)S(1)} %copy-done), channel_id=1, source_target_pairs={{0,16},{16,32},{32,48},{48,0},{1,17},{17,33},{33,49},{49,1},{2,18}... | collective-permute-start | bytes 1572872 | tf_op jit(solution)/shard_map/ppermute | solution.py:133
  28.0 2.2 %collective-permute-start.6 = (bf16[1024,256]{1,0:T(8,128)(2,1)S(1)}, bf16[1024,256]{1,0:T(8,128)(2,1)S(1)}, u32[]{:S(2)}, u32[]{:S(2)}) collective-permute-start(bf16[1024,256]{1,0:T(8,128)(2,1)S(1)} %copy-done), channel_id=1, source_target_pairs={{0,48},{16,0},{32,16},{48,32},{1,49},{17,1},{33,17},{49,33},{2,50}... | collective-permute-start | bytes 1572872 | tf_op jit(solution)/shard_map/ppermute | solution.py:133
  30.2 5.2 %collective-permute-done.1.before_ref = bf16[256,1024]{1,0:T(8,128)(2,1)S(1)} collective-permute-done((bf16[256,1024]{1,0:T(8,128)(2,1)}, bf16[256,1024]{1,0:T(8,128)(2,1)S(1)}, u32[]{:S(2)}, u32[]{:S(2)}) %collective-permute-start.1) | collective-permute-done | bytes 524320 | tf_op jit(solution)/shard_map/ppermute | solution.py:133
  35.5 0.7 slice.46
  36.2 3.6 %collective-permute-start.3 = (bf16[128,1024]{1,0:T(8,128)(2,1)}, bf16[128,1024]{1,0:T(8,128)(2,1)}, u32[]{:S(2)}, u32[]{:S(2)}) collective-permute-start(bf16[128,1024]{1,0:T(8,128)(2,1)} %slice.46), channel_id=1, source_target_pairs={{0,16},{16,32},{32,48},{48,0},{1,17},{17,33},{33,49},{49,1},{2,18}... | collective-permute-start | bytes 786440 | tf_op jit(solution)/shard_map/ppermute | solution.py:138
  39.8 0.7 slice.47
  40.5 2.2 %collective-permute-start.4 = (bf16[128,1024]{1,0:T(8,128)(2,1)}, bf16[128,1024]{1,0:T(8,128)(2,1)}, u32[]{:S(2)}, u32[]{:S(2)}) collective-permute-start(bf16[128,1024]{1,0:T(8,128)(2,1)} %slice.47), channel_id=1, source_target_pairs={{0,48},{16,0},{32,16},{48,32},{1,49},{17,1},{33,17},{49,33},{2,50}... | collective-permute-start | bytes 786440 | tf_op jit(solution)/shard_map/ppermute | solution.py:138
  42.8 4.3 %collective-permute-start = (bf16[96,256]{1,0:T(8,128)(2,1)S(1)}, bf16[96,256]{1,0:T(8,128)(2,1)S(1)}, u32[]{:S(2)}, u32[]{:S(2)}) collective-permute-start(bf16[96,256]{1,0:T(8,128)(2,1)S(1)} %copy-done.8), channel_id=1, source_target_pairs={{0,0},{16,128},{32,256},{48,384},{128,400},{144,16},{160,144},{176... | collective-permute-start | bytes 147464 | tf_op jit(solution)/shard_map/ppermute | solution.py:148
  47.1 10.9 %collective-permute-done = bf16[96,256]{1,0:T(8,128)(2,1)S(1)} collective-permute-done((bf16[96,256]{1,0:T(8,128)(2,1)S(1)}, bf16[96,256]{1,0:T(8,128)(2,1)S(1)}, u32[]{:S(2)}, u32[]{:S(2)}) %collective-permute-start) | collective-permute-done | bytes 49184 | tf_op jit(solution)/shard_map/ppermute | solution.py:148
  58.0 0.0 collective-permute-done.3.far0_ref
  58.0 3.5 %shard_map.77 = (f32[4,96,256]{2,1,0:T(8,128)S(1)}, f32[4,96,256]{2,1,0:T(8,128)S(1)}, bf16[2,192,1024]{2,1,0:T(8,128)(2,1)}) custom-call(s32[1]{0:T(128)} %bitcast.core_ref, bf16[16,48,512]{2,1,0:T(8,128)(2,1)S(1)} %all-to-all-done.both_ref, bf16[256,1024]{1,0:T(8,128)(2,1)} %own_ref.2, bf16[256,1024]{1,0:T(8,128)(2,1)S(1)} %collective-permute-done.2.after_ref, ...), custom_call_target="tpu_custom_call" | custom-call | flops 402653184 | bytes 4456452 | tf_op jit(solution)/shard_map/pallas_call | solution.py:32
  61.6 1.9 %collective-permute-start.7 = (f32[4,96,256]{2,1,0:T(8,128)S(1)}, f32[4,96,256]{2,1,0:T(8,128)S(1)}, u32[]{:S(2)}, u32[]{:S(2)}) collective-permute-start(f32[4,96,256]{2,1,0:T(8,128)S(1)} %get-tuple-element.33), channel_id=1, source_target_pairs={{0,64},{64,0},{1,65},{65,1},{2,66},{66,2},{3,67},{67,3},{4,68},{68... | collective-permute-start | bytes 1179656 | tf_op jit(solution)/shard_map/ppermute | solution.py:165
  63.5 1.7 %collective-permute-done.7 = f32[4,96,256]{2,1,0:T(8,128)S(1)} collective-permute-done((f32[4,96,256]{2,1,0:T(8,128)S(1)}, f32[4,96,256]{2,1,0:T(8,128)S(1)}, u32[]{:S(2)}, u32[]{:S(2)}) %collective-permute-start.7) | collective-permute-done | bytes 393248 | tf_op jit(solution)/shard_map/ppermute | solution.py:165
  65.2 0.1 add_convert_fusion
  65.3 1.2 broadcast_in_dim.21
  66.5 4.7 %all-to-all-start.1 = ((bf16[4,6,96,256]{3,2,1,0:T(8,128)(2,1)}), bf16[4,6,96,256]{3,2,1,0:T(8,128)(2,1)}, u32[]{:S(2)}, u32[]{:S(2)}) async-start(bf16[4,6,96,256]{3,2,1,0:T(8,128)(2,1)} %broadcast_in_dim.21), calls=%async_computation.1 | async-start | bytes 2359296 | tf_op jit(solution)/shard_map/all_to_all | solution.py:22
  71.2 2.7 %collective-permute-start.9 = (bf16[512,256]{1,0:T(8,128)(2,1)S(1)}, bf16[512,256]{1,0:T(8,128)(2,1)S(1)}, u32[]{:S(2)}, u32[]{:S(2)}) collective-permute-start(bf16[512,256]{1,0:T(8,128)(2,1)S(1)} %slice.37), channel_id=1, source_target_pairs={{0,48},{16,0},{32,16},{48,32},{1,49},{17,1},{33,17},{49,33},{2,50}... | collective-permute-start | bytes 786440 | tf_op jit(solution)/shard_map/ppermute | solution.py:138
  73.9 4.3 %collective-permute-start.8 = (bf16[512,256]{1,0:T(8,128)(2,1)S(1)}, bf16[512,256]{1,0:T(8,128)(2,1)S(1)}, u32[]{:S(2)}, u32[]{:S(2)}) collective-permute-start(bf16[512,256]{1,0:T(8,128)(2,1)S(1)} %slice.36), channel_id=1, source_target_pairs={{0,16},{16,32},{32,48},{48,0},{1,17},{17,33},{33,49},{49,1},{2,18}... | collective-permute-start | bytes 786440 | tf_op jit(solution)/shard_map/ppermute | solution.py:138
  78.3 1.9 %collective-permute-start.11 = (bf16[2,192,1024]{2,1,0:T(8,128)(2,1)}, bf16[2,192,1024]{2,1,0:T(8,128)(2,1)S(1)}, u32[]{:S(2)}, u32[]{:S(2)}) collective-permute-start(bf16[2,192,1024]{2,1,0:T(8,128)(2,1)} %get-tuple-element.40.tokens_ref), channel_id=1, source_target_pairs={{0,48},{16,0},{32,16},{48,32},{1,49},{17,1},{33,17},{49,33},{2,50}... | collective-permute-start | bytes 2359304 | tf_op jit(solution)/shard_map/ppermute | solution.py:133
  80.2 5.1 %collective-permute-start.10 = (bf16[2,192,1024]{2,1,0:T(8,128)(2,1)}, bf16[2,192,1024]{2,1,0:T(8,128)(2,1)S(1)}, u32[]{:S(2)}, u32[]{:S(2)}) collective-permute-start(bf16[2,192,1024]{2,1,0:T(8,128)(2,1)} %get-tuple-element.40.tokens_ref), channel_id=1, source_target_pairs={{0,16},{16,32},{32,48},{48,0},{1,17},{17,33},{33,49},{49,1},{2,18}... | collective-permute-start | bytes 2359304 | tf_op jit(solution)/shard_map/ppermute | solution.py:133
  85.3 0.0 copy-start.2
  85.4 0.7 copy-done.2
  86.0 0.7 copy-done.4
  86.8 0.9 slice_bitcast_fusion
  87.7 1.5 %fusion.7 = bf16[4,96,256]{2,1,0:T(8,128)(2,1)S(1)} fusion(bf16[4,6,96,256]{3,2,1,0:T(8,128)(2,1)} %all-to-all-done.1), kind=kLoop, calls=%fused_computation.13 | loop fusion | flops 1769472 | bytes 1179648 | tf_op jit(solution)/shard_map/convert_element_type | solution.py:173
  89.2 0.0 copy-start.1
  89.3 0.0 copy-start.3
  89.3 0.0 copy-start.5
  89.3 2.5 %all-gather.pregrad_ref.own_ref = bf16[8,192,256]{2,1,0:T(8,128)(2,1)S(1)} all-gather(bf16[8,96,256]{2,1,0:T(8,128)(2,1)S(1)} %pad_maximum_fusion), channel_id=2, replica_groups=mesh['y'=4,'c'=2,'x'=4,'za'=4,'zb'=4] {'c'}, dimensions={1}, use_global_device_ids=true | all-gather | bytes 1179648 | tf_op jit(solution)/shard_map/all_gather | solution.py:174
  91.8 1.6 %shard_map.78 = bf16[16,24,512]{2,1,0:T(8,128)(2,1)} custom-call(bf16[8,192,256]{2,1,0:T(8,128)(2,1)S(1)} %all-gather.pregrad_ref.own_ref, bf16[1024,256]{1,0:T(8,128)(2,1)S(1)} %copy-done.1, bf16[1024,256]{1,0:T(8,128)(2,1)S(1)} %collective-permute-done.6.after_ref, bf16[512,256]{1,0:T(8,128)(2,1)S(1)} %copy-done.5, bf16[512,256]{1,0:T(8,128)(2,1)S(1)} %copy-done.3, ...), custom_call_target="tpu_custom_call" | custom-call | flops 402653184 | bytes 3276800 | tf_op jit(solution)/shard_map/pallas_call | solution.py:32
  93.5 6.7 %collective-permute-done.11.after_ref = bf16[2,192,1024]{2,1,0:T(8,128)(2,1)S(1)} collective-permute-done((bf16[2,192,1024]{2,1,0:T(8,128)(2,1)}, bf16[2,192,1024]{2,1,0:T(8,128)(2,1)S(1)}, u32[]{:S(2)}, u32[]{:S(2)}) %collective-permute-start.11) | collective-permute-done | bytes 786464 | tf_op jit(solution)/shard_map/ppermute | solution.py:133
  100.2 1.3 collective-permute-done.10.before_ref
  101.5 11.7 %all-to-all-start.2 = ((bf16[16,24,512]{2,1,0:T(8,128)(2,1)}), bf16[16,24,512]{2,1,0:T(8,128)(2,1)S(1)}, u32[]{:S(2)}, u32[]{:S(2)}) async-start(bf16[16,24,512]{2,1,0:T(8,128)(2,1)} %shard_map.78), calls=%async_computation.2 | async-start | bytes 786432 | tf_op jit(solution)/shard_map/all_to_all | solution.py:22
  113.2 1.0 shard_map.79
  114.2 5.5 %collective-permute-start.12 = (bf16[192,1280]{1,0:T(8,128)(2,1)}, bf16[192,1280]{1,0:T(8,128)(2,1)S(1)}, u32[]{:S(2)}, u32[]{:S(2)}) collective-permute-start(bf16[192,1280]{1,0:T(8,128)(2,1)} %get-tuple-element.44), channel_id=1, source_target_pairs={{0,16},{16,32},{32,48},{48,0},{1,17},{17,33},{33,49},{49,1},{2,18}... | collective-permute-start | bytes 1474568 | tf_op jit(solution)/shard_map/ppermute | solution.py:188
  119.7 1.9 %collective-permute-start.13 = (bf16[192,1280]{1,0:T(8,128)(2,1)}, bf16[192,1280]{1,0:T(8,128)(2,1)}, u32[]{:S(2)}, u32[]{:S(2)}) collective-permute-start(bf16[192,1280]{1,0:T(8,128)(2,1)} %get-tuple-element.45), channel_id=1, source_target_pairs={{0,48},{16,0},{32,16},{48,32},{1,49},{17,1},{33,17},{49,33},{2,50}... | collective-permute-start | bytes 1474568 | tf_op jit(solution)/shard_map/ppermute | solution.py:188
  121.7 3.4 %collective-permute-start.14 = (bf16[192,256]{1,0:T(8,128)(2,1)S(1)}, bf16[192,256]{1,0:T(8,128)(2,1)S(1)}, u32[]{:S(2)}, u32[]{:S(2)}) collective-permute-start(bf16[192,256]{1,0:T(8,128)(2,1)S(1)} %slice_bitcast_fusion.2), channel_id=1, source_target_pairs={{0,32},{16,48},{32,0},{48,16},{1,33},{17,49},{33,1},{49,17},{2,34}... | collective-permute-start | bytes 294920 | tf_op jit(solution)/shard_map/ppermute | solution.py:189
  125.0 9.7 %collective-permute-done.14.two_ref = bf16[192,256]{1,0:T(8,128)(2,1)S(1)} collective-permute-done((bf16[192,256]{1,0:T(8,128)(2,1)S(1)}, bf16[192,256]{1,0:T(8,128)(2,1)S(1)}, u32[]{:S(2)}, u32[]{:S(2)}) %collective-permute-start.14) | collective-permute-done | bytes 98336 | tf_op jit(solution)/shard_map/ppermute | solution.py:189
  134.7 1.5 %collective-permute-done.13.minus_ref = bf16[192,1280]{1,0:T(8,128)(2,1)} collective-permute-done((bf16[192,1280]{1,0:T(8,128)(2,1)}, bf16[192,1280]{1,0:T(8,128)(2,1)}, u32[]{:S(2)}, u32[]{:S(2)}) %collective-permute-start.13) | collective-permute-done | bytes 491552 | tf_op jit(solution)/shard_map/ppermute | solution.py:188
  136.2 3.9 %shard_map.80 = (f32[1024,256]{1,0:T(8,128)}, f32[256,1024]{1,0:T(8,128)}) custom-call(s32[1]{0:T(128)} %bitcast.7.x_ref, bf16[2,192,1024]{2,1,0:T(8,128)(2,1)} %get-tuple-element.40.tokens_ref, bf16[2,192,1024]{2,1,0:T(8,128)(2,1)S(1)} %collective-permute-done.11.after_ref, bf16[192,1280]{1,0:T(8,128)(2,1)S(1)} %collective-permute-done.12.plus_ref, ...), custom_call_target="tpu_custom_call" | custom-call | flops 805306368 | bytes 6324228 | tf_op jit(solution)/shard_map/pallas_call | solution.py:32
  140.1 0.7 shard_map.81
  (25 shorter events, 0.2 us)
Async XLA Ops:
  0.6 23.7 %copy-start = (bf16[1024,256]{1,0:T(8,128)(2,1)S(1)}, bf16[1024,256]{1,0:T(8,128)(2,1)}, u32[]{:S(2)}) copy-start(bf16[1024,256]{1,0:T(8,128)(2,1)} %own_ref.3) | copy-start | bytes 1572868
  0.6 0.8 copy-start.6
  1.5 0.8 copy-start.7
  3.2 39.6 %copy-start.8 = (bf16[96,256]{1,0:T(8,128)(2,1)S(1)}, bf16[96,256]{1,0:T(8,128)(2,1)}, u32[]{:S(2)}) copy-start(bf16[96,256]{1,0:T(8,128)(2,1)} %param.7) | copy-start | bytes 147460
  3.2 54.9 %all-to-all-start = ((bf16[16,48,512]{2,1,0:T(8,128)(2,1)}), bf16[16,48,512]{2,1,0:T(8,128)(2,1)S(1)}, u32[]{:S(2)}, u32[]{:S(2)}) async-start(bf16[16,48,512]{2,1,0:T(8,128)(2,1)} %shard_map.76), calls=%async_computation | async-start | bytes 1572864 | tf_op jit(solution)/shard_map/all_to_all | solution.py:22
  18.5 17.0 %collective-permute-start.1 = (bf16[256,1024]{1,0:T(8,128)(2,1)}, bf16[256,1024]{1,0:T(8,128)(2,1)S(1)}, u32[]{:S(2)}, u32[]{:S(2)}) collective-permute-start(bf16[256,1024]{1,0:T(8,128)(2,1)} %own_ref.2), channel_id=1, source_target_pairs={{0,16},{16,32},{32,48},{48,0},{1,17},{17,33},{33,49},{49,1},{2,18}... | collective-permute-start | bytes 1572872 | tf_op jit(solution)/shard_map/ppermute | solution.py:133
  20.9 18.9 %collective-permute-start.2 = (bf16[256,1024]{1,0:T(8,128)(2,1)}, bf16[256,1024]{1,0:T(8,128)(2,1)S(1)}, u32[]{:S(2)}, u32[]{:S(2)}) collective-permute-start(bf16[256,1024]{1,0:T(8,128)(2,1)} %own_ref.2), channel_id=1, source_target_pairs={{0,48},{16,0},{32,16},{48,32},{1,49},{17,1},{33,17},{49,33},{2,50}... | collective-permute-start | bytes 1572872 | tf_op jit(solution)/shard_map/ppermute | solution.py:133
  24.4 33.6 %collective-permute-start.5 = (bf16[1024,256]{1,0:T(8,128)(2,1)S(1)}, bf16[1024,256]{1,0:T(8,128)(2,1)S(1)}, u32[]{:S(2)}, u32[]{:S(2)}) collective-permute-start(bf16[1024,256]{1,0:T(8,128)(2,1)S(1)} %copy-done), channel_id=1, source_target_pairs={{0,16},{16,32},{32,48},{48,0},{1,17},{17,33},{33,49},{49,1},{2,18}... | collective-permute-start | bytes 1572872 | tf_op jit(solution)/shard_map/ppermute | solution.py:133
  28.0 30.0 %collective-permute-start.6 = (bf16[1024,256]{1,0:T(8,128)(2,1)S(1)}, bf16[1024,256]{1,0:T(8,128)(2,1)S(1)}, u32[]{:S(2)}, u32[]{:S(2)}) collective-permute-start(bf16[1024,256]{1,0:T(8,128)(2,1)S(1)} %copy-done), channel_id=1, source_target_pairs={{0,48},{16,0},{32,16},{48,32},{1,49},{17,1},{33,17},{49,33},{2,50}... | collective-permute-start | bytes 1572872 | tf_op jit(solution)/shard_map/ppermute | solution.py:133
  36.2 21.8 %collective-permute-start.3 = (bf16[128,1024]{1,0:T(8,128)(2,1)}, bf16[128,1024]{1,0:T(8,128)(2,1)}, u32[]{:S(2)}, u32[]{:S(2)}) collective-permute-start(bf16[128,1024]{1,0:T(8,128)(2,1)} %slice.46), channel_id=1, source_target_pairs={{0,16},{16,32},{32,48},{48,0},{1,17},{17,33},{33,49},{49,1},{2,18}... | collective-permute-start | bytes 786440 | tf_op jit(solution)/shard_map/ppermute | solution.py:138
  40.5 17.5 %collective-permute-start.4 = (bf16[128,1024]{1,0:T(8,128)(2,1)}, bf16[128,1024]{1,0:T(8,128)(2,1)}, u32[]{:S(2)}, u32[]{:S(2)}) collective-permute-start(bf16[128,1024]{1,0:T(8,128)(2,1)} %slice.47), channel_id=1, source_target_pairs={{0,48},{16,0},{32,16},{48,32},{1,49},{17,1},{33,17},{49,33},{2,50}... | collective-permute-start | bytes 786440 | tf_op jit(solution)/shard_map/ppermute | solution.py:138
  42.8 15.2 %collective-permute-start = (bf16[96,256]{1,0:T(8,128)(2,1)S(1)}, bf16[96,256]{1,0:T(8,128)(2,1)S(1)}, u32[]{:S(2)}, u32[]{:S(2)}) collective-permute-start(bf16[96,256]{1,0:T(8,128)(2,1)S(1)} %copy-done.8), channel_id=1, source_target_pairs={{0,0},{16,128},{32,256},{48,384},{128,400},{144,16},{160,144},{176... | collective-permute-start | bytes 147464 | tf_op jit(solution)/shard_map/ppermute | solution.py:148
  61.6 3.6 %collective-permute-start.7 = (f32[4,96,256]{2,1,0:T(8,128)S(1)}, f32[4,96,256]{2,1,0:T(8,128)S(1)}, u32[]{:S(2)}, u32[]{:S(2)}) collective-permute-start(f32[4,96,256]{2,1,0:T(8,128)S(1)} %get-tuple-element.33), channel_id=1, source_target_pairs={{0,64},{64,0},{1,65},{65,1},{2,66},{66,2},{3,67},{67,3},{4,68},{68... | collective-permute-start | bytes 1179656 | tf_op jit(solution)/shard_map/ppermute | solution.py:165
  66.5 20.3 %all-to-all-start.1 = ((bf16[4,6,96,256]{3,2,1,0:T(8,128)(2,1)}), bf16[4,6,96,256]{3,2,1,0:T(8,128)(2,1)}, u32[]{:S(2)}, u32[]{:S(2)}) async-start(bf16[4,6,96,256]{3,2,1,0:T(8,128)(2,1)} %broadcast_in_dim.21), calls=%async_computation.1 | async-start | bytes 2359296 | tf_op jit(solution)/shard_map/all_to_all | solution.py:22
  71.2 14.1 %collective-permute-start.9 = (bf16[512,256]{1,0:T(8,128)(2,1)S(1)}, bf16[512,256]{1,0:T(8,128)(2,1)S(1)}, u32[]{:S(2)}, u32[]{:S(2)}) collective-permute-start(bf16[512,256]{1,0:T(8,128)(2,1)S(1)} %slice.37), channel_id=1, source_target_pairs={{0,48},{16,0},{32,16},{48,32},{1,49},{17,1},{33,17},{49,33},{2,50}... | collective-permute-start | bytes 786440 | tf_op jit(solution)/shard_map/ppermute | solution.py:138
  73.9 12.1 %collective-permute-start.8 = (bf16[512,256]{1,0:T(8,128)(2,1)S(1)}, bf16[512,256]{1,0:T(8,128)(2,1)S(1)}, u32[]{:S(2)}, u32[]{:S(2)}) collective-permute-start(bf16[512,256]{1,0:T(8,128)(2,1)S(1)} %slice.36), channel_id=1, source_target_pairs={{0,16},{16,32},{32,48},{48,0},{1,17},{17,33},{33,49},{49,1},{2,18}... | collective-permute-start | bytes 786440 | tf_op jit(solution)/shard_map/ppermute | solution.py:138
  78.3 21.9 %collective-permute-start.11 = (bf16[2,192,1024]{2,1,0:T(8,128)(2,1)}, bf16[2,192,1024]{2,1,0:T(8,128)(2,1)S(1)}, u32[]{:S(2)}, u32[]{:S(2)}) collective-permute-start(bf16[2,192,1024]{2,1,0:T(8,128)(2,1)} %get-tuple-element.40.tokens_ref), channel_id=1, source_target_pairs={{0,48},{16,0},{32,16},{48,32},{1,49},{17,1},{33,17},{49,33},{2,50}... | collective-permute-start | bytes 2359304 | tf_op jit(solution)/shard_map/ppermute | solution.py:133
  80.2 21.3 %collective-permute-start.10 = (bf16[2,192,1024]{2,1,0:T(8,128)(2,1)}, bf16[2,192,1024]{2,1,0:T(8,128)(2,1)S(1)}, u32[]{:S(2)}, u32[]{:S(2)}) collective-permute-start(bf16[2,192,1024]{2,1,0:T(8,128)(2,1)} %get-tuple-element.40.tokens_ref), channel_id=1, source_target_pairs={{0,16},{16,32},{32,48},{48,0},{1,17},{17,33},{33,49},{49,1},{2,18}... | collective-permute-start | bytes 2359304 | tf_op jit(solution)/shard_map/ppermute | solution.py:133
  85.3 0.7 copy-start.2
  86.0 0.7 copy-start.4
  89.2 2.6 %copy-start.1 = (bf16[1024,256]{1,0:T(8,128)(2,1)S(1)}, bf16[1024,256]{1,0:T(8,128)(2,1)}, u32[]{:S(2)}) copy-start(bf16[1024,256]{1,0:T(8,128)(2,1)} %own_ref.3) | copy-start | bytes 1572868
  89.3 2.6 %copy-start.3 = (bf16[512,256]{1,0:T(8,128)(2,1)S(1)}, bf16[512,256]{1,0:T(8,128)(2,1)}, u32[]{:S(2)}) copy-start(bf16[512,256]{1,0:T(8,128)(2,1)} %copy-done.2) | copy-start | bytes 786436
  89.3 2.6 %copy-start.5 = (bf16[512,256]{1,0:T(8,128)(2,1)S(1)}, bf16[512,256]{1,0:T(8,128)(2,1)}, u32[]{:S(2)}) copy-start(bf16[512,256]{1,0:T(8,128)(2,1)} %copy-done.4) | copy-start | bytes 786436
  101.5 38.6 %all-to-all-start.2 = ((bf16[16,24,512]{2,1,0:T(8,128)(2,1)}), bf16[16,24,512]{2,1,0:T(8,128)(2,1)S(1)}, u32[]{:S(2)}, u32[]{:S(2)}) async-start(bf16[16,24,512]{2,1,0:T(8,128)(2,1)} %shard_map.78), calls=%async_computation.2 | async-start | bytes 786432 | tf_op jit(solution)/shard_map/all_to_all | solution.py:22
  114.2 20.5 %collective-permute-start.12 = (bf16[192,1280]{1,0:T(8,128)(2,1)}, bf16[192,1280]{1,0:T(8,128)(2,1)S(1)}, u32[]{:S(2)}, u32[]{:S(2)}) collective-permute-start(bf16[192,1280]{1,0:T(8,128)(2,1)} %get-tuple-element.44), channel_id=1, source_target_pairs={{0,16},{16,32},{32,48},{48,0},{1,17},{17,33},{33,49},{49,1},{2,18}... | collective-permute-start | bytes 1474568 | tf_op jit(solution)/shard_map/ppermute | solution.py:188
  119.7 16.5 %collective-permute-start.13 = (bf16[192,1280]{1,0:T(8,128)(2,1)}, bf16[192,1280]{1,0:T(8,128)(2,1)}, u32[]{:S(2)}, u32[]{:S(2)}) collective-permute-start(bf16[192,1280]{1,0:T(8,128)(2,1)} %get-tuple-element.45), channel_id=1, source_target_pairs={{0,48},{16,0},{32,16},{48,32},{1,49},{17,1},{33,17},{49,33},{2,50}... | collective-permute-start | bytes 1474568 | tf_op jit(solution)/shard_map/ppermute | solution.py:188
  121.7 13.0 %collective-permute-start.14 = (bf16[192,256]{1,0:T(8,128)(2,1)S(1)}, bf16[192,256]{1,0:T(8,128)(2,1)S(1)}, u32[]{:S(2)}, u32[]{:S(2)}) collective-permute-start(bf16[192,256]{1,0:T(8,128)(2,1)S(1)} %slice_bitcast_fusion.2), channel_id=1, source_target_pairs={{0,32},{16,48},{32,0},{48,16},{1,33},{17,49},{33,1},{49,17},{2,34}... | collective-permute-start | bytes 294920 | tf_op jit(solution)/shard_map/ppermute | solution.py:189

commit v12 on v11

--- a/solution.py
+++ b/solution.py
@@ -26,8 +26,9 @@
     return exchange(jnp.broadcast_to(block[None], (n,) + block.shape), axis)
 
 
-def call(body, outs, scratch, flops, operands, smem=0):
-    moved = sum(a.size * a.dtype.itemsize for a in (*operands, *outs))
+def call(body, outs, scratch, flops, operands, smem=0, moved=None):
+    if moved is None:
+        moved = sum(a.size * a.dtype.itemsize for a in (*operands, *outs))
     spaces = [pltpu.SMEM] * smem + [pltpu.VMEM] * (len(operands) - smem)
     return pl.pallas_call(
         body,
@@ -149,8 +150,10 @@
     before, after = near_x(down_weight)
     far = far_x(before, after)
     up_before, up_after = near_x(up_weight)
-    both, turned, before, after, far, up_before, up_after = lax.optimization_barrier(
-        (both, turned, before, after, far, up_before, up_after)
+    turned, far_before, far_after = lax.optimization_barrier((turned, up_before, up_after))
+    up_far = far_x(far_before, far_after)
+    both, before, after, far, up_before, up_after = lax.optimization_barrier(
+        (both, before, after, far, up_before, up_after)
     )
 
     half = jax.ShapeDtypeStruct((4, 96, 256), F32)
@@ -162,12 +165,11 @@
         (core[None], both, down_weight, after, *far, before),
         smem=1,
     )
+    theirs, up_far = lax.optimization_barrier((theirs, up_far))
     pair = (mine + lax.ppermute(theirs, "c", [(0, 1), (1, 0)])).astype(BF)
     activ, _ = gelu_parts(preact)
     own = spread(jnp.concatenate([pair, activ.astype(BF)[None], turned[None]]), "y")
-    up_far = far_x(up_before, up_after)
     tok_before, tok_after = near_x(tokens)
-    own, up_far = lax.optimization_barrier((own, up_far))
     hidden_grad = sum((own[k, :4].astype(F32) for k in range(1, 4)), own[0, :4].astype(F32))
     _, slope = gelu_parts(own[:, 5])
     own = jnp.concatenate([(hidden_grad * slope).astype(BF), own[:, 4]])
@@ -180,7 +182,7 @@
         2 * 192 * 1024 * 1024,
         (own, up_weight, up_after, *up_far, up_before),
     )
-    part, tok_before, tok_after = lax.optimization_barrier((part, tok_before, tok_after))
+    _, tok_before, tok_after = lax.optimization_barrier((part, tok_before, tok_after))
     part = exchange(part, ("za", "zb"))
 
     packed = jax.ShapeDtypeStruct((192, 1280), BF)
@@ -191,7 +193,7 @@
         weights_kernel,
         [jax.ShapeDtypeStruct((1024, 256), F32), jax.ShapeDtypeStruct((256, 1024), F32)],
         [],
-        4 * 768 * 1024 * 256,
+        8 * 4 * 768 * 1024 * 256,
         (at_x[None], tokens, tok_after, plus, minus, tok_before, own, two),
         smem=1,
     )

time: 142 us -> 140 us (0.986)
  the two profiles are of different devices: /device:TPU:14 before, /device:TPU:24 now
where the time goes in v12:
time: 140 us; the launch traced here: 138 us
  starting transfers between devices  80.4 us (57%)
  waiting for transfers between devices  34.3 us (24%)
  Pallas kernels  11.7 us (8%)
  local copies, waits for them, and re-layouts  6.72 us (5%)
  blocking collectives  2.37 us (2%)
  other arithmetic  1.7 us (1%)
    all_to_all x3, starting transfers between devices, exchange(): lax.all_to_all(blocks, axis, split_axis=0, concat_axis=0, tiled=False)  33.1 us
    pallas_call x6, Pallas kernels, call(): pl.pallas_call(body, out_shape=outs, in_specs=[pl.BlockSpec(memory_space=...  11.7 us
    all_to_all x3, waiting for transfers between devices, exchange(): lax.all_to_all(blocks, axis, split_axis=0, concat_axis=0, tiled=False)  10.5 us
    ppermute x3, starting transfers between devices, near_x(): lax.ppermute(block, 'x', shift(-1))  10.4 us
    ppermute x2, starting transfers between devices, far_x(): lax.ppermute(after[half:], 'x', shift(-1))  9.52 us
    ppermute x3, starting transfers between devices, near_x(): lax.ppermute(block, 'x', shift(1))  9.51 us
    ppermute x1, waiting for transfers between devices, local(): two = lax.ppermute(own[2], 'x', shift(2))  7.37 us
    ppermute x1, waiting for transfers between devices, local(): turned = lax.ppermute(preact, ('y', 'x'), swap)  6.18 us
  transfers between devices with their start and end apart: 18, of which 8 were waited for; matrix products, arithmetic and copies ran while one was open for 4% of the time, Pallas kernels for 7%

profile of v12, /device:TPU:24, one launch (start us, length us, event | category | flops | bytes accessed | tf_op | source)
XLA Modules:
  0.0 138.1 jit_solution(8810612657651082428)
XLA Ops:
  0.6 0.0 copy-start
  0.7 0.8 copy-done.6
  1.5 0.8 copy-done.7
  2.2 0.9 shard_map.76
  3.2 15.2 %all-to-all-start = ((bf16[16,48,512]{2,1,0:T(8,128)(2,1)}), bf16[16,48,512]{2,1,0:T(8,128)(2,1)S(1)}, u32[]{:S(2)}, u32[]{:S(2)}) async-start(bf16[16,48,512]{2,1,0:T(8,128)(2,1)} %shard_map.76), calls=%async_computation | async-start | bytes 1572864 | tf_op jit(solution)/shard_map/all_to_all | solution.py:22
  18.4 3.4 %collective-permute-start = (bf16[256,1024]{1,0:T(8,128)(2,1)}, bf16[256,1024]{1,0:T(8,128)(2,1)S(1)}, u32[]{:S(2)}, u32[]{:S(2)}) collective-permute-start(bf16[256,1024]{1,0:T(8,128)(2,1)} %own_ref.2), channel_id=1, source_target_pairs={{0,16},{16,32},{32,48},{48,0},{1,17},{17,33},{33,49},{49,1},{2,18}... | collective-permute-start | bytes 1572872 | tf_op jit(solution)/shard_map/ppermute | solution.py:134
  21.8 3.7 %collective-permute-start.1 = (bf16[256,1024]{1,0:T(8,128)(2,1)}, bf16[256,1024]{1,0:T(8,128)(2,1)S(1)}, u32[]{:S(2)}, u32[]{:S(2)}) collective-permute-start(bf16[256,1024]{1,0:T(8,128)(2,1)} %own_ref.2), channel_id=1, source_target_pairs={{0,48},{16,0},{32,16},{48,32},{1,49},{17,1},{33,17},{49,33},{2,50}... | collective-permute-start | bytes 1572872 | tf_op jit(solution)/shard_map/ppermute | solution.py:134
  25.5 2.2 %collective-permute-start.4 = (bf16[1024,256]{1,0:T(8,128)(2,1)S(1)}, bf16[1024,256]{1,0:T(8,128)(2,1)S(1)}, u32[]{:S(2)}, u32[]{:S(2)}) collective-permute-start(bf16[1024,256]{1,0:T(8,128)(2,1)S(1)} %copy-done), channel_id=1, source_target_pairs={{0,16},{16,32},{32,48},{48,0},{1,17},{17,33},{33,49},{49,1},{2,18}... | collective-permute-start | bytes 1572872 | tf_op jit(solution)/shard_map/ppermute | solution.py:134
  27.6 4.9 %collective-permute-start.5 = (bf16[1024,256]{1,0:T(8,128)(2,1)S(1)}, bf16[1024,256]{1,0:T(8,128)(2,1)S(1)}, u32[]{:S(2)}, u32[]{:S(2)}) collective-permute-start(bf16[1024,256]{1,0:T(8,128)(2,1)S(1)} %copy-done), channel_id=1, source_target_pairs={{0,48},{16,0},{32,16},{48,32},{1,49},{17,1},{33,17},{49,33},{2,50}... | collective-permute-start | bytes 1572872 | tf_op jit(solution)/shard_map/ppermute | solution.py:134
  32.5 2.9 %collective-permute-start.6 = (bf16[96,256]{1,0:T(8,128)(2,1)S(1)}, bf16[96,256]{1,0:T(8,128)(2,1)S(1)}, u32[]{:S(2)}, u32[]{:S(2)}) collective-permute-start(bf16[96,256]{1,0:T(8,128)(2,1)S(1)} %copy-done.8), channel_id=1, source_target_pairs={{0,0},{16,128},{32,256},{48,384},{128,400},{144,16},{160,144},{176... | collective-permute-start | bytes 147464 | tf_op jit(solution)/shard_map/ppermute | solution.py:149
  35.5 1.1 collective-permute-done.before_ref
  36.5 0.7 slice.46
  37.3 2.2 %collective-permute-start.2 = (bf16[128,1024]{1,0:T(8,128)(2,1)}, bf16[128,1024]{1,0:T(8,128)(2,1)}, u32[]{:S(2)}, u32[]{:S(2)}) collective-permute-start(bf16[128,1024]{1,0:T(8,128)(2,1)} %slice.46), channel_id=1, source_target_pairs={{0,16},{16,32},{32,48},{48,0},{1,17},{17,33},{33,49},{49,1},{2,18}... | collective-permute-start | bytes 786440 | tf_op jit(solution)/shard_map/ppermute | solution.py:139
  39.4 0.0 collective-permute-done.1.after_ref
  39.5 0.7 slice.47
  40.2 4.9 %collective-permute-start.3 = (bf16[128,1024]{1,0:T(8,128)(2,1)}, bf16[128,1024]{1,0:T(8,128)(2,1)}, u32[]{:S(2)}, u32[]{:S(2)}) collective-permute-start(bf16[128,1024]{1,0:T(8,128)(2,1)} %slice.47), channel_id=1, source_target_pairs={{0,48},{16,0},{32,16},{48,32},{1,49},{17,1},{33,17},{49,33},{2,50}... | collective-permute-start | bytes 786440 | tf_op jit(solution)/shard_map/ppermute | solution.py:139
  45.0 6.2 %collective-permute-done.6 = bf16[96,256]{1,0:T(8,128)(2,1)S(1)} collective-permute-done((bf16[96,256]{1,0:T(8,128)(2,1)S(1)}, bf16[96,256]{1,0:T(8,128)(2,1)S(1)}, u32[]{:S(2)}, u32[]{:S(2)}) %collective-permute-start.6) | collective-permute-done | bytes 49184 | tf_op jit(solution)/shard_map/ppermute | solution.py:149
  51.2 0.7 slice.36
  51.9 0.7 slice.37
  52.7 4.7 %collective-permute-start.8 = (bf16[512,256]{1,0:T(8,128)(2,1)}, bf16[512,256]{1,0:T(8,128)(2,1)S(1)}, u32[]{:S(2)}, u32[]{:S(2)}) collective-permute-start(bf16[512,256]{1,0:T(8,128)(2,1)} %slice.37), channel_id=1, source_target_pairs={{0,48},{16,0},{32,16},{48,32},{1,49},{17,1},{33,17},{49,33},{2,50}... | collective-permute-start | bytes 786440 | tf_op jit(solution)/shard_map/ppermute | solution.py:139
  57.4 1.9 %collective-permute-start.7 = (bf16[512,256]{1,0:T(8,128)(2,1)}, bf16[512,256]{1,0:T(8,128)(2,1)S(1)}, u32[]{:S(2)}, u32[]{:S(2)}) collective-permute-start(bf16[512,256]{1,0:T(8,128)(2,1)} %slice.36), channel_id=1, source_target_pairs={{0,16},{16,32},{32,48},{48,0},{1,17},{17,33},{33,49},{49,1},{2,18}... | collective-permute-start | bytes 786440 | tf_op jit(solution)/shard_map/ppermute | solution.py:139
  59.3 3.5 %shard_map.77 = (f32[4,96,256]{2,1,0:T(8,128)S(1)}, f32[4,96,256]{2,1,0:T(8,128)S(1)}, bf16[2,192,1024]{2,1,0:T(8,128)(2,1)}) custom-call(s32[1]{0:T(128)} %bitcast.core_ref, bf16[16,48,512]{2,1,0:T(8,128)(2,1)S(1)} %all-to-all-done.both_ref, bf16[256,1024]{1,0:T(8,128)(2,1)} %own_ref.2, bf16[256,1024]{1,0:T(8,128)(2,1)S(1)} %collective-permute-done.1.after_ref, ...), custom_call_target="tpu_custom_call" | custom-call | flops 402653184 | bytes 4456452 | tf_op jit(solution)/shard_map/pallas_call | solution.py:33
  62.9 4.2 %collective-permute-done.7.far0_ref = bf16[512,256]{1,0:T(8,128)(2,1)S(1)} collective-permute-done((bf16[512,256]{1,0:T(8,128)(2,1)}, bf16[512,256]{1,0:T(8,128)(2,1)S(1)}, u32[]{:S(2)}, u32[]{:S(2)}) %collective-permute-start.7) | collective-permute-done | bytes 262176 | tf_op jit(solution)/shard_map/ppermute | solution.py:139
  67.1 1.9 %collective-permute-start.9 = (f32[4,96,256]{2,1,0:T(8,128)S(1)}, f32[4,96,256]{2,1,0:T(8,128)S(1)}, u32[]{:S(2)}, u32[]{:S(2)}) collective-permute-start(f32[4,96,256]{2,1,0:T(8,128)S(1)} %get-tuple-element.37), channel_id=1, source_target_pairs={{0,64},{64,0},{1,65},{65,1},{2,66},{66,2},{3,67},{67,3},{4,68},{68... | collective-permute-start | bytes 1179656 | tf_op jit(solution)/shard_map/ppermute | solution.py:169
  69.0 1.7 %collective-permute-done.9 = f32[4,96,256]{2,1,0:T(8,128)S(1)} collective-permute-done((f32[4,96,256]{2,1,0:T(8,128)S(1)}, f32[4,96,256]{2,1,0:T(8,128)S(1)}, u32[]{:S(2)}, u32[]{:S(2)}) %collective-permute-start.9) | collective-permute-done | bytes 393248 | tf_op jit(solution)/shard_map/ppermute | solution.py:169
  70.7 0.1 add_convert_fusion
  70.8 1.2 broadcast_in_dim.21
  71.9 5.9 %all-to-all-start.1 = ((bf16[4,6,96,256]{3,2,1,0:T(8,128)(2,1)}), bf16[4,6,96,256]{3,2,1,0:T(8,128)(2,1)}, u32[]{:S(2)}, u32[]{:S(2)}) async-start(bf16[4,6,96,256]{3,2,1,0:T(8,128)(2,1)} %broadcast_in_dim.21), calls=%async_computation.1 | async-start | bytes 2359296 | tf_op jit(solution)/shard_map/all_to_all | solution.py:22
  77.8 1.9 %collective-permute-start.11 = (bf16[2,192,1024]{2,1,0:T(8,128)(2,1)}, bf16[2,192,1024]{2,1,0:T(8,128)(2,1)S(1)}, u32[]{:S(2)}, u32[]{:S(2)}) collective-permute-start(bf16[2,192,1024]{2,1,0:T(8,128)(2,1)} %get-tuple-element.43.tokens_ref), channel_id=1, source_target_pairs={{0,48},{16,0},{32,16},{48,32},{1,49},{17,1},{33,17},{49,33},{2,50}... | collective-permute-start | bytes 2359304 | tf_op jit(solution)/shard_map/ppermute | solution.py:134
  79.7 3.9 %collective-permute-start.10 = (bf16[2,192,1024]{2,1,0:T(8,128)(2,1)}, bf16[2,192,1024]{2,1,0:T(8,128)(2,1)S(1)}, u32[]{:S(2)}, u32[]{:S(2)}) collective-permute-start(bf16[2,192,1024]{2,1,0:T(8,128)(2,1)} %get-tuple-element.43.tokens_ref), channel_id=1, source_target_pairs={{0,16},{16,32},{32,48},{48,0},{1,17},{17,33},{33,49},{49,1},{2,18}... | collective-permute-start | bytes 2359304 | tf_op jit(solution)/shard_map/ppermute | solution.py:134
  83.6 10.5 %all-to-all-done.1 = bf16[4,6,96,256]{3,2,1,0:T(8,128)(2,1)} async-done(((bf16[4,6,96,256]{3,2,1,0:T(8,128)(2,1)}), bf16[4,6,96,256]{3,2,1,0:T(8,128)(2,1)}, u32[]{:S(2)}, u32[]{:S(2)}) %all-to-all-start.1) | async-done | bytes 1179680 | tf_op jit(solution)/shard_map/all_to_all | solution.py:22
  94.2 1.5 %fusion.7 = bf16[4,96,256]{2,1,0:T(8,128)(2,1)S(1)} fusion(bf16[4,6,96,256]{3,2,1,0:T(8,128)(2,1)} %all-to-all-done.1), kind=kLoop, calls=%fused_computation.13 | loop fusion | flops 1769472 | bytes 1179648 | tf_op jit(solution)/shard_map/convert_element_type | solution.py:175
  95.7 0.0 copy-start.1
  95.7 0.0 copy-start.3
  95.7 0.0 copy-start.5
  95.7 1.0 slice_bitcast_fusion
  96.8 2.4 %all-gather.pregrad_ref.own_ref = bf16[8,192,256]{2,1,0:T(8,128)(2,1)S(1)} all-gather(bf16[8,96,256]{2,1,0:T(8,128)(2,1)S(1)} %pad_maximum_fusion), channel_id=2, replica_groups=mesh['y'=4,'c'=2,'x'=4,'za'=4,'zb'=4] {'c'}, dimensions={1}, use_global_device_ids=true | all-gather | bytes 1179648 | tf_op jit(solution)/shard_map/all_gather | solution.py:176
  99.2 1.6 %shard_map.78 = bf16[16,24,512]{2,1,0:T(8,128)(2,1)} custom-call(bf16[8,192,256]{2,1,0:T(8,128)(2,1)S(1)} %all-gather.pregrad_ref.own_ref, bf16[1024,256]{1,0:T(8,128)(2,1)S(1)} %copy-done.1, bf16[1024,256]{1,0:T(8,128)(2,1)S(1)} %collective-permute-done.5.after_ref, bf16[512,256]{1,0:T(8,128)(2,1)S(1)} %copy-done.5, bf16[512,256]{1,0:T(8,128)(2,1)S(1)} %copy-done.3, ...), custom_call_target="tpu_custom_call" | custom-call | flops 402653184 | bytes 3276800 | tf_op jit(solution)/shard_map/pallas_call | solution.py:33
  100.8 12.0 %all-to-all-start.2 = ((bf16[16,24,512]{2,1,0:T(8,128)(2,1)}), bf16[16,24,512]{2,1,0:T(8,128)(2,1)S(1)}, u32[]{:S(2)}, u32[]{:S(2)}) async-start(bf16[16,24,512]{2,1,0:T(8,128)(2,1)} %shard_map.78), calls=%async_computation.2 | async-start | bytes 786432 | tf_op jit(solution)/shard_map/all_to_all | solution.py:22
  112.9 1.0 shard_map.79
  113.9 1.9 %collective-permute-start.12 = (bf16[192,1280]{1,0:T(8,128)(2,1)}, bf16[192,1280]{1,0:T(8,128)(2,1)S(1)}, u32[]{:S(2)}, u32[]{:S(2)}) collective-permute-start(bf16[192,1280]{1,0:T(8,128)(2,1)} %get-tuple-element.46), channel_id=1, source_target_pairs={{0,16},{16,32},{32,48},{48,0},{1,17},{17,33},{33,49},{49,1},{2,18}... | collective-permute-start | bytes 1474568 | tf_op jit(solution)/shard_map/ppermute | solution.py:190
  115.8 5.1 %collective-permute-start.13 = (bf16[192,1280]{1,0:T(8,128)(2,1)}, bf16[192,1280]{1,0:T(8,128)(2,1)}, u32[]{:S(2)}, u32[]{:S(2)}) collective-permute-start(bf16[192,1280]{1,0:T(8,128)(2,1)} %get-tuple-element.47), channel_id=1, source_target_pairs={{0,48},{16,0},{32,16},{48,32},{1,49},{17,1},{33,17},{49,33},{2,50}... | collective-permute-start | bytes 1474568 | tf_op jit(solution)/shard_map/ppermute | solution.py:190
  120.9 1.9 %collective-permute-start.14 = (bf16[192,256]{1,0:T(8,128)(2,1)S(1)}, bf16[192,256]{1,0:T(8,128)(2,1)S(1)}, u32[]{:S(2)}, u32[]{:S(2)}) collective-permute-start(bf16[192,256]{1,0:T(8,128)(2,1)S(1)} %slice_bitcast_fusion.2), channel_id=1, source_target_pairs={{0,32},{16,48},{32,0},{48,16},{1,33},{17,49},{33,1},{49,17},{2,34}... | collective-permute-start | bytes 294920 | tf_op jit(solution)/shard_map/ppermute | solution.py:191
  122.9 7.4 %collective-permute-done.14.two_ref = bf16[192,256]{1,0:T(8,128)(2,1)S(1)} collective-permute-done((bf16[192,256]{1,0:T(8,128)(2,1)S(1)}, bf16[192,256]{1,0:T(8,128)(2,1)S(1)}, u32[]{:S(2)}, u32[]{:S(2)}) %collective-permute-start.14) | collective-permute-done | bytes 98336 | tf_op jit(solution)/shard_map/ppermute | solution.py:191
  130.2 2.0 %collective-permute-done.12.plus_ref = bf16[192,1280]{1,0:T(8,128)(2,1)S(1)} collective-permute-done((bf16[192,1280]{1,0:T(8,128)(2,1)}, bf16[192,1280]{1,0:T(8,128)(2,1)S(1)}, u32[]{:S(2)}, u32[]{:S(2)}) %collective-permute-start.12) | collective-permute-done | bytes 491552 | tf_op jit(solution)/shard_map/ppermute | solution.py:190
  132.3 1.3 collective-permute-done.13.minus_ref
  133.5 3.9 %shard_map.80 = (f32[1024,256]{1,0:T(8,128)}, f32[256,1024]{1,0:T(8,128)}) custom-call(s32[1]{0:T(128)} %bitcast.7.x_ref, bf16[2,192,1024]{2,1,0:T(8,128)(2,1)} %get-tuple-element.43.tokens_ref, bf16[2,192,1024]{2,1,0:T(8,128)(2,1)S(1)} %collective-permute-done.11.after_ref, bf16[192,1280]{1,0:T(8,128)(2,1)S(1)} %collective-permute-done.12.plus_ref, ...), custom_call_target="tpu_custom_call" | custom-call | flops 6442450944 | bytes 6324228 | tf_op jit(solution)/shard_map/pallas_call | solution.py:33
  137.5 0.7 shard_map.81
  (25 shorter events, 0.2 us)
Async XLA Ops:
  0.6 24.8 %copy-start = (bf16[1024,256]{1,0:T(8,128)(2,1)S(1)}, bf16[1024,256]{1,0:T(8,128)(2,1)}, u32[]{:S(2)}) copy-start(bf16[1024,256]{1,0:T(8,128)(2,1)} %own_ref.3) | copy-start | bytes 1572868
  0.6 0.8 copy-start.6
  1.5 0.8 copy-start.7
  2.2 30.3 %copy-start.8 = (bf16[96,256]{1,0:T(8,128)(2,1)S(1)}, bf16[96,256]{1,0:T(8,128)(2,1)}, u32[]{:S(2)}) copy-start(bf16[96,256]{1,0:T(8,128)(2,1)} %param.7) | copy-start | bytes 147460
  3.2 56.2 %all-to-all-start = ((bf16[16,48,512]{2,1,0:T(8,128)(2,1)}), bf16[16,48,512]{2,1,0:T(8,128)(2,1)S(1)}, u32[]{:S(2)}, u32[]{:S(2)}) async-start(bf16[16,48,512]{2,1,0:T(8,128)(2,1)} %shard_map.76), calls=%async_computation | async-start | bytes 1572864 | tf_op jit(solution)/shard_map/all_to_all | solution.py:22
  18.4 18.2 %collective-permute-start = (bf16[256,1024]{1,0:T(8,128)(2,1)}, bf16[256,1024]{1,0:T(8,128)(2,1)S(1)}, u32[]{:S(2)}, u32[]{:S(2)}) collective-permute-start(bf16[256,1024]{1,0:T(8,128)(2,1)} %own_ref.2), channel_id=1, source_target_pairs={{0,16},{16,32},{32,48},{48,0},{1,17},{17,33},{33,49},{49,1},{2,18}... | collective-permute-start | bytes 1572872 | tf_op jit(solution)/shard_map/ppermute | solution.py:134
  21.8 17.7 %collective-permute-start.1 = (bf16[256,1024]{1,0:T(8,128)(2,1)}, bf16[256,1024]{1,0:T(8,128)(2,1)S(1)}, u32[]{:S(2)}, u32[]{:S(2)}) collective-permute-start(bf16[256,1024]{1,0:T(8,128)(2,1)} %own_ref.2), channel_id=1, source_target_pairs={{0,48},{16,0},{32,16},{48,32},{1,49},{17,1},{33,17},{49,33},{2,50}... | collective-permute-start | bytes 1572872 | tf_op jit(solution)/shard_map/ppermute | solution.py:134
  25.5 25.8 %collective-permute-start.4 = (bf16[1024,256]{1,0:T(8,128)(2,1)S(1)}, bf16[1024,256]{1,0:T(8,128)(2,1)S(1)}, u32[]{:S(2)}, u32[]{:S(2)}) collective-permute-start(bf16[1024,256]{1,0:T(8,128)(2,1)S(1)} %copy-done), channel_id=1, source_target_pairs={{0,16},{16,32},{32,48},{48,0},{1,17},{17,33},{33,49},{49,1},{2,18}... | collective-permute-start | bytes 1572872 | tf_op jit(solution)/shard_map/ppermute | solution.py:134
  27.6 23.6 %collective-permute-start.5 = (bf16[1024,256]{1,0:T(8,128)(2,1)S(1)}, bf16[1024,256]{1,0:T(8,128)(2,1)S(1)}, u32[]{:S(2)}, u32[]{:S(2)}) collective-permute-start(bf16[1024,256]{1,0:T(8,128)(2,1)S(1)} %copy-done), channel_id=1, source_target_pairs={{0,48},{16,0},{32,16},{48,32},{1,49},{17,1},{33,17},{49,33},{2,50}... | collective-permute-start | bytes 1572872 | tf_op jit(solution)/shard_map/ppermute | solution.py:134
  32.5 18.7 %collective-permute-start.6 = (bf16[96,256]{1,0:T(8,128)(2,1)S(1)}, bf16[96,256]{1,0:T(8,128)(2,1)S(1)}, u32[]{:S(2)}, u32[]{:S(2)}) collective-permute-start(bf16[96,256]{1,0:T(8,128)(2,1)S(1)} %copy-done.8), channel_id=1, source_target_pairs={{0,0},{16,128},{32,256},{48,384},{128,400},{144,16},{160,144},{176... | collective-permute-start | bytes 147464 | tf_op jit(solution)/shard_map/ppermute | solution.py:149
  37.3 22.0 %collective-permute-start.2 = (bf16[128,1024]{1,0:T(8,128)(2,1)}, bf16[128,1024]{1,0:T(8,128)(2,1)}, u32[]{:S(2)}, u32[]{:S(2)}) collective-permute-start(bf16[128,1024]{1,0:T(8,128)(2,1)} %slice.46), channel_id=1, source_target_pairs={{0,16},{16,32},{32,48},{48,0},{1,17},{17,33},{33,49},{49,1},{2,18}... | collective-permute-start | bytes 786440 | tf_op jit(solution)/shard_map/ppermute | solution.py:139
  40.2 19.1 %collective-permute-start.3 = (bf16[128,1024]{1,0:T(8,128)(2,1)}, bf16[128,1024]{1,0:T(8,128)(2,1)}, u32[]{:S(2)}, u32[]{:S(2)}) collective-permute-start(bf16[128,1024]{1,0:T(8,128)(2,1)} %slice.47), channel_id=1, source_target_pairs={{0,48},{16,0},{32,16},{48,32},{1,49},{17,1},{33,17},{49,33},{2,50}... | collective-permute-start | bytes 786440 | tf_op jit(solution)/shard_map/ppermute | solution.py:139
  52.7 10.2 %collective-permute-start.8 = (bf16[512,256]{1,0:T(8,128)(2,1)}, bf16[512,256]{1,0:T(8,128)(2,1)S(1)}, u32[]{:S(2)}, u32[]{:S(2)}) collective-permute-start(bf16[512,256]{1,0:T(8,128)(2,1)} %slice.37), channel_id=1, source_target_pairs={{0,48},{16,0},{32,16},{48,32},{1,49},{17,1},{33,17},{49,33},{2,50}... | collective-permute-start | bytes 786440 | tf_op jit(solution)/shard_map/ppermute | solution.py:139
  57.4 9.7 %collective-permute-start.7 = (bf16[512,256]{1,0:T(8,128)(2,1)}, bf16[512,256]{1,0:T(8,128)(2,1)S(1)}, u32[]{:S(2)}, u32[]{:S(2)}) collective-permute-start(bf16[512,256]{1,0:T(8,128)(2,1)} %slice.36), channel_id=1, source_target_pairs={{0,16},{16,32},{32,48},{48,0},{1,17},{17,33},{33,49},{49,1},{2,18}... | collective-permute-start | bytes 786440 | tf_op jit(solution)/shard_map/ppermute | solution.py:139
  62.9 9.1 %copy-start.2 = (bf16[512,256]{1,0:T(8,128)(2,1)}, bf16[512,256]{1,0:T(8,128)(2,1)S(1)}, u32[]{:S(2)}) copy-start(bf16[512,256]{1,0:T(8,128)(2,1)S(1)} %collective-permute-done.8.far1_ref) | copy-start | bytes 786436
  67.1 4.9 %copy-start.4 = (bf16[512,256]{1,0:T(8,128)(2,1)}, bf16[512,256]{1,0:T(8,128)(2,1)S(1)}, u32[]{:S(2)}) copy-start(bf16[512,256]{1,0:T(8,128)(2,1)S(1)} %collective-permute-done.7.far0_ref) | copy-start | bytes 786436
  67.1 3.6 %collective-permute-start.9 = (f32[4,96,256]{2,1,0:T(8,128)S(1)}, f32[4,96,256]{2,1,0:T(8,128)S(1)}, u32[]{:S(2)}, u32[]{:S(2)}) collective-permute-start(f32[4,96,256]{2,1,0:T(8,128)S(1)} %get-tuple-element.37), channel_id=1, source_target_pairs={{0,64},{64,0},{1,65},{65,1},{2,66},{66,2},{3,67},{67,3},{4,68},{68... | collective-permute-start | bytes 1179656 | tf_op jit(solution)/shard_map/ppermute | solution.py:169
  71.9 22.2 %all-to-all-start.1 = ((bf16[4,6,96,256]{3,2,1,0:T(8,128)(2,1)}), bf16[4,6,96,256]{3,2,1,0:T(8,128)(2,1)}, u32[]{:S(2)}, u32[]{:S(2)}) async-start(bf16[4,6,96,256]{3,2,1,0:T(8,128)(2,1)} %broadcast_in_dim.21), calls=%async_computation.1 | async-start | bytes 2359296 | tf_op jit(solution)/shard_map/all_to_all | solution.py:22
  77.8 35.0 %collective-permute-start.11 = (bf16[2,192,1024]{2,1,0:T(8,128)(2,1)}, bf16[2,192,1024]{2,1,0:T(8,128)(2,1)S(1)}, u32[]{:S(2)}, u32[]{:S(2)}) collective-permute-start(bf16[2,192,1024]{2,1,0:T(8,128)(2,1)} %get-tuple-element.43.tokens_ref), channel_id=1, source_target_pairs={{0,48},{16,0},{32,16},{48,32},{1,49},{17,1},{33,17},{49,33},{2,50}... | collective-permute-start | bytes 2359304 | tf_op jit(solution)/shard_map/ppermute | solution.py:134
  79.7 33.1 %collective-permute-start.10 = (bf16[2,192,1024]{2,1,0:T(8,128)(2,1)}, bf16[2,192,1024]{2,1,0:T(8,128)(2,1)S(1)}, u32[]{:S(2)}, u32[]{:S(2)}) collective-permute-start(bf16[2,192,1024]{2,1,0:T(8,128)(2,1)} %get-tuple-element.43.tokens_ref), channel_id=1, source_target_pairs={{0,16},{16,32},{32,48},{48,0},{1,17},{17,33},{33,49},{49,1},{2,18}... | collective-permute-start | bytes 2359304 | tf_op jit(solution)/shard_map/ppermute | solution.py:134
  95.7 3.5 %copy-start.1 = (bf16[1024,256]{1,0:T(8,128)(2,1)S(1)}, bf16[1024,256]{1,0:T(8,128)(2,1)}, u32[]{:S(2)}) copy-start(bf16[1024,256]{1,0:T(8,128)(2,1)} %own_ref.3) | copy-start | bytes 1572868
  95.7 3.5 %copy-start.3 = (bf16[512,256]{1,0:T(8,128)(2,1)S(1)}, bf16[512,256]{1,0:T(8,128)(2,1)}, u32[]{:S(2)}) copy-start(bf16[512,256]{1,0:T(8,128)(2,1)} %copy-done.2) | copy-start | bytes 786436
  95.7 3.5 %copy-start.5 = (bf16[512,256]{1,0:T(8,128)(2,1)S(1)}, bf16[512,256]{1,0:T(8,128)(2,1)}, u32[]{:S(2)}) copy-start(bf16[512,256]{1,0:T(8,128)(2,1)} %copy-done.4) | copy-start | bytes 786436
  100.8 36.6 %all-to-all-start.2 = ((bf16[16,24,512]{2,1,0:T(8,128)(2,1)}), bf16[16,24,512]{2,1,0:T(8,128)(2,1)S(1)}, u32[]{:S(2)}, u32[]{:S(2)}) async-start(bf16[16,24,512]{2,1,0:T(8,128)(2,1)} %shard_map.78), calls=%async_computation.2 | async-start | bytes 786432 | tf_op jit(solution)/shard_map/all_to_all | solution.py:22
  113.9 18.4 %collective-permute-start.12 = (bf16[192,1280]{1,0:T(8,128)(2,1)}, bf16[192,1280]{1,0:T(8,128)(2,1)S(1)}, u32[]{:S(2)}, u32[]{:S(2)}) collective-permute-start(bf16[192,1280]{1,0:T(8,128)(2,1)} %get-tuple-element.46), channel_id=1, source_target_pairs={{0,16},{16,32},{32,48},{48,0},{1,17},{17,33},{33,49},{49,1},{2,18}... | collective-permute-start | bytes 1474568 | tf_op jit(solution)/shard_map/ppermute | solution.py:190
  115.8 17.8 %collective-permute-start.13 = (bf16[192,1280]{1,0:T(8,128)(2,1)}, bf16[192,1280]{1,0:T(8,128)(2,1)}, u32[]{:S(2)}, u32[]{:S(2)}) collective-permute-start(bf16[192,1280]{1,0:T(8,128)(2,1)} %get-tuple-element.47), channel_id=1, source_target_pairs={{0,48},{16,0},{32,16},{48,32},{1,49},{17,1},{33,17},{49,33},{2,50}... | collective-permute-start | bytes 1474568 | tf_op jit(solution)/shard_map/ppermute | solution.py:190
  120.9 9.3 %collective-permute-start.14 = (bf16[192,256]{1,0:T(8,128)(2,1)S(1)}, bf16[192,256]{1,0:T(8,128)(2,1)S(1)}, u32[]{:S(2)}, u32[]{:S(2)}) collective-permute-start(bf16[192,256]{1,0:T(8,128)(2,1)S(1)} %slice_bitcast_fusion.2), channel_id=1, source_target_pairs={{0,32},{16,48},{32,0},{48,16},{1,33},{17,49},{33,1},{49,17},{2,34}... | collective-permute-start | bytes 294920 | tf_op jit(solution)/shard_map/ppermute | solution.py:191

commit v13 on v12

--- a/solution.py
+++ b/solution.py
@@ -20,10 +20,6 @@
 
 def exchange(blocks, axis):
     return lax.all_to_all(blocks, axis, split_axis=0, concat_axis=0, tiled=False)
-
-
-def spread(block, axis, n=4):
-    return exchange(jnp.broadcast_to(block[None], (n,) + block.shape), axis)
 
 
 def call(body, outs, scratch, flops, operands, smem=0, moved=None):
@@ -77,6 +73,26 @@
         out_ref[3] = times_transposed(half, before_ref[...])
 
 
+def payload_kernel(mine_ref, theirs_ref, activ_ref, preact_ref, out_ref):
+    for k in range(6):
+        if k < 4:
+            block = (mine_ref[k] + theirs_ref[k]).astype(BF)
+        else:
+            block = activ_ref[...] if k == 4 else preact_ref[...]
+        for y in range(4):
+            out_ref[y, k] = block
+
+
+def slope_kernel(own_ref, out_ref):
+    for d in range(4):
+        hidden = own_ref[0, d].astype(F32)
+        for y in range(1, 4):
+            hidden = hidden + own_ref[y, d].astype(F32)
+        _, slope = gelu_parts(own_ref[d, 5])
+        out_ref[d] = (hidden * slope).astype(BF)
+        out_ref[4 + d] = own_ref[d, 4]
+
+
 def part_kernel(pregrad_ref, own_ref, after_ref, far0_ref, far1_ref, before_ref, out_ref, total, rows):
     total[...] = times_transposed(pregrad_ref[0], own_ref[...])
     total[...] += times_transposed(pregrad_ref[1], after_ref[...])
@@ -90,31 +106,17 @@
         out_ref[z] = rows[z].astype(BF)
 
 
-def pack_kernel(before_ref, after_ref, own_ref, plus_ref, minus_ref):
-    plus_ref[:, :1024] = before_ref[0]
-    plus_ref[:, 1024:] = own_ref[1]
-    minus_ref[:, :1024] = after_ref[1]
-    minus_ref[:, 1024:] = own_ref[3]
-
-
 def times_tokens(a, b):
     return lax.dot_general(a, b, (((0,), (0,)), ((), ())), preferred_element_type=F32)
 
 
-def weights_kernel(x_ref, tokens_ref, after_ref, plus_ref, minus_ref, before_ref, own_ref, two_ref, *outs):
-    up_ref, down_ref = outs
-    up_ref[...] = times_tokens(tokens_ref[1], own_ref[0])
-    up_ref[...] += times_tokens(after_ref[1], minus_ref[:, 1024:])
-    up_ref[...] += times_tokens(minus_ref[:, :1024], two_ref[...])
-    up_ref[...] += times_tokens(before_ref[1], plus_ref[:, 1024:])
-
-    def activ(d):
-        return own_ref[4 + lax.rem(x_ref[0] + d, 4)]
-
-    down_ref[...] = times_tokens(activ(0), tokens_ref[0])
-    down_ref[...] += times_tokens(activ(1), after_ref[0])
-    down_ref[...] += times_tokens(activ(2), plus_ref[:, :1024])
-    down_ref[...] += times_tokens(activ(3), before_ref[0])
+def weights_kernel(x_ref, own_ref, *refs):
+    tokens, pregrad, (up_ref, down_ref) = refs[:4], (own_ref.at[0], *refs[4:7]), refs[7:]
+    for d in range(4):
+        up = times_tokens(tokens[d][1], pregrad[d][...])
+        down = times_tokens(own_ref[4 + lax.rem(x_ref[0] + d, 4)], tokens[d][0])
+        up_ref[...] = up if d == 0 else up_ref[...] + up
+        down_ref[...] = down if d == 0 else down_ref[...] + down
 
 
 def sum_kernel(part_ref, out_ref, rows):
@@ -150,8 +152,7 @@
     before, after = near_x(down_weight)
     far = far_x(before, after)
     up_before, up_after = near_x(up_weight)
-    turned, far_before, far_after = lax.optimization_barrier((turned, up_before, up_after))
-    up_far = far_x(far_before, far_after)
+    up_far = far_x(up_before, up_after)
     both, before, after, far, up_before, up_after = lax.optimization_barrier(
         (both, before, after, far, up_before, up_after)
     )
@@ -165,14 +166,12 @@
         (core[None], both, down_weight, after, *far, before),
         smem=1,
     )
-    theirs, up_far = lax.optimization_barrier((theirs, up_far))
-    pair = (mine + lax.ppermute(theirs, "c", [(0, 1), (1, 0)])).astype(BF)
-    activ, _ = gelu_parts(preact)
-    own = spread(jnp.concatenate([pair, activ.astype(BF)[None], turned[None]]), "y")
-    tok_before, tok_after = near_x(tokens)
-    hidden_grad = sum((own[k, :4].astype(F32) for k in range(1, 4)), own[0, :4].astype(F32))
-    _, slope = gelu_parts(own[:, 5])
-    own = jnp.concatenate([(hidden_grad * slope).astype(BF), own[:, 4]])
+    theirs, turned, up_far = lax.optimization_barrier((theirs, turned, up_far))
+    theirs = lax.ppermute(theirs, "c", [(0, 1), (1, 0)])
+    activ = gelu_parts(preact)[0].astype(BF)
+    (own,) = call(payload_kernel, [jax.ShapeDtypeStruct((4, 6, 96, 256), BF)], [], 0, (mine, theirs, activ, turned))
+    own = exchange(own, "y")
+    (own,) = call(slope_kernel, [jax.ShapeDtypeStruct((8, 96, 256), BF)], [], 0, (own,))
     own = lax.all_gather(own, "c", axis=1, tiled=False).reshape(8, 192, 256)
 
     (part,) = call(
@@ -182,19 +181,16 @@
         2 * 192 * 1024 * 1024,
         (own, up_weight, up_after, *up_far, up_before),
     )
-    _, tok_before, tok_after = lax.optimization_barrier((part, tok_before, tok_after))
     part = exchange(part, ("za", "zb"))
 
-    packed = jax.ShapeDtypeStruct((192, 1280), BF)
-    plus, minus = call(pack_kernel, [packed, packed], [], 0, (tok_before, tok_after, own))
-    plus, minus = lax.ppermute(plus, "x", shift(1)), lax.ppermute(minus, "x", shift(-1))
-    two = lax.ppermute(own[2], "x", shift(2))
+    all_tokens = [tokens] + [lax.ppermute(tokens, "x", shift(k)) for k in (3, 2, 1)]
+    all_pregrad = [lax.ppermute(own[k], "x", shift(k)) for k in (3, 2, 1)]
     up_grad, down_grad = call(
         weights_kernel,
         [jax.ShapeDtypeStruct((1024, 256), F32), jax.ShapeDtypeStruct((256, 1024), F32)],
         [],
-        8 * 4 * 768 * 1024 * 256,
-        (at_x[None], tokens, tok_after, plus, minus, tok_before, own, two),
+        16 * 4 * 768 * 1024 * 256,
+        (at_x[None], own, *all_tokens, *all_pregrad),
         smem=1,
     )
     part, up_grad, down_grad = lax.optimization_barrier((part, up_grad, down_grad))

time: 140 us -> 136 us (0.971)
  waiting for transfers between devices: 34.3 us -> 22.3 us
  starting transfers between devices: 80.4 us -> 87 us
  Pallas kernels: 11.7 us -> 13.5 us
    ppermute x4 -> x7, starting transfers between devices: 10.9 us -> 23.3 us  [the longest x3 10.8 us: local(): all_pregrad = [lax.ppermute(own[k], 'x', shift(k)) for k in (3, 2, 1)]]
    ppermute x4 -> x7, waiting for transfers between devices: 12.3 us -> 3.79 us  [the longest x3 2.92 us: local(): all_pregrad = [lax.ppermute(own[k], 'x', shift(k)) for k in (3, 2, 1)]]
    ppermute x3 -> x2, waiting for transfers between devices: 1.08 us -> 6.75 us  [near_x(): lax.ppermute(block, 'x', shift(1))]
    ppermute x1, waiting for transfers between devices: 6.18 us -> 1.38 us  [local(): turned = lax.ppermute(preact, ('y', 'x'), swap)]
    ppermute x2, waiting for transfers between devices: 4.18 us -> 0.01 us  [far_x(): lax.ppermute(before[:half], 'x', shift(1))]
    ppermute x3 -> x2, starting transfers between devices: 9.51 us -> 5.59 us  [near_x(): lax.ppermute(block, 'x', shift(1))]
    unnamed x18 -> x12, local copies, waits for them, and re-layouts: 1.6 us -> 4.04 us
    ppermute x3 -> x2, starting transfers between devices: 10.4 us -> 8.52 us  [near_x(): lax.ppermute(block, 'x', shift(-1))]
  transfers between devices with their start and end apart: 18 -> 19, of which waited for: 8 -> 8; matrix products, arithmetic and copies ran while one was open for 4% -> 3% of each run, Pallas kernels for 7% -> 7%
where the time goes in v13:
time: 136 us; the launch traced here: 134 us
  starting transfers between devices  87 us (64%)
  waiting for transfers between devices  22.3 us (16%)
  Pallas kernels  13.5 us (10%)
  local copies, waits for them, and re-layouts  6.98 us (5%)
  blocking collectives  2.37 us (2%)
    all_to_all x3, starting transfers between devices, exchange(): lax.all_to_all(blocks, axis, split_axis=0, concat_axis=0, tiled=False)  32.7 us
    pallas_call x7, Pallas kernels, call(): pl.pallas_call(body, out_shape=outs, in_specs=[pl.BlockSpec(memory_space=...  13.5 us
    ppermute x3, starting transfers between devices, local(): all_pregrad = [lax.ppermute(own[k], 'x', shift(k)) for k in (3, 2, 1)]  10.8 us
    ppermute x3, starting transfers between devices, local(): lax.ppermute(tokens, 'x', shift(k))  10.5 us
    all_to_all x3, waiting for transfers between devices, exchange(): lax.all_to_all(blocks, axis, split_axis=0, concat_axis=0, tiled=False)  10.4 us
    ppermute x2, starting transfers between devices, far_x(): lax.ppermute(after[half:], 'x', shift(-1))  9.71 us
    ppermute x2, starting transfers between devices, near_x(): lax.ppermute(block, 'x', shift(-1))  8.52 us
    ppermute x2, waiting for transfers between devices, near_x(): lax.ppermute(block, 'x', shift(1))  6.75 us
  transfers between devices with their start and end apart: 19, of which 8 were waited for; matrix products, arithmetic and copies ran while one was open for 3% of the time, Pallas kernels for 7%

profile of v13, /device:TPU:24, one launch (start us, length us, event | category | flops | bytes accessed | tf_op | source)
XLA Modules:
  0.0 134.0 jit_solution(11262391566493969355)
XLA Ops:
  0.6 0.7 copy-done.2
  1.4 0.8 copy-done.3
  2.1 0.9 shard_map.76
  3.1 15.2 %all-to-all-start = ((bf16[16,48,512]{2,1,0:T(8,128)(2,1)}), bf16[16,48,512]{2,1,0:T(8,128)(2,1)S(1)}, u32[]{:S(2)}, u32[]{:S(2)}) async-start(bf16[16,48,512]{2,1,0:T(8,128)(2,1)} %shard_map.76), calls=%async_computation | async-start | bytes 1572864 | tf_op jit(solution)/shard_map/all_to_all | solution.py:22
  18.3 3.4 %collective-permute-start = (bf16[256,1024]{1,0:T(8,128)(2,1)}, bf16[256,1024]{1,0:T(8,128)(2,1)S(1)}, u32[]{:S(2)}, u32[]{:S(2)}) collective-permute-start(bf16[256,1024]{1,0:T(8,128)(2,1)} %own_ref.2), channel_id=1, source_target_pairs={{0,16},{16,32},{32,48},{48,0},{1,17},{17,33},{33,49},{49,1},{2,18}... | collective-permute-start | bytes 1572872 | tf_op jit(solution)/shard_map/ppermute | solution.py:136
  21.7 3.7 %collective-permute-start.1 = (bf16[256,1024]{1,0:T(8,128)(2,1)}, bf16[256,1024]{1,0:T(8,128)(2,1)S(1)}, u32[]{:S(2)}, u32[]{:S(2)}) collective-permute-start(bf16[256,1024]{1,0:T(8,128)(2,1)} %own_ref.2), channel_id=1, source_target_pairs={{0,48},{16,0},{32,16},{48,32},{1,49},{17,1},{33,17},{49,33},{2,50}... | collective-permute-start | bytes 1572872 | tf_op jit(solution)/shard_map/ppermute | solution.py:136
  25.4 2.2 %collective-permute-start.4 = (bf16[1024,256]{1,0:T(8,128)(2,1)}, bf16[1024,256]{1,0:T(8,128)(2,1)S(1)}, u32[]{:S(2)}, u32[]{:S(2)}) collective-permute-start(bf16[1024,256]{1,0:T(8,128)(2,1)} %own_ref.3), channel_id=1, source_target_pairs={{0,16},{16,32},{32,48},{48,0},{1,17},{17,33},{33,49},{49,1},{2,18}... | collective-permute-start | bytes 1572872 | tf_op jit(solution)/shard_map/ppermute | solution.py:136
  27.6 4.9 %collective-permute-start.5 = (bf16[1024,256]{1,0:T(8,128)(2,1)}, bf16[1024,256]{1,0:T(8,128)(2,1)S(1)}, u32[]{:S(2)}, u32[]{:S(2)}) collective-permute-start(bf16[1024,256]{1,0:T(8,128)(2,1)} %own_ref.3), channel_id=1, source_target_pairs={{0,48},{16,0},{32,16},{48,32},{1,49},{17,1},{33,17},{49,33},{2,50}... | collective-permute-start | bytes 1572872 | tf_op jit(solution)/shard_map/ppermute | solution.py:136
  32.4 4.0 %collective-permute-done.before_ref = bf16[256,1024]{1,0:T(8,128)(2,1)S(1)} collective-permute-done((bf16[256,1024]{1,0:T(8,128)(2,1)}, bf16[256,1024]{1,0:T(8,128)(2,1)S(1)}, u32[]{:S(2)}, u32[]{:S(2)}) %collective-permute-start) | collective-permute-done | bytes 524320 | tf_op jit(solution)/shard_map/ppermute | solution.py:136
  36.5 0.7 slice.34
  37.2 2.2 %collective-permute-start.2 = (bf16[128,1024]{1,0:T(8,128)(2,1)}, bf16[128,1024]{1,0:T(8,128)(2,1)S(1)}, u32[]{:S(2)}, u32[]{:S(2)}) collective-permute-start(bf16[128,1024]{1,0:T(8,128)(2,1)} %slice.34), channel_id=1, source_target_pairs={{0,16},{16,32},{32,48},{48,0},{1,17},{17,33},{33,49},{49,1},{2,18}... | collective-permute-start | bytes 786440 | tf_op jit(solution)/shard_map/ppermute | solution.py:141
  39.4 0.7 slice.35
  40.1 4.9 %collective-permute-start.3 = (bf16[128,1024]{1,0:T(8,128)(2,1)}, bf16[128,1024]{1,0:T(8,128)(2,1)}, u32[]{:S(2)}, u32[]{:S(2)}) collective-permute-start(bf16[128,1024]{1,0:T(8,128)(2,1)} %slice.35), channel_id=1, source_target_pairs={{0,48},{16,0},{32,16},{48,32},{1,49},{17,1},{33,17},{49,33},{2,50}... | collective-permute-start | bytes 786440 | tf_op jit(solution)/shard_map/ppermute | solution.py:141
  45.0 2.7 %collective-permute-done.4.before_ref = bf16[1024,256]{1,0:T(8,128)(2,1)S(1)} collective-permute-done((bf16[1024,256]{1,0:T(8,128)(2,1)}, bf16[1024,256]{1,0:T(8,128)(2,1)S(1)}, u32[]{:S(2)}, u32[]{:S(2)}) %collective-permute-start.4) | collective-permute-done | bytes 524320 | tf_op jit(solution)/shard_map/ppermute | solution.py:136
  47.7 0.7 slice.36
  48.4 2.2 %collective-permute-start.7 = (bf16[512,256]{1,0:T(8,128)(2,1)}, bf16[512,256]{1,0:T(8,128)(2,1)S(1)}, u32[]{:S(2)}, u32[]{:S(2)}) collective-permute-start(bf16[512,256]{1,0:T(8,128)(2,1)} %slice.36), channel_id=1, source_target_pairs={{0,16},{16,32},{32,48},{48,0},{1,17},{17,33},{33,49},{49,1},{2,18}... | collective-permute-start | bytes 786440 | tf_op jit(solution)/shard_map/ppermute | solution.py:141
  50.6 0.7 slice.37
  51.4 4.9 %collective-permute-start.8 = (bf16[512,256]{1,0:T(8,128)(2,1)}, bf16[512,256]{1,0:T(8,128)(2,1)}, u32[]{:S(2)}, u32[]{:S(2)}) collective-permute-start(bf16[512,256]{1,0:T(8,128)(2,1)} %slice.37), channel_id=1, source_target_pairs={{0,48},{16,0},{32,16},{48,32},{1,49},{17,1},{33,17},{49,33},{2,50}... | collective-permute-start | bytes 786440 | tf_op jit(solution)/shard_map/ppermute | solution.py:141
  56.2 2.9 %collective-permute-start.6 = (bf16[96,256]{1,0:T(8,128)(2,1)}, bf16[96,256]{1,0:T(8,128)(2,1)}, u32[]{:S(2)}, u32[]{:S(2)}) collective-permute-start(bf16[96,256]{1,0:T(8,128)(2,1)} %param.7), channel_id=1, source_target_pairs={{0,0},{16,128},{32,256},{48,384},{128,400},{144,16},{160,144},{176... | collective-permute-start | bytes 147464 | tf_op jit(solution)/shard_map/ppermute | solution.py:151
  59.2 0.0 collective-permute-done.2.far0_ref
  59.2 0.0 copy-start
  59.2 0.7 copy-done
  59.9 0.9 copy-done.1
  60.8 2.8 %shard_map.77 = (f32[4,96,256]{2,1,0:T(8,128)S(1)}, f32[4,96,256]{2,1,0:T(8,128)S(1)}, bf16[2,192,1024]{2,1,0:T(8,128)(2,1)S(1)}) custom-call(s32[1]{0:T(128)} %bitcast.core_ref, bf16[16,48,512]{2,1,0:T(8,128)(2,1)S(1)} %all-to-all-done.both_ref, bf16[256,1024]{1,0:T(8,128)(2,1)} %own_ref.2, bf16[256,1024]{1,0:T(8,128)(2,1)S(1)} %collective-permute-done.1.after_ref, ...), custom_call_target="tpu_custom_call" | custom-call | flops 402653184 | bytes 4456452 | tf_op jit(solution)/shard_map/pallas_call | solution.py:29
  63.6 0.0 copy-start.4
  63.6 0.9 copy-done.4
  64.5 1.4 %collective-permute-done.6.preact_ref = bf16[96,256]{1,0:T(8,128)(2,1)} collective-permute-done((bf16[96,256]{1,0:T(8,128)(2,1)}, bf16[96,256]{1,0:T(8,128)(2,1)}, u32[]{:S(2)}, u32[]{:S(2)}) %collective-permute-start.6) | collective-permute-done | bytes 49184 | tf_op jit(solution)/shard_map/ppermute | solution.py:151
  65.9 1.9 %collective-permute-start.9 = (f32[4,96,256]{2,1,0:T(8,128)S(1)}, f32[4,96,256]{2,1,0:T(8,128)S(1)}, u32[]{:S(2)}, u32[]{:S(2)}) collective-permute-start(f32[4,96,256]{2,1,0:T(8,128)S(1)} %get-tuple-element.29), channel_id=1, source_target_pairs={{0,64},{64,0},{1,65},{65,1},{2,66},{66,2},{3,67},{67,3},{4,68},{68... | collective-permute-start | bytes 1179656 | tf_op jit(solution)/shard_map/ppermute | solution.py:170
  67.8 0.8 fusion.3.activ_ref
  68.6 0.9 collective-permute-done.9.theirs_ref
  69.5 1.9 %shard_map.78 = bf16[4,6,96,256]{3,2,1,0:T(8,128)(2,1)} custom-call(f32[4,96,256]{2,1,0:T(8,128)S(1)} %get-tuple-element.27.mine_ref, f32[4,96,256]{2,1,0:T(8,128)S(1)} %collective-permute-done.9.theirs_ref, bf16[96,256]{1,0:T(8,128)(2,1)S(1)} %fusion.3.activ_ref, bf16[96,256]{1,0:T(8,128)(2,1)} %collective-permute-done.6.preact_ref), custom_call_target="tpu_custom_call" | custom-call | bytes 2064384 | tf_op jit(solution)/shard_map/pallas_call | solution.py:29
  71.4 5.4 %all-to-all-start.1 = ((bf16[4,6,96,256]{3,2,1,0:T(8,128)(2,1)}), bf16[4,6,96,256]{3,2,1,0:T(8,128)(2,1)S(1)}, u32[]{:S(2)}, u32[]{:S(2)}) async-start(bf16[4,6,96,256]{3,2,1,0:T(8,128)(2,1)} %shard_map.78), calls=%async_computation.1 | async-start | bytes 2359296 | tf_op jit(solution)/shard_map/all_to_all | solution.py:22
  76.8 1.9 %collective-permute-start.12 = (bf16[2,192,1024]{2,1,0:T(8,128)(2,1)S(1)}, bf16[2,192,1024]{2,1,0:T(8,128)(2,1)}, u32[]{:S(2)}, u32[]{:S(2)}) collective-permute-start(bf16[2,192,1024]{2,1,0:T(8,128)(2,1)S(1)} %copy-done.5), channel_id=1, source_target_pairs={{0,16},{16,32},{32,48},{48,0},{1,17},{17,33},{33,49},{49,1},{2,18}... | collective-permute-start | bytes 2359304 | tf_op jit(solution)/shard_map/ppermute | solution.py:186
  78.8 5.1 %collective-permute-start.11 = (bf16[2,192,1024]{2,1,0:T(8,128)(2,1)S(1)}, bf16[2,192,1024]{2,1,0:T(8,128)(2,1)}, u32[]{:S(2)}, u32[]{:S(2)}) collective-permute-start(bf16[2,192,1024]{2,1,0:T(8,128)(2,1)S(1)} %copy-done.5), channel_id=1, source_target_pairs={{0,32},{16,48},{32,0},{48,16},{1,33},{17,49},{33,1},{49,17},{2,34}... | collective-permute-start | bytes 2359304 | tf_op jit(solution)/shard_map/ppermute | solution.py:186
  83.8 3.5 %collective-permute-start.10 = (bf16[2,192,1024]{2,1,0:T(8,128)(2,1)S(1)}, bf16[2,192,1024]{2,1,0:T(8,128)(2,1)}, u32[]{:S(2)}, u32[]{:S(2)}) collective-permute-start(bf16[2,192,1024]{2,1,0:T(8,128)(2,1)S(1)} %copy-done.5), channel_id=1, source_target_pairs={{0,48},{16,0},{32,16},{48,32},{1,49},{17,1},{33,17},{49,33},{2,50}... | collective-permute-start | bytes 2359304 | tf_op jit(solution)/shard_map/ppermute | solution.py:186
  87.4 4.2 %all-to-all-done.1.own_ref = bf16[4,6,96,256]{3,2,1,0:T(8,128)(2,1)S(1)} async-done(((bf16[4,6,96,256]{3,2,1,0:T(8,128)(2,1)}), bf16[4,6,96,256]{3,2,1,0:T(8,128)(2,1)S(1)}, u32[]{:S(2)}, u32[]{:S(2)}) %all-to-all-start.1) | async-done | bytes 1179680 | tf_op jit(solution)/shard_map/all_to_all | solution.py:22
  91.6 0.3 shard_map.79
  91.8 2.4 %all-gather.pregrad_ref.own_ref = bf16[8,192,256]{2,1,0:T(8,128)(2,1)S(1)} all-gather(bf16[8,96,256]{2,1,0:T(8,128)(2,1)S(1)} %shard_map.79), channel_id=2, replica_groups=mesh['y'=4,'c'=2,'x'=4,'za'=4,'zb'=4] {'c'}, dimensions={1}, use_global_device_ids=true | all-gather | bytes 1179648 | tf_op jit(solution)/shard_map/all_gather | solution.py:175
  94.2 2.7 %shard_map.80 = bf16[16,24,512]{2,1,0:T(8,128)(2,1)} custom-call(bf16[8,192,256]{2,1,0:T(8,128)(2,1)S(1)} %all-gather.pregrad_ref.own_ref, bf16[1024,256]{1,0:T(8,128)(2,1)} %own_ref.3, bf16[1024,256]{1,0:T(8,128)(2,1)S(1)} %collective-permute-done.5.after_ref, bf16[512,256]{1,0:T(8,128)(2,1)S(1)} %collective-permute-done.7.far0_ref, ...), custom_call_target="tpu_custom_call" | custom-call | flops 402653184 | bytes 3276800 | tf_op jit(solution)/shard_map/pallas_call | solution.py:29
  96.9 12.0 %all-to-all-start.2 = ((bf16[16,24,512]{2,1,0:T(8,128)(2,1)}), bf16[16,24,512]{2,1,0:T(8,128)(2,1)S(1)}, u32[]{:S(2)}, u32[]{:S(2)}) async-start(bf16[16,24,512]{2,1,0:T(8,128)(2,1)} %shard_map.80), calls=%async_computation.2 | async-start | bytes 786432 | tf_op jit(solution)/shard_map/all_to_all | solution.py:22
  109.0 1.9 %collective-permute-start.15 = (bf16[192,256]{1,0:T(8,128)(2,1)S(1)}, bf16[192,256]{1,0:T(8,128)(2,1)S(1)}, u32[]{:S(2)}, u32[]{:S(2)}) collective-permute-start(bf16[192,256]{1,0:T(8,128)(2,1)S(1)} %get-tuple-element.41), channel_id=1, source_target_pairs={{0,16},{16,32},{32,48},{48,0},{1,17},{17,33},{33,49},{49,1},{2,18}... | collective-permute-start | bytes 294920 | tf_op jit(solution)/shard_map/ppermute | solution.py:187
  110.9 5.4 %collective-permute-start.14 = (bf16[192,256]{1,0:T(8,128)(2,1)S(1)}, bf16[192,256]{1,0:T(8,128)(2,1)S(1)}, u32[]{:S(2)}, u32[]{:S(2)}) collective-permute-start(bf16[192,256]{1,0:T(8,128)(2,1)S(1)} %get-tuple-element.42), channel_id=1, source_target_pairs={{0,32},{16,48},{32,0},{48,16},{1,33},{17,49},{33,1},{49,17},{2,34}... | collective-permute-start | bytes 294920 | tf_op jit(solution)/shard_map/ppermute | solution.py:187
  116.3 3.5 %collective-permute-start.13 = (bf16[192,256]{1,0:T(8,128)(2,1)S(1)}, bf16[192,256]{1,0:T(8,128)(2,1)S(1)}, u32[]{:S(2)}, u32[]{:S(2)}) collective-permute-start(bf16[192,256]{1,0:T(8,128)(2,1)S(1)} %get-tuple-element.43), channel_id=1, source_target_pairs={{0,48},{16,0},{32,16},{48,32},{1,49},{17,1},{33,17},{49,33},{2,50}... | collective-permute-start | bytes 294920 | tf_op jit(solution)/shard_map/ppermute | solution.py:187
  119.9 0.3 collective-permute-done.14.refs_5_
  120.2 2.6 %collective-permute-done.13.refs_4_ = bf16[192,256]{1,0:T(8,128)(2,1)S(1)} collective-permute-done((bf16[192,256]{1,0:T(8,128)(2,1)S(1)}, bf16[192,256]{1,0:T(8,128)(2,1)S(1)}, u32[]{:S(2)}, u32[]{:S(2)}) %collective-permute-start.13) | collective-permute-done | bytes 98336 | tf_op jit(solution)/shard_map/ppermute | solution.py:187
  122.8 4.2 %shard_map.81 = (f32[1024,256]{1,0:T(8,128)}, f32[256,1024]{1,0:T(8,128)}) custom-call(s32[1]{0:T(128)} %bitcast.1.x_ref, bf16[8,192,256]{2,1,0:T(8,128)(2,1)S(1)} %all-gather.pregrad_ref.own_ref, bf16[2,192,1024]{2,1,0:T(8,128)(2,1)S(1)} %copy-done.5, bf16[2,192,1024]{2,1,0:T(8,128)(2,1)} %collective-permute-done.10.refs_1_, ...), custom_call_target="tpu_custom_call" | custom-call | flops 12884901888 | bytes 6324228 | tf_op jit(solution)/shard_map/pallas_call | solution.py:29
  127.1 6.2 %all-to-all-done.2.part_ref = bf16[16,24,512]{2,1,0:T(8,128)(2,1)S(1)} async-done(((bf16[16,24,512]{2,1,0:T(8,128)(2,1)}), bf16[16,24,512]{2,1,0:T(8,128)(2,1)S(1)}, u32[]{:S(2)}, u32[]{:S(2)}) %all-to-all-start.2) | async-done | bytes 393248 | tf_op jit(solution)/shard_map/all_to_all | solution.py:22
  133.3 0.7 shard_map.82
  (16 shorter events, 0.1 us)
Async XLA Ops:
  0.6 0.8 copy-start.2
  1.4 0.8 copy-start.3
  3.1 56.8 %all-to-all-start = ((bf16[16,48,512]{2,1,0:T(8,128)(2,1)}), bf16[16,48,512]{2,1,0:T(8,128)(2,1)S(1)}, u32[]{:S(2)}, u32[]{:S(2)}) async-start(bf16[16,48,512]{2,1,0:T(8,128)(2,1)} %shard_map.76), calls=%async_computation | async-start | bytes 1572864 | tf_op jit(solution)/shard_map/all_to_all | solution.py:22
  18.3 18.2 %collective-permute-start = (bf16[256,1024]{1,0:T(8,128)(2,1)}, bf16[256,1024]{1,0:T(8,128)(2,1)S(1)}, u32[]{:S(2)}, u32[]{:S(2)}) collective-permute-start(bf16[256,1024]{1,0:T(8,128)(2,1)} %own_ref.2), channel_id=1, source_target_pairs={{0,16},{16,32},{32,48},{48,0},{1,17},{17,33},{33,49},{49,1},{2,18}... | collective-permute-start | bytes 1572872 | tf_op jit(solution)/shard_map/ppermute | solution.py:136
  21.7 17.7 %collective-permute-start.1 = (bf16[256,1024]{1,0:T(8,128)(2,1)}, bf16[256,1024]{1,0:T(8,128)(2,1)S(1)}, u32[]{:S(2)}, u32[]{:S(2)}) collective-permute-start(bf16[256,1024]{1,0:T(8,128)(2,1)} %own_ref.2), channel_id=1, source_target_pairs={{0,48},{16,0},{32,16},{48,32},{1,49},{17,1},{33,17},{49,33},{2,50}... | collective-permute-start | bytes 1572872 | tf_op jit(solution)/shard_map/ppermute | solution.py:136
  25.4 22.3 %collective-permute-start.4 = (bf16[1024,256]{1,0:T(8,128)(2,1)}, bf16[1024,256]{1,0:T(8,128)(2,1)S(1)}, u32[]{:S(2)}, u32[]{:S(2)}) collective-permute-start(bf16[1024,256]{1,0:T(8,128)(2,1)} %own_ref.3), channel_id=1, source_target_pairs={{0,16},{16,32},{32,48},{48,0},{1,17},{17,33},{33,49},{49,1},{2,18}... | collective-permute-start | bytes 1572872 | tf_op jit(solution)/shard_map/ppermute | solution.py:136
  27.6 23.1 %collective-permute-start.5 = (bf16[1024,256]{1,0:T(8,128)(2,1)}, bf16[1024,256]{1,0:T(8,128)(2,1)S(1)}, u32[]{:S(2)}, u32[]{:S(2)}) collective-permute-start(bf16[1024,256]{1,0:T(8,128)(2,1)} %own_ref.3), channel_id=1, source_target_pairs={{0,48},{16,0},{32,16},{48,32},{1,49},{17,1},{33,17},{49,33},{2,50}... | collective-permute-start | bytes 1572872 | tf_op jit(solution)/shard_map/ppermute | solution.py:136
  37.2 22.0 %collective-permute-start.2 = (bf16[128,1024]{1,0:T(8,128)(2,1)}, bf16[128,1024]{1,0:T(8,128)(2,1)S(1)}, u32[]{:S(2)}, u32[]{:S(2)}) collective-permute-start(bf16[128,1024]{1,0:T(8,128)(2,1)} %slice.34), channel_id=1, source_target_pairs={{0,16},{16,32},{32,48},{48,0},{1,17},{17,33},{33,49},{49,1},{2,18}... | collective-permute-start | bytes 786440 | tf_op jit(solution)/shard_map/ppermute | solution.py:141
  40.1 19.8 %collective-permute-start.3 = (bf16[128,1024]{1,0:T(8,128)(2,1)}, bf16[128,1024]{1,0:T(8,128)(2,1)}, u32[]{:S(2)}, u32[]{:S(2)}) collective-permute-start(bf16[128,1024]{1,0:T(8,128)(2,1)} %slice.35), channel_id=1, source_target_pairs={{0,48},{16,0},{32,16},{48,32},{1,49},{17,1},{33,17},{49,33},{2,50}... | collective-permute-start | bytes 786440 | tf_op jit(solution)/shard_map/ppermute | solution.py:141
  48.4 17.4 %collective-permute-start.7 = (bf16[512,256]{1,0:T(8,128)(2,1)}, bf16[512,256]{1,0:T(8,128)(2,1)S(1)}, u32[]{:S(2)}, u32[]{:S(2)}) collective-permute-start(bf16[512,256]{1,0:T(8,128)(2,1)} %slice.36), channel_id=1, source_target_pairs={{0,16},{16,32},{32,48},{48,0},{1,17},{17,33},{33,49},{49,1},{2,18}... | collective-permute-start | bytes 786440 | tf_op jit(solution)/shard_map/ppermute | solution.py:141
  51.4 14.5 %collective-permute-start.8 = (bf16[512,256]{1,0:T(8,128)(2,1)}, bf16[512,256]{1,0:T(8,128)(2,1)}, u32[]{:S(2)}, u32[]{:S(2)}) collective-permute-start(bf16[512,256]{1,0:T(8,128)(2,1)} %slice.37), channel_id=1, source_target_pairs={{0,48},{16,0},{32,16},{48,32},{1,49},{17,1},{33,17},{49,33},{2,50}... | collective-permute-start | bytes 786440 | tf_op jit(solution)/shard_map/ppermute | solution.py:141
  56.2 9.6 %collective-permute-start.6 = (bf16[96,256]{1,0:T(8,128)(2,1)}, bf16[96,256]{1,0:T(8,128)(2,1)}, u32[]{:S(2)}, u32[]{:S(2)}) collective-permute-start(bf16[96,256]{1,0:T(8,128)(2,1)} %param.7), channel_id=1, source_target_pairs={{0,0},{16,128},{32,256},{48,384},{128,400},{144,16},{160,144},{176... | collective-permute-start | bytes 147464 | tf_op jit(solution)/shard_map/ppermute | solution.py:151
  59.2 0.7 copy-start
  59.9 1.0 copy-start.1
  63.6 0.9 copy-start.4
  65.9 3.6 %collective-permute-start.9 = (f32[4,96,256]{2,1,0:T(8,128)S(1)}, f32[4,96,256]{2,1,0:T(8,128)S(1)}, u32[]{:S(2)}, u32[]{:S(2)}) collective-permute-start(f32[4,96,256]{2,1,0:T(8,128)S(1)} %get-tuple-element.29), channel_id=1, source_target_pairs={{0,64},{64,0},{1,65},{65,1},{2,66},{66,2},{3,67},{67,3},{4,68},{68... | collective-permute-start | bytes 1179656 | tf_op jit(solution)/shard_map/ppermute | solution.py:170
  71.4 5.4 %copy-start.5 = (bf16[2,192,1024]{2,1,0:T(8,128)(2,1)S(1)}, bf16[2,192,1024]{2,1,0:T(8,128)(2,1)}, u32[]{:S(2)}) copy-start(bf16[2,192,1024]{2,1,0:T(8,128)(2,1)} %copy-done.4) | copy-start | bytes 2359300
  71.4 20.2 %all-to-all-start.1 = ((bf16[4,6,96,256]{3,2,1,0:T(8,128)(2,1)}), bf16[4,6,96,256]{3,2,1,0:T(8,128)(2,1)S(1)}, u32[]{:S(2)}, u32[]{:S(2)}) async-start(bf16[4,6,96,256]{3,2,1,0:T(8,128)(2,1)} %shard_map.78), calls=%async_computation.1 | async-start | bytes 2359296 | tf_op jit(solution)/shard_map/all_to_all | solution.py:22
  76.8 39.5 %collective-permute-start.12 = (bf16[2,192,1024]{2,1,0:T(8,128)(2,1)S(1)}, bf16[2,192,1024]{2,1,0:T(8,128)(2,1)}, u32[]{:S(2)}, u32[]{:S(2)}) collective-permute-start(bf16[2,192,1024]{2,1,0:T(8,128)(2,1)S(1)} %copy-done.5), channel_id=1, source_target_pairs={{0,16},{16,32},{32,48},{48,0},{1,17},{17,33},{33,49},{49,1},{2,18}... | collective-permute-start | bytes 2359304 | tf_op jit(solution)/shard_map/ppermute | solution.py:186
  78.8 41.1 %collective-permute-start.11 = (bf16[2,192,1024]{2,1,0:T(8,128)(2,1)S(1)}, bf16[2,192,1024]{2,1,0:T(8,128)(2,1)}, u32[]{:S(2)}, u32[]{:S(2)}) collective-permute-start(bf16[2,192,1024]{2,1,0:T(8,128)(2,1)S(1)} %copy-done.5), channel_id=1, source_target_pairs={{0,32},{16,48},{32,0},{48,16},{1,33},{17,49},{33,1},{49,17},{2,34}... | collective-permute-start | bytes 2359304 | tf_op jit(solution)/shard_map/ppermute | solution.py:186
  83.8 36.0 %collective-permute-start.10 = (bf16[2,192,1024]{2,1,0:T(8,128)(2,1)S(1)}, bf16[2,192,1024]{2,1,0:T(8,128)(2,1)}, u32[]{:S(2)}, u32[]{:S(2)}) collective-permute-start(bf16[2,192,1024]{2,1,0:T(8,128)(2,1)S(1)} %copy-done.5), channel_id=1, source_target_pairs={{0,48},{16,0},{32,16},{48,32},{1,49},{17,1},{33,17},{49,33},{2,50}... | collective-permute-start | bytes 2359304 | tf_op jit(solution)/shard_map/ppermute | solution.py:186
  96.9 36.3 %all-to-all-start.2 = ((bf16[16,24,512]{2,1,0:T(8,128)(2,1)}), bf16[16,24,512]{2,1,0:T(8,128)(2,1)S(1)}, u32[]{:S(2)}, u32[]{:S(2)}) async-start(bf16[16,24,512]{2,1,0:T(8,128)(2,1)} %shard_map.80), calls=%async_computation.2 | async-start | bytes 786432 | tf_op jit(solution)/shard_map/all_to_all | solution.py:22
  109.0 10.9 %collective-permute-start.15 = (bf16[192,256]{1,0:T(8,128)(2,1)S(1)}, bf16[192,256]{1,0:T(8,128)(2,1)S(1)}, u32[]{:S(2)}, u32[]{:S(2)}) collective-permute-start(bf16[192,256]{1,0:T(8,128)(2,1)S(1)} %get-tuple-element.41), channel_id=1, source_target_pairs={{0,16},{16,32},{32,48},{48,0},{1,17},{17,33},{33,49},{49,1},{2,18}... | collective-permute-start | bytes 294920 | tf_op jit(solution)/shard_map/ppermute | solution.py:187
  110.9 9.3 %collective-permute-start.14 = (bf16[192,256]{1,0:T(8,128)(2,1)S(1)}, bf16[192,256]{1,0:T(8,128)(2,1)S(1)}, u32[]{:S(2)}, u32[]{:S(2)}) collective-permute-start(bf16[192,256]{1,0:T(8,128)(2,1)S(1)} %get-tuple-element.42), channel_id=1, source_target_pairs={{0,32},{16,48},{32,0},{48,16},{1,33},{17,49},{33,1},{49,17},{2,34}... | collective-permute-start | bytes 294920 | tf_op jit(solution)/shard_map/ppermute | solution.py:187
  116.3 6.5 %collective-permute-start.13 = (bf16[192,256]{1,0:T(8,128)(2,1)S(1)}, bf16[192,256]{1,0:T(8,128)(2,1)S(1)}, u32[]{:S(2)}, u32[]{:S(2)}) collective-permute-start(bf16[192,256]{1,0:T(8,128)(2,1)S(1)} %get-tuple-element.43), channel_id=1, source_target_pairs={{0,48},{16,0},{32,16},{48,32},{1,49},{17,1},{33,17},{49,33},{2,50}... | collective-permute-start | bytes 294920 | tf_op jit(solution)/shard_map/ppermute | solution.py:187

commit v14 on v13

--- a/solution.py
+++ b/solution.py
@@ -22,9 +22,8 @@
     return lax.all_to_all(blocks, axis, split_axis=0, concat_axis=0, tiled=False)
 
 
-def call(body, outs, scratch, flops, operands, smem=0, moved=None):
-    if moved is None:
-        moved = sum(a.size * a.dtype.itemsize for a in (*operands, *outs))
+def call(body, outs, scratch, flops, operands, smem=0):
+    moved = sum(a.size * a.dtype.itemsize for a in (*operands, *outs))
     spaces = [pltpu.SMEM] * smem + [pltpu.VMEM] * (len(operands) - smem)
     return pl.pallas_call(
         body,
@@ -33,7 +32,7 @@
         out_specs=[pl.BlockSpec(memory_space=pltpu.VMEM)] * len(outs),
         scratch_shapes=[pltpu.VMEM(shape, F32) for shape in scratch],
         cost_estimate=pl.CostEstimate(flops=flops, bytes_accessed=moved, transcendentals=0),
-        compiler_params=pltpu.CompilerParams(vmem_limit_bytes=40 * 2**20),
+        compiler_params=pltpu.CompilerParams(vmem_limit_bytes=16 * 2**20),
     )(*operands)
 
 
@@ -73,12 +72,12 @@
         out_ref[3] = times_transposed(half, before_ref[...])
 
 
-def payload_kernel(mine_ref, theirs_ref, activ_ref, preact_ref, out_ref):
+def payload_kernel(mine_ref, theirs_ref, preact_ref, turned_ref, out_ref):
     for k in range(6):
         if k < 4:
             block = (mine_ref[k] + theirs_ref[k]).astype(BF)
         else:
-            block = activ_ref[...] if k == 4 else preact_ref[...]
+            block = gelu_parts(preact_ref[...])[0].astype(BF) if k == 4 else turned_ref[...]
         for y in range(4):
             out_ref[y, k] = block
 
@@ -93,11 +92,10 @@
         out_ref[4 + d] = own_ref[d, 4]
 
 
-def part_kernel(pregrad_ref, own_ref, after_ref, far0_ref, far1_ref, before_ref, out_ref, total, rows):
+def part_kernel(pregrad_ref, own_ref, after_ref, far_ref, before_ref, out_ref, total, rows):
     total[...] = times_transposed(pregrad_ref[0], own_ref[...])
     total[...] += times_transposed(pregrad_ref[1], after_ref[...])
-    total[:, :512] += times_transposed(pregrad_ref[2], far0_ref[...])
-    total[:, 512:] += times_transposed(pregrad_ref[2], far1_ref[...])
+    total[...] += times_transposed(pregrad_ref[2], far_ref[...])
     total[...] += times_transposed(pregrad_ref[3], before_ref[...])
     for z in range(16):
         here = slice(12 * z, 12 * z + 12)
@@ -152,7 +150,7 @@
     before, after = near_x(down_weight)
     far = far_x(before, after)
     up_before, up_after = near_x(up_weight)
-    up_far = far_x(up_before, up_after)
+    up_far = lax.ppermute(up_weight, "x", shift(2))
     both, before, after, far, up_before, up_after = lax.optimization_barrier(
         (both, before, after, far, up_before, up_after)
     )
@@ -168,8 +166,7 @@
     )
     theirs, turned, up_far = lax.optimization_barrier((theirs, turned, up_far))
     theirs = lax.ppermute(theirs, "c", [(0, 1), (1, 0)])
-    activ = gelu_parts(preact)[0].astype(BF)
-    (own,) = call(payload_kernel, [jax.ShapeDtypeStruct((4, 6, 96, 256), BF)], [], 0, (mine, theirs, activ, turned))
+    (own,) = call(payload_kernel, [jax.ShapeDtypeStruct((4, 6, 96, 256), BF)], [], 0, (mine, theirs, preact, turned))
     own = exchange(own, "y")
     (own,) = call(slope_kernel, [jax.ShapeDtypeStruct((8, 96, 256), BF)], [], 0, (own,))
     own = lax.all_gather(own, "c", axis=1, tiled=False).reshape(8, 192, 256)
@@ -179,7 +176,7 @@
         [jax.ShapeDtypeStruct((16, 24, 512), BF)],
         [(192, 1024), (16, 24, 512)],
         2 * 192 * 1024 * 1024,
-        (own, up_weight, up_after, *up_far, up_before),
+        (own, up_weight, up_after, up_far, up_before),
     )
     part = exchange(part, ("za", "zb"))
 

time: 136 us -> 139 us (1.022)
  waiting for transfers between devices: 22.3 us -> 32.8 us
  local copies, waits for them, and re-layouts: 6.98 us -> 3.93 us
  starting transfers between devices: 87 us -> 84.4 us
    ppermute x2, waiting for transfers between devices: 0.01 us -> 15.2 us  [near_x(): lax.ppermute(block, 'x', shift(-1))]
    ppermute x2, waiting for transfers between devices: 6.75 us -> 1.5 us  [near_x(): lax.ppermute(block, 'x', shift(1))]
    ppermute x2 -> x1, starting transfers between devices: 9.71 us -> 4.81 us  [far_x(): lax.ppermute(after[half:], 'x', shift(-1))]
    ppermute x0 -> x1, starting transfers between devices: none -> 3.72 us  [local(): up_far = lax.ppermute(up_weight, 'x', shift(2))]
    ppermute x1, starting transfers between devices: 2.92 us -> 6.52 us  [local(): turned = lax.ppermute(preact, ('y', 'x'), swap)]
    ppermute x2 -> x1, starting transfers between devices: 4.35 us -> 2.22 us  [far_x(): lax.ppermute(before[:half], 'x', shift(1))]
    unnamed x12, local copies, waits for them, and re-layouts: 4.04 us -> 2.46 us
    ppermute x2, starting transfers between devices: 8.52 us -> 7.11 us  [near_x(): lax.ppermute(block, 'x', shift(-1))]
  transfers between devices with their start and end apart: 19 -> 18, of which waited for: 8 -> 8; matrix products, arithmetic and copies ran while one was open for 3% -> 1% of each run, Pallas kernels for 7% -> 7%
where the time goes in v14:
time: 139 us; the launch traced here: 137 us
  starting transfers between devices  84.4 us (61%)
  waiting for transfers between devices  32.8 us (24%)
  Pallas kernels  12.8 us (9%)
  local copies, waits for them, and re-layouts  3.93 us (3%)
  blocking collectives  2.37 us (2%)
    all_to_all x3, starting transfers between devices, exchange(): lax.all_to_all(blocks, axis, split_axis=0, concat_axis=0, tiled=False)  32 us
    ppermute x2, waiting for transfers between devices, near_x(): lax.ppermute(block, 'x', shift(-1))  15.2 us
    pallas_call x7, Pallas kernels, call(): pl.pallas_call(body, out_shape=outs, in_specs=[pl.BlockSpec(memory_space=...  12.8 us
    ppermute x3, starting transfers between devices, local(): lax.ppermute(tokens, 'x', shift(k))  10.2 us
    ppermute x3, starting transfers between devices, local(): all_pregrad = [lax.ppermute(own[k], 'x', shift(k)) for k in (3, 2, 1)]  10.1 us
    all_to_all x3, waiting for transfers between devices, exchange(): lax.all_to_all(blocks, axis, split_axis=0, concat_axis=0, tiled=False)  9.81 us
    ppermute x2, starting transfers between devices, near_x(): lax.ppermute(block, 'x', shift(-1))  7.11 us
    ppermute x1, starting transfers between devices, local(): turned = lax.ppermute(preact, ('y', 'x'), swap)  6.52 us
  transfers between devices with their start and end apart: 18, of which 8 were waited for; matrix products, arithmetic and copies ran while one was open for 1% of the time, Pallas kernels for 7%

profile of v14, /device:TPU:24, one launch (start us, length us, event | category | flops | bytes accessed | tf_op | source)
XLA Modules:
  0.0 137.1 jit_solution(8260670368794579434)
XLA Ops:
  0.7 0.8 copy-done.2
  1.5 0.8 copy-done.3
  2.2 0.9 shard_map.76
  3.2 15.3 %all-to-all-start = ((bf16[16,48,512]{2,1,0:T(8,128)(2,1)}), bf16[16,48,512]{2,1,0:T(8,128)(2,1)S(1)}, u32[]{:S(2)}, u32[]{:S(2)}) async-start(bf16[16,48,512]{2,1,0:T(8,128)(2,1)} %shard_map.76), calls=%async_computation | async-start | bytes 1572864 | tf_op jit(solution)/shard_map/all_to_all | solution.py:22
  18.5 3.4 %collective-permute-start = (bf16[256,1024]{1,0:T(8,128)(2,1)}, bf16[256,1024]{1,0:T(8,128)(2,1)S(1)}, u32[]{:S(2)}, u32[]{:S(2)}) collective-permute-start(bf16[256,1024]{1,0:T(8,128)(2,1)} %own_ref.2), channel_id=1, source_target_pairs={{0,16},{16,32},{32,48},{48,0},{1,17},{17,33},{33,49},{49,1},{2,18}... | collective-permute-start | bytes 1572872 | tf_op jit(solution)/shard_map/ppermute | solution.py:134
  21.9 3.7 %collective-permute-start.1 = (bf16[256,1024]{1,0:T(8,128)(2,1)}, bf16[256,1024]{1,0:T(8,128)(2,1)S(1)}, u32[]{:S(2)}, u32[]{:S(2)}) collective-permute-start(bf16[256,1024]{1,0:T(8,128)(2,1)} %own_ref.2), channel_id=1, source_target_pairs={{0,48},{16,0},{32,16},{48,32},{1,49},{17,1},{33,17},{49,33},{2,50}... | collective-permute-start | bytes 1572872 | tf_op jit(solution)/shard_map/ppermute | solution.py:134
  25.6 3.5 %collective-permute-start.5 = (bf16[1024,256]{1,0:T(8,128)(2,1)S(1)}, bf16[1024,256]{1,0:T(8,128)(2,1)S(1)}, u32[]{:S(2)}, u32[]{:S(2)}) collective-permute-start(bf16[1024,256]{1,0:T(8,128)(2,1)S(1)} %copy-done), channel_id=1, source_target_pairs={{0,48},{16,0},{32,16},{48,32},{1,49},{17,1},{33,17},{49,33},{2,50}... | collective-permute-start | bytes 1572872 | tf_op jit(solution)/shard_map/ppermute | solution.py:134
  29.0 2.4 %collective-permute-start.4 = (bf16[1024,256]{1,0:T(8,128)(2,1)S(1)}, bf16[1024,256]{1,0:T(8,128)(2,1)S(1)}, u32[]{:S(2)}, u32[]{:S(2)}) collective-permute-start(bf16[1024,256]{1,0:T(8,128)(2,1)S(1)} %copy-done), channel_id=1, source_target_pairs={{0,16},{16,32},{32,48},{48,0},{1,17},{17,33},{33,49},{49,1},{2,18}... | collective-permute-start | bytes 1572872 | tf_op jit(solution)/shard_map/ppermute | solution.py:134
  31.4 3.7 %collective-permute-start.7 = (bf16[1024,256]{1,0:T(8,128)(2,1)S(1)}, bf16[1024,256]{1,0:T(8,128)(2,1)}, u32[]{:S(2)}, u32[]{:S(2)}) collective-permute-start(bf16[1024,256]{1,0:T(8,128)(2,1)S(1)} %copy-done), channel_id=1, source_target_pairs={{0,32},{16,48},{32,0},{48,16},{1,33},{17,49},{33,1},{49,17},{2,34}... | collective-permute-start | bytes 1572872 | tf_op jit(solution)/shard_map/ppermute | solution.py:153
  35.2 1.5 %collective-permute-done.before_ref = bf16[256,1024]{1,0:T(8,128)(2,1)S(1)} collective-permute-done((bf16[256,1024]{1,0:T(8,128)(2,1)}, bf16[256,1024]{1,0:T(8,128)(2,1)S(1)}, u32[]{:S(2)}, u32[]{:S(2)}) %collective-permute-start) | collective-permute-done | bytes 524320 | tf_op jit(solution)/shard_map/ppermute | solution.py:134
  36.7 0.7 slice.26
  37.4 2.2 %collective-permute-start.2 = (bf16[128,1024]{1,0:T(8,128)(2,1)}, bf16[128,1024]{1,0:T(8,128)(2,1)}, u32[]{:S(2)}, u32[]{:S(2)}) collective-permute-start(bf16[128,1024]{1,0:T(8,128)(2,1)} %slice.26), channel_id=1, source_target_pairs={{0,16},{16,32},{32,48},{48,0},{1,17},{17,33},{33,49},{49,1},{2,18}... | collective-permute-start | bytes 786440 | tf_op jit(solution)/shard_map/ppermute | solution.py:139
  39.6 0.0 collective-permute-done.1.after_ref
  39.6 0.7 slice.27
  40.4 4.8 %collective-permute-start.3 = (bf16[128,1024]{1,0:T(8,128)(2,1)}, bf16[128,1024]{1,0:T(8,128)(2,1)}, u32[]{:S(2)}, u32[]{:S(2)}) collective-permute-start(bf16[128,1024]{1,0:T(8,128)(2,1)} %slice.27), channel_id=1, source_target_pairs={{0,48},{16,0},{32,16},{48,32},{1,49},{17,1},{33,17},{49,33},{2,50}... | collective-permute-start | bytes 786440 | tf_op jit(solution)/shard_map/ppermute | solution.py:139
  45.2 15.2 %collective-permute-done.5.after_ref = bf16[1024,256]{1,0:T(8,128)(2,1)S(1)} collective-permute-done((bf16[1024,256]{1,0:T(8,128)(2,1)S(1)}, bf16[1024,256]{1,0:T(8,128)(2,1)S(1)}, u32[]{:S(2)}, u32[]{:S(2)}) %collective-permute-start.5) | collective-permute-done | bytes 524320 | tf_op jit(solution)/shard_map/ppermute | solution.py:134
  60.4 6.5 %collective-permute-start.6 = (bf16[96,256]{1,0:T(8,128)(2,1)S(1)}, bf16[96,256]{1,0:T(8,128)(2,1)S(1)}, u32[]{:S(2)}, u32[]{:S(2)}) collective-permute-start(bf16[96,256]{1,0:T(8,128)(2,1)S(1)} %copy-done.1), channel_id=1, source_target_pairs={{0,0},{16,128},{32,256},{48,384},{128,400},{144,16},{160,144},{176... | collective-permute-start | bytes 147464 | tf_op jit(solution)/shard_map/ppermute | solution.py:149
  66.9 0.0 collective-permute-done.4.before_ref
  66.9 0.0 collective-permute-done.2.far0_ref
  66.9 0.0 collective-permute-done.3.far1_ref
  66.9 0.0 all-to-all-done.both_ref
  66.9 2.8 %shard_map.77 = (f32[4,96,256]{2,1,0:T(8,128)S(1)}, f32[4,96,256]{2,1,0:T(8,128)S(1)}, bf16[2,192,1024]{2,1,0:T(8,128)(2,1)S(1)}) custom-call(s32[1]{0:T(128)} %bitcast.core_ref, bf16[16,48,512]{2,1,0:T(8,128)(2,1)S(1)} %all-to-all-done.both_ref, bf16[256,1024]{1,0:T(8,128)(2,1)} %own_ref.2, bf16[256,1024]{1,0:T(8,128)(2,1)S(1)} %collective-permute-done.1.after_ref, ...), custom_call_target="tpu_custom_call" | custom-call | flops 402653184 | bytes 4456452 | tf_op jit(solution)/shard_map/pallas_call | solution.py:28
  69.8 0.0 copy-start.4
  69.8 0.9 copy-done.4
  70.7 0.0 collective-permute-done.6.turned_ref
  70.7 0.0 collective-permute-done.7.far_ref
  70.7 1.9 %collective-permute-start.8 = (f32[4,96,256]{2,1,0:T(8,128)S(1)}, f32[4,96,256]{2,1,0:T(8,128)S(1)}, u32[]{:S(2)}, u32[]{:S(2)}) collective-permute-start(f32[4,96,256]{2,1,0:T(8,128)S(1)} %get-tuple-element.28), channel_id=1, source_target_pairs={{0,64},{64,0},{1,65},{65,1},{2,66},{66,2},{3,67},{67,3},{4,68},{68... | collective-permute-start | bytes 1179656 | tf_op jit(solution)/shard_map/ppermute | solution.py:168
  72.6 1.7 %collective-permute-done.8.theirs_ref = f32[4,96,256]{2,1,0:T(8,128)S(1)} collective-permute-done((f32[4,96,256]{2,1,0:T(8,128)S(1)}, f32[4,96,256]{2,1,0:T(8,128)S(1)}, u32[]{:S(2)}, u32[]{:S(2)}) %collective-permute-start.8) | collective-permute-done | bytes 393248 | tf_op jit(solution)/shard_map/ppermute | solution.py:168
  74.3 1.1 shard_map.78
  75.4 4.6 %all-to-all-start.1 = ((bf16[4,6,96,256]{3,2,1,0:T(8,128)(2,1)}), bf16[4,6,96,256]{3,2,1,0:T(8,128)(2,1)S(1)}, u32[]{:S(2)}, u32[]{:S(2)}) async-start(bf16[4,6,96,256]{3,2,1,0:T(8,128)(2,1)} %shard_map.78), calls=%async_computation.1 | async-start | bytes 2359296 | tf_op jit(solution)/shard_map/all_to_all | solution.py:22
  80.0 2.3 %collective-permute-start.11 = (bf16[2,192,1024]{2,1,0:T(8,128)(2,1)S(1)}, bf16[2,192,1024]{2,1,0:T(8,128)(2,1)}, u32[]{:S(2)}, u32[]{:S(2)}) collective-permute-start(bf16[2,192,1024]{2,1,0:T(8,128)(2,1)S(1)} %copy-done.5), channel_id=1, source_target_pairs={{0,16},{16,32},{32,48},{48,0},{1,17},{17,33},{33,49},{49,1},{2,18}... | collective-permute-start | bytes 2359304 | tf_op jit(solution)/shard_map/ppermute | solution.py:183
  82.3 5.4 %collective-permute-start.10 = (bf16[2,192,1024]{2,1,0:T(8,128)(2,1)S(1)}, bf16[2,192,1024]{2,1,0:T(8,128)(2,1)}, u32[]{:S(2)}, u32[]{:S(2)}) collective-permute-start(bf16[2,192,1024]{2,1,0:T(8,128)(2,1)S(1)} %copy-done.5), channel_id=1, source_target_pairs={{0,32},{16,48},{32,0},{48,16},{1,33},{17,49},{33,1},{49,17},{2,34}... | collective-permute-start | bytes 2359304 | tf_op jit(solution)/shard_map/ppermute | solution.py:183
  87.7 2.6 %collective-permute-start.9 = (bf16[2,192,1024]{2,1,0:T(8,128)(2,1)S(1)}, bf16[2,192,1024]{2,1,0:T(8,128)(2,1)}, u32[]{:S(2)}, u32[]{:S(2)}) collective-permute-start(bf16[2,192,1024]{2,1,0:T(8,128)(2,1)S(1)} %copy-done.5), channel_id=1, source_target_pairs={{0,48},{16,0},{32,16},{48,32},{1,49},{17,1},{33,17},{49,33},{2,50}... | collective-permute-start | bytes 2359304 | tf_op jit(solution)/shard_map/ppermute | solution.py:183
  90.3 4.5 %all-to-all-done.1.own_ref = bf16[4,6,96,256]{3,2,1,0:T(8,128)(2,1)S(1)} async-done(((bf16[4,6,96,256]{3,2,1,0:T(8,128)(2,1)}), bf16[4,6,96,256]{3,2,1,0:T(8,128)(2,1)S(1)}, u32[]{:S(2)}, u32[]{:S(2)}) %all-to-all-start.1) | async-done | bytes 1179680 | tf_op jit(solution)/shard_map/all_to_all | solution.py:22
  94.8 0.3 shard_map.79
  95.0 2.4 %all-gather.pregrad_ref.own_ref = bf16[8,192,256]{2,1,0:T(8,128)(2,1)S(1)} all-gather(bf16[8,96,256]{2,1,0:T(8,128)(2,1)S(1)} %shard_map.79), channel_id=2, replica_groups=mesh['y'=4,'c'=2,'x'=4,'za'=4,'zb'=4] {'c'}, dimensions={1}, use_global_device_ids=true | all-gather | bytes 1179648 | tf_op jit(solution)/shard_map/all_gather | solution.py:172
  97.4 2.7 %shard_map.80 = bf16[16,24,512]{2,1,0:T(8,128)(2,1)} custom-call(bf16[8,192,256]{2,1,0:T(8,128)(2,1)S(1)} %all-gather.pregrad_ref.own_ref, bf16[1024,256]{1,0:T(8,128)(2,1)S(1)} %copy-done, bf16[1024,256]{1,0:T(8,128)(2,1)S(1)} %collective-permute-done.5.after_ref, bf16[1024,256]{1,0:T(8,128)(2,1)} %collective-permute-done.7.far_ref, ...), custom_call_target="tpu_custom_call" | custom-call | flops 402653184 | bytes 3276800 | tf_op jit(solution)/shard_map/pallas_call | solution.py:28
  100.1 12.0 %all-to-all-start.2 = ((bf16[16,24,512]{2,1,0:T(8,128)(2,1)}), bf16[16,24,512]{2,1,0:T(8,128)(2,1)S(1)}, u32[]{:S(2)}, u32[]{:S(2)}) async-start(bf16[16,24,512]{2,1,0:T(8,128)(2,1)} %shard_map.80), calls=%async_computation.2 | async-start | bytes 786432 | tf_op jit(solution)/shard_map/all_to_all | solution.py:22
  112.1 2.3 %collective-permute-start.14 = (bf16[192,256]{1,0:T(8,128)(2,1)S(1)}, bf16[192,256]{1,0:T(8,128)(2,1)S(1)}, u32[]{:S(2)}, u32[]{:S(2)}) collective-permute-start(bf16[192,256]{1,0:T(8,128)(2,1)S(1)} %get-tuple-element.39), channel_id=1, source_target_pairs={{0,16},{16,32},{32,48},{48,0},{1,17},{17,33},{33,49},{49,1},{2,18}... | collective-permute-start | bytes 294920 | tf_op jit(solution)/shard_map/ppermute | solution.py:184
  114.4 5.9 %collective-permute-start.13 = (bf16[192,256]{1,0:T(8,128)(2,1)S(1)}, bf16[192,256]{1,0:T(8,128)(2,1)S(1)}, u32[]{:S(2)}, u32[]{:S(2)}) collective-permute-start(bf16[192,256]{1,0:T(8,128)(2,1)S(1)} %get-tuple-element.40), channel_id=1, source_target_pairs={{0,32},{16,48},{32,0},{48,16},{1,33},{17,49},{33,1},{49,17},{2,34}... | collective-permute-start | bytes 294920 | tf_op jit(solution)/shard_map/ppermute | solution.py:184
  120.3 1.9 %collective-permute-start.12 = (bf16[192,256]{1,0:T(8,128)(2,1)S(1)}, bf16[192,256]{1,0:T(8,128)(2,1)S(1)}, u32[]{:S(2)}, u32[]{:S(2)}) collective-permute-start(bf16[192,256]{1,0:T(8,128)(2,1)S(1)} %get-tuple-element.41), channel_id=1, source_target_pairs={{0,48},{16,0},{32,16},{48,32},{1,49},{17,1},{33,17},{49,33},{2,50}... | collective-permute-start | bytes 294920 | tf_op jit(solution)/shard_map/ppermute | solution.py:184
  122.3 0.4 collective-permute-done.9.refs_1_
  122.7 0.0 collective-permute-done.14.refs_6_
  122.7 1.1 collective-permute-done.13.refs_5_
  123.8 3.0 %collective-permute-done.12.refs_4_ = bf16[192,256]{1,0:T(8,128)(2,1)S(1)} collective-permute-done((bf16[192,256]{1,0:T(8,128)(2,1)S(1)}, bf16[192,256]{1,0:T(8,128)(2,1)S(1)}, u32[]{:S(2)}, u32[]{:S(2)}) %collective-permute-start.12) | collective-permute-done | bytes 98336 | tf_op jit(solution)/shard_map/ppermute | solution.py:184
  126.8 4.2 %shard_map.81 = (f32[1024,256]{1,0:T(8,128)}, f32[256,1024]{1,0:T(8,128)}) custom-call(s32[1]{0:T(128)} %bitcast.1.x_ref, bf16[8,192,256]{2,1,0:T(8,128)(2,1)S(1)} %all-gather.pregrad_ref.own_ref, bf16[2,192,1024]{2,1,0:T(8,128)(2,1)S(1)} %copy-done.5, bf16[2,192,1024]{2,1,0:T(8,128)(2,1)} %collective-permute-done.9.refs_1_, ...), custom_call_target="tpu_custom_call" | custom-call | flops 12884901888 | bytes 6324228 | tf_op jit(solution)/shard_map/pallas_call | solution.py:28
  131.1 5.3 %all-to-all-done.2.part_ref = bf16[16,24,512]{2,1,0:T(8,128)(2,1)S(1)} async-done(((bf16[16,24,512]{2,1,0:T(8,128)(2,1)}), bf16[16,24,512]{2,1,0:T(8,128)(2,1)S(1)}, u32[]{:S(2)}, u32[]{:S(2)}) %all-to-all-start.2) | async-done | bytes 393248 | tf_op jit(solution)/shard_map/all_to_all | solution.py:22
  136.4 0.7 shard_map.82
  (11 shorter events, 0.0 us)
Async XLA Ops:
  0.6 24.9 %copy-start = (bf16[1024,256]{1,0:T(8,128)(2,1)S(1)}, bf16[1024,256]{1,0:T(8,128)(2,1)}, u32[]{:S(2)}) copy-start(bf16[1024,256]{1,0:T(8,128)(2,1)} %own_ref.3) | copy-start | bytes 1572868
  0.6 0.8 copy-start.2
  1.5 0.8 copy-start.3
  3.2 57.2 %copy-start.1 = (bf16[96,256]{1,0:T(8,128)(2,1)S(1)}, bf16[96,256]{1,0:T(8,128)(2,1)}, u32[]{:S(2)}) copy-start(bf16[96,256]{1,0:T(8,128)(2,1)} %preact_ref.1) | copy-start | bytes 147460
  3.2 63.8 %all-to-all-start = ((bf16[16,48,512]{2,1,0:T(8,128)(2,1)}), bf16[16,48,512]{2,1,0:T(8,128)(2,1)S(1)}, u32[]{:S(2)}, u32[]{:S(2)}) async-start(bf16[16,48,512]{2,1,0:T(8,128)(2,1)} %shard_map.76), calls=%async_computation | async-start | bytes 1572864 | tf_op jit(solution)/shard_map/all_to_all | solution.py:22
  18.5 18.2 %collective-permute-start = (bf16[256,1024]{1,0:T(8,128)(2,1)}, bf16[256,1024]{1,0:T(8,128)(2,1)S(1)}, u32[]{:S(2)}, u32[]{:S(2)}) collective-permute-start(bf16[256,1024]{1,0:T(8,128)(2,1)} %own_ref.2), channel_id=1, source_target_pairs={{0,16},{16,32},{32,48},{48,0},{1,17},{17,33},{33,49},{49,1},{2,18}... | collective-permute-start | bytes 1572872 | tf_op jit(solution)/shard_map/ppermute | solution.py:134
  21.9 17.7 %collective-permute-start.1 = (bf16[256,1024]{1,0:T(8,128)(2,1)}, bf16[256,1024]{1,0:T(8,128)(2,1)S(1)}, u32[]{:S(2)}, u32[]{:S(2)}) collective-permute-start(bf16[256,1024]{1,0:T(8,128)(2,1)} %own_ref.2), channel_id=1, source_target_pairs={{0,48},{16,0},{32,16},{48,32},{1,49},{17,1},{33,17},{49,33},{2,50}... | collective-permute-start | bytes 1572872 | tf_op jit(solution)/shard_map/ppermute | solution.py:134
  25.6 34.8 %collective-permute-start.5 = (bf16[1024,256]{1,0:T(8,128)(2,1)S(1)}, bf16[1024,256]{1,0:T(8,128)(2,1)S(1)}, u32[]{:S(2)}, u32[]{:S(2)}) collective-permute-start(bf16[1024,256]{1,0:T(8,128)(2,1)S(1)} %copy-done), channel_id=1, source_target_pairs={{0,48},{16,0},{32,16},{48,32},{1,49},{17,1},{33,17},{49,33},{2,50}... | collective-permute-start | bytes 1572872 | tf_op jit(solution)/shard_map/ppermute | solution.py:134
  29.0 37.8 %collective-permute-start.4 = (bf16[1024,256]{1,0:T(8,128)(2,1)S(1)}, bf16[1024,256]{1,0:T(8,128)(2,1)S(1)}, u32[]{:S(2)}, u32[]{:S(2)}) collective-permute-start(bf16[1024,256]{1,0:T(8,128)(2,1)S(1)} %copy-done), channel_id=1, source_target_pairs={{0,16},{16,32},{32,48},{48,0},{1,17},{17,33},{33,49},{49,1},{2,18}... | collective-permute-start | bytes 1572872 | tf_op jit(solution)/shard_map/ppermute | solution.py:134
  31.4 39.2 %collective-permute-start.7 = (bf16[1024,256]{1,0:T(8,128)(2,1)S(1)}, bf16[1024,256]{1,0:T(8,128)(2,1)}, u32[]{:S(2)}, u32[]{:S(2)}) collective-permute-start(bf16[1024,256]{1,0:T(8,128)(2,1)S(1)} %copy-done), channel_id=1, source_target_pairs={{0,32},{16,48},{32,0},{48,16},{1,33},{17,49},{33,1},{49,17},{2,34}... | collective-permute-start | bytes 1572872 | tf_op jit(solution)/shard_map/ppermute | solution.py:153
  37.4 29.5 %collective-permute-start.2 = (bf16[128,1024]{1,0:T(8,128)(2,1)}, bf16[128,1024]{1,0:T(8,128)(2,1)}, u32[]{:S(2)}, u32[]{:S(2)}) collective-permute-start(bf16[128,1024]{1,0:T(8,128)(2,1)} %slice.26), channel_id=1, source_target_pairs={{0,16},{16,32},{32,48},{48,0},{1,17},{17,33},{33,49},{49,1},{2,18}... | collective-permute-start | bytes 786440 | tf_op jit(solution)/shard_map/ppermute | solution.py:139
  40.4 26.6 %collective-permute-start.3 = (bf16[128,1024]{1,0:T(8,128)(2,1)}, bf16[128,1024]{1,0:T(8,128)(2,1)}, u32[]{:S(2)}, u32[]{:S(2)}) collective-permute-start(bf16[128,1024]{1,0:T(8,128)(2,1)} %slice.27), channel_id=1, source_target_pairs={{0,48},{16,0},{32,16},{48,32},{1,49},{17,1},{33,17},{49,33},{2,50}... | collective-permute-start | bytes 786440 | tf_op jit(solution)/shard_map/ppermute | solution.py:139
  60.4 10.3 %collective-permute-start.6 = (bf16[96,256]{1,0:T(8,128)(2,1)S(1)}, bf16[96,256]{1,0:T(8,128)(2,1)S(1)}, u32[]{:S(2)}, u32[]{:S(2)}) collective-permute-start(bf16[96,256]{1,0:T(8,128)(2,1)S(1)} %copy-done.1), channel_id=1, source_target_pairs={{0,0},{16,128},{32,256},{48,384},{128,400},{144,16},{160,144},{176... | collective-permute-start | bytes 147464 | tf_op jit(solution)/shard_map/ppermute | solution.py:149
  69.8 0.9 copy-start.4
  70.7 3.6 %collective-permute-start.8 = (f32[4,96,256]{2,1,0:T(8,128)S(1)}, f32[4,96,256]{2,1,0:T(8,128)S(1)}, u32[]{:S(2)}, u32[]{:S(2)}) collective-permute-start(f32[4,96,256]{2,1,0:T(8,128)S(1)} %get-tuple-element.28), channel_id=1, source_target_pairs={{0,64},{64,0},{1,65},{65,1},{2,66},{66,2},{3,67},{67,3},{4,68},{68... | collective-permute-start | bytes 1179656 | tf_op jit(solution)/shard_map/ppermute | solution.py:168
  75.4 4.6 %copy-start.5 = (bf16[2,192,1024]{2,1,0:T(8,128)(2,1)S(1)}, bf16[2,192,1024]{2,1,0:T(8,128)(2,1)}, u32[]{:S(2)}) copy-start(bf16[2,192,1024]{2,1,0:T(8,128)(2,1)} %copy-done.4) | copy-start | bytes 2359300
  75.4 19.4 %all-to-all-start.1 = ((bf16[4,6,96,256]{3,2,1,0:T(8,128)(2,1)}), bf16[4,6,96,256]{3,2,1,0:T(8,128)(2,1)S(1)}, u32[]{:S(2)}, u32[]{:S(2)}) async-start(bf16[4,6,96,256]{3,2,1,0:T(8,128)(2,1)} %shard_map.78), calls=%async_computation.1 | async-start | bytes 2359296 | tf_op jit(solution)/shard_map/all_to_all | solution.py:22
  80.0 40.3 %collective-permute-start.11 = (bf16[2,192,1024]{2,1,0:T(8,128)(2,1)S(1)}, bf16[2,192,1024]{2,1,0:T(8,128)(2,1)}, u32[]{:S(2)}, u32[]{:S(2)}) collective-permute-start(bf16[2,192,1024]{2,1,0:T(8,128)(2,1)S(1)} %copy-done.5), channel_id=1, source_target_pairs={{0,16},{16,32},{32,48},{48,0},{1,17},{17,33},{33,49},{49,1},{2,18}... | collective-permute-start | bytes 2359304 | tf_op jit(solution)/shard_map/ppermute | solution.py:183
  82.3 40.0 %collective-permute-start.10 = (bf16[2,192,1024]{2,1,0:T(8,128)(2,1)S(1)}, bf16[2,192,1024]{2,1,0:T(8,128)(2,1)}, u32[]{:S(2)}, u32[]{:S(2)}) collective-permute-start(bf16[2,192,1024]{2,1,0:T(8,128)(2,1)S(1)} %copy-done.5), channel_id=1, source_target_pairs={{0,32},{16,48},{32,0},{48,16},{1,33},{17,49},{33,1},{49,17},{2,34}... | collective-permute-start | bytes 2359304 | tf_op jit(solution)/shard_map/ppermute | solution.py:183
  87.7 35.0 %collective-permute-start.9 = (bf16[2,192,1024]{2,1,0:T(8,128)(2,1)S(1)}, bf16[2,192,1024]{2,1,0:T(8,128)(2,1)}, u32[]{:S(2)}, u32[]{:S(2)}) collective-permute-start(bf16[2,192,1024]{2,1,0:T(8,128)(2,1)S(1)} %copy-done.5), channel_id=1, source_target_pairs={{0,48},{16,0},{32,16},{48,32},{1,49},{17,1},{33,17},{49,33},{2,50}... | collective-permute-start | bytes 2359304 | tf_op jit(solution)/shard_map/ppermute | solution.py:183
  100.1 36.3 %all-to-all-start.2 = ((bf16[16,24,512]{2,1,0:T(8,128)(2,1)}), bf16[16,24,512]{2,1,0:T(8,128)(2,1)S(1)}, u32[]{:S(2)}, u32[]{:S(2)}) async-start(bf16[16,24,512]{2,1,0:T(8,128)(2,1)} %shard_map.80), calls=%async_computation.2 | async-start | bytes 786432 | tf_op jit(solution)/shard_map/all_to_all | solution.py:22
  112.1 10.6 %collective-permute-start.14 = (bf16[192,256]{1,0:T(8,128)(2,1)S(1)}, bf16[192,256]{1,0:T(8,128)(2,1)S(1)}, u32[]{:S(2)}, u32[]{:S(2)}) collective-permute-start(bf16[192,256]{1,0:T(8,128)(2,1)S(1)} %get-tuple-element.39), channel_id=1, source_target_pairs={{0,16},{16,32},{32,48},{48,0},{1,17},{17,33},{33,49},{49,1},{2,18}... | collective-permute-start | bytes 294920 | tf_op jit(solution)/shard_map/ppermute | solution.py:184
  114.4 9.4 %collective-permute-start.13 = (bf16[192,256]{1,0:T(8,128)(2,1)S(1)}, bf16[192,256]{1,0:T(8,128)(2,1)S(1)}, u32[]{:S(2)}, u32[]{:S(2)}) collective-permute-start(bf16[192,256]{1,0:T(8,128)(2,1)S(1)} %get-tuple-element.40), channel_id=1, source_target_pairs={{0,32},{16,48},{32,0},{48,16},{1,33},{17,49},{33,1},{49,17},{2,34}... | collective-permute-start | bytes 294920 | tf_op jit(solution)/shard_map/ppermute | solution.py:184
  120.3 6.5 %collective-permute-start.12 = (bf16[192,256]{1,0:T(8,128)(2,1)S(1)}, bf16[192,256]{1,0:T(8,128)(2,1)S(1)}, u32[]{:S(2)}, u32[]{:S(2)}) collective-permute-start(bf16[192,256]{1,0:T(8,128)(2,1)S(1)} %get-tuple-element.41), channel_id=1, source_target_pairs={{0,48},{16,0},{32,16},{48,32},{1,49},{17,1},{33,17},{49,33},{2,50}... | collective-permute-start | bytes 294920 | tf_op jit(solution)/shard_map/ppermute | solution.py:184

commit v15 on v14

--- a/solution.py
+++ b/solution.py
@@ -50,17 +50,23 @@
         out_ref[z] = block
 
 
-def hidden_kernel(core_ref, both_ref, own_ref, after_ref, far0_ref, far1_ref, before_ref, *refs):
-    mine_ref, theirs_ref, tokens_ref, rows, grads, ins = refs
+def put_back(both_ref, start, rows, tokens):
     for z in range(16):
         rows[z] = both_ref[z].astype(F32)
         here = slice(12 * z, 12 * z + 12)
-        grads[here, :512] = rows[z, 0:12]
-        grads[here, 512:] = rows[z, 12:24]
-        ins[here, :512] = rows[z, 24:36]
-        ins[here, 512:] = rows[z, 36:48]
-    tokens_ref[0] = grads[...].astype(BF)
-    tokens_ref[1] = ins[...].astype(BF)
+        tokens[here, :512] = rows[z, start : start + 12]
+        tokens[here, 512:] = rows[z, start + 12 : start + 24]
+
+
+def tokens_kernel(both_ref, tokens_ref, rows, tokens):
+    for k in range(2):
+        put_back(both_ref, 24 * k, rows, tokens)
+        tokens_ref[k] = tokens[...].astype(BF)
+
+
+def hidden_kernel(core_ref, both_ref, own_ref, after_ref, far0_ref, far1_ref, before_ref, *refs):
+    mine_ref, theirs_ref, rows, grads = refs
+    put_back(both_ref, 0, rows, grads)
     first = pl.multiple_of(core_ref[0] * 96, 96)
     second = pl.multiple_of(96 - core_ref[0] * 96, 96)
     for start, out_ref in ((second, theirs_ref), (first, mine_ref)):
@@ -92,10 +98,11 @@
         out_ref[4 + d] = own_ref[d, 4]
 
 
-def part_kernel(pregrad_ref, own_ref, after_ref, far_ref, before_ref, out_ref, total, rows):
+def part_kernel(pregrad_ref, own_ref, after_ref, far0_ref, far1_ref, before_ref, out_ref, total, rows):
     total[...] = times_transposed(pregrad_ref[0], own_ref[...])
     total[...] += times_transposed(pregrad_ref[1], after_ref[...])
-    total[...] += times_transposed(pregrad_ref[2], far_ref[...])
+    total[:, :512] += times_transposed(pregrad_ref[2], far0_ref[...])
+    total[:, 512:] += times_transposed(pregrad_ref[2], far1_ref[...])
     total[...] += times_transposed(pregrad_ref[3], before_ref[...])
     for z in range(16):
         here = slice(12 * z, 12 * z + 12)
@@ -150,16 +157,16 @@
     before, after = near_x(down_weight)
     far = far_x(before, after)
     up_before, up_after = near_x(up_weight)
-    up_far = lax.ppermute(up_weight, "x", shift(2))
+    up_far = far_x(up_before, up_after)
     both, before, after, far, up_before, up_after = lax.optimization_barrier(
         (both, before, after, far, up_before, up_after)
     )
 
     half = jax.ShapeDtypeStruct((4, 96, 256), F32)
-    mine, theirs, tokens = call(
+    mine, theirs = call(
         hidden_kernel,
-        [half, half, jax.ShapeDtypeStruct((2, 192, 1024), BF)],
-        [(16, 48, 512), (192, 1024), (192, 1024)],
+        [half, half],
+        [(16, 48, 512), (192, 1024)],
         2 * 192 * 1024 * 1024,
         (core[None], both, down_weight, after, *far, before),
         smem=1,
@@ -176,10 +183,12 @@
         [jax.ShapeDtypeStruct((16, 24, 512), BF)],
         [(192, 1024), (16, 24, 512)],
         2 * 192 * 1024 * 1024,
-        (own, up_weight, up_after, up_far, up_before),
+        (own, up_weight, up_after, *up_far, up_before),
     )
     part = exchange(part, ("za", "zb"))
 
+    tokens = jax.ShapeDtypeStruct((2, 192, 1024), BF)
+    (tokens,) = call(tokens_kernel, [tokens], [(16, 48, 512), (192, 1024)], 0, (both,))
     all_tokens = [tokens] + [lax.ppermute(tokens, "x", shift(k)) for k in (3, 2, 1)]
     all_pregrad = [lax.ppermute(own[k], "x", shift(k)) for k in (3, 2, 1)]
     up_grad, down_grad = call(

time: 139 us -> 135 us (0.971)
  waiting for transfers between devices: 32.8 us -> 29.5 us
  starting transfers between devices: 84.4 us -> 81.6 us
    ppermute x2, waiting for transfers between devices: 15.2 us -> 0.01 us  [near_x(): lax.ppermute(block, 'x', shift(-1))]
    ppermute x3, waiting for transfers between devices: 0.43 us -> 6.48 us  [local(): lax.ppermute(tokens, 'x', shift(k))]
    ppermute x2, waiting for transfers between devices: 1.5 us -> 6.73 us  [near_x(): lax.ppermute(block, 'x', shift(1))]
    ppermute x1 -> x2, starting transfers between devices: 4.81 us -> 9.71 us  [far_x(): lax.ppermute(after[half:], 'x', shift(-1))]
    ppermute x1, waiting for transfers between devices: 0.01 us -> 3.73 us  [local(): turned = lax.ppermute(preact, ('y', 'x'), swap)]
    ppermute x1 -> x0, starting transfers between devices: 3.72 us -> none  [local(): up_far = lax.ppermute(up_weight, 'x', shift(2))]
    ppermute x1, starting transfers between devices: 6.52 us -> 2.92 us  [local(): turned = lax.ppermute(preact, ('y', 'x'), swap)]
    all_to_all x3, waiting for transfers between devices: 9.81 us -> 6.31 us  [exchange(): lax.all_to_all(blocks, axis, split_axis=0, concat_axis=0, tiled=False)]
  transfers between devices with their start and end apart: 18 -> 19, of which waited for: 8 -> 8; matrix products, arithmetic and copies ran while one was open for 1% -> 2% of each run, Pallas kernels for 7% -> 8%
where the time goes in v15:
time: 135 us; the launch traced here: 133 us
  starting transfers between devices  81.6 us (60%)
  waiting for transfers between devices  29.5 us (22%)
  Pallas kernels  14 us (10%)
  local copies, waits for them, and re-layouts  4.51 us (3%)
  blocking collectives  2.37 us (2%)
    all_to_all x3, starting transfers between devices, exchange(): lax.all_to_all(blocks, axis, split_axis=0, concat_axis=0, tiled=False)  32.6 us
    pallas_call x8, Pallas kernels, call(): pl.pallas_call(body, out_shape=outs, in_specs=[pl.BlockSpec(memory_space=...  14 us
    ppermute x2, starting transfers between devices, far_x(): lax.ppermute(after[half:], 'x', shift(-1))  9.71 us
    ppermute x3, starting transfers between devices, local(): lax.ppermute(tokens, 'x', shift(k))  8.96 us
    ppermute x2, starting transfers between devices, near_x(): lax.ppermute(block, 'x', shift(-1))  8.52 us
    ppermute x3, starting transfers between devices, local(): all_pregrad = [lax.ppermute(own[k], 'x', shift(k)) for k in (3, 2, 1)]  6.95 us
    ppermute x2, waiting for transfers between devices, near_x(): lax.ppermute(block, 'x', shift(1))  6.73 us
    ppermute x3, waiting for transfers between devices, local(): lax.ppermute(tokens, 'x', shift(k))  6.48 us
  transfers between devices with their start and end apart: 19, of which 8 were waited for; matrix products, arithmetic and copies ran while one was open for 2% of the time, Pallas kernels for 8%

profile of v15, /device:TPU:24, one launch (start us, length us, event | category | flops | bytes accessed | tf_op | source)
XLA Modules:
  0.0 132.8 jit_solution(14816865640236904706)
XLA Ops:
  0.7 0.8 copy-done.2
  1.5 0.8 copy-done.3
  2.2 0.9 shard_map.76
  3.2 15.2 %all-to-all-start = ((bf16[16,48,512]{2,1,0:T(8,128)(2,1)}), bf16[16,48,512]{2,1,0:T(8,128)(2,1)S(1)}, u32[]{:S(2)}, u32[]{:S(2)}) async-start(bf16[16,48,512]{2,1,0:T(8,128)(2,1)} %shard_map.76), calls=%async_computation | async-start | bytes 1572864 | tf_op jit(solution)/shard_map/all_to_all | solution.py:22
  18.4 0.0 copy-start.1
  18.4 3.5 %collective-permute-start = (bf16[256,1024]{1,0:T(8,128)(2,1)}, bf16[256,1024]{1,0:T(8,128)(2,1)S(1)}, u32[]{:S(2)}, u32[]{:S(2)}) collective-permute-start(bf16[256,1024]{1,0:T(8,128)(2,1)} %own_ref.2), channel_id=1, source_target_pairs={{0,16},{16,32},{32,48},{48,0},{1,17},{17,33},{33,49},{49,1},{2,18}... | collective-permute-start | bytes 1572872 | tf_op jit(solution)/shard_map/ppermute | solution.py:141
  21.9 3.7 %collective-permute-start.1 = (bf16[256,1024]{1,0:T(8,128)(2,1)}, bf16[256,1024]{1,0:T(8,128)(2,1)S(1)}, u32[]{:S(2)}, u32[]{:S(2)}) collective-permute-start(bf16[256,1024]{1,0:T(8,128)(2,1)} %own_ref.2), channel_id=1, source_target_pairs={{0,48},{16,0},{32,16},{48,32},{1,49},{17,1},{33,17},{49,33},{2,50}... | collective-permute-start | bytes 1572872 | tf_op jit(solution)/shard_map/ppermute | solution.py:141
  25.6 2.2 %collective-permute-start.4 = (bf16[1024,256]{1,0:T(8,128)(2,1)S(1)}, bf16[1024,256]{1,0:T(8,128)(2,1)S(1)}, u32[]{:S(2)}, u32[]{:S(2)}) collective-permute-start(bf16[1024,256]{1,0:T(8,128)(2,1)S(1)} %copy-done), channel_id=1, source_target_pairs={{0,16},{16,32},{32,48},{48,0},{1,17},{17,33},{33,49},{49,1},{2,18}... | collective-permute-start | bytes 1572872 | tf_op jit(solution)/shard_map/ppermute | solution.py:141
  27.8 4.9 %collective-permute-start.5 = (bf16[1024,256]{1,0:T(8,128)(2,1)S(1)}, bf16[1024,256]{1,0:T(8,128)(2,1)S(1)}, u32[]{:S(2)}, u32[]{:S(2)}) collective-permute-start(bf16[1024,256]{1,0:T(8,128)(2,1)S(1)} %copy-done), channel_id=1, source_target_pairs={{0,48},{16,0},{32,16},{48,32},{1,49},{17,1},{33,17},{49,33},{2,50}... | collective-permute-start | bytes 1572872 | tf_op jit(solution)/shard_map/ppermute | solution.py:141
  32.7 4.0 %collective-permute-done.before_ref = bf16[256,1024]{1,0:T(8,128)(2,1)S(1)} collective-permute-done((bf16[256,1024]{1,0:T(8,128)(2,1)}, bf16[256,1024]{1,0:T(8,128)(2,1)S(1)}, u32[]{:S(2)}, u32[]{:S(2)}) %collective-permute-start) | collective-permute-done | bytes 524320 | tf_op jit(solution)/shard_map/ppermute | solution.py:141
  36.7 0.7 slice.34
  37.4 2.2 %collective-permute-start.2 = (bf16[128,1024]{1,0:T(8,128)(2,1)}, bf16[128,1024]{1,0:T(8,128)(2,1)}, u32[]{:S(2)}, u32[]{:S(2)}) collective-permute-start(bf16[128,1024]{1,0:T(8,128)(2,1)} %slice.34), channel_id=1, source_target_pairs={{0,16},{16,32},{32,48},{48,0},{1,17},{17,33},{33,49},{49,1},{2,18}... | collective-permute-start | bytes 786440 | tf_op jit(solution)/shard_map/ppermute | solution.py:146
  39.6 0.7 slice.35
  40.3 4.9 %collective-permute-start.3 = (bf16[128,1024]{1,0:T(8,128)(2,1)}, bf16[128,1024]{1,0:T(8,128)(2,1)}, u32[]{:S(2)}, u32[]{:S(2)}) collective-permute-start(bf16[128,1024]{1,0:T(8,128)(2,1)} %slice.35), channel_id=1, source_target_pairs={{0,48},{16,0},{32,16},{48,32},{1,49},{17,1},{33,17},{49,33},{2,50}... | collective-permute-start | bytes 786440 | tf_op jit(solution)/shard_map/ppermute | solution.py:146
  45.2 2.7 %collective-permute-done.4.before_ref = bf16[1024,256]{1,0:T(8,128)(2,1)S(1)} collective-permute-done((bf16[1024,256]{1,0:T(8,128)(2,1)S(1)}, bf16[1024,256]{1,0:T(8,128)(2,1)S(1)}, u32[]{:S(2)}, u32[]{:S(2)}) %collective-permute-start.4) | collective-permute-done | bytes 524320 | tf_op jit(solution)/shard_map/ppermute | solution.py:141
  47.9 0.7 slice.36
  48.6 2.2 %collective-permute-start.7 = (bf16[512,256]{1,0:T(8,128)(2,1)}, bf16[512,256]{1,0:T(8,128)(2,1)}, u32[]{:S(2)}, u32[]{:S(2)}) collective-permute-start(bf16[512,256]{1,0:T(8,128)(2,1)} %slice.36), channel_id=1, source_target_pairs={{0,16},{16,32},{32,48},{48,0},{1,17},{17,33},{33,49},{49,1},{2,18}... | collective-permute-start | bytes 786440 | tf_op jit(solution)/shard_map/ppermute | solution.py:146
  50.8 0.0 collective-permute-done.5.after_ref
  50.8 0.7 slice.37
  51.6 4.9 %collective-permute-start.8 = (bf16[512,256]{1,0:T(8,128)(2,1)}, bf16[512,256]{1,0:T(8,128)(2,1)}, u32[]{:S(2)}, u32[]{:S(2)}) collective-permute-start(bf16[512,256]{1,0:T(8,128)(2,1)} %slice.37), channel_id=1, source_target_pairs={{0,48},{16,0},{32,16},{48,32},{1,49},{17,1},{33,17},{49,33},{2,50}... | collective-permute-start | bytes 786440 | tf_op jit(solution)/shard_map/ppermute | solution.py:146
  56.4 2.9 %collective-permute-start.6 = (bf16[96,256]{1,0:T(8,128)(2,1)S(1)}, bf16[96,256]{1,0:T(8,128)(2,1)S(1)}, u32[]{:S(2)}, u32[]{:S(2)}) collective-permute-start(bf16[96,256]{1,0:T(8,128)(2,1)S(1)} %copy-done.1), channel_id=1, source_target_pairs={{0,0},{16,128},{32,256},{48,384},{128,400},{144,16},{160,144},{176... | collective-permute-start | bytes 147464 | tf_op jit(solution)/shard_map/ppermute | solution.py:156
  59.4 0.0 collective-permute-done.2.far0_ref
  59.4 0.0 collective-permute-done.3.far1_ref
  59.4 2.6 %shard_map.77 = (f32[4,96,256]{2,1,0:T(8,128)S(1)}, f32[4,96,256]{2,1,0:T(8,128)S(1)}) custom-call(s32[1]{0:T(128)} %bitcast.core_ref, bf16[16,48,512]{2,1,0:T(8,128)(2,1)S(1)} %all-to-all-done.both_ref, bf16[256,1024]{1,0:T(8,128)(2,1)} %own_ref.2, bf16[256,1024]{1,0:T(8,128)(2,1)S(1)} %collective-permute-done.1.after_ref, ...), custom_call_target="tpu_custom_call" | custom-call | flops 402653184 | bytes 3670020 | tf_op jit(solution)/shard_map/pallas_call | solution.py:28
  62.0 3.7 %collective-permute-done.6.turned_ref = bf16[96,256]{1,0:T(8,128)(2,1)S(1)} collective-permute-done((bf16[96,256]{1,0:T(8,128)(2,1)S(1)}, bf16[96,256]{1,0:T(8,128)(2,1)S(1)}, u32[]{:S(2)}, u32[]{:S(2)}) %collective-permute-start.6) | collective-permute-done | bytes 49184 | tf_op jit(solution)/shard_map/ppermute | solution.py:156
  65.7 0.0 collective-permute-done.7.far0_ref
  65.7 0.0 collective-permute-done.8.far1_ref
  65.8 1.9 %collective-permute-start.9 = (f32[4,96,256]{2,1,0:T(8,128)S(1)}, f32[4,96,256]{2,1,0:T(8,128)S(1)}, u32[]{:S(2)}, u32[]{:S(2)}) collective-permute-start(f32[4,96,256]{2,1,0:T(8,128)S(1)} %get-tuple-element.28), channel_id=1, source_target_pairs={{0,64},{64,0},{1,65},{65,1},{2,66},{66,2},{3,67},{67,3},{4,68},{68... | collective-permute-start | bytes 1179656 | tf_op jit(solution)/shard_map/ppermute | solution.py:175
  67.7 1.7 %collective-permute-done.9.theirs_ref = f32[4,96,256]{2,1,0:T(8,128)S(1)} collective-permute-done((f32[4,96,256]{2,1,0:T(8,128)S(1)}, f32[4,96,256]{2,1,0:T(8,128)S(1)}, u32[]{:S(2)}, u32[]{:S(2)}) %collective-permute-start.9) | collective-permute-done | bytes 393248 | tf_op jit(solution)/shard_map/ppermute | solution.py:175
  69.4 1.1 shard_map.78
  70.5 5.3 %all-to-all-start.1 = ((bf16[4,6,96,256]{3,2,1,0:T(8,128)(2,1)}), bf16[4,6,96,256]{3,2,1,0:T(8,128)(2,1)S(1)}, u32[]{:S(2)}, u32[]{:S(2)}) async-start(bf16[4,6,96,256]{3,2,1,0:T(8,128)(2,1)} %shard_map.78), calls=%async_computation.1 | async-start | bytes 2359296 | tf_op jit(solution)/shard_map/all_to_all | solution.py:22
  75.8 1.2 shard_map.81.refs_0_
  77.0 1.9 %collective-permute-start.12 = (bf16[2,192,1024]{2,1,0:T(8,128)(2,1)}, bf16[2,192,1024]{2,1,0:T(8,128)(2,1)}, u32[]{:S(2)}, u32[]{:S(2)}) collective-permute-start(bf16[2,192,1024]{2,1,0:T(8,128)(2,1)} %shard_map.81.refs_0_), channel_id=1, source_target_pairs={{0,16},{16,32},{32,48},{48,0},{1,17},{17,33},{33,49},{49,1},{2,18}... | collective-permute-start | bytes 2359304 | tf_op jit(solution)/shard_map/ppermute | solution.py:192
  78.9 2.7 %collective-permute-start.11 = (bf16[2,192,1024]{2,1,0:T(8,128)(2,1)}, bf16[2,192,1024]{2,1,0:T(8,128)(2,1)}, u32[]{:S(2)}, u32[]{:S(2)}) collective-permute-start(bf16[2,192,1024]{2,1,0:T(8,128)(2,1)} %shard_map.81.refs_0_), channel_id=1, source_target_pairs={{0,32},{16,48},{32,0},{48,16},{1,33},{17,49},{33,1},{49,17},{2,34}... | collective-permute-start | bytes 2359304 | tf_op jit(solution)/shard_map/ppermute | solution.py:192
  81.7 4.3 %collective-permute-start.10 = (bf16[2,192,1024]{2,1,0:T(8,128)(2,1)}, bf16[2,192,1024]{2,1,0:T(8,128)(2,1)}, u32[]{:S(2)}, u32[]{:S(2)}) collective-permute-start(bf16[2,192,1024]{2,1,0:T(8,128)(2,1)} %shard_map.81.refs_0_), channel_id=1, source_target_pairs={{0,48},{16,0},{32,16},{48,32},{1,49},{17,1},{33,17},{49,33},{2,50}... | collective-permute-start | bytes 2359304 | tf_op jit(solution)/shard_map/ppermute | solution.py:192
  86.0 4.6 %all-to-all-done.1.own_ref = bf16[4,6,96,256]{3,2,1,0:T(8,128)(2,1)S(1)} async-done(((bf16[4,6,96,256]{3,2,1,0:T(8,128)(2,1)}), bf16[4,6,96,256]{3,2,1,0:T(8,128)(2,1)S(1)}, u32[]{:S(2)}, u32[]{:S(2)}) %all-to-all-start.1) | async-done | bytes 1179680 | tf_op jit(solution)/shard_map/all_to_all | solution.py:22
  90.5 0.3 shard_map.79
  90.8 2.4 %all-gather.pregrad_ref.own_ref = bf16[8,192,256]{2,1,0:T(8,128)(2,1)S(1)} all-gather(bf16[8,96,256]{2,1,0:T(8,128)(2,1)S(1)} %shard_map.79), channel_id=2, replica_groups=mesh['y'=4,'c'=2,'x'=4,'za'=4,'zb'=4] {'c'}, dimensions={1}, use_global_device_ids=true | all-gather | bytes 1179648 | tf_op jit(solution)/shard_map/all_gather | solution.py:179
  93.2 2.6 %shard_map.80 = bf16[16,24,512]{2,1,0:T(8,128)(2,1)} custom-call(bf16[8,192,256]{2,1,0:T(8,128)(2,1)S(1)} %all-gather.pregrad_ref.own_ref, bf16[1024,256]{1,0:T(8,128)(2,1)S(1)} %copy-done, bf16[1024,256]{1,0:T(8,128)(2,1)S(1)} %collective-permute-done.5.after_ref, bf16[512,256]{1,0:T(8,128)(2,1)} %collective-permute-done.7.far0_ref, ...), custom_call_target="tpu_custom_call" | custom-call | flops 402653184 | bytes 3276800 | tf_op jit(solution)/shard_map/pallas_call | solution.py:28
  95.8 12.0 %all-to-all-start.2 = ((bf16[16,24,512]{2,1,0:T(8,128)(2,1)}), bf16[16,24,512]{2,1,0:T(8,128)(2,1)S(1)}, u32[]{:S(2)}, u32[]{:S(2)}) async-start(bf16[16,24,512]{2,1,0:T(8,128)(2,1)} %shard_map.80), calls=%async_computation.2 | async-start | bytes 786432 | tf_op jit(solution)/shard_map/all_to_all | solution.py:22
  107.9 1.9 %collective-permute-start.15 = (bf16[192,256]{1,0:T(8,128)(2,1)S(1)}, bf16[192,256]{1,0:T(8,128)(2,1)S(1)}, u32[]{:S(2)}, u32[]{:S(2)}) collective-permute-start(bf16[192,256]{1,0:T(8,128)(2,1)S(1)} %get-tuple-element.39), channel_id=1, source_target_pairs={{0,16},{16,32},{32,48},{48,0},{1,17},{17,33},{33,49},{49,1},{2,18}... | collective-permute-start | bytes 294920 | tf_op jit(solution)/shard_map/ppermute | solution.py:193
  109.8 3.1 %collective-permute-start.14 = (bf16[192,256]{1,0:T(8,128)(2,1)S(1)}, bf16[192,256]{1,0:T(8,128)(2,1)S(1)}, u32[]{:S(2)}, u32[]{:S(2)}) collective-permute-start(bf16[192,256]{1,0:T(8,128)(2,1)S(1)} %get-tuple-element.40), channel_id=1, source_target_pairs={{0,32},{16,48},{32,0},{48,16},{1,33},{17,49},{33,1},{49,17},{2,34}... | collective-permute-start | bytes 294920 | tf_op jit(solution)/shard_map/ppermute | solution.py:193
  113.0 6.5 %collective-permute-done.12.refs_3_ = bf16[2,192,1024]{2,1,0:T(8,128)(2,1)} collective-permute-done((bf16[2,192,1024]{2,1,0:T(8,128)(2,1)}, bf16[2,192,1024]{2,1,0:T(8,128)(2,1)}, u32[]{:S(2)}, u32[]{:S(2)}) %collective-permute-start.12) | collective-permute-done | bytes 786464 | tf_op jit(solution)/shard_map/ppermute | solution.py:192
  119.4 1.9 %collective-permute-start.13 = (bf16[192,256]{1,0:T(8,128)(2,1)S(1)}, bf16[192,256]{1,0:T(8,128)(2,1)S(1)}, u32[]{:S(2)}, u32[]{:S(2)}) collective-permute-start(bf16[192,256]{1,0:T(8,128)(2,1)S(1)} %get-tuple-element.41), channel_id=1, source_target_pairs={{0,48},{16,0},{32,16},{48,32},{1,49},{17,1},{33,17},{49,33},{2,50}... | collective-permute-start | bytes 294920 | tf_op jit(solution)/shard_map/ppermute | solution.py:193
  121.4 4.5 %collective-permute-done.13.refs_4_ = bf16[192,256]{1,0:T(8,128)(2,1)S(1)} collective-permute-done((bf16[192,256]{1,0:T(8,128)(2,1)S(1)}, bf16[192,256]{1,0:T(8,128)(2,1)S(1)}, u32[]{:S(2)}, u32[]{:S(2)}) %collective-permute-start.13) | collective-permute-done | bytes 98336 | tf_op jit(solution)/shard_map/ppermute | solution.py:193
  125.9 4.5 %shard_map.82 = (f32[1024,256]{1,0:T(8,128)}, f32[256,1024]{1,0:T(8,128)}) custom-call(s32[1]{0:T(128)} %bitcast.1.x_ref, bf16[8,192,256]{2,1,0:T(8,128)(2,1)S(1)} %all-gather.pregrad_ref.own_ref, bf16[2,192,1024]{2,1,0:T(8,128)(2,1)} %shard_map.81.refs_0_, bf16[2,192,1024]{2,1,0:T(8,128)(2,1)} %collective-permute-done.10.refs_1_, ...), custom_call_target="tpu_custom_call" | custom-call | flops 12884901888 | bytes 6324228 | tf_op jit(solution)/shard_map/pallas_call | solution.py:28
  130.4 1.7 %all-to-all-done.2.part_ref = bf16[16,24,512]{2,1,0:T(8,128)(2,1)S(1)} async-done(((bf16[16,24,512]{2,1,0:T(8,128)(2,1)}), bf16[16,24,512]{2,1,0:T(8,128)(2,1)S(1)}, u32[]{:S(2)}, u32[]{:S(2)}) %all-to-all-start.2) | async-done | bytes 393248 | tf_op jit(solution)/shard_map/all_to_all | solution.py:22
  132.2 0.7 shard_map.83
  (12 shorter events, 0.0 us)
Async XLA Ops:
  0.6 25.0 %copy-start = (bf16[1024,256]{1,0:T(8,128)(2,1)S(1)}, bf16[1024,256]{1,0:T(8,128)(2,1)}, u32[]{:S(2)}) copy-start(bf16[1024,256]{1,0:T(8,128)(2,1)} %own_ref.3) | copy-start | bytes 1572868
  0.6 0.8 copy-start.2
  1.5 0.8 copy-start.3
  3.2 56.2 %all-to-all-start = ((bf16[16,48,512]{2,1,0:T(8,128)(2,1)}), bf16[16,48,512]{2,1,0:T(8,128)(2,1)S(1)}, u32[]{:S(2)}, u32[]{:S(2)}) async-start(bf16[16,48,512]{2,1,0:T(8,128)(2,1)} %shard_map.76), calls=%async_computation | async-start | bytes 1572864 | tf_op jit(solution)/shard_map/all_to_all | solution.py:22
  18.4 38.1 %copy-start.1 = (bf16[96,256]{1,0:T(8,128)(2,1)S(1)}, bf16[96,256]{1,0:T(8,128)(2,1)}, u32[]{:S(2)}) copy-start(bf16[96,256]{1,0:T(8,128)(2,1)} %preact_ref.1) | copy-start | bytes 147460
  18.4 18.3 %collective-permute-start = (bf16[256,1024]{1,0:T(8,128)(2,1)}, bf16[256,1024]{1,0:T(8,128)(2,1)S(1)}, u32[]{:S(2)}, u32[]{:S(2)}) collective-permute-start(bf16[256,1024]{1,0:T(8,128)(2,1)} %own_ref.2), channel_id=1, source_target_pairs={{0,16},{16,32},{32,48},{48,0},{1,17},{17,33},{33,49},{49,1},{2,18}... | collective-permute-start | bytes 1572872 | tf_op jit(solution)/shard_map/ppermute | solution.py:141
  21.9 17.7 %collective-permute-start.1 = (bf16[256,1024]{1,0:T(8,128)(2,1)}, bf16[256,1024]{1,0:T(8,128)(2,1)S(1)}, u32[]{:S(2)}, u32[]{:S(2)}) collective-permute-start(bf16[256,1024]{1,0:T(8,128)(2,1)} %own_ref.2), channel_id=1, source_target_pairs={{0,48},{16,0},{32,16},{48,32},{1,49},{17,1},{33,17},{49,33},{2,50}... | collective-permute-start | bytes 1572872 | tf_op jit(solution)/shard_map/ppermute | solution.py:141
  25.6 22.3 %collective-permute-start.4 = (bf16[1024,256]{1,0:T(8,128)(2,1)S(1)}, bf16[1024,256]{1,0:T(8,128)(2,1)S(1)}, u32[]{:S(2)}, u32[]{:S(2)}) collective-permute-start(bf16[1024,256]{1,0:T(8,128)(2,1)S(1)} %copy-done), channel_id=1, source_target_pairs={{0,16},{16,32},{32,48},{48,0},{1,17},{17,33},{33,49},{49,1},{2,18}... | collective-permute-start | bytes 1572872 | tf_op jit(solution)/shard_map/ppermute | solution.py:141
  27.8 23.0 %collective-permute-start.5 = (bf16[1024,256]{1,0:T(8,128)(2,1)S(1)}, bf16[1024,256]{1,0:T(8,128)(2,1)S(1)}, u32[]{:S(2)}, u32[]{:S(2)}) collective-permute-start(bf16[1024,256]{1,0:T(8,128)(2,1)S(1)} %copy-done), channel_id=1, source_target_pairs={{0,48},{16,0},{32,16},{48,32},{1,49},{17,1},{33,17},{49,33},{2,50}... | collective-permute-start | bytes 1572872 | tf_op jit(solution)/shard_map/ppermute | solution.py:141
  37.4 22.0 %collective-permute-start.2 = (bf16[128,1024]{1,0:T(8,128)(2,1)}, bf16[128,1024]{1,0:T(8,128)(2,1)}, u32[]{:S(2)}, u32[]{:S(2)}) collective-permute-start(bf16[128,1024]{1,0:T(8,128)(2,1)} %slice.34), channel_id=1, source_target_pairs={{0,16},{16,32},{32,48},{48,0},{1,17},{17,33},{33,49},{49,1},{2,18}... | collective-permute-start | bytes 786440 | tf_op jit(solution)/shard_map/ppermute | solution.py:146
  40.3 19.0 %collective-permute-start.3 = (bf16[128,1024]{1,0:T(8,128)(2,1)}, bf16[128,1024]{1,0:T(8,128)(2,1)}, u32[]{:S(2)}, u32[]{:S(2)}) collective-permute-start(bf16[128,1024]{1,0:T(8,128)(2,1)} %slice.35), channel_id=1, source_target_pairs={{0,48},{16,0},{32,16},{48,32},{1,49},{17,1},{33,17},{49,33},{2,50}... | collective-permute-start | bytes 786440 | tf_op jit(solution)/shard_map/ppermute | solution.py:146
  48.6 17.1 %collective-permute-start.7 = (bf16[512,256]{1,0:T(8,128)(2,1)}, bf16[512,256]{1,0:T(8,128)(2,1)}, u32[]{:S(2)}, u32[]{:S(2)}) collective-permute-start(bf16[512,256]{1,0:T(8,128)(2,1)} %slice.36), channel_id=1, source_target_pairs={{0,16},{16,32},{32,48},{48,0},{1,17},{17,33},{33,49},{49,1},{2,18}... | collective-permute-start | bytes 786440 | tf_op jit(solution)/shard_map/ppermute | solution.py:146
  51.6 14.2 %collective-permute-start.8 = (bf16[512,256]{1,0:T(8,128)(2,1)}, bf16[512,256]{1,0:T(8,128)(2,1)}, u32[]{:S(2)}, u32[]{:S(2)}) collective-permute-start(bf16[512,256]{1,0:T(8,128)(2,1)} %slice.37), channel_id=1, source_target_pairs={{0,48},{16,0},{32,16},{48,32},{1,49},{17,1},{33,17},{49,33},{2,50}... | collective-permute-start | bytes 786440 | tf_op jit(solution)/shard_map/ppermute | solution.py:146
  56.4 9.3 %collective-permute-start.6 = (bf16[96,256]{1,0:T(8,128)(2,1)S(1)}, bf16[96,256]{1,0:T(8,128)(2,1)S(1)}, u32[]{:S(2)}, u32[]{:S(2)}) collective-permute-start(bf16[96,256]{1,0:T(8,128)(2,1)S(1)} %copy-done.1), channel_id=1, source_target_pairs={{0,0},{16,128},{32,256},{48,384},{128,400},{144,16},{160,144},{176... | collective-permute-start | bytes 147464 | tf_op jit(solution)/shard_map/ppermute | solution.py:156
  65.8 3.6 %collective-permute-start.9 = (f32[4,96,256]{2,1,0:T(8,128)S(1)}, f32[4,96,256]{2,1,0:T(8,128)S(1)}, u32[]{:S(2)}, u32[]{:S(2)}) collective-permute-start(f32[4,96,256]{2,1,0:T(8,128)S(1)} %get-tuple-element.28), channel_id=1, source_target_pairs={{0,64},{64,0},{1,65},{65,1},{2,66},{66,2},{3,67},{67,3},{4,68},{68... | collective-permute-start | bytes 1179656 | tf_op jit(solution)/shard_map/ppermute | solution.py:175
  70.5 20.0 %all-to-all-start.1 = ((bf16[4,6,96,256]{3,2,1,0:T(8,128)(2,1)}), bf16[4,6,96,256]{3,2,1,0:T(8,128)(2,1)S(1)}, u32[]{:S(2)}, u32[]{:S(2)}) async-start(bf16[4,6,96,256]{3,2,1,0:T(8,128)(2,1)} %shard_map.78), calls=%async_computation.1 | async-start | bytes 2359296 | tf_op jit(solution)/shard_map/all_to_all | solution.py:22
  77.0 42.4 %collective-permute-start.12 = (bf16[2,192,1024]{2,1,0:T(8,128)(2,1)}, bf16[2,192,1024]{2,1,0:T(8,128)(2,1)}, u32[]{:S(2)}, u32[]{:S(2)}) collective-permute-start(bf16[2,192,1024]{2,1,0:T(8,128)(2,1)} %shard_map.81.refs_0_), channel_id=1, source_target_pairs={{0,16},{16,32},{32,48},{48,0},{1,17},{17,33},{33,49},{49,1},{2,18}... | collective-permute-start | bytes 2359304 | tf_op jit(solution)/shard_map/ppermute | solution.py:192
  78.9 42.5 %collective-permute-start.11 = (bf16[2,192,1024]{2,1,0:T(8,128)(2,1)}, bf16[2,192,1024]{2,1,0:T(8,128)(2,1)}, u32[]{:S(2)}, u32[]{:S(2)}) collective-permute-start(bf16[2,192,1024]{2,1,0:T(8,128)(2,1)} %shard_map.81.refs_0_), channel_id=1, source_target_pairs={{0,32},{16,48},{32,0},{48,16},{1,33},{17,49},{33,1},{49,17},{2,34}... | collective-permute-start | bytes 2359304 | tf_op jit(solution)/shard_map/ppermute | solution.py:192
  81.7 39.7 %collective-permute-start.10 = (bf16[2,192,1024]{2,1,0:T(8,128)(2,1)}, bf16[2,192,1024]{2,1,0:T(8,128)(2,1)}, u32[]{:S(2)}, u32[]{:S(2)}) collective-permute-start(bf16[2,192,1024]{2,1,0:T(8,128)(2,1)} %shard_map.81.refs_0_), channel_id=1, source_target_pairs={{0,48},{16,0},{32,16},{48,32},{1,49},{17,1},{33,17},{49,33},{2,50}... | collective-permute-start | bytes 2359304 | tf_op jit(solution)/shard_map/ppermute | solution.py:192
  95.8 36.3 %all-to-all-start.2 = ((bf16[16,24,512]{2,1,0:T(8,128)(2,1)}), bf16[16,24,512]{2,1,0:T(8,128)(2,1)S(1)}, u32[]{:S(2)}, u32[]{:S(2)}) async-start(bf16[16,24,512]{2,1,0:T(8,128)(2,1)} %shard_map.80), calls=%async_computation.2 | async-start | bytes 786432 | tf_op jit(solution)/shard_map/all_to_all | solution.py:22
  107.9 13.5 %collective-permute-start.15 = (bf16[192,256]{1,0:T(8,128)(2,1)S(1)}, bf16[192,256]{1,0:T(8,128)(2,1)S(1)}, u32[]{:S(2)}, u32[]{:S(2)}) collective-permute-start(bf16[192,256]{1,0:T(8,128)(2,1)S(1)} %get-tuple-element.39), channel_id=1, source_target_pairs={{0,16},{16,32},{32,48},{48,0},{1,17},{17,33},{33,49},{49,1},{2,18}... | collective-permute-start | bytes 294920 | tf_op jit(solution)/shard_map/ppermute | solution.py:193
  109.8 11.6 %collective-permute-start.14 = (bf16[192,256]{1,0:T(8,128)(2,1)S(1)}, bf16[192,256]{1,0:T(8,128)(2,1)S(1)}, u32[]{:S(2)}, u32[]{:S(2)}) collective-permute-start(bf16[192,256]{1,0:T(8,128)(2,1)S(1)} %get-tuple-element.40), channel_id=1, source_target_pairs={{0,32},{16,48},{32,0},{48,16},{1,33},{17,49},{33,1},{49,17},{2,34}... | collective-permute-start | bytes 294920 | tf_op jit(solution)/shard_map/ppermute | solution.py:193
  119.4 6.5 %collective-permute-start.13 = (bf16[192,256]{1,0:T(8,128)(2,1)S(1)}, bf16[192,256]{1,0:T(8,128)(2,1)S(1)}, u32[]{:S(2)}, u32[]{:S(2)}) collective-permute-start(bf16[192,256]{1,0:T(8,128)(2,1)S(1)} %get-tuple-element.41), channel_id=1, source_target_pairs={{0,48},{16,0},{32,16},{48,32},{1,49},{17,1},{33,17},{49,33},{2,50}... | collective-permute-start | bytes 294920 | tf_op jit(solution)/shard_map/ppermute | solution.py:193

commit v16 on v15

--- a/solution.py
+++ b/solution.py
@@ -64,7 +64,7 @@
         tokens_ref[k] = tokens[...].astype(BF)
 
 
-def hidden_kernel(core_ref, both_ref, own_ref, after_ref, far0_ref, far1_ref, before_ref, *refs):
+def hidden_kernel(core_ref, both_ref, own_ref, after_ref, far_ref, before_ref, *refs):
     mine_ref, theirs_ref, rows, grads = refs
     put_back(both_ref, 0, rows, grads)
     first = pl.multiple_of(core_ref[0] * 96, 96)
@@ -73,17 +73,13 @@
         half = grads[pl.ds(start, 96)].astype(BF)
         out_ref[0] = times_transposed(half, own_ref[...])
         out_ref[1] = times_transposed(half, after_ref[...])
-        out_ref[2, :, :128] = times_transposed(half, far0_ref[...])
-        out_ref[2, :, 128:] = times_transposed(half, far1_ref[...])
+        out_ref[2] = times_transposed(half, far_ref[...])
         out_ref[3] = times_transposed(half, before_ref[...])
 
 
-def payload_kernel(mine_ref, theirs_ref, preact_ref, turned_ref, out_ref):
-    for k in range(6):
-        if k < 4:
-            block = (mine_ref[k] + theirs_ref[k]).astype(BF)
-        else:
-            block = gelu_parts(preact_ref[...])[0].astype(BF) if k == 4 else turned_ref[...]
+def payload_kernel(mine_ref, theirs_ref, turned_ref, out_ref):
+    for k in range(5):
+        block = (mine_ref[k] + theirs_ref[k]).astype(BF) if k < 4 else turned_ref[...]
         for y in range(4):
             out_ref[y, k] = block
 
@@ -93,17 +89,16 @@
         hidden = own_ref[0, d].astype(F32)
         for y in range(1, 4):
             hidden = hidden + own_ref[y, d].astype(F32)
-        _, slope = gelu_parts(own_ref[d, 5])
-        out_ref[d] = (hidden * slope).astype(BF)
-        out_ref[4 + d] = own_ref[d, 4]
-
-
-def part_kernel(pregrad_ref, own_ref, after_ref, far0_ref, far1_ref, before_ref, out_ref, total, rows):
-    total[...] = times_transposed(pregrad_ref[0], own_ref[...])
-    total[...] += times_transposed(pregrad_ref[1], after_ref[...])
-    total[:, :512] += times_transposed(pregrad_ref[2], far0_ref[...])
-    total[:, 512:] += times_transposed(pregrad_ref[2], far1_ref[...])
-    total[...] += times_transposed(pregrad_ref[3], before_ref[...])
+        activ, slope = gelu_parts(own_ref[d, 4])
+        out_ref[2 * d] = (hidden * slope).astype(BF)
+        out_ref[2 * d + 1] = activ.astype(BF)
+
+
+def part_kernel(pregrad_ref, own_ref, after_ref, far_ref, before_ref, out_ref, total, rows):
+    total[...] = times_transposed(pregrad_ref[0, 0], own_ref[...])
+    total[...] += times_transposed(pregrad_ref[1, 0], after_ref[...])
+    total[...] += times_transposed(pregrad_ref[2, 0], far_ref[...])
+    total[...] += times_transposed(pregrad_ref[3, 0], before_ref[...])
     for z in range(16):
         here = slice(12 * z, 12 * z + 12)
         rows[z, 0:12] = total[here, :512]
@@ -115,11 +110,11 @@
     return lax.dot_general(a, b, (((0,), (0,)), ((), ())), preferred_element_type=F32)
 
 
-def weights_kernel(x_ref, own_ref, *refs):
-    tokens, pregrad, (up_ref, down_ref) = refs[:4], (own_ref.at[0], *refs[4:7]), refs[7:]
+def weights_kernel(own_ref, *refs):
+    tokens, units, (up_ref, down_ref) = refs[:4], (own_ref.at[0], *refs[4:7]), refs[7:]
     for d in range(4):
-        up = times_tokens(tokens[d][1], pregrad[d][...])
-        down = times_tokens(own_ref[4 + lax.rem(x_ref[0] + d, 4)], tokens[d][0])
+        up = times_tokens(tokens[d][1], units[d][0])
+        down = times_tokens(units[d][1], tokens[d][0])
         up_ref[...] = up if d == 0 else up_ref[...] + up
         down_ref[...] = down if d == 0 else down_ref[...] + down
 
@@ -141,13 +136,8 @@
     return lax.ppermute(block, "x", shift(1)), lax.ppermute(block, "x", shift(-1))
 
 
-def far_x(before, after):
-    half = before.shape[0] // 2
-    return lax.ppermute(before[:half], "x", shift(1)), lax.ppermute(after[half:], "x", shift(-1))
-
-
 def local(inputs, out_grad, preact, up_weight, down_weight):
-    core, at_x = lax.axis_index("c"), lax.axis_index("x")
+    core = lax.axis_index("c")
 
     sixteen = jax.ShapeDtypeStruct((16, 48, 512), BF)
     (both,) = call(lay_out_kernel, [sixteen], [(48, 512)], 0, (out_grad, inputs))
@@ -155,9 +145,9 @@
     swap = [(4 * a + b, 4 * ((b - a) % 4) + a) for a in range(4) for b in range(4)]
     turned = lax.ppermute(preact, ("y", "x"), swap)
     before, after = near_x(down_weight)
-    far = far_x(before, after)
+    far = lax.ppermute(before, "x", shift(1))
     up_before, up_after = near_x(up_weight)
-    up_far = far_x(up_before, up_after)
+    up_far = lax.ppermute(up_after, "x", shift(-1))
     both, before, after, far, up_before, up_after = lax.optimization_barrier(
         (both, before, after, far, up_before, up_after)
     )
@@ -168,36 +158,35 @@
         [half, half],
         [(16, 48, 512), (192, 1024)],
         2 * 192 * 1024 * 1024,
-        (core[None], both, down_weight, after, *far, before),
+        (core[None], both, down_weight, after, far, before),
         smem=1,
     )
     theirs, turned, up_far = lax.optimization_barrier((theirs, turned, up_far))
     theirs = lax.ppermute(theirs, "c", [(0, 1), (1, 0)])
-    (own,) = call(payload_kernel, [jax.ShapeDtypeStruct((4, 6, 96, 256), BF)], [], 0, (mine, theirs, preact, turned))
+    (own,) = call(payload_kernel, [jax.ShapeDtypeStruct((4, 5, 96, 256), BF)], [], 0, (mine, theirs, turned))
     own = exchange(own, "y")
     (own,) = call(slope_kernel, [jax.ShapeDtypeStruct((8, 96, 256), BF)], [], 0, (own,))
-    own = lax.all_gather(own, "c", axis=1, tiled=False).reshape(8, 192, 256)
+    own = lax.all_gather(own, "c", axis=1, tiled=False).reshape(4, 2, 192, 256)
 
     (part,) = call(
         part_kernel,
         [jax.ShapeDtypeStruct((16, 24, 512), BF)],
         [(192, 1024), (16, 24, 512)],
         2 * 192 * 1024 * 1024,
-        (own, up_weight, up_after, *up_far, up_before),
+        (own, up_weight, up_after, up_far, up_before),
     )
     part = exchange(part, ("za", "zb"))
 
     tokens = jax.ShapeDtypeStruct((2, 192, 1024), BF)
     (tokens,) = call(tokens_kernel, [tokens], [(16, 48, 512), (192, 1024)], 0, (both,))
     all_tokens = [tokens] + [lax.ppermute(tokens, "x", shift(k)) for k in (3, 2, 1)]
-    all_pregrad = [lax.ppermute(own[k], "x", shift(k)) for k in (3, 2, 1)]
+    all_units = [lax.ppermute(own[k], "x", shift(k)) for k in (3, 2, 1)]
     up_grad, down_grad = call(
         weights_kernel,
         [jax.ShapeDtypeStruct((1024, 256), F32), jax.ShapeDtypeStruct((256, 1024), F32)],
         [],
         16 * 4 * 768 * 1024 * 256,
-        (at_x[None], own, *all_tokens, *all_pregrad),
-        smem=1,
+        (own, *all_tokens, *all_units),
     )
     part, up_grad, down_grad = lax.optimization_barrier((part, up_grad, down_grad))
     (input_grad,) = call(sum_kernel, [jax.ShapeDtypeStruct((12, 1024), BF)], [(24, 512)], 0, (part,))

time: 135 us -> 128 us (0.948)
  local copies, waits for them, and re-layouts: 4.51 us -> 1.58 us
  Pallas kernels: 14 us -> 12.1 us
    ppermute x7 -> x5, waiting for transfers between devices: 4.55 us -> 14.7 us  [the longest x1 7.76 us: local(): far = lax.ppermute(before, 'x', shift(1))]
    all_to_all x3, waiting for transfers between devices: 6.31 us -> 0.95 us  [exchange(): lax.all_to_all(blocks, axis, split_axis=0, concat_axis=0, tiled=False)]
    ppermute x1, waiting for transfers between devices: 3.73 us -> 0.01 us  [local(): turned = lax.ppermute(preact, ('y', 'x'), swap)]
    ppermute x3, waiting for transfers between devices: 6.48 us -> 3.51 us  [local(): lax.ppermute(tokens, 'x', shift(k))]
    slice x4 -> x1, local copies, waits for them, and re-layouts: 2.91 us -> 0.04 us  [local(): all_units = [lax.ppermute(own[k], 'x', shift(k)) for k in (3, 2, 1)]]
    ppermute x3, starting transfers between devices: 8.96 us -> 11.7 us  [local(): lax.ppermute(tokens, 'x', shift(k))]
    ppermute x7 -> x5, starting transfers between devices: 21 us -> 18.4 us  [the longest x3 11.4 us: local(): all_units = [lax.ppermute(own[k], 'x', shift(k)) for k in (3, 2, 1)]]
    ppermute x2, waiting for transfers between devices: 0.01 us -> 2.12 us  [near_x(): lax.ppermute(block, 'x', shift(-1))]
  transfers between devices with their start and end apart: 19 -> 17, of which waited for: 8 -> 11; matrix products, arithmetic and copies ran while one was open for 2% -> 0% of each run, Pallas kernels for 8% -> 7%
where the time goes in v16:
time: 128 us; the launch traced here: 126 us
  starting transfers between devices  80.9 us (63%)
  waiting for transfers between devices  28.2 us (22%)
  Pallas kernels  12.1 us (9%)
  blocking collectives  2.5 us (2%)
  local copies, waits for them, and re-layouts  1.58 us (1%)
    all_to_all x3, starting transfers between devices, exchange(): lax.all_to_all(blocks, axis, split_axis=0, concat_axis=0, tiled=False)  31.8 us
    pallas_call x8, Pallas kernels, call(): pl.pallas_call(body, out_shape=outs, in_specs=[pl.BlockSpec(memory_space=...  12.1 us
    ppermute x3, starting transfers between devices, local(): lax.ppermute(tokens, 'x', shift(k))  11.7 us
    ppermute x3, starting transfers between devices, local(): all_units = [lax.ppermute(own[k], 'x', shift(k)) for k in (3, 2, 1)]  11.4 us
    ppermute x2, starting transfers between devices, near_x(): lax.ppermute(block, 'x', shift(-1))  8.52 us
    ppermute x1, waiting for transfers between devices, local(): far = lax.ppermute(before, 'x', shift(1))  7.76 us
    ppermute x3, waiting for transfers between devices, local(): all_units = [lax.ppermute(own[k], 'x', shift(k)) for k in (3, 2, 1)]  6.92 us
    ppermute x2, starting transfers between devices, near_x(): lax.ppermute(block, 'x', shift(1))  5.59 us
  transfers between devices with their start and end apart: 17, of which 11 were waited for; matrix products, arithmetic and copies ran while one was open for 0% of the time, Pallas kernels for 7%

profile of v16, /device:TPU:24, one launch (start us, length us, event | category | flops | bytes accessed | tf_op | source)
XLA Modules:
  0.0 126.1 jit_solution(1006865622050135353)
XLA Ops:
  0.6 0.7 copy-done.7
  1.4 0.8 copy-done.8
  2.1 0.9 shard_map.76
  3.1 15.3 %all-to-all-start = ((bf16[16,48,512]{2,1,0:T(8,128)(2,1)}), bf16[16,48,512]{2,1,0:T(8,128)(2,1)S(1)}, u32[]{:S(2)}, u32[]{:S(2)}) async-start(bf16[16,48,512]{2,1,0:T(8,128)(2,1)} %shard_map.76), calls=%async_computation | async-start | bytes 1572864 | tf_op jit(solution)/shard_map/all_to_all | solution.py:22
  18.4 3.4 %collective-permute-start = (bf16[256,1024]{1,0:T(8,128)(2,1)}, bf16[256,1024]{1,0:T(8,128)(2,1)}, u32[]{:S(2)}, u32[]{:S(2)}) collective-permute-start(bf16[256,1024]{1,0:T(8,128)(2,1)} %own_ref.2), channel_id=1, source_target_pairs={{0,16},{16,32},{32,48},{48,0},{1,17},{17,33},{33,49},{49,1},{2,18}... | collective-permute-start | bytes 1572872 | tf_op jit(solution)/shard_map/ppermute | solution.py:136
  21.9 3.7 %collective-permute-start.4 = (bf16[1024,256]{1,0:T(8,128)(2,1)S(1)}, bf16[1024,256]{1,0:T(8,128)(2,1)S(1)}, u32[]{:S(2)}, u32[]{:S(2)}) collective-permute-start(bf16[1024,256]{1,0:T(8,128)(2,1)S(1)} %copy-done), channel_id=1, source_target_pairs={{0,48},{16,0},{32,16},{48,32},{1,49},{17,1},{33,17},{49,33},{2,50}... | collective-permute-start | bytes 1572872 | tf_op jit(solution)/shard_map/ppermute | solution.py:136
  25.5 2.2 %collective-permute-start.3 = (bf16[1024,256]{1,0:T(8,128)(2,1)S(1)}, bf16[1024,256]{1,0:T(8,128)(2,1)S(1)}, u32[]{:S(2)}, u32[]{:S(2)}) collective-permute-start(bf16[1024,256]{1,0:T(8,128)(2,1)S(1)} %copy-done), channel_id=1, source_target_pairs={{0,16},{16,32},{32,48},{48,0},{1,17},{17,33},{33,49},{49,1},{2,18}... | collective-permute-start | bytes 1572872 | tf_op jit(solution)/shard_map/ppermute | solution.py:136
  27.7 4.9 %collective-permute-start.1 = (bf16[256,1024]{1,0:T(8,128)(2,1)}, bf16[256,1024]{1,0:T(8,128)(2,1)}, u32[]{:S(2)}, u32[]{:S(2)}) collective-permute-start(bf16[256,1024]{1,0:T(8,128)(2,1)} %own_ref.2), channel_id=1, source_target_pairs={{0,48},{16,0},{32,16},{48,32},{1,49},{17,1},{33,17},{49,33},{2,50}... | collective-permute-start | bytes 1572872 | tf_op jit(solution)/shard_map/ppermute | solution.py:136
  32.6 4.1 %collective-permute-done.before_ref = bf16[256,1024]{1,0:T(8,128)(2,1)} collective-permute-done((bf16[256,1024]{1,0:T(8,128)(2,1)}, bf16[256,1024]{1,0:T(8,128)(2,1)}, u32[]{:S(2)}, u32[]{:S(2)}) %collective-permute-start) | collective-permute-done | bytes 524320 | tf_op jit(solution)/shard_map/ppermute | solution.py:136
  36.7 2.2 %collective-permute-start.2 = (bf16[256,1024]{1,0:T(8,128)(2,1)}, bf16[256,1024]{1,0:T(8,128)(2,1)}, u32[]{:S(2)}, u32[]{:S(2)}) collective-permute-start(bf16[256,1024]{1,0:T(8,128)(2,1)} %collective-permute-done.before_ref), channel_id=1, source_target_pairs={{0,16},{16,32},{32,48},{48,0},{1,17},{17,33},{33,49},{49,1},{2,18}... | collective-permute-start | bytes 1572872 | tf_op jit(solution)/shard_map/ppermute | solution.py:148
  38.9 0.0 collective-permute-done.4.after_ref
  38.9 0.0 copy-start.1
  38.9 4.9 %collective-permute-start.6 = (bf16[1024,256]{1,0:T(8,128)(2,1)S(1)}, bf16[1024,256]{1,0:T(8,128)(2,1)S(1)}, u32[]{:S(2)}, u32[]{:S(2)}) collective-permute-start(bf16[1024,256]{1,0:T(8,128)(2,1)S(1)} %collective-permute-done.4.after_ref), channel_id=1, source_target_pairs={{0,48},{16,0},{32,16},{48,32},{1,49},{17,1},{33,17},{49,33},{2,50}... | collective-permute-start | bytes 1572872 | tf_op jit(solution)/shard_map/ppermute | solution.py:150
  43.8 0.0 copy-done.9
  43.8 2.9 %collective-permute-start.5 = (bf16[96,256]{1,0:T(8,128)(2,1)S(1)}, bf16[96,256]{1,0:T(8,128)(2,1)S(1)}, u32[]{:S(2)}, u32[]{:S(2)}) collective-permute-start(bf16[96,256]{1,0:T(8,128)(2,1)S(1)} %copy-done.9), channel_id=1, source_target_pairs={{0,0},{16,128},{32,256},{48,384},{128,400},{144,16},{160,144},{176... | collective-permute-start | bytes 147464 | tf_op jit(solution)/shard_map/ppermute | solution.py:146
  46.7 1.1 collective-permute-done.3.before_ref
  47.8 2.1 %collective-permute-done.1.after_ref = bf16[256,1024]{1,0:T(8,128)(2,1)} collective-permute-done((bf16[256,1024]{1,0:T(8,128)(2,1)}, bf16[256,1024]{1,0:T(8,128)(2,1)}, u32[]{:S(2)}, u32[]{:S(2)}) %collective-permute-start.1) | collective-permute-done | bytes 524320 | tf_op jit(solution)/shard_map/ppermute | solution.py:136
  50.0 7.8 %collective-permute-done.2.far_ref = bf16[256,1024]{1,0:T(8,128)(2,1)} collective-permute-done((bf16[256,1024]{1,0:T(8,128)(2,1)}, bf16[256,1024]{1,0:T(8,128)(2,1)}, u32[]{:S(2)}, u32[]{:S(2)}) %collective-permute-start.2) | collective-permute-done | bytes 524320 | tf_op jit(solution)/shard_map/ppermute | solution.py:148
  57.7 0.0 all-to-all-done.both_ref
  57.7 3.0 %shard_map.77 = (f32[4,96,256]{2,1,0:T(8,128)S(1)}, f32[4,96,256]{2,1,0:T(8,128)S(1)}) custom-call(s32[1]{0:T(128)} %bitcast.core_ref, bf16[16,48,512]{2,1,0:T(8,128)(2,1)S(1)} %all-to-all-done.both_ref, bf16[256,1024]{1,0:T(8,128)(2,1)} %own_ref.2, bf16[256,1024]{1,0:T(8,128)(2,1)} %collective-permute-done.1.after_ref, ...), custom_call_target="tpu_custom_call" | custom-call | flops 402653184 | bytes 3670020 | tf_op jit(solution)/shard_map/pallas_call | solution.py:28
  60.8 0.0 collective-permute-done.5.turned_ref
  60.8 0.0 collective-permute-done.6.far_ref
  60.8 1.9 %collective-permute-start.7 = (f32[4,96,256]{2,1,0:T(8,128)S(1)}, f32[4,96,256]{2,1,0:T(8,128)S(1)}, u32[]{:S(2)}, u32[]{:S(2)}) collective-permute-start(f32[4,96,256]{2,1,0:T(8,128)S(1)} %get-tuple-element.25), channel_id=1, source_target_pairs={{0,64},{64,0},{1,65},{65,1},{2,66},{66,2},{3,67},{67,3},{4,68},{68... | collective-permute-start | bytes 1179656 | tf_op jit(solution)/shard_map/ppermute | solution.py:165
  62.7 1.7 %collective-permute-done.7.theirs_ref = f32[4,96,256]{2,1,0:T(8,128)S(1)} collective-permute-done((f32[4,96,256]{2,1,0:T(8,128)S(1)}, f32[4,96,256]{2,1,0:T(8,128)S(1)}, u32[]{:S(2)}, u32[]{:S(2)}) %collective-permute-start.7) | collective-permute-done | bytes 393248 | tf_op jit(solution)/shard_map/ppermute | solution.py:165
  64.4 1.0 shard_map.78
  65.4 4.7 %all-to-all-start.1 = ((bf16[4,5,96,256]{3,2,1,0:T(8,128)(2,1)}), bf16[4,5,96,256]{3,2,1,0:T(8,128)(2,1)S(1)}, u32[]{:S(2)}, u32[]{:S(2)}) async-start(bf16[4,5,96,256]{3,2,1,0:T(8,128)(2,1)} %shard_map.78), calls=%async_computation.1 | async-start | bytes 1966080 | tf_op jit(solution)/shard_map/all_to_all | solution.py:22
  70.2 0.3 shard_map.81.refs_0_
  70.4 3.6 %collective-permute-start.10 = (bf16[2,192,1024]{2,1,0:T(8,128)(2,1)S(1)}, bf16[2,192,1024]{2,1,0:T(8,128)(2,1)}, u32[]{:S(2)}, u32[]{:S(2)}) collective-permute-start(bf16[2,192,1024]{2,1,0:T(8,128)(2,1)S(1)} %shard_map.81.refs_0_), channel_id=1, source_target_pairs={{0,16},{16,32},{32,48},{48,0},{1,17},{17,33},{33,49},{49,1},{2,18}... | collective-permute-start | bytes 2359304 | tf_op jit(solution)/shard_map/ppermute | solution.py:182
  74.0 5.4 %collective-permute-start.9 = (bf16[2,192,1024]{2,1,0:T(8,128)(2,1)S(1)}, bf16[2,192,1024]{2,1,0:T(8,128)(2,1)}, u32[]{:S(2)}, u32[]{:S(2)}) collective-permute-start(bf16[2,192,1024]{2,1,0:T(8,128)(2,1)S(1)} %shard_map.81.refs_0_), channel_id=1, source_target_pairs={{0,32},{16,48},{32,0},{48,16},{1,33},{17,49},{33,1},{49,17},{2,34}... | collective-permute-start | bytes 2359304 | tf_op jit(solution)/shard_map/ppermute | solution.py:182
  79.4 2.7 %collective-permute-start.8 = (bf16[2,192,1024]{2,1,0:T(8,128)(2,1)S(1)}, bf16[2,192,1024]{2,1,0:T(8,128)(2,1)}, u32[]{:S(2)}, u32[]{:S(2)}) collective-permute-start(bf16[2,192,1024]{2,1,0:T(8,128)(2,1)S(1)} %shard_map.81.refs_0_), channel_id=1, source_target_pairs={{0,48},{16,0},{32,16},{48,32},{1,49},{17,1},{33,17},{49,33},{2,50}... | collective-permute-start | bytes 2359304 | tf_op jit(solution)/shard_map/ppermute | solution.py:182
  82.1 0.9 all-to-all-done.1.own_ref
  83.1 0.3 shard_map.79
  83.3 0.0 copy-start.2
  83.4 2.5 %all-gather = bf16[8,192,256]{2,1,0:T(8,128)(2,1)S(1)} all-gather(bf16[8,96,256]{2,1,0:T(8,128)(2,1)S(1)} %shard_map.79), channel_id=2, replica_groups=mesh['y'=4,'c'=2,'x'=4,'za'=4,'zb'=4] {'c'}, dimensions={1}, use_global_device_ids=true | all-gather | bytes 1179648 | tf_op jit(solution)/shard_map/all_gather | solution.py:169
  85.9 1.6 %shard_map.80 = bf16[16,24,512]{2,1,0:T(8,128)(2,1)} custom-call(bf16[4,2,192,256]{3,2,1,0:T(8,128)(2,1)S(1)} %bitcast.2, bf16[1024,256]{1,0:T(8,128)(2,1)S(1)} %copy-done, bf16[1024,256]{1,0:T(8,128)(2,1)S(1)} %copy-done.2, bf16[1024,256]{1,0:T(8,128)(2,1)S(1)} %copy-done.6, bf16[1024,256]{1,0:T(8,128)(2,1)S(1)} %copy-done.4), custom_call_target="tpu_custom_call" | custom-call | flops 402653184 | bytes 3276800 | tf_op jit(solution)/shard_map/pallas_call | solution.py:28
  87.5 11.7 %all-to-all-start.2 = ((bf16[16,24,512]{2,1,0:T(8,128)(2,1)}), bf16[16,24,512]{2,1,0:T(8,128)(2,1)S(1)}, u32[]{:S(2)}, u32[]{:S(2)}) async-start(bf16[16,24,512]{2,1,0:T(8,128)(2,1)} %shard_map.80), calls=%async_computation.2 | async-start | bytes 786432 | tf_op jit(solution)/shard_map/all_to_all | solution.py:22
  99.3 3.3 %collective-permute-start.13 = (bf16[2,192,256]{2,1,0:T(8,128)(2,1)S(1)}, bf16[2,192,256]{2,1,0:T(8,128)(2,1)S(1)}, u32[]{:S(2)}, u32[]{:S(2)}) collective-permute-start(bf16[2,192,256]{2,1,0:T(8,128)(2,1)S(1)} %get-tuple-element.35), channel_id=1, source_target_pairs={{0,16},{16,32},{32,48},{48,0},{1,17},{17,33},{33,49},{49,1},{2,18}... | collective-permute-start | bytes 589832 | tf_op jit(solution)/shard_map/ppermute | solution.py:183
  102.6 6.1 %collective-permute-start.12 = (bf16[2,192,256]{2,1,0:T(8,128)(2,1)S(1)}, bf16[2,192,256]{2,1,0:T(8,128)(2,1)S(1)}, u32[]{:S(2)}, u32[]{:S(2)}) collective-permute-start(bf16[2,192,256]{2,1,0:T(8,128)(2,1)S(1)} %get-tuple-element.36), channel_id=1, source_target_pairs={{0,32},{16,48},{32,0},{48,16},{1,33},{17,49},{33,1},{49,17},{2,34}... | collective-permute-start | bytes 589832 | tf_op jit(solution)/shard_map/ppermute | solution.py:183
  108.7 0.0 collective-permute-done.10.refs_3_
  108.7 2.0 %collective-permute-start.11 = (bf16[2,192,256]{2,1,0:T(8,128)(2,1)S(1)}, bf16[2,192,256]{2,1,0:T(8,128)(2,1)S(1)}, u32[]{:S(2)}, u32[]{:S(2)}) collective-permute-start(bf16[2,192,256]{2,1,0:T(8,128)(2,1)S(1)} %get-tuple-element.37), channel_id=1, source_target_pairs={{0,48},{16,0},{32,16},{48,32},{1,49},{17,1},{33,17},{49,33},{2,50}... | collective-permute-start | bytes 589832 | tf_op jit(solution)/shard_map/ppermute | solution.py:183
  110.7 2.2 %collective-permute-done.9.refs_2_ = bf16[2,192,1024]{2,1,0:T(8,128)(2,1)} collective-permute-done((bf16[2,192,1024]{2,1,0:T(8,128)(2,1)S(1)}, bf16[2,192,1024]{2,1,0:T(8,128)(2,1)}, u32[]{:S(2)}, u32[]{:S(2)}) %collective-permute-start.9) | collective-permute-done | bytes 786464 | tf_op jit(solution)/shard_map/ppermute | solution.py:182
  112.9 1.3 %collective-permute-done.8.refs_1_ = bf16[2,192,1024]{2,1,0:T(8,128)(2,1)} collective-permute-done((bf16[2,192,1024]{2,1,0:T(8,128)(2,1)S(1)}, bf16[2,192,1024]{2,1,0:T(8,128)(2,1)}, u32[]{:S(2)}, u32[]{:S(2)}) %collective-permute-start.8) | collective-permute-done | bytes 786464 | tf_op jit(solution)/shard_map/ppermute | solution.py:182
  114.2 2.7 %collective-permute-done.13.refs_6_ = bf16[2,192,256]{2,1,0:T(8,128)(2,1)S(1)} collective-permute-done((bf16[2,192,256]{2,1,0:T(8,128)(2,1)S(1)}, bf16[2,192,256]{2,1,0:T(8,128)(2,1)S(1)}, u32[]{:S(2)}, u32[]{:S(2)}) %collective-permute-start.13) | collective-permute-done | bytes 196640 | tf_op jit(solution)/shard_map/ppermute | solution.py:183
  116.9 2.9 %collective-permute-done.12.refs_5_ = bf16[2,192,256]{2,1,0:T(8,128)(2,1)S(1)} collective-permute-done((bf16[2,192,256]{2,1,0:T(8,128)(2,1)S(1)}, bf16[2,192,256]{2,1,0:T(8,128)(2,1)S(1)}, u32[]{:S(2)}, u32[]{:S(2)}) %collective-permute-start.12) | collective-permute-done | bytes 196640 | tf_op jit(solution)/shard_map/ppermute | solution.py:183
  119.8 1.4 %collective-permute-done.11.refs_4_ = bf16[2,192,256]{2,1,0:T(8,128)(2,1)S(1)} collective-permute-done((bf16[2,192,256]{2,1,0:T(8,128)(2,1)S(1)}, bf16[2,192,256]{2,1,0:T(8,128)(2,1)S(1)}, u32[]{:S(2)}, u32[]{:S(2)}) %collective-permute-start.11) | collective-permute-done | bytes 196640 | tf_op jit(solution)/shard_map/ppermute | solution.py:183
  121.1 4.2 %shard_map.82 = (f32[1024,256]{1,0:T(8,128)}, f32[256,1024]{1,0:T(8,128)}) custom-call(bf16[4,2,192,256]{3,2,1,0:T(8,128)(2,1)S(1)} %bitcast.3, bf16[2,192,1024]{2,1,0:T(8,128)(2,1)S(1)} %shard_map.81.refs_0_, bf16[2,192,1024]{2,1,0:T(8,128)(2,1)} %collective-permute-done.8.refs_1_, bf16[2,192,1024]{2,1,0:T(8,128)(2,1)} %collective-permute-done.9.refs_2_, ...), custom_call_target="tpu_custom_call" | custom-call | flops 12884901888 | bytes 6619136 | tf_op jit(solution)/shard_map/pallas_call | solution.py:28
  125.4 0.0 all-to-all-done.2.part_ref
  125.4 0.7 shard_map.83
  (16 shorter events, 0.1 us)
Async XLA Ops:
  0.6 0.8 copy-start.7
  1.4 0.8 copy-start.8
  3.1 18.8 %copy-start = (bf16[1024,256]{1,0:T(8,128)(2,1)S(1)}, bf16[1024,256]{1,0:T(8,128)(2,1)}, u32[]{:S(2)}) copy-start(bf16[1024,256]{1,0:T(8,128)(2,1)} %own_ref.3) | copy-start | bytes 1572868
  3.1 40.7 %copy-start.9 = (bf16[96,256]{1,0:T(8,128)(2,1)S(1)}, bf16[96,256]{1,0:T(8,128)(2,1)}, u32[]{:S(2)}) copy-start(bf16[96,256]{1,0:T(8,128)(2,1)} %param.7) | copy-start | bytes 147460
  3.1 54.6 %all-to-all-start = ((bf16[16,48,512]{2,1,0:T(8,128)(2,1)}), bf16[16,48,512]{2,1,0:T(8,128)(2,1)S(1)}, u32[]{:S(2)}, u32[]{:S(2)}) async-start(bf16[16,48,512]{2,1,0:T(8,128)(2,1)} %shard_map.76), calls=%async_computation | async-start | bytes 1572864 | tf_op jit(solution)/shard_map/all_to_all | solution.py:22
  18.4 18.3 %collective-permute-start = (bf16[256,1024]{1,0:T(8,128)(2,1)}, bf16[256,1024]{1,0:T(8,128)(2,1)}, u32[]{:S(2)}, u32[]{:S(2)}) collective-permute-start(bf16[256,1024]{1,0:T(8,128)(2,1)} %own_ref.2), channel_id=1, source_target_pairs={{0,16},{16,32},{32,48},{48,0},{1,17},{17,33},{33,49},{49,1},{2,18}... | collective-permute-start | bytes 1572872 | tf_op jit(solution)/shard_map/ppermute | solution.py:136
  21.9 17.0 %collective-permute-start.4 = (bf16[1024,256]{1,0:T(8,128)(2,1)S(1)}, bf16[1024,256]{1,0:T(8,128)(2,1)S(1)}, u32[]{:S(2)}, u32[]{:S(2)}) collective-permute-start(bf16[1024,256]{1,0:T(8,128)(2,1)S(1)} %copy-done), channel_id=1, source_target_pairs={{0,48},{16,0},{32,16},{48,32},{1,49},{17,1},{33,17},{49,33},{2,50}... | collective-permute-start | bytes 1572872 | tf_op jit(solution)/shard_map/ppermute | solution.py:136
  25.5 22.3 %collective-permute-start.3 = (bf16[1024,256]{1,0:T(8,128)(2,1)S(1)}, bf16[1024,256]{1,0:T(8,128)(2,1)S(1)}, u32[]{:S(2)}, u32[]{:S(2)}) collective-permute-start(bf16[1024,256]{1,0:T(8,128)(2,1)S(1)} %copy-done), channel_id=1, source_target_pairs={{0,16},{16,32},{32,48},{48,0},{1,17},{17,33},{33,49},{49,1},{2,18}... | collective-permute-start | bytes 1572872 | tf_op jit(solution)/shard_map/ppermute | solution.py:136
  27.7 22.2 %collective-permute-start.1 = (bf16[256,1024]{1,0:T(8,128)(2,1)}, bf16[256,1024]{1,0:T(8,128)(2,1)}, u32[]{:S(2)}, u32[]{:S(2)}) collective-permute-start(bf16[256,1024]{1,0:T(8,128)(2,1)} %own_ref.2), channel_id=1, source_target_pairs={{0,48},{16,0},{32,16},{48,32},{1,49},{17,1},{33,17},{49,33},{2,50}... | collective-permute-start | bytes 1572872 | tf_op jit(solution)/shard_map/ppermute | solution.py:136
  36.7 21.0 %collective-permute-start.2 = (bf16[256,1024]{1,0:T(8,128)(2,1)}, bf16[256,1024]{1,0:T(8,128)(2,1)}, u32[]{:S(2)}, u32[]{:S(2)}) collective-permute-start(bf16[256,1024]{1,0:T(8,128)(2,1)} %collective-permute-done.before_ref), channel_id=1, source_target_pairs={{0,16},{16,32},{32,48},{48,0},{1,17},{17,33},{33,49},{49,1},{2,18}... | collective-permute-start | bytes 1572872 | tf_op jit(solution)/shard_map/ppermute | solution.py:148
  38.9 21.8 %copy-start.1 = (bf16[1024,256]{1,0:T(8,128)(2,1)}, bf16[1024,256]{1,0:T(8,128)(2,1)S(1)}, u32[]{:S(2)}) copy-start(bf16[1024,256]{1,0:T(8,128)(2,1)S(1)} %collective-permute-done.4.after_ref) | copy-start | bytes 1572868
  38.9 21.9 %collective-permute-start.6 = (bf16[1024,256]{1,0:T(8,128)(2,1)S(1)}, bf16[1024,256]{1,0:T(8,128)(2,1)S(1)}, u32[]{:S(2)}, u32[]{:S(2)}) collective-permute-start(bf16[1024,256]{1,0:T(8,128)(2,1)S(1)} %collective-permute-done.4.after_ref), channel_id=1, source_target_pairs={{0,48},{16,0},{32,16},{48,32},{1,49},{17,1},{33,17},{49,33},{2,50}... | collective-permute-start | bytes 1572872 | tf_op jit(solution)/shard_map/ppermute | solution.py:150
  43.8 17.0 %collective-permute-start.5 = (bf16[96,256]{1,0:T(8,128)(2,1)S(1)}, bf16[96,256]{1,0:T(8,128)(2,1)S(1)}, u32[]{:S(2)}, u32[]{:S(2)}) collective-permute-start(bf16[96,256]{1,0:T(8,128)(2,1)S(1)} %copy-done.9), channel_id=1, source_target_pairs={{0,0},{16,128},{32,256},{48,384},{128,400},{144,16},{160,144},{176... | collective-permute-start | bytes 147464 | tf_op jit(solution)/shard_map/ppermute | solution.py:146
  47.8 12.9 %copy-start.3 = (bf16[1024,256]{1,0:T(8,128)(2,1)}, bf16[1024,256]{1,0:T(8,128)(2,1)S(1)}, u32[]{:S(2)}) copy-start(bf16[1024,256]{1,0:T(8,128)(2,1)S(1)} %collective-permute-done.3.before_ref) | copy-start | bytes 1572868
  60.8 4.6 %copy-start.5 = (bf16[1024,256]{1,0:T(8,128)(2,1)}, bf16[1024,256]{1,0:T(8,128)(2,1)S(1)}, u32[]{:S(2)}) copy-start(bf16[1024,256]{1,0:T(8,128)(2,1)S(1)} %collective-permute-done.6.far_ref) | copy-start | bytes 1572868
  60.8 3.6 %collective-permute-start.7 = (f32[4,96,256]{2,1,0:T(8,128)S(1)}, f32[4,96,256]{2,1,0:T(8,128)S(1)}, u32[]{:S(2)}, u32[]{:S(2)}) collective-permute-start(f32[4,96,256]{2,1,0:T(8,128)S(1)} %get-tuple-element.25), channel_id=1, source_target_pairs={{0,64},{64,0},{1,65},{65,1},{2,66},{66,2},{3,67},{67,3},{4,68},{68... | collective-permute-start | bytes 1179656 | tf_op jit(solution)/shard_map/ppermute | solution.py:165
  65.4 17.6 %all-to-all-start.1 = ((bf16[4,5,96,256]{3,2,1,0:T(8,128)(2,1)}), bf16[4,5,96,256]{3,2,1,0:T(8,128)(2,1)S(1)}, u32[]{:S(2)}, u32[]{:S(2)}) async-start(bf16[4,5,96,256]{3,2,1,0:T(8,128)(2,1)} %shard_map.78), calls=%async_computation.1 | async-start | bytes 1966080 | tf_op jit(solution)/shard_map/all_to_all | solution.py:22
  70.4 38.3 %collective-permute-start.10 = (bf16[2,192,1024]{2,1,0:T(8,128)(2,1)S(1)}, bf16[2,192,1024]{2,1,0:T(8,128)(2,1)}, u32[]{:S(2)}, u32[]{:S(2)}) collective-permute-start(bf16[2,192,1024]{2,1,0:T(8,128)(2,1)S(1)} %shard_map.81.refs_0_), channel_id=1, source_target_pairs={{0,16},{16,32},{32,48},{48,0},{1,17},{17,33},{33,49},{49,1},{2,18}... | collective-permute-start | bytes 2359304 | tf_op jit(solution)/shard_map/ppermute | solution.py:182
  74.0 38.9 %collective-permute-start.9 = (bf16[2,192,1024]{2,1,0:T(8,128)(2,1)S(1)}, bf16[2,192,1024]{2,1,0:T(8,128)(2,1)}, u32[]{:S(2)}, u32[]{:S(2)}) collective-permute-start(bf16[2,192,1024]{2,1,0:T(8,128)(2,1)S(1)} %shard_map.81.refs_0_), channel_id=1, source_target_pairs={{0,32},{16,48},{32,0},{48,16},{1,33},{17,49},{33,1},{49,17},{2,34}... | collective-permute-start | bytes 2359304 | tf_op jit(solution)/shard_map/ppermute | solution.py:182
  79.4 34.8 %collective-permute-start.8 = (bf16[2,192,1024]{2,1,0:T(8,128)(2,1)S(1)}, bf16[2,192,1024]{2,1,0:T(8,128)(2,1)}, u32[]{:S(2)}, u32[]{:S(2)}) collective-permute-start(bf16[2,192,1024]{2,1,0:T(8,128)(2,1)S(1)} %shard_map.81.refs_0_), channel_id=1, source_target_pairs={{0,48},{16,0},{32,16},{48,32},{1,49},{17,1},{33,17},{49,33},{2,50}... | collective-permute-start | bytes 2359304 | tf_op jit(solution)/shard_map/ppermute | solution.py:182
  83.1 2.8 %copy-start.6 = (bf16[1024,256]{1,0:T(8,128)(2,1)S(1)}, bf16[1024,256]{1,0:T(8,128)(2,1)}, u32[]{:S(2)}) copy-start(bf16[1024,256]{1,0:T(8,128)(2,1)} %copy-done.5) | copy-start | bytes 1572868
  83.3 2.5 %copy-start.2 = (bf16[1024,256]{1,0:T(8,128)(2,1)S(1)}, bf16[1024,256]{1,0:T(8,128)(2,1)}, u32[]{:S(2)}) copy-start(bf16[1024,256]{1,0:T(8,128)(2,1)} %copy-done.1) | copy-start | bytes 1572868
  83.4 2.5 %copy-start.4 = (bf16[1024,256]{1,0:T(8,128)(2,1)S(1)}, bf16[1024,256]{1,0:T(8,128)(2,1)}, u32[]{:S(2)}) copy-start(bf16[1024,256]{1,0:T(8,128)(2,1)} %copy-done.3) | copy-start | bytes 1572868
  87.5 37.9 %all-to-all-start.2 = ((bf16[16,24,512]{2,1,0:T(8,128)(2,1)}), bf16[16,24,512]{2,1,0:T(8,128)(2,1)S(1)}, u32[]{:S(2)}, u32[]{:S(2)}) async-start(bf16[16,24,512]{2,1,0:T(8,128)(2,1)} %shard_map.80), calls=%async_computation.2 | async-start | bytes 786432 | tf_op jit(solution)/shard_map/all_to_all | solution.py:22
  99.3 17.6 %collective-permute-start.13 = (bf16[2,192,256]{2,1,0:T(8,128)(2,1)S(1)}, bf16[2,192,256]{2,1,0:T(8,128)(2,1)S(1)}, u32[]{:S(2)}, u32[]{:S(2)}) collective-permute-start(bf16[2,192,256]{2,1,0:T(8,128)(2,1)S(1)} %get-tuple-element.35), channel_id=1, source_target_pairs={{0,16},{16,32},{32,48},{48,0},{1,17},{17,33},{33,49},{49,1},{2,18}... | collective-permute-start | bytes 589832 | tf_op jit(solution)/shard_map/ppermute | solution.py:183
  102.6 17.2 %collective-permute-start.12 = (bf16[2,192,256]{2,1,0:T(8,128)(2,1)S(1)}, bf16[2,192,256]{2,1,0:T(8,128)(2,1)S(1)}, u32[]{:S(2)}, u32[]{:S(2)}) collective-permute-start(bf16[2,192,256]{2,1,0:T(8,128)(2,1)S(1)} %get-tuple-element.36), channel_id=1, source_target_pairs={{0,32},{16,48},{32,0},{48,16},{1,33},{17,49},{33,1},{49,17},{2,34}... | collective-permute-start | bytes 589832 | tf_op jit(solution)/shard_map/ppermute | solution.py:183
  108.7 12.4 %collective-permute-start.11 = (bf16[2,192,256]{2,1,0:T(8,128)(2,1)S(1)}, bf16[2,192,256]{2,1,0:T(8,128)(2,1)S(1)}, u32[]{:S(2)}, u32[]{:S(2)}) collective-permute-start(bf16[2,192,256]{2,1,0:T(8,128)(2,1)S(1)} %get-tuple-element.37), channel_id=1, source_target_pairs={{0,48},{16,0},{32,16},{48,32},{1,49},{17,1},{33,17},{49,33},{2,50}... | collective-permute-start | bytes 589832 | tf_op jit(solution)/shard_map/ppermute | solution.py:183

commit v17 on v16

--- a/solution.py
+++ b/solution.py
@@ -112,11 +112,12 @@
 
 def weights_kernel(own_ref, *refs):
     tokens, units, (up_ref, down_ref) = refs[:4], (own_ref.at[0], *refs[4:7]), refs[7:]
-    for d in range(4):
-        up = times_tokens(tokens[d][1], units[d][0])
-        down = times_tokens(units[d][1], tokens[d][0])
-        up_ref[...] = up if d == 0 else up_ref[...] + up
-        down_ref[...] = down if d == 0 else down_ref[...] + down
+    pregrad = jnp.concatenate([ref[0] for ref in units])
+    activ = jnp.concatenate([ref[1] for ref in units])
+    for part in range(4):
+        here = slice(256 * part, 256 * part + 256)
+        up_ref[here] = times_tokens(jnp.concatenate([ref[1, :, here] for ref in tokens]), pregrad)
+        down_ref[:, here] = times_tokens(activ, jnp.concatenate([ref[0, :, here] for ref in tokens]))
 
 
 def sum_kernel(part_ref, out_ref, rows):
@@ -148,9 +149,7 @@
     far = lax.ppermute(before, "x", shift(1))
     up_before, up_after = near_x(up_weight)
     up_far = lax.ppermute(up_after, "x", shift(-1))
-    both, before, after, far, up_before, up_after = lax.optimization_barrier(
-        (both, before, after, far, up_before, up_after)
-    )
+    both, before, after, far, up_after = lax.optimization_barrier((both, before, after, far, up_after))
 
     half = jax.ShapeDtypeStruct((4, 96, 256), F32)
     mine, theirs = call(
@@ -161,7 +160,7 @@
         (core[None], both, down_weight, after, far, before),
         smem=1,
     )
-    theirs, turned, up_far = lax.optimization_barrier((theirs, turned, up_far))
+    theirs, turned, up_before, up_far = lax.optimization_barrier((theirs, turned, up_before, up_far))
     theirs = lax.ppermute(theirs, "c", [(0, 1), (1, 0)])
     (own,) = call(payload_kernel, [jax.ShapeDtypeStruct((4, 5, 96, 256), BF)], [], 0, (mine, theirs, turned))
     own = exchange(own, "y")

time: 128 us -> 129 us (level)
  waiting for transfers between devices: 28.2 us -> 35.7 us
  starting transfers between devices: 80.9 us -> 75.7 us
    all_to_all x3, waiting for transfers between devices: 0.95 us -> 7.07 us  [exchange(): lax.all_to_all(blocks, axis, split_axis=0, concat_axis=0, tiled=False)]
    ppermute x1, waiting for transfers between devices: 7.76 us -> 3.56 us  [local(): far = lax.ppermute(before, 'x', shift(1))]
    ppermute x1, waiting for transfers between devices: 0.01 us -> 3.27 us  [local(): turned = lax.ppermute(preact, ('y', 'x'), swap)]
    ppermute x3, waiting for transfers between devices: 3.51 us -> 6.15 us  [local(): lax.ppermute(tokens, 'x', shift(k))]
    ppermute x3, starting transfers between devices: 11.4 us -> 8.91 us  [local(): all_units = [lax.ppermute(own[k], 'x', shift(k)) for k in (3, 2, 1)]]
    ppermute x3, starting transfers between devices: 11.7 us -> 9.48 us  [local(): lax.ppermute(tokens, 'x', shift(k))]
    ppermute x1, starting transfers between devices: 2.92 us -> 4.32 us  [local(): turned = lax.ppermute(preact, ('y', 'x'), swap)]
    ppermute x2, starting transfers between devices: 8.52 us -> 7.11 us  [near_x(): lax.ppermute(block, 'x', shift(-1))]
where the time goes in v17:
time: 129 us; the launch traced here: 128 us
  starting transfers between devices  75.7 us (59%)
  waiting for transfers between devices  35.7 us (28%)
  Pallas kernels  11.8 us (9%)
  blocking collectives  2.5 us (2%)
  local copies, waits for them, and re-layouts  1.58 us (1%)
    all_to_all x3, starting transfers between devices, exchange(): lax.all_to_all(blocks, axis, split_axis=0, concat_axis=0, tiled=False)  31.3 us
    pallas_call x8, Pallas kernels, call(): pl.pallas_call(body, out_shape=outs, in_specs=[pl.BlockSpec(memory_space=...  11.8 us
    ppermute x3, starting transfers between devices, local(): lax.ppermute(tokens, 'x', shift(k))  9.48 us
    ppermute x3, starting transfers between devices, local(): all_units = [lax.ppermute(own[k], 'x', shift(k)) for k in (3, 2, 1)]  8.91 us
    ppermute x2, starting transfers between devices, near_x(): lax.ppermute(block, 'x', shift(-1))  7.11 us
    all_to_all x3, waiting for transfers between devices, exchange(): lax.all_to_all(blocks, axis, split_axis=0, concat_axis=0, tiled=False)  7.07 us
    ppermute x2, starting transfers between devices, near_x(): lax.ppermute(block, 'x', shift(1))  6.8 us
    ppermute x3, waiting for transfers between devices, local(): all_units = [lax.ppermute(own[k], 'x', shift(k)) for k in (3, 2, 1)]  6.58 us
  transfers between devices with their start and end apart: 17, of which 11 were waited for; matrix products, arithmetic and copies ran while one was open for 0% of the time, Pallas kernels for 7%

profile of v17, /device:TPU:24, one launch (start us, length us, event | category | flops | bytes accessed | tf_op | source)
XLA Modules:
  0.0 128.0 jit_solution(9996102223429497563)
XLA Ops:
  0.6 0.7 copy-done.7
  1.4 0.8 copy-done.8
  2.1 0.9 shard_map.76
  3.1 15.3 %all-to-all-start = ((bf16[16,48,512]{2,1,0:T(8,128)(2,1)}), bf16[16,48,512]{2,1,0:T(8,128)(2,1)S(1)}, u32[]{:S(2)}, u32[]{:S(2)}) async-start(bf16[16,48,512]{2,1,0:T(8,128)(2,1)} %shard_map.76), calls=%async_computation | async-start | bytes 1572864 | tf_op jit(solution)/shard_map/all_to_all | solution.py:22
  18.4 3.4 %collective-permute-start = (bf16[256,1024]{1,0:T(8,128)(2,1)}, bf16[256,1024]{1,0:T(8,128)(2,1)}, u32[]{:S(2)}, u32[]{:S(2)}) collective-permute-start(bf16[256,1024]{1,0:T(8,128)(2,1)} %own_ref.2), channel_id=1, source_target_pairs={{0,16},{16,32},{32,48},{48,0},{1,17},{17,33},{33,49},{49,1},{2,18}... | collective-permute-start | bytes 1572872 | tf_op jit(solution)/shard_map/ppermute | solution.py:137
  21.9 3.7 %collective-permute-start.3 = (bf16[1024,256]{1,0:T(8,128)(2,1)S(1)}, bf16[1024,256]{1,0:T(8,128)(2,1)S(1)}, u32[]{:S(2)}, u32[]{:S(2)}) collective-permute-start(bf16[1024,256]{1,0:T(8,128)(2,1)S(1)} %copy-done), channel_id=1, source_target_pairs={{0,48},{16,0},{32,16},{48,32},{1,49},{17,1},{33,17},{49,33},{2,50}... | collective-permute-start | bytes 1572872 | tf_op jit(solution)/shard_map/ppermute | solution.py:137
  25.5 3.5 %collective-permute-start.1 = (bf16[256,1024]{1,0:T(8,128)(2,1)}, bf16[256,1024]{1,0:T(8,128)(2,1)}, u32[]{:S(2)}, u32[]{:S(2)}) collective-permute-start(bf16[256,1024]{1,0:T(8,128)(2,1)} %own_ref.2), channel_id=1, source_target_pairs={{0,48},{16,0},{32,16},{48,32},{1,49},{17,1},{33,17},{49,33},{2,50}... | collective-permute-start | bytes 1572872 | tf_op jit(solution)/shard_map/ppermute | solution.py:137
  29.0 6.3 %collective-permute-done.before_ref = bf16[256,1024]{1,0:T(8,128)(2,1)} collective-permute-done((bf16[256,1024]{1,0:T(8,128)(2,1)}, bf16[256,1024]{1,0:T(8,128)(2,1)}, u32[]{:S(2)}, u32[]{:S(2)}) %collective-permute-start) | collective-permute-done | bytes 524320 | tf_op jit(solution)/shard_map/ppermute | solution.py:137
  35.2 2.2 %collective-permute-start.2 = (bf16[256,1024]{1,0:T(8,128)(2,1)}, bf16[256,1024]{1,0:T(8,128)(2,1)}, u32[]{:S(2)}, u32[]{:S(2)}) collective-permute-start(bf16[256,1024]{1,0:T(8,128)(2,1)} %collective-permute-done.before_ref), channel_id=1, source_target_pairs={{0,16},{16,32},{32,48},{48,0},{1,17},{17,33},{33,49},{49,1},{2,18}... | collective-permute-start | bytes 1572872 | tf_op jit(solution)/shard_map/ppermute | solution.py:149
  37.4 3.4 %collective-permute-start.5 = (bf16[1024,256]{1,0:T(8,128)(2,1)S(1)}, bf16[1024,256]{1,0:T(8,128)(2,1)S(1)}, u32[]{:S(2)}, u32[]{:S(2)}) collective-permute-start(bf16[1024,256]{1,0:T(8,128)(2,1)S(1)} %copy-done), channel_id=1, source_target_pairs={{0,16},{16,32},{32,48},{48,0},{1,17},{17,33},{33,49},{49,1},{2,18}... | collective-permute-start | bytes 1572872 | tf_op jit(solution)/shard_map/ppermute | solution.py:137
  40.8 0.0 collective-permute-done.3.after_ref
  40.8 0.0 copy-start.1
  40.9 3.7 %collective-permute-start.6 = (bf16[1024,256]{1,0:T(8,128)(2,1)S(1)}, bf16[1024,256]{1,0:T(8,128)(2,1)S(1)}, u32[]{:S(2)}, u32[]{:S(2)}) collective-permute-start(bf16[1024,256]{1,0:T(8,128)(2,1)S(1)} %collective-permute-done.3.after_ref), channel_id=1, source_target_pairs={{0,48},{16,0},{32,16},{48,32},{1,49},{17,1},{33,17},{49,33},{2,50}... | collective-permute-start | bytes 1572872 | tf_op jit(solution)/shard_map/ppermute | solution.py:151
  44.5 4.3 %collective-permute-start.4 = (bf16[96,256]{1,0:T(8,128)(2,1)S(1)}, bf16[96,256]{1,0:T(8,128)(2,1)S(1)}, u32[]{:S(2)}, u32[]{:S(2)}) collective-permute-start(bf16[96,256]{1,0:T(8,128)(2,1)S(1)} %copy-done.9), channel_id=1, source_target_pairs={{0,0},{16,128},{32,256},{48,384},{128,400},{144,16},{160,144},{176... | collective-permute-start | bytes 147464 | tf_op jit(solution)/shard_map/ppermute | solution.py:147
  48.9 1.1 collective-permute-done.1.after_ref
  50.0 3.6 %collective-permute-done.2.far_ref = bf16[256,1024]{1,0:T(8,128)(2,1)} collective-permute-done((bf16[256,1024]{1,0:T(8,128)(2,1)}, bf16[256,1024]{1,0:T(8,128)(2,1)}, u32[]{:S(2)}, u32[]{:S(2)}) %collective-permute-start.2) | collective-permute-done | bytes 524320 | tf_op jit(solution)/shard_map/ppermute | solution.py:149
  53.5 4.2 %all-to-all-done.both_ref = bf16[16,48,512]{2,1,0:T(8,128)(2,1)S(1)} async-done(((bf16[16,48,512]{2,1,0:T(8,128)(2,1)}), bf16[16,48,512]{2,1,0:T(8,128)(2,1)S(1)}, u32[]{:S(2)}, u32[]{:S(2)}) %all-to-all-start) | async-done | bytes 786464 | tf_op jit(solution)/shard_map/all_to_all | solution.py:22
  57.7 3.0 %shard_map.77 = (f32[4,96,256]{2,1,0:T(8,128)S(1)}, f32[4,96,256]{2,1,0:T(8,128)S(1)}) custom-call(s32[1]{0:T(128)} %bitcast.core_ref, bf16[16,48,512]{2,1,0:T(8,128)(2,1)S(1)} %all-to-all-done.both_ref, bf16[256,1024]{1,0:T(8,128)(2,1)} %own_ref.2, bf16[256,1024]{1,0:T(8,128)(2,1)} %collective-permute-done.1.after_ref, ...), custom_call_target="tpu_custom_call" | custom-call | flops 402653184 | bytes 3670020 | tf_op jit(solution)/shard_map/pallas_call | solution.py:28
  60.8 3.3 %collective-permute-done.4.turned_ref = bf16[96,256]{1,0:T(8,128)(2,1)S(1)} collective-permute-done((bf16[96,256]{1,0:T(8,128)(2,1)S(1)}, bf16[96,256]{1,0:T(8,128)(2,1)S(1)}, u32[]{:S(2)}, u32[]{:S(2)}) %collective-permute-start.4) | collective-permute-done | bytes 49184 | tf_op jit(solution)/shard_map/ppermute | solution.py:147
  64.0 0.0 collective-permute-done.5.before_ref
  64.0 0.0 collective-permute-done.6.far_ref
  64.0 1.9 %collective-permute-start.7 = (f32[4,96,256]{2,1,0:T(8,128)S(1)}, f32[4,96,256]{2,1,0:T(8,128)S(1)}, u32[]{:S(2)}, u32[]{:S(2)}) collective-permute-start(f32[4,96,256]{2,1,0:T(8,128)S(1)} %get-tuple-element.25), channel_id=1, source_target_pairs={{0,64},{64,0},{1,65},{65,1},{2,66},{66,2},{3,67},{67,3},{4,68},{68... | collective-permute-start | bytes 1179656 | tf_op jit(solution)/shard_map/ppermute | solution.py:164
  66.0 1.7 %collective-permute-done.7.theirs_ref = f32[4,96,256]{2,1,0:T(8,128)S(1)} collective-permute-done((f32[4,96,256]{2,1,0:T(8,128)S(1)}, f32[4,96,256]{2,1,0:T(8,128)S(1)}, u32[]{:S(2)}, u32[]{:S(2)}) %collective-permute-start.7) | collective-permute-done | bytes 393248 | tf_op jit(solution)/shard_map/ppermute | solution.py:164
  67.7 1.0 shard_map.78
  68.7 0.0 copy-done.5
  68.7 4.5 %all-to-all-start.1 = ((bf16[4,5,96,256]{3,2,1,0:T(8,128)(2,1)}), bf16[4,5,96,256]{3,2,1,0:T(8,128)(2,1)S(1)}, u32[]{:S(2)}, u32[]{:S(2)}) async-start(bf16[4,5,96,256]{3,2,1,0:T(8,128)(2,1)} %shard_map.78), calls=%async_computation.1 | async-start | bytes 1966080 | tf_op jit(solution)/shard_map/all_to_all | solution.py:22
  73.2 0.3 shard_map.81.refs_0_
  73.5 1.9 %collective-permute-start.10 = (bf16[2,192,1024]{2,1,0:T(8,128)(2,1)S(1)}, bf16[2,192,1024]{2,1,0:T(8,128)(2,1)}, u32[]{:S(2)}, u32[]{:S(2)}) collective-permute-start(bf16[2,192,1024]{2,1,0:T(8,128)(2,1)S(1)} %shard_map.81.refs_0_), channel_id=1, source_target_pairs={{0,16},{16,32},{32,48},{48,0},{1,17},{17,33},{33,49},{49,1},{2,18}... | collective-permute-start | bytes 2359304 | tf_op jit(solution)/shard_map/ppermute | solution.py:181
  75.4 4.0 %collective-permute-start.9 = (bf16[2,192,1024]{2,1,0:T(8,128)(2,1)S(1)}, bf16[2,192,1024]{2,1,0:T(8,128)(2,1)}, u32[]{:S(2)}, u32[]{:S(2)}) collective-permute-start(bf16[2,192,1024]{2,1,0:T(8,128)(2,1)S(1)} %shard_map.81.refs_0_), channel_id=1, source_target_pairs={{0,32},{16,48},{32,0},{48,16},{1,33},{17,49},{33,1},{49,17},{2,34}... | collective-permute-start | bytes 2359304 | tf_op jit(solution)/shard_map/ppermute | solution.py:181
  79.4 3.5 %collective-permute-start.8 = (bf16[2,192,1024]{2,1,0:T(8,128)(2,1)S(1)}, bf16[2,192,1024]{2,1,0:T(8,128)(2,1)}, u32[]{:S(2)}, u32[]{:S(2)}) collective-permute-start(bf16[2,192,1024]{2,1,0:T(8,128)(2,1)S(1)} %shard_map.81.refs_0_), channel_id=1, source_target_pairs={{0,48},{16,0},{32,16},{48,32},{1,49},{17,1},{33,17},{49,33},{2,50}... | collective-permute-start | bytes 2359304 | tf_op jit(solution)/shard_map/ppermute | solution.py:181
  83.0 2.8 %all-to-all-done.1.own_ref = bf16[4,5,96,256]{3,2,1,0:T(8,128)(2,1)S(1)} async-done(((bf16[4,5,96,256]{3,2,1,0:T(8,128)(2,1)}), bf16[4,5,96,256]{3,2,1,0:T(8,128)(2,1)S(1)}, u32[]{:S(2)}, u32[]{:S(2)}) %all-to-all-start.1) | async-done | bytes 983072 | tf_op jit(solution)/shard_map/all_to_all | solution.py:22
  85.8 0.3 shard_map.79
  86.1 0.0 copy-start.2
  86.1 2.5 %all-gather = bf16[8,192,256]{2,1,0:T(8,128)(2,1)S(1)} all-gather(bf16[8,96,256]{2,1,0:T(8,128)(2,1)S(1)} %shard_map.79), channel_id=2, replica_groups=mesh['y'=4,'c'=2,'x'=4,'za'=4,'zb'=4] {'c'}, dimensions={1}, use_global_device_ids=true | all-gather | bytes 1179648 | tf_op jit(solution)/shard_map/all_gather | solution.py:168
  88.6 1.6 %shard_map.80 = bf16[16,24,512]{2,1,0:T(8,128)(2,1)} custom-call(bf16[4,2,192,256]{3,2,1,0:T(8,128)(2,1)S(1)} %bitcast.2, bf16[1024,256]{1,0:T(8,128)(2,1)S(1)} %copy-done, bf16[1024,256]{1,0:T(8,128)(2,1)S(1)} %copy-done.2, bf16[1024,256]{1,0:T(8,128)(2,1)S(1)} %copy-done.6, bf16[1024,256]{1,0:T(8,128)(2,1)S(1)} %copy-done.4), custom_call_target="tpu_custom_call" | custom-call | flops 402653184 | bytes 3276800 | tf_op jit(solution)/shard_map/pallas_call | solution.py:28
  90.3 11.4 %all-to-all-start.2 = ((bf16[16,24,512]{2,1,0:T(8,128)(2,1)}), bf16[16,24,512]{2,1,0:T(8,128)(2,1)S(1)}, u32[]{:S(2)}, u32[]{:S(2)}) async-start(bf16[16,24,512]{2,1,0:T(8,128)(2,1)} %shard_map.80), calls=%async_computation.2 | async-start | bytes 786432 | tf_op jit(solution)/shard_map/all_to_all | solution.py:22
  101.7 1.9 %collective-permute-start.13 = (bf16[2,192,256]{2,1,0:T(8,128)(2,1)S(1)}, bf16[2,192,256]{2,1,0:T(8,128)(2,1)S(1)}, u32[]{:S(2)}, u32[]{:S(2)}) collective-permute-start(bf16[2,192,256]{2,1,0:T(8,128)(2,1)S(1)} %get-tuple-element.35), channel_id=1, source_target_pairs={{0,16},{16,32},{32,48},{48,0},{1,17},{17,33},{33,49},{49,1},{2,18}... | collective-permute-start | bytes 589832 | tf_op jit(solution)/shard_map/ppermute | solution.py:182
  103.7 5.1 %collective-permute-start.12 = (bf16[2,192,256]{2,1,0:T(8,128)(2,1)S(1)}, bf16[2,192,256]{2,1,0:T(8,128)(2,1)S(1)}, u32[]{:S(2)}, u32[]{:S(2)}) collective-permute-start(bf16[2,192,256]{2,1,0:T(8,128)(2,1)S(1)} %get-tuple-element.36), channel_id=1, source_target_pairs={{0,32},{16,48},{32,0},{48,16},{1,33},{17,49},{33,1},{49,17},{2,34}... | collective-permute-start | bytes 589832 | tf_op jit(solution)/shard_map/ppermute | solution.py:182
  108.8 4.7 %collective-permute-done.10.refs_3_ = bf16[2,192,1024]{2,1,0:T(8,128)(2,1)} collective-permute-done((bf16[2,192,1024]{2,1,0:T(8,128)(2,1)S(1)}, bf16[2,192,1024]{2,1,0:T(8,128)(2,1)}, u32[]{:S(2)}, u32[]{:S(2)}) %collective-permute-start.10) | collective-permute-done | bytes 786464 | tf_op jit(solution)/shard_map/ppermute | solution.py:181
  113.5 1.9 %collective-permute-start.11 = (bf16[2,192,256]{2,1,0:T(8,128)(2,1)S(1)}, bf16[2,192,256]{2,1,0:T(8,128)(2,1)S(1)}, u32[]{:S(2)}, u32[]{:S(2)}) collective-permute-start(bf16[2,192,256]{2,1,0:T(8,128)(2,1)S(1)} %get-tuple-element.37), channel_id=1, source_target_pairs={{0,48},{16,0},{32,16},{48,32},{1,49},{17,1},{33,17},{49,33},{2,50}... | collective-permute-start | bytes 589832 | tf_op jit(solution)/shard_map/ppermute | solution.py:182
  115.4 0.0 collective-permute-done.9.refs_2_
  115.4 1.4 %collective-permute-done.8.refs_1_ = bf16[2,192,1024]{2,1,0:T(8,128)(2,1)} collective-permute-done((bf16[2,192,1024]{2,1,0:T(8,128)(2,1)S(1)}, bf16[2,192,1024]{2,1,0:T(8,128)(2,1)}, u32[]{:S(2)}, u32[]{:S(2)}) %collective-permute-start.8) | collective-permute-done | bytes 786464 | tf_op jit(solution)/shard_map/ppermute | solution.py:181
  116.8 4.0 %collective-permute-done.13.refs_6_ = bf16[2,192,256]{2,1,0:T(8,128)(2,1)S(1)} collective-permute-done((bf16[2,192,256]{2,1,0:T(8,128)(2,1)S(1)}, bf16[2,192,256]{2,1,0:T(8,128)(2,1)S(1)}, u32[]{:S(2)}, u32[]{:S(2)}) %collective-permute-start.13) | collective-permute-done | bytes 196640 | tf_op jit(solution)/shard_map/ppermute | solution.py:182
  120.9 0.0 collective-permute-done.12.refs_5_
  120.9 2.5 %collective-permute-done.11.refs_4_ = bf16[2,192,256]{2,1,0:T(8,128)(2,1)S(1)} collective-permute-done((bf16[2,192,256]{2,1,0:T(8,128)(2,1)S(1)}, bf16[2,192,256]{2,1,0:T(8,128)(2,1)S(1)}, u32[]{:S(2)}, u32[]{:S(2)}) %collective-permute-start.11) | collective-permute-done | bytes 196640 | tf_op jit(solution)/shard_map/ppermute | solution.py:182
  123.4 4.0 %shard_map.82 = (f32[1024,256]{1,0:T(8,128)}, f32[256,1024]{1,0:T(8,128)}) custom-call(bf16[4,2,192,256]{3,2,1,0:T(8,128)(2,1)S(1)} %bitcast.3, bf16[2,192,1024]{2,1,0:T(8,128)(2,1)S(1)} %shard_map.81.refs_0_, bf16[2,192,1024]{2,1,0:T(8,128)(2,1)} %collective-permute-done.8.refs_1_, bf16[2,192,1024]{2,1,0:T(8,128)(2,1)} %collective-permute-done.9.refs_2_, ...), custom_call_target="tpu_custom_call" | custom-call | flops 12884901888 | bytes 6619136 | tf_op jit(solution)/shard_map/pallas_call | solution.py:28
  127.4 0.0 all-to-all-done.2.part_ref
  127.4 0.7 shard_map.83
  (16 shorter events, 0.1 us)
Async XLA Ops:
  0.6 0.8 copy-start.7
  1.4 0.8 copy-start.8
  3.1 18.8 %copy-start = (bf16[1024,256]{1,0:T(8,128)(2,1)S(1)}, bf16[1024,256]{1,0:T(8,128)(2,1)}, u32[]{:S(2)}) copy-start(bf16[1024,256]{1,0:T(8,128)(2,1)} %own_ref.3) | copy-start | bytes 1572868
  3.1 41.4 %copy-start.9 = (bf16[96,256]{1,0:T(8,128)(2,1)S(1)}, bf16[96,256]{1,0:T(8,128)(2,1)}, u32[]{:S(2)}) copy-start(bf16[96,256]{1,0:T(8,128)(2,1)} %param.7) | copy-start | bytes 147460
  3.1 54.6 %all-to-all-start = ((bf16[16,48,512]{2,1,0:T(8,128)(2,1)}), bf16[16,48,512]{2,1,0:T(8,128)(2,1)S(1)}, u32[]{:S(2)}, u32[]{:S(2)}) async-start(bf16[16,48,512]{2,1,0:T(8,128)(2,1)} %shard_map.76), calls=%async_computation | async-start | bytes 1572864 | tf_op jit(solution)/shard_map/all_to_all | solution.py:22
  18.4 16.8 %collective-permute-start = (bf16[256,1024]{1,0:T(8,128)(2,1)}, bf16[256,1024]{1,0:T(8,128)(2,1)}, u32[]{:S(2)}, u32[]{:S(2)}) collective-permute-start(bf16[256,1024]{1,0:T(8,128)(2,1)} %own_ref.2), channel_id=1, source_target_pairs={{0,16},{16,32},{32,48},{48,0},{1,17},{17,33},{33,49},{49,1},{2,18}... | collective-permute-start | bytes 1572872 | tf_op jit(solution)/shard_map/ppermute | solution.py:137
  21.9 19.0 %collective-permute-start.3 = (bf16[1024,256]{1,0:T(8,128)(2,1)S(1)}, bf16[1024,256]{1,0:T(8,128)(2,1)S(1)}, u32[]{:S(2)}, u32[]{:S(2)}) collective-permute-start(bf16[1024,256]{1,0:T(8,128)(2,1)S(1)} %copy-done), channel_id=1, source_target_pairs={{0,48},{16,0},{32,16},{48,32},{1,49},{17,1},{33,17},{49,33},{2,50}... | collective-permute-start | bytes 1572872 | tf_op jit(solution)/shard_map/ppermute | solution.py:137
  25.5 24.4 %collective-permute-start.1 = (bf16[256,1024]{1,0:T(8,128)(2,1)}, bf16[256,1024]{1,0:T(8,128)(2,1)}, u32[]{:S(2)}, u32[]{:S(2)}) collective-permute-start(bf16[256,1024]{1,0:T(8,128)(2,1)} %own_ref.2), channel_id=1, source_target_pairs={{0,48},{16,0},{32,16},{48,32},{1,49},{17,1},{33,17},{49,33},{2,50}... | collective-permute-start | bytes 1572872 | tf_op jit(solution)/shard_map/ppermute | solution.py:137
  35.2 18.3 %collective-permute-start.2 = (bf16[256,1024]{1,0:T(8,128)(2,1)}, bf16[256,1024]{1,0:T(8,128)(2,1)}, u32[]{:S(2)}, u32[]{:S(2)}) collective-permute-start(bf16[256,1024]{1,0:T(8,128)(2,1)} %collective-permute-done.before_ref), channel_id=1, source_target_pairs={{0,16},{16,32},{32,48},{48,0},{1,17},{17,33},{33,49},{49,1},{2,18}... | collective-permute-start | bytes 1572872 | tf_op jit(solution)/shard_map/ppermute | solution.py:149
  37.4 26.6 %collective-permute-start.5 = (bf16[1024,256]{1,0:T(8,128)(2,1)S(1)}, bf16[1024,256]{1,0:T(8,128)(2,1)S(1)}, u32[]{:S(2)}, u32[]{:S(2)}) collective-permute-start(bf16[1024,256]{1,0:T(8,128)(2,1)S(1)} %copy-done), channel_id=1, source_target_pairs={{0,16},{16,32},{32,48},{48,0},{1,17},{17,33},{33,49},{49,1},{2,18}... | collective-permute-start | bytes 1572872 | tf_op jit(solution)/shard_map/ppermute | solution.py:137
  40.8 19.9 %copy-start.1 = (bf16[1024,256]{1,0:T(8,128)(2,1)}, bf16[1024,256]{1,0:T(8,128)(2,1)S(1)}, u32[]{:S(2)}) copy-start(bf16[1024,256]{1,0:T(8,128)(2,1)S(1)} %collective-permute-done.3.after_ref) | copy-start | bytes 1572868
  40.9 23.2 %collective-permute-start.6 = (bf16[1024,256]{1,0:T(8,128)(2,1)S(1)}, bf16[1024,256]{1,0:T(8,128)(2,1)S(1)}, u32[]{:S(2)}, u32[]{:S(2)}) collective-permute-start(bf16[1024,256]{1,0:T(8,128)(2,1)S(1)} %collective-permute-done.3.after_ref), channel_id=1, source_target_pairs={{0,48},{16,0},{32,16},{48,32},{1,49},{17,1},{33,17},{49,33},{2,50}... | collective-permute-start | bytes 1572872 | tf_op jit(solution)/shard_map/ppermute | solution.py:151
  44.5 19.5 %collective-permute-start.4 = (bf16[96,256]{1,0:T(8,128)(2,1)S(1)}, bf16[96,256]{1,0:T(8,128)(2,1)S(1)}, u32[]{:S(2)}, u32[]{:S(2)}) collective-permute-start(bf16[96,256]{1,0:T(8,128)(2,1)S(1)} %copy-done.9), channel_id=1, source_target_pairs={{0,0},{16,128},{32,256},{48,384},{128,400},{144,16},{160,144},{176... | collective-permute-start | bytes 147464 | tf_op jit(solution)/shard_map/ppermute | solution.py:147
  64.0 4.6 %copy-start.3 = (bf16[1024,256]{1,0:T(8,128)(2,1)}, bf16[1024,256]{1,0:T(8,128)(2,1)S(1)}, u32[]{:S(2)}) copy-start(bf16[1024,256]{1,0:T(8,128)(2,1)S(1)} %collective-permute-done.5.before_ref) | copy-start | bytes 1572868
  64.0 4.6 %copy-start.5 = (bf16[1024,256]{1,0:T(8,128)(2,1)}, bf16[1024,256]{1,0:T(8,128)(2,1)S(1)}, u32[]{:S(2)}) copy-start(bf16[1024,256]{1,0:T(8,128)(2,1)S(1)} %collective-permute-done.6.far_ref) | copy-start | bytes 1572868
  64.0 3.6 %collective-permute-start.7 = (f32[4,96,256]{2,1,0:T(8,128)S(1)}, f32[4,96,256]{2,1,0:T(8,128)S(1)}, u32[]{:S(2)}, u32[]{:S(2)}) collective-permute-start(f32[4,96,256]{2,1,0:T(8,128)S(1)} %get-tuple-element.25), channel_id=1, source_target_pairs={{0,64},{64,0},{1,65},{65,1},{2,66},{66,2},{3,67},{67,3},{4,68},{68... | collective-permute-start | bytes 1179656 | tf_op jit(solution)/shard_map/ppermute | solution.py:164
  68.7 17.1 %all-to-all-start.1 = ((bf16[4,5,96,256]{3,2,1,0:T(8,128)(2,1)}), bf16[4,5,96,256]{3,2,1,0:T(8,128)(2,1)S(1)}, u32[]{:S(2)}, u32[]{:S(2)}) async-start(bf16[4,5,96,256]{3,2,1,0:T(8,128)(2,1)} %shard_map.78), calls=%async_computation.1 | async-start | bytes 1966080 | tf_op jit(solution)/shard_map/all_to_all | solution.py:22
  73.5 40.0 %collective-permute-start.10 = (bf16[2,192,1024]{2,1,0:T(8,128)(2,1)S(1)}, bf16[2,192,1024]{2,1,0:T(8,128)(2,1)}, u32[]{:S(2)}, u32[]{:S(2)}) collective-permute-start(bf16[2,192,1024]{2,1,0:T(8,128)(2,1)S(1)} %shard_map.81.refs_0_), channel_id=1, source_target_pairs={{0,16},{16,32},{32,48},{48,0},{1,17},{17,33},{33,49},{49,1},{2,18}... | collective-permute-start | bytes 2359304 | tf_op jit(solution)/shard_map/ppermute | solution.py:181
  75.4 40.0 %collective-permute-start.9 = (bf16[2,192,1024]{2,1,0:T(8,128)(2,1)S(1)}, bf16[2,192,1024]{2,1,0:T(8,128)(2,1)}, u32[]{:S(2)}, u32[]{:S(2)}) collective-permute-start(bf16[2,192,1024]{2,1,0:T(8,128)(2,1)S(1)} %shard_map.81.refs_0_), channel_id=1, source_target_pairs={{0,32},{16,48},{32,0},{48,16},{1,33},{17,49},{33,1},{49,17},{2,34}... | collective-permute-start | bytes 2359304 | tf_op jit(solution)/shard_map/ppermute | solution.py:181
  79.4 37.4 %collective-permute-start.8 = (bf16[2,192,1024]{2,1,0:T(8,128)(2,1)S(1)}, bf16[2,192,1024]{2,1,0:T(8,128)(2,1)}, u32[]{:S(2)}, u32[]{:S(2)}) collective-permute-start(bf16[2,192,1024]{2,1,0:T(8,128)(2,1)S(1)} %shard_map.81.refs_0_), channel_id=1, source_target_pairs={{0,48},{16,0},{32,16},{48,32},{1,49},{17,1},{33,17},{49,33},{2,50}... | collective-permute-start | bytes 2359304 | tf_op jit(solution)/shard_map/ppermute | solution.py:181
  85.8 2.8 %copy-start.6 = (bf16[1024,256]{1,0:T(8,128)(2,1)S(1)}, bf16[1024,256]{1,0:T(8,128)(2,1)}, u32[]{:S(2)}) copy-start(bf16[1024,256]{1,0:T(8,128)(2,1)} %copy-done.5) | copy-start | bytes 1572868
  86.1 2.5 %copy-start.2 = (bf16[1024,256]{1,0:T(8,128)(2,1)S(1)}, bf16[1024,256]{1,0:T(8,128)(2,1)}, u32[]{:S(2)}) copy-start(bf16[1024,256]{1,0:T(8,128)(2,1)} %copy-done.1) | copy-start | bytes 1572868
  86.1 2.5 %copy-start.4 = (bf16[1024,256]{1,0:T(8,128)(2,1)S(1)}, bf16[1024,256]{1,0:T(8,128)(2,1)}, u32[]{:S(2)}) copy-start(bf16[1024,256]{1,0:T(8,128)(2,1)} %copy-done.3) | copy-start | bytes 1572868
  90.3 37.1 %all-to-all-start.2 = ((bf16[16,24,512]{2,1,0:T(8,128)(2,1)}), bf16[16,24,512]{2,1,0:T(8,128)(2,1)S(1)}, u32[]{:S(2)}, u32[]{:S(2)}) async-start(bf16[16,24,512]{2,1,0:T(8,128)(2,1)} %shard_map.80), calls=%async_computation.2 | async-start | bytes 786432 | tf_op jit(solution)/shard_map/all_to_all | solution.py:22
  101.7 19.1 %collective-permute-start.13 = (bf16[2,192,256]{2,1,0:T(8,128)(2,1)S(1)}, bf16[2,192,256]{2,1,0:T(8,128)(2,1)S(1)}, u32[]{:S(2)}, u32[]{:S(2)}) collective-permute-start(bf16[2,192,256]{2,1,0:T(8,128)(2,1)S(1)} %get-tuple-element.35), channel_id=1, source_target_pairs={{0,16},{16,32},{32,48},{48,0},{1,17},{17,33},{33,49},{49,1},{2,18}... | collective-permute-start | bytes 589832 | tf_op jit(solution)/shard_map/ppermute | solution.py:182
  103.7 17.2 %collective-permute-start.12 = (bf16[2,192,256]{2,1,0:T(8,128)(2,1)S(1)}, bf16[2,192,256]{2,1,0:T(8,128)(2,1)S(1)}, u32[]{:S(2)}, u32[]{:S(2)}) collective-permute-start(bf16[2,192,256]{2,1,0:T(8,128)(2,1)S(1)} %get-tuple-element.36), channel_id=1, source_target_pairs={{0,32},{16,48},{32,0},{48,16},{1,33},{17,49},{33,1},{49,17},{2,34}... | collective-permute-start | bytes 589832 | tf_op jit(solution)/shard_map/ppermute | solution.py:182
  113.5 9.9 %collective-permute-start.11 = (bf16[2,192,256]{2,1,0:T(8,128)(2,1)S(1)}, bf16[2,192,256]{2,1,0:T(8,128)(2,1)S(1)}, u32[]{:S(2)}, u32[]{:S(2)}) collective-permute-start(bf16[2,192,256]{2,1,0:T(8,128)(2,1)S(1)} %get-tuple-element.37), channel_id=1, source_target_pairs={{0,48},{16,0},{32,16},{48,32},{1,49},{17,1},{33,17},{49,33},{2,50}... | collective-permute-start | bytes 589832 | tf_op jit(solution)/shard_map/ppermute | solution.py:182

commit v18 on v17

--- a/solution.py
+++ b/solution.py
@@ -64,17 +64,21 @@
         tokens_ref[k] = tokens[...].astype(BF)
 
 
-def hidden_kernel(core_ref, both_ref, own_ref, after_ref, far_ref, before_ref, *refs):
-    mine_ref, theirs_ref, rows, grads = refs
+def products(half, weights, out_ref):
+    for d, ref in enumerate(weights):
+        out_ref[d] = times_transposed(half, ref[...])
+
+
+def theirs_kernel(core_ref, both_ref, own_ref, after_ref, far_ref, before_ref, *refs):
+    theirs_ref, half_ref, rows, grads = refs
     put_back(both_ref, 0, rows, grads)
-    first = pl.multiple_of(core_ref[0] * 96, 96)
-    second = pl.multiple_of(96 - core_ref[0] * 96, 96)
-    for start, out_ref in ((second, theirs_ref), (first, mine_ref)):
-        half = grads[pl.ds(start, 96)].astype(BF)
-        out_ref[0] = times_transposed(half, own_ref[...])
-        out_ref[1] = times_transposed(half, after_ref[...])
-        out_ref[2] = times_transposed(half, far_ref[...])
-        out_ref[3] = times_transposed(half, before_ref[...])
+    half_ref[...] = grads[pl.ds(pl.multiple_of(core_ref[0] * 96, 96), 96)].astype(BF)
+    theirs = grads[pl.ds(pl.multiple_of(96 - core_ref[0] * 96, 96), 96)].astype(BF)
+    products(theirs, (own_ref, after_ref, far_ref, before_ref), theirs_ref)
+
+
+def mine_kernel(half_ref, own_ref, after_ref, far_ref, before_ref, mine_ref):
+    products(half_ref[...], (own_ref, after_ref, far_ref, before_ref), mine_ref)
 
 
 def payload_kernel(mine_ref, theirs_ref, turned_ref, out_ref):
@@ -149,18 +153,22 @@
     far = lax.ppermute(before, "x", shift(1))
     up_before, up_after = near_x(up_weight)
     up_far = lax.ppermute(up_after, "x", shift(-1))
-    both, before, after, far, up_after = lax.optimization_barrier((both, before, after, far, up_after))
+    both, before, after, far, up_before, up_after = lax.optimization_barrier(
+        (both, before, after, far, up_before, up_after)
+    )
 
     half = jax.ShapeDtypeStruct((4, 96, 256), F32)
-    mine, theirs = call(
-        hidden_kernel,
-        [half, half],
+    weights = (down_weight, after, far, before)
+    theirs, own_half = call(
+        theirs_kernel,
+        [half, jax.ShapeDtypeStruct((96, 1024), BF)],
         [(16, 48, 512), (192, 1024)],
-        2 * 192 * 1024 * 1024,
-        (core[None], both, down_weight, after, far, before),
+        2 * 96 * 1024 * 1024,
+        (core[None], both, *weights),
         smem=1,
     )
-    theirs, turned, up_before, up_far = lax.optimization_barrier((theirs, turned, up_before, up_far))
+    (mine,) = call(mine_kernel, [half], [], 2 * 96 * 1024 * 1024, (own_half, *weights))
+    theirs, turned, up_far = lax.optimization_barrier((theirs, turned, up_far))
     theirs = lax.ppermute(theirs, "c", [(0, 1), (1, 0)])
     (own,) = call(payload_kernel, [jax.ShapeDtypeStruct((4, 5, 96, 256), BF)], [], 0, (mine, theirs, turned))
     own = exchange(own, "y")

time: 129 us -> 129 us (level)
  the two profiles are of different devices: /device:TPU:24 before, /device:TPU:6 now
where the time goes in v18:
time: 129 us; the launch traced here: 128 us
  starting transfers between devices  76 us (59%)
  waiting for transfers between devices  35.4 us (27%)
  Pallas kernels  11.8 us (9%)
  blocking collectives  2.37 us (2%)
  local copies, waits for them, and re-layouts  1.56 us (1%)
    all_to_all x3, starting transfers between devices, exchange(): lax.all_to_all(blocks, axis, split_axis=0, concat_axis=0, tiled=False)  33.6 us
    pallas_call x9, Pallas kernels, call(): pl.pallas_call(body, out_shape=outs, in_specs=[pl.BlockSpec(memory_space=...  11.8 us
    all_to_all x3, waiting for transfers between devices, exchange(): lax.all_to_all(blocks, axis, split_axis=0, concat_axis=0, tiled=False)  9.83 us
    ppermute x3, starting transfers between devices, local(): all_units = [lax.ppermute(own[k], 'x', shift(k)) for k in (3, 2, 1)]  7.82 us
    ppermute x3, starting transfers between devices, local(): lax.ppermute(tokens, 'x', shift(k))  7.82 us
    ppermute x1, starting transfers between devices, local(): turned = lax.ppermute(preact, ('y', 'x'), swap)  7.26 us
    ppermute x3, waiting for transfers between devices, local(): all_units = [lax.ppermute(own[k], 'x', shift(k)) for k in (3, 2, 1)]  7.24 us
    ppermute x1, waiting for transfers between devices, local(): far = lax.ppermute(before, 'x', shift(1))  6.66 us
  transfers between devices with their start and end apart: 17, of which 13 were waited for; matrix products, arithmetic and copies ran while one was open for 0% of the time, Pallas kernels for 7%

profile of v18, /device:TPU:6, one launch (start us, length us, event | category | flops | bytes accessed | tf_op | source)
XLA Modules:
  0.0 127.9 jit_solution(11073332560055016020)
XLA Ops:
  0.6 0.0 copy-start.2
  0.6 0.7 copy-done.2
  1.4 0.8 copy-done.3
  2.1 0.9 shard_map.76
  3.1 15.3 %all-to-all-start = ((bf16[16,48,512]{2,1,0:T(8,128)(2,1)}), bf16[16,48,512]{2,1,0:T(8,128)(2,1)S(1)}, u32[]{:S(2)}, u32[]{:S(2)}) async-start(bf16[16,48,512]{2,1,0:T(8,128)(2,1)} %shard_map.76), calls=%async_computation | async-start | bytes 1572864 | tf_op jit(solution)/shard_map/all_to_all | solution.py:22
  18.4 2.4 %collective-permute-start = (bf16[256,1024]{1,0:T(8,128)(2,1)S(1)}, bf16[256,1024]{1,0:T(8,128)(2,1)S(1)}, u32[]{:S(2)}, u32[]{:S(2)}) collective-permute-start(bf16[256,1024]{1,0:T(8,128)(2,1)S(1)} %copy-done), channel_id=1, source_target_pairs={{0,16},{16,32},{32,48},{48,0},{1,17},{17,33},{33,49},{49,1},{2,18}... | collective-permute-start | bytes 1572872 | tf_op jit(solution)/shard_map/ppermute | solution.py:141
  20.8 3.5 %collective-permute-start.4 = (bf16[1024,256]{1,0:T(8,128)(2,1)S(1)}, bf16[1024,256]{1,0:T(8,128)(2,1)}, u32[]{:S(2)}, u32[]{:S(2)}) collective-permute-start(bf16[1024,256]{1,0:T(8,128)(2,1)S(1)} %copy-done.1), channel_id=1, source_target_pairs={{0,48},{16,0},{32,16},{48,32},{1,49},{17,1},{33,17},{49,33},{2,50}... | collective-permute-start | bytes 1572872 | tf_op jit(solution)/shard_map/ppermute | solution.py:141
  24.3 3.6 %collective-permute-start.3 = (bf16[1024,256]{1,0:T(8,128)(2,1)S(1)}, bf16[1024,256]{1,0:T(8,128)(2,1)}, u32[]{:S(2)}, u32[]{:S(2)}) collective-permute-start(bf16[1024,256]{1,0:T(8,128)(2,1)S(1)} %copy-done.1), channel_id=1, source_target_pairs={{0,16},{16,32},{32,48},{48,0},{1,17},{17,33},{33,49},{49,1},{2,18}... | collective-permute-start | bytes 1572872 | tf_op jit(solution)/shard_map/ppermute | solution.py:141
  27.9 2.2 %collective-permute-start.1 = (bf16[256,1024]{1,0:T(8,128)(2,1)S(1)}, bf16[256,1024]{1,0:T(8,128)(2,1)S(1)}, u32[]{:S(2)}, u32[]{:S(2)}) collective-permute-start(bf16[256,1024]{1,0:T(8,128)(2,1)S(1)} %copy-done), channel_id=1, source_target_pairs={{0,48},{16,0},{32,16},{48,32},{1,49},{17,1},{33,17},{49,33},{2,50}... | collective-permute-start | bytes 1572872 | tf_op jit(solution)/shard_map/ppermute | solution.py:141
  30.2 5.0 %collective-permute-done.before_ref = bf16[256,1024]{1,0:T(8,128)(2,1)S(1)} collective-permute-done((bf16[256,1024]{1,0:T(8,128)(2,1)S(1)}, bf16[256,1024]{1,0:T(8,128)(2,1)S(1)}, u32[]{:S(2)}, u32[]{:S(2)}) %collective-permute-start) | collective-permute-done | bytes 524320 | tf_op jit(solution)/shard_map/ppermute | solution.py:141
  35.2 3.6 %collective-permute-start.2 = (bf16[256,1024]{1,0:T(8,128)(2,1)S(1)}, bf16[256,1024]{1,0:T(8,128)(2,1)S(1)}, u32[]{:S(2)}, u32[]{:S(2)}) collective-permute-start(bf16[256,1024]{1,0:T(8,128)(2,1)S(1)} %collective-permute-done.before_ref), channel_id=1, source_target_pairs={{0,16},{16,32},{32,48},{48,0},{1,17},{17,33},{33,49},{49,1},{2,18}... | collective-permute-start | bytes 1572872 | tf_op jit(solution)/shard_map/ppermute | solution.py:153
  38.8 0.1 collective-permute-done.4.after_ref
  38.9 2.2 %collective-permute-start.6 = (bf16[1024,256]{1,0:T(8,128)(2,1)}, bf16[1024,256]{1,0:T(8,128)(2,1)}, u32[]{:S(2)}, u32[]{:S(2)}) collective-permute-start(bf16[1024,256]{1,0:T(8,128)(2,1)} %collective-permute-done.4.after_ref), channel_id=1, source_target_pairs={{0,48},{16,0},{32,16},{48,32},{1,49},{17,1},{33,17},{49,33},{2,50}... | collective-permute-start | bytes 1572872 | tf_op jit(solution)/shard_map/ppermute | solution.py:155
  41.2 0.0 copy-done.4
  41.2 7.3 %collective-permute-start.5 = (bf16[96,256]{1,0:T(8,128)(2,1)S(1)}, bf16[96,256]{1,0:T(8,128)(2,1)S(1)}, u32[]{:S(2)}, u32[]{:S(2)}) collective-permute-start(bf16[96,256]{1,0:T(8,128)(2,1)S(1)} %copy-done.4), channel_id=1, source_target_pairs={{0,0},{16,128},{32,256},{48,384},{128,400},{144,16},{160,144},{176... | collective-permute-start | bytes 147464 | tf_op jit(solution)/shard_map/ppermute | solution.py:151
  48.4 0.0 collective-permute-done.3.before_ref
  48.5 1.6 %collective-permute-done.1.after_ref = bf16[256,1024]{1,0:T(8,128)(2,1)S(1)} collective-permute-done((bf16[256,1024]{1,0:T(8,128)(2,1)S(1)}, bf16[256,1024]{1,0:T(8,128)(2,1)S(1)}, u32[]{:S(2)}, u32[]{:S(2)}) %collective-permute-start.1) | collective-permute-done | bytes 524320 | tf_op jit(solution)/shard_map/ppermute | solution.py:141
  50.1 6.7 %collective-permute-done.2.far_ref = bf16[256,1024]{1,0:T(8,128)(2,1)S(1)} collective-permute-done((bf16[256,1024]{1,0:T(8,128)(2,1)S(1)}, bf16[256,1024]{1,0:T(8,128)(2,1)S(1)}, u32[]{:S(2)}, u32[]{:S(2)}) %collective-permute-start.2) | collective-permute-done | bytes 524320 | tf_op jit(solution)/shard_map/ppermute | solution.py:153
  56.7 1.0 all-to-all-done.both_ref
  57.8 0.9 shard_map.77
  58.6 0.0 collective-permute-done.5.turned_ref
  58.6 1.0 collective-permute-done.6.far_ref
  59.6 1.9 %collective-permute-start.7 = (f32[4,96,256]{2,1,0:T(8,128)S(1)}, f32[4,96,256]{2,1,0:T(8,128)S(1)}, u32[]{:S(2)}, u32[]{:S(2)}) collective-permute-start(f32[4,96,256]{2,1,0:T(8,128)S(1)} %get-tuple-element.25), channel_id=1, source_target_pairs={{0,64},{64,0},{1,65},{65,1},{2,66},{66,2},{3,67},{67,3},{4,68},{68... | collective-permute-start | bytes 1179656 | tf_op jit(solution)/shard_map/ppermute | solution.py:172
  61.6 0.8 shard_map.78.mine_ref
  62.3 0.9 collective-permute-done.7.theirs_ref
  63.2 1.0 shard_map.79
  64.3 6.6 %all-to-all-start.1 = ((bf16[4,5,96,256]{3,2,1,0:T(8,128)(2,1)}), bf16[4,5,96,256]{3,2,1,0:T(8,128)(2,1)S(1)}, u32[]{:S(2)}, u32[]{:S(2)}) async-start(bf16[4,5,96,256]{3,2,1,0:T(8,128)(2,1)} %shard_map.79), calls=%async_computation.1 | async-start | bytes 1966080 | tf_op jit(solution)/shard_map/all_to_all | solution.py:22
  70.8 0.3 shard_map.82.refs_0_
  71.1 1.9 %collective-permute-start.10 = (bf16[2,192,1024]{2,1,0:T(8,128)(2,1)S(1)}, bf16[2,192,1024]{2,1,0:T(8,128)(2,1)}, u32[]{:S(2)}, u32[]{:S(2)}) collective-permute-start(bf16[2,192,1024]{2,1,0:T(8,128)(2,1)S(1)} %shard_map.82.refs_0_), channel_id=1, source_target_pairs={{0,16},{16,32},{32,48},{48,0},{1,17},{17,33},{33,49},{49,1},{2,18}... | collective-permute-start | bytes 2359304 | tf_op jit(solution)/shard_map/ppermute | solution.py:189
  73.1 2.7 %collective-permute-start.9 = (bf16[2,192,1024]{2,1,0:T(8,128)(2,1)S(1)}, bf16[2,192,1024]{2,1,0:T(8,128)(2,1)}, u32[]{:S(2)}, u32[]{:S(2)}) collective-permute-start(bf16[2,192,1024]{2,1,0:T(8,128)(2,1)S(1)} %shard_map.82.refs_0_), channel_id=1, source_target_pairs={{0,32},{16,48},{32,0},{48,16},{1,33},{17,49},{33,1},{49,17},{2,34}... | collective-permute-start | bytes 2359304 | tf_op jit(solution)/shard_map/ppermute | solution.py:189
  75.8 3.2 %collective-permute-start.8 = (bf16[2,192,1024]{2,1,0:T(8,128)(2,1)S(1)}, bf16[2,192,1024]{2,1,0:T(8,128)(2,1)}, u32[]{:S(2)}, u32[]{:S(2)}) collective-permute-start(bf16[2,192,1024]{2,1,0:T(8,128)(2,1)S(1)} %shard_map.82.refs_0_), channel_id=1, source_target_pairs={{0,48},{16,0},{32,16},{48,32},{1,49},{17,1},{33,17},{49,33},{2,50}... | collective-permute-start | bytes 2359304 | tf_op jit(solution)/shard_map/ppermute | solution.py:189
  79.0 6.6 %all-to-all-done.1.own_ref = bf16[4,5,96,256]{3,2,1,0:T(8,128)(2,1)S(1)} async-done(((bf16[4,5,96,256]{3,2,1,0:T(8,128)(2,1)}), bf16[4,5,96,256]{3,2,1,0:T(8,128)(2,1)S(1)}, u32[]{:S(2)}, u32[]{:S(2)}) %all-to-all-start.1) | async-done | bytes 983072 | tf_op jit(solution)/shard_map/all_to_all | solution.py:22
  85.5 0.3 shard_map.80
  85.8 2.4 %all-gather = bf16[8,192,256]{2,1,0:T(8,128)(2,1)S(1)} all-gather(bf16[8,96,256]{2,1,0:T(8,128)(2,1)S(1)} %shard_map.80), channel_id=2, replica_groups=mesh['y'=4,'c'=2,'x'=4,'za'=4,'zb'=4] {'c'}, dimensions={1}, use_global_device_ids=true | all-gather | bytes 1179648 | tf_op jit(solution)/shard_map/all_gather | solution.py:176
  88.2 3.0 %shard_map.81 = bf16[16,24,512]{2,1,0:T(8,128)(2,1)} custom-call(bf16[4,2,192,256]{3,2,1,0:T(8,128)(2,1)S(1)} %bitcast.2, bf16[1024,256]{1,0:T(8,128)(2,1)S(1)} %copy-done.1, bf16[1024,256]{1,0:T(8,128)(2,1)} %collective-permute-done.4.after_ref, bf16[1024,256]{1,0:T(8,128)(2,1)} %collective-permute-done.6.far_ref, ...), custom_call_target="tpu_custom_call" | custom-call | flops 402653184 | bytes 3276800 | tf_op jit(solution)/shard_map/pallas_call | solution.py:28
  91.2 11.7 %all-to-all-start.2 = ((bf16[16,24,512]{2,1,0:T(8,128)(2,1)}), bf16[16,24,512]{2,1,0:T(8,128)(2,1)S(1)}, u32[]{:S(2)}, u32[]{:S(2)}) async-start(bf16[16,24,512]{2,1,0:T(8,128)(2,1)} %shard_map.81), calls=%async_computation.2 | async-start | bytes 786432 | tf_op jit(solution)/shard_map/all_to_all | solution.py:22
  103.0 1.9 %collective-permute-start.13 = (bf16[2,192,256]{2,1,0:T(8,128)(2,1)S(1)}, bf16[2,192,256]{2,1,0:T(8,128)(2,1)S(1)}, u32[]{:S(2)}, u32[]{:S(2)}) collective-permute-start(bf16[2,192,256]{2,1,0:T(8,128)(2,1)S(1)} %get-tuple-element.35), channel_id=1, source_target_pairs={{0,16},{16,32},{32,48},{48,0},{1,17},{17,33},{33,49},{49,1},{2,18}... | collective-permute-start | bytes 589832 | tf_op jit(solution)/shard_map/ppermute | solution.py:190
  104.9 2.7 %collective-permute-start.12 = (bf16[2,192,256]{2,1,0:T(8,128)(2,1)S(1)}, bf16[2,192,256]{2,1,0:T(8,128)(2,1)S(1)}, u32[]{:S(2)}, u32[]{:S(2)}) collective-permute-start(bf16[2,192,256]{2,1,0:T(8,128)(2,1)S(1)} %get-tuple-element.36), channel_id=1, source_target_pairs={{0,32},{16,48},{32,0},{48,16},{1,33},{17,49},{33,1},{49,17},{2,34}... | collective-permute-start | bytes 589832 | tf_op jit(solution)/shard_map/ppermute | solution.py:190
  107.6 0.0 collective-permute-done.10.refs_3_
  107.6 3.2 %collective-permute-start.11 = (bf16[2,192,256]{2,1,0:T(8,128)(2,1)S(1)}, bf16[2,192,256]{2,1,0:T(8,128)(2,1)S(1)}, u32[]{:S(2)}, u32[]{:S(2)}) collective-permute-start(bf16[2,192,256]{2,1,0:T(8,128)(2,1)S(1)} %get-tuple-element.37), channel_id=1, source_target_pairs={{0,48},{16,0},{32,16},{48,32},{1,49},{17,1},{33,17},{49,33},{2,50}... | collective-permute-start | bytes 589832 | tf_op jit(solution)/shard_map/ppermute | solution.py:190
  110.8 0.0 collective-permute-done.9.refs_2_
  110.8 3.0 %collective-permute-done.8.refs_1_ = bf16[2,192,1024]{2,1,0:T(8,128)(2,1)} collective-permute-done((bf16[2,192,1024]{2,1,0:T(8,128)(2,1)S(1)}, bf16[2,192,1024]{2,1,0:T(8,128)(2,1)}, u32[]{:S(2)}, u32[]{:S(2)}) %collective-permute-start.8) | collective-permute-done | bytes 786464 | tf_op jit(solution)/shard_map/ppermute | solution.py:189
  113.8 0.8 collective-permute-done.13.refs_6_
  114.6 3.5 %collective-permute-done.12.refs_5_ = bf16[2,192,256]{2,1,0:T(8,128)(2,1)S(1)} collective-permute-done((bf16[2,192,256]{2,1,0:T(8,128)(2,1)S(1)}, bf16[2,192,256]{2,1,0:T(8,128)(2,1)S(1)}, u32[]{:S(2)}, u32[]{:S(2)}) %collective-permute-start.12) | collective-permute-done | bytes 196640 | tf_op jit(solution)/shard_map/ppermute | solution.py:190
  118.0 3.0 %collective-permute-done.11.refs_4_ = bf16[2,192,256]{2,1,0:T(8,128)(2,1)S(1)} collective-permute-done((bf16[2,192,256]{2,1,0:T(8,128)(2,1)S(1)}, bf16[2,192,256]{2,1,0:T(8,128)(2,1)S(1)}, u32[]{:S(2)}, u32[]{:S(2)}) %collective-permute-start.11) | collective-permute-done | bytes 196640 | tf_op jit(solution)/shard_map/ppermute | solution.py:190
  121.0 4.0 %shard_map.83 = (f32[1024,256]{1,0:T(8,128)}, f32[256,1024]{1,0:T(8,128)}) custom-call(bf16[4,2,192,256]{3,2,1,0:T(8,128)(2,1)S(1)} %bitcast.3, bf16[2,192,1024]{2,1,0:T(8,128)(2,1)S(1)} %shard_map.82.refs_0_, bf16[2,192,1024]{2,1,0:T(8,128)(2,1)} %collective-permute-done.8.refs_1_, bf16[2,192,1024]{2,1,0:T(8,128)(2,1)} %collective-permute-done.9.refs_2_, ...), custom_call_target="tpu_custom_call" | custom-call | flops 12884901888 | bytes 6619136 | tf_op jit(solution)/shard_map/pallas_call | solution.py:28
  125.0 2.2 %all-to-all-done.2.part_ref = bf16[16,24,512]{2,1,0:T(8,128)(2,1)S(1)} async-done(((bf16[16,24,512]{2,1,0:T(8,128)(2,1)}), bf16[16,24,512]{2,1,0:T(8,128)(2,1)S(1)}, u32[]{:S(2)}, u32[]{:S(2)}) %all-to-all-start.2) | async-done | bytes 393248 | tf_op jit(solution)/shard_map/all_to_all | solution.py:22
  127.2 0.7 shard_map.84
  (7 shorter events, 0.1 us)
Async XLA Ops:
  0.6 0.8 copy-start.2
  1.4 0.8 copy-start.3
  3.1 15.3 %copy-start = (bf16[256,1024]{1,0:T(8,128)(2,1)S(1)}, bf16[256,1024]{1,0:T(8,128)(2,1)}, u32[]{:S(2)}) copy-start(bf16[256,1024]{1,0:T(8,128)(2,1)} %own_ref.4) | copy-start | bytes 1572868
  3.1 17.7 %copy-start.1 = (bf16[1024,256]{1,0:T(8,128)(2,1)S(1)}, bf16[1024,256]{1,0:T(8,128)(2,1)}, u32[]{:S(2)}) copy-start(bf16[1024,256]{1,0:T(8,128)(2,1)} %own_ref.5) | copy-start | bytes 1572868
  3.1 38.1 %copy-start.4 = (bf16[96,256]{1,0:T(8,128)(2,1)S(1)}, bf16[96,256]{1,0:T(8,128)(2,1)}, u32[]{:S(2)}) copy-start(bf16[96,256]{1,0:T(8,128)(2,1)} %param.7) | copy-start | bytes 147460
  3.1 54.6 %all-to-all-start = ((bf16[16,48,512]{2,1,0:T(8,128)(2,1)}), bf16[16,48,512]{2,1,0:T(8,128)(2,1)S(1)}, u32[]{:S(2)}, u32[]{:S(2)}) async-start(bf16[16,48,512]{2,1,0:T(8,128)(2,1)} %shard_map.76), calls=%async_computation | async-start | bytes 1572864 | tf_op jit(solution)/shard_map/all_to_all | solution.py:22
  18.4 16.7 %collective-permute-start = (bf16[256,1024]{1,0:T(8,128)(2,1)S(1)}, bf16[256,1024]{1,0:T(8,128)(2,1)S(1)}, u32[]{:S(2)}, u32[]{:S(2)}) collective-permute-start(bf16[256,1024]{1,0:T(8,128)(2,1)S(1)} %copy-done), channel_id=1, source_target_pairs={{0,16},{16,32},{32,48},{48,0},{1,17},{17,33},{33,49},{49,1},{2,18}... | collective-permute-start | bytes 1572872 | tf_op jit(solution)/shard_map/ppermute | solution.py:141
  20.8 18.1 %collective-permute-start.4 = (bf16[1024,256]{1,0:T(8,128)(2,1)S(1)}, bf16[1024,256]{1,0:T(8,128)(2,1)}, u32[]{:S(2)}, u32[]{:S(2)}) collective-permute-start(bf16[1024,256]{1,0:T(8,128)(2,1)S(1)} %copy-done.1), channel_id=1, source_target_pairs={{0,48},{16,0},{32,16},{48,32},{1,49},{17,1},{33,17},{49,33},{2,50}... | collective-permute-start | bytes 1572872 | tf_op jit(solution)/shard_map/ppermute | solution.py:141
  24.3 24.1 %collective-permute-start.3 = (bf16[1024,256]{1,0:T(8,128)(2,1)S(1)}, bf16[1024,256]{1,0:T(8,128)(2,1)}, u32[]{:S(2)}, u32[]{:S(2)}) collective-permute-start(bf16[1024,256]{1,0:T(8,128)(2,1)S(1)} %copy-done.1), channel_id=1, source_target_pairs={{0,16},{16,32},{32,48},{48,0},{1,17},{17,33},{33,49},{49,1},{2,18}... | collective-permute-start | bytes 1572872 | tf_op jit(solution)/shard_map/ppermute | solution.py:141
  27.9 22.1 %collective-permute-start.1 = (bf16[256,1024]{1,0:T(8,128)(2,1)S(1)}, bf16[256,1024]{1,0:T(8,128)(2,1)S(1)}, u32[]{:S(2)}, u32[]{:S(2)}) collective-permute-start(bf16[256,1024]{1,0:T(8,128)(2,1)S(1)} %copy-done), channel_id=1, source_target_pairs={{0,48},{16,0},{32,16},{48,32},{1,49},{17,1},{33,17},{49,33},{2,50}... | collective-permute-start | bytes 1572872 | tf_op jit(solution)/shard_map/ppermute | solution.py:141
  35.2 21.5 %collective-permute-start.2 = (bf16[256,1024]{1,0:T(8,128)(2,1)S(1)}, bf16[256,1024]{1,0:T(8,128)(2,1)S(1)}, u32[]{:S(2)}, u32[]{:S(2)}) collective-permute-start(bf16[256,1024]{1,0:T(8,128)(2,1)S(1)} %collective-permute-done.before_ref), channel_id=1, source_target_pairs={{0,16},{16,32},{32,48},{48,0},{1,17},{17,33},{33,49},{49,1},{2,18}... | collective-permute-start | bytes 1572872 | tf_op jit(solution)/shard_map/ppermute | solution.py:153
  38.9 20.7 %collective-permute-start.6 = (bf16[1024,256]{1,0:T(8,128)(2,1)}, bf16[1024,256]{1,0:T(8,128)(2,1)}, u32[]{:S(2)}, u32[]{:S(2)}) collective-permute-start(bf16[1024,256]{1,0:T(8,128)(2,1)} %collective-permute-done.4.after_ref), channel_id=1, source_target_pairs={{0,48},{16,0},{32,16},{48,32},{1,49},{17,1},{33,17},{49,33},{2,50}... | collective-permute-start | bytes 1572872 | tf_op jit(solution)/shard_map/ppermute | solution.py:155
  41.2 17.5 %collective-permute-start.5 = (bf16[96,256]{1,0:T(8,128)(2,1)S(1)}, bf16[96,256]{1,0:T(8,128)(2,1)S(1)}, u32[]{:S(2)}, u32[]{:S(2)}) collective-permute-start(bf16[96,256]{1,0:T(8,128)(2,1)S(1)} %copy-done.4), channel_id=1, source_target_pairs={{0,0},{16,128},{32,256},{48,384},{128,400},{144,16},{160,144},{176... | collective-permute-start | bytes 147464 | tf_op jit(solution)/shard_map/ppermute | solution.py:151
  59.6 3.6 %collective-permute-start.7 = (f32[4,96,256]{2,1,0:T(8,128)S(1)}, f32[4,96,256]{2,1,0:T(8,128)S(1)}, u32[]{:S(2)}, u32[]{:S(2)}) collective-permute-start(f32[4,96,256]{2,1,0:T(8,128)S(1)} %get-tuple-element.25), channel_id=1, source_target_pairs={{0,64},{64,0},{1,65},{65,1},{2,66},{66,2},{3,67},{67,3},{4,68},{68... | collective-permute-start | bytes 1179656 | tf_op jit(solution)/shard_map/ppermute | solution.py:172
  64.3 21.3 %all-to-all-start.1 = ((bf16[4,5,96,256]{3,2,1,0:T(8,128)(2,1)}), bf16[4,5,96,256]{3,2,1,0:T(8,128)(2,1)S(1)}, u32[]{:S(2)}, u32[]{:S(2)}) async-start(bf16[4,5,96,256]{3,2,1,0:T(8,128)(2,1)} %shard_map.79), calls=%async_computation.1 | async-start | bytes 1966080 | tf_op jit(solution)/shard_map/all_to_all | solution.py:22
  71.1 36.5 %collective-permute-start.10 = (bf16[2,192,1024]{2,1,0:T(8,128)(2,1)S(1)}, bf16[2,192,1024]{2,1,0:T(8,128)(2,1)}, u32[]{:S(2)}, u32[]{:S(2)}) collective-permute-start(bf16[2,192,1024]{2,1,0:T(8,128)(2,1)S(1)} %shard_map.82.refs_0_), channel_id=1, source_target_pairs={{0,16},{16,32},{32,48},{48,0},{1,17},{17,33},{33,49},{49,1},{2,18}... | collective-permute-start | bytes 2359304 | tf_op jit(solution)/shard_map/ppermute | solution.py:189
  73.1 37.8 %collective-permute-start.9 = (bf16[2,192,1024]{2,1,0:T(8,128)(2,1)S(1)}, bf16[2,192,1024]{2,1,0:T(8,128)(2,1)}, u32[]{:S(2)}, u32[]{:S(2)}) collective-permute-start(bf16[2,192,1024]{2,1,0:T(8,128)(2,1)S(1)} %shard_map.82.refs_0_), channel_id=1, source_target_pairs={{0,32},{16,48},{32,0},{48,16},{1,33},{17,49},{33,1},{49,17},{2,34}... | collective-permute-start | bytes 2359304 | tf_op jit(solution)/shard_map/ppermute | solution.py:189
  75.8 38.0 %collective-permute-start.8 = (bf16[2,192,1024]{2,1,0:T(8,128)(2,1)S(1)}, bf16[2,192,1024]{2,1,0:T(8,128)(2,1)}, u32[]{:S(2)}, u32[]{:S(2)}) collective-permute-start(bf16[2,192,1024]{2,1,0:T(8,128)(2,1)S(1)} %shard_map.82.refs_0_), channel_id=1, source_target_pairs={{0,48},{16,0},{32,16},{48,32},{1,49},{17,1},{33,17},{49,33},{2,50}... | collective-permute-start | bytes 2359304 | tf_op jit(solution)/shard_map/ppermute | solution.py:189
  91.2 36.0 %all-to-all-start.2 = ((bf16[16,24,512]{2,1,0:T(8,128)(2,1)}), bf16[16,24,512]{2,1,0:T(8,128)(2,1)S(1)}, u32[]{:S(2)}, u32[]{:S(2)}) async-start(bf16[16,24,512]{2,1,0:T(8,128)(2,1)} %shard_map.81), calls=%async_computation.2 | async-start | bytes 786432 | tf_op jit(solution)/shard_map/all_to_all | solution.py:22
  103.0 11.6 %collective-permute-start.13 = (bf16[2,192,256]{2,1,0:T(8,128)(2,1)S(1)}, bf16[2,192,256]{2,1,0:T(8,128)(2,1)S(1)}, u32[]{:S(2)}, u32[]{:S(2)}) collective-permute-start(bf16[2,192,256]{2,1,0:T(8,128)(2,1)S(1)} %get-tuple-element.35), channel_id=1, source_target_pairs={{0,16},{16,32},{32,48},{48,0},{1,17},{17,33},{33,49},{49,1},{2,18}... | collective-permute-start | bytes 589832 | tf_op jit(solution)/shard_map/ppermute | solution.py:190
  104.9 13.1 %collective-permute-start.12 = (bf16[2,192,256]{2,1,0:T(8,128)(2,1)S(1)}, bf16[2,192,256]{2,1,0:T(8,128)(2,1)S(1)}, u32[]{:S(2)}, u32[]{:S(2)}) collective-permute-start(bf16[2,192,256]{2,1,0:T(8,128)(2,1)S(1)} %get-tuple-element.36), channel_id=1, source_target_pairs={{0,32},{16,48},{32,0},{48,16},{1,33},{17,49},{33,1},{49,17},{2,34}... | collective-permute-start | bytes 589832 | tf_op jit(solution)/shard_map/ppermute | solution.py:190
  107.6 13.4 %collective-permute-start.11 = (bf16[2,192,256]{2,1,0:T(8,128)(2,1)S(1)}, bf16[2,192,256]{2,1,0:T(8,128)(2,1)S(1)}, u32[]{:S(2)}, u32[]{:S(2)}) collective-permute-start(bf16[2,192,256]{2,1,0:T(8,128)(2,1)S(1)} %get-tuple-element.37), channel_id=1, source_target_pairs={{0,48},{16,0},{32,16},{48,32},{1,49},{17,1},{33,17},{49,33},{2,50}... | collective-permute-start | bytes 589832 | tf_op jit(solution)/shard_map/ppermute | solution.py:190

commit v19 on v18

--- a/solution.py
+++ b/solution.py
@@ -22,15 +22,17 @@
     return lax.all_to_all(blocks, axis, split_axis=0, concat_axis=0, tiled=False)
 
 
-def call(body, outs, scratch, flops, operands, smem=0):
+def call(body, outs, scratch, flops, operands, smem=0, copied=0):
     moved = sum(a.size * a.dtype.itemsize for a in (*operands, *outs))
-    spaces = [pltpu.SMEM] * smem + [pltpu.VMEM] * (len(operands) - smem)
+    spaces = [pltpu.SMEM] * smem + [pltpu.VMEM] * (len(operands) - smem - copied) + [pl.ANY] * copied
     return pl.pallas_call(
         body,
         out_shape=outs,
         in_specs=[pl.BlockSpec(memory_space=space) for space in spaces],
         out_specs=[pl.BlockSpec(memory_space=pltpu.VMEM)] * len(outs),
-        scratch_shapes=[pltpu.VMEM(shape, F32) for shape in scratch],
+        scratch_shapes=[pltpu.VMEM(shape, F32) for shape in scratch]
+        + [pltpu.VMEM(a.shape, a.dtype) for a in operands[len(operands) - copied :]]
+        + [pltpu.SemaphoreType.DMA] * copied,
         cost_estimate=pl.CostEstimate(flops=flops, bytes_accessed=moved, transcendentals=0),
         compiler_params=pltpu.CompilerParams(vmem_limit_bytes=16 * 2**20),
     )(*operands)
@@ -98,11 +100,18 @@
         out_ref[2 * d + 1] = activ.astype(BF)
 
 
-def part_kernel(pregrad_ref, own_ref, after_ref, far_ref, before_ref, out_ref, total, rows):
-    total[...] = times_transposed(pregrad_ref[0, 0], own_ref[...])
-    total[...] += times_transposed(pregrad_ref[1, 0], after_ref[...])
-    total[...] += times_transposed(pregrad_ref[2, 0], far_ref[...])
-    total[...] += times_transposed(pregrad_ref[3, 0], before_ref[...])
+def part_kernel(pregrad_ref, own_ref, after_ref, far_ref, before_ref, out_ref, total, rows, *copies):
+    blocks = copies[:4]
+    moves = [
+        pltpu.make_async_copy(*move)
+        for move in zip((own_ref, after_ref, far_ref, before_ref), blocks, copies[4:])
+    ]
+    for move in moves:
+        move.start()
+    for d in range(4):
+        moves[d].wait()
+        product = times_transposed(pregrad_ref[d, 0], blocks[d][...])
+        total[...] = product if d == 0 else total[...] + product
     for z in range(16):
         here = slice(12 * z, 12 * z + 12)
         rows[z, 0:12] = total[here, :512]
@@ -181,6 +190,7 @@
         [(192, 1024), (16, 24, 512)],
         2 * 192 * 1024 * 1024,
         (own, up_weight, up_after, up_far, up_before),
+        copied=4,
     )
     part = exchange(part, ("za", "zb"))
 

time: 129 us -> 129 us (level)
  no operation moved by 1% of the time
where the time goes in v19:
time: 129 us; the launch traced here: 128 us
  starting transfers between devices  76 us (59%)
  waiting for transfers between devices  35.4 us (27%)
  Pallas kernels  11.5 us (9%)
  blocking collectives  2.37 us (2%)
  local copies, waits for them, and re-layouts  1.56 us (1%)
    all_to_all x3, starting transfers between devices, exchange(): lax.all_to_all(blocks, axis, split_axis=0, concat_axis=0, tiled=False)  33.7 us
    pallas_call x9, Pallas kernels, call(): pl.pallas_call(body, out_shape=outs, in_specs=[pl.BlockSpec(memory_space=...  11.5 us
    all_to_all x3, waiting for transfers between devices, exchange(): lax.all_to_all(blocks, axis, split_axis=0, concat_axis=0, tiled=False)  9.51 us
    ppermute x3, starting transfers between devices, local(): lax.ppermute(tokens, 'x', shift(k))  7.82 us
    ppermute x3, starting transfers between devices, local(): all_units = [lax.ppermute(own[k], 'x', shift(k)) for k in (3, 2, 1)]  7.82 us
    ppermute x1, starting transfers between devices, local(): turned = lax.ppermute(preact, ('y', 'x'), swap)  7.26 us
    ppermute x3, waiting for transfers between devices, local(): all_units = [lax.ppermute(own[k], 'x', shift(k)) for k in (3, 2, 1)]  7.09 us
    ppermute x1, waiting for transfers between devices, local(): far = lax.ppermute(before, 'x', shift(1))  6.66 us
  transfers between devices with their start and end apart: 17, of which 13 were waited for; matrix products, arithmetic and copies ran while one was open for 0% of the time, Pallas kernels for 7%

profile of v19, /device:TPU:6, one launch (start us, length us, event | category | flops | bytes accessed | tf_op | source)
XLA Modules:
  0.0 127.6 jit_solution(8131385520283751822)
XLA Ops:
  0.6 0.0 copy-start.2
  0.6 0.7 copy-done.2
  1.4 0.8 copy-done.3
  2.1 0.9 shard_map.76
  3.1 15.3 %all-to-all-start = ((bf16[16,48,512]{2,1,0:T(8,128)(2,1)}), bf16[16,48,512]{2,1,0:T(8,128)(2,1)S(1)}, u32[]{:S(2)}, u32[]{:S(2)}) async-start(bf16[16,48,512]{2,1,0:T(8,128)(2,1)} %shard_map.76), calls=%async_computation | async-start | bytes 1572864 | tf_op jit(solution)/shard_map/all_to_all | solution.py:22
  18.4 0.0 copy-done
  18.4 2.4 %collective-permute-start = (bf16[256,1024]{1,0:T(8,128)(2,1)S(1)}, bf16[256,1024]{1,0:T(8,128)(2,1)S(1)}, u32[]{:S(2)}, u32[]{:S(2)}) collective-permute-start(bf16[256,1024]{1,0:T(8,128)(2,1)S(1)} %copy-done), channel_id=1, source_target_pairs={{0,16},{16,32},{32,48},{48,0},{1,17},{17,33},{33,49},{49,1},{2,18}... | collective-permute-start | bytes 1572872 | tf_op jit(solution)/shard_map/ppermute | solution.py:150
  20.8 3.5 %collective-permute-start.4 = (bf16[1024,256]{1,0:T(8,128)(2,1)S(1)}, bf16[1024,256]{1,0:T(8,128)(2,1)}, u32[]{:S(2)}, u32[]{:S(2)}) collective-permute-start(bf16[1024,256]{1,0:T(8,128)(2,1)S(1)} %copy-done.1), channel_id=1, source_target_pairs={{0,48},{16,0},{32,16},{48,32},{1,49},{17,1},{33,17},{49,33},{2,50}... | collective-permute-start | bytes 1572872 | tf_op jit(solution)/shard_map/ppermute | solution.py:150
  24.3 3.6 %collective-permute-start.3 = (bf16[1024,256]{1,0:T(8,128)(2,1)S(1)}, bf16[1024,256]{1,0:T(8,128)(2,1)}, u32[]{:S(2)}, u32[]{:S(2)}) collective-permute-start(bf16[1024,256]{1,0:T(8,128)(2,1)S(1)} %copy-done.1), channel_id=1, source_target_pairs={{0,16},{16,32},{32,48},{48,0},{1,17},{17,33},{33,49},{49,1},{2,18}... | collective-permute-start | bytes 1572872 | tf_op jit(solution)/shard_map/ppermute | solution.py:150
  27.9 2.2 %collective-permute-start.1 = (bf16[256,1024]{1,0:T(8,128)(2,1)S(1)}, bf16[256,1024]{1,0:T(8,128)(2,1)S(1)}, u32[]{:S(2)}, u32[]{:S(2)}) collective-permute-start(bf16[256,1024]{1,0:T(8,128)(2,1)S(1)} %copy-done), channel_id=1, source_target_pairs={{0,48},{16,0},{32,16},{48,32},{1,49},{17,1},{33,17},{49,33},{2,50}... | collective-permute-start | bytes 1572872 | tf_op jit(solution)/shard_map/ppermute | solution.py:150
  30.2 5.0 %collective-permute-done.before_ref = bf16[256,1024]{1,0:T(8,128)(2,1)S(1)} collective-permute-done((bf16[256,1024]{1,0:T(8,128)(2,1)S(1)}, bf16[256,1024]{1,0:T(8,128)(2,1)S(1)}, u32[]{:S(2)}, u32[]{:S(2)}) %collective-permute-start) | collective-permute-done | bytes 524320 | tf_op jit(solution)/shard_map/ppermute | solution.py:150
  35.2 3.6 %collective-permute-start.2 = (bf16[256,1024]{1,0:T(8,128)(2,1)S(1)}, bf16[256,1024]{1,0:T(8,128)(2,1)S(1)}, u32[]{:S(2)}, u32[]{:S(2)}) collective-permute-start(bf16[256,1024]{1,0:T(8,128)(2,1)S(1)} %collective-permute-done.before_ref), channel_id=1, source_target_pairs={{0,16},{16,32},{32,48},{48,0},{1,17},{17,33},{33,49},{49,1},{2,18}... | collective-permute-start | bytes 1572872 | tf_op jit(solution)/shard_map/ppermute | solution.py:162
  38.8 0.1 collective-permute-done.4.after_ref
  38.9 2.2 %collective-permute-start.6 = (bf16[1024,256]{1,0:T(8,128)(2,1)}, bf16[1024,256]{1,0:T(8,128)(2,1)}, u32[]{:S(2)}, u32[]{:S(2)}) collective-permute-start(bf16[1024,256]{1,0:T(8,128)(2,1)} %collective-permute-done.4.after_ref), channel_id=1, source_target_pairs={{0,48},{16,0},{32,16},{48,32},{1,49},{17,1},{33,17},{49,33},{2,50}... | collective-permute-start | bytes 1572872 | tf_op jit(solution)/shard_map/ppermute | solution.py:164
  41.2 7.3 %collective-permute-start.5 = (bf16[96,256]{1,0:T(8,128)(2,1)S(1)}, bf16[96,256]{1,0:T(8,128)(2,1)S(1)}, u32[]{:S(2)}, u32[]{:S(2)}) collective-permute-start(bf16[96,256]{1,0:T(8,128)(2,1)S(1)} %copy-done.4), channel_id=1, source_target_pairs={{0,0},{16,128},{32,256},{48,384},{128,400},{144,16},{160,144},{176... | collective-permute-start | bytes 147464 | tf_op jit(solution)/shard_map/ppermute | solution.py:160
  48.4 0.0 collective-permute-done.3.before_ref
  48.5 1.6 %collective-permute-done.1.after_ref = bf16[256,1024]{1,0:T(8,128)(2,1)S(1)} collective-permute-done((bf16[256,1024]{1,0:T(8,128)(2,1)S(1)}, bf16[256,1024]{1,0:T(8,128)(2,1)S(1)}, u32[]{:S(2)}, u32[]{:S(2)}) %collective-permute-start.1) | collective-permute-done | bytes 524320 | tf_op jit(solution)/shard_map/ppermute | solution.py:150
  50.1 6.7 %collective-permute-done.2.far_ref = bf16[256,1024]{1,0:T(8,128)(2,1)S(1)} collective-permute-done((bf16[256,1024]{1,0:T(8,128)(2,1)S(1)}, bf16[256,1024]{1,0:T(8,128)(2,1)S(1)}, u32[]{:S(2)}, u32[]{:S(2)}) %collective-permute-start.2) | collective-permute-done | bytes 524320 | tf_op jit(solution)/shard_map/ppermute | solution.py:162
  56.7 1.0 all-to-all-done.both_ref
  57.8 0.9 shard_map.77
  58.6 0.0 collective-permute-done.5.turned_ref
  58.6 1.0 collective-permute-done.6.far_ref
  59.6 1.9 %collective-permute-start.7 = (f32[4,96,256]{2,1,0:T(8,128)S(1)}, f32[4,96,256]{2,1,0:T(8,128)S(1)}, u32[]{:S(2)}, u32[]{:S(2)}) collective-permute-start(f32[4,96,256]{2,1,0:T(8,128)S(1)} %get-tuple-element.25), channel_id=1, source_target_pairs={{0,64},{64,0},{1,65},{65,1},{2,66},{66,2},{3,67},{67,3},{4,68},{68... | collective-permute-start | bytes 1179656 | tf_op jit(solution)/shard_map/ppermute | solution.py:181
  61.6 0.8 shard_map.78.mine_ref
  62.3 0.9 collective-permute-done.7.theirs_ref
  63.2 1.0 shard_map.79
  64.3 6.6 %all-to-all-start.1 = ((bf16[4,5,96,256]{3,2,1,0:T(8,128)(2,1)}), bf16[4,5,96,256]{3,2,1,0:T(8,128)(2,1)S(1)}, u32[]{:S(2)}, u32[]{:S(2)}) async-start(bf16[4,5,96,256]{3,2,1,0:T(8,128)(2,1)} %shard_map.79), calls=%async_computation.1 | async-start | bytes 1966080 | tf_op jit(solution)/shard_map/all_to_all | solution.py:22
  70.8 0.3 shard_map.82.refs_0_
  71.1 1.9 %collective-permute-start.10 = (bf16[2,192,1024]{2,1,0:T(8,128)(2,1)S(1)}, bf16[2,192,1024]{2,1,0:T(8,128)(2,1)}, u32[]{:S(2)}, u32[]{:S(2)}) collective-permute-start(bf16[2,192,1024]{2,1,0:T(8,128)(2,1)S(1)} %shard_map.82.refs_0_), channel_id=1, source_target_pairs={{0,16},{16,32},{32,48},{48,0},{1,17},{17,33},{33,49},{49,1},{2,18}... | collective-permute-start | bytes 2359304 | tf_op jit(solution)/shard_map/ppermute | solution.py:199
  73.1 2.7 %collective-permute-start.9 = (bf16[2,192,1024]{2,1,0:T(8,128)(2,1)S(1)}, bf16[2,192,1024]{2,1,0:T(8,128)(2,1)}, u32[]{:S(2)}, u32[]{:S(2)}) collective-permute-start(bf16[2,192,1024]{2,1,0:T(8,128)(2,1)S(1)} %shard_map.82.refs_0_), channel_id=1, source_target_pairs={{0,32},{16,48},{32,0},{48,16},{1,33},{17,49},{33,1},{49,17},{2,34}... | collective-permute-start | bytes 2359304 | tf_op jit(solution)/shard_map/ppermute | solution.py:199
  75.8 3.2 %collective-permute-start.8 = (bf16[2,192,1024]{2,1,0:T(8,128)(2,1)S(1)}, bf16[2,192,1024]{2,1,0:T(8,128)(2,1)}, u32[]{:S(2)}, u32[]{:S(2)}) collective-permute-start(bf16[2,192,1024]{2,1,0:T(8,128)(2,1)S(1)} %shard_map.82.refs_0_), channel_id=1, source_target_pairs={{0,48},{16,0},{32,16},{48,32},{1,49},{17,1},{33,17},{49,33},{2,50}... | collective-permute-start | bytes 2359304 | tf_op jit(solution)/shard_map/ppermute | solution.py:199
  79.0 6.6 %all-to-all-done.1.own_ref = bf16[4,5,96,256]{3,2,1,0:T(8,128)(2,1)S(1)} async-done(((bf16[4,5,96,256]{3,2,1,0:T(8,128)(2,1)}), bf16[4,5,96,256]{3,2,1,0:T(8,128)(2,1)S(1)}, u32[]{:S(2)}, u32[]{:S(2)}) %all-to-all-start.1) | async-done | bytes 983072 | tf_op jit(solution)/shard_map/all_to_all | solution.py:22
  85.5 0.3 shard_map.80
  85.8 2.4 %all-gather = bf16[8,192,256]{2,1,0:T(8,128)(2,1)S(1)} all-gather(bf16[8,96,256]{2,1,0:T(8,128)(2,1)S(1)} %shard_map.80), channel_id=2, replica_groups=mesh['y'=4,'c'=2,'x'=4,'za'=4,'zb'=4] {'c'}, dimensions={1}, use_global_device_ids=true | all-gather | bytes 1179648 | tf_op jit(solution)/shard_map/all_gather | solution.py:185
  88.2 2.7 %shard_map.81 = bf16[16,24,512]{2,1,0:T(8,128)(2,1)} custom-call(bf16[4,2,192,256]{3,2,1,0:T(8,128)(2,1)S(1)} %bitcast.2, bf16[1024,256]{1,0:T(8,128)(2,1)S(1)} %copy-done.1, bf16[1024,256]{1,0:T(8,128)(2,1)} %collective-permute-done.4.after_ref, bf16[1024,256]{1,0:T(8,128)(2,1)} %collective-permute-done.6.far_ref, ...), custom_call_target="tpu_custom_call" | custom-call | flops 402653184 | bytes 3276800 | tf_op jit(solution)/shard_map/pallas_call | solution.py:28
  90.9 11.7 %all-to-all-start.2 = ((bf16[16,24,512]{2,1,0:T(8,128)(2,1)}), bf16[16,24,512]{2,1,0:T(8,128)(2,1)S(1)}, u32[]{:S(2)}, u32[]{:S(2)}) async-start(bf16[16,24,512]{2,1,0:T(8,128)(2,1)} %shard_map.81), calls=%async_computation.2 | async-start | bytes 786432 | tf_op jit(solution)/shard_map/all_to_all | solution.py:22
  102.7 1.9 %collective-permute-start.13 = (bf16[2,192,256]{2,1,0:T(8,128)(2,1)S(1)}, bf16[2,192,256]{2,1,0:T(8,128)(2,1)S(1)}, u32[]{:S(2)}, u32[]{:S(2)}) collective-permute-start(bf16[2,192,256]{2,1,0:T(8,128)(2,1)S(1)} %get-tuple-element.35), channel_id=1, source_target_pairs={{0,16},{16,32},{32,48},{48,0},{1,17},{17,33},{33,49},{49,1},{2,18}... | collective-permute-start | bytes 589832 | tf_op jit(solution)/shard_map/ppermute | solution.py:200
  104.6 2.7 %collective-permute-start.12 = (bf16[2,192,256]{2,1,0:T(8,128)(2,1)S(1)}, bf16[2,192,256]{2,1,0:T(8,128)(2,1)S(1)}, u32[]{:S(2)}, u32[]{:S(2)}) collective-permute-start(bf16[2,192,256]{2,1,0:T(8,128)(2,1)S(1)} %get-tuple-element.36), channel_id=1, source_target_pairs={{0,32},{16,48},{32,0},{48,16},{1,33},{17,49},{33,1},{49,17},{2,34}... | collective-permute-start | bytes 589832 | tf_op jit(solution)/shard_map/ppermute | solution.py:200
  107.3 0.0 collective-permute-done.10.refs_3_
  107.3 3.2 %collective-permute-start.11 = (bf16[2,192,256]{2,1,0:T(8,128)(2,1)S(1)}, bf16[2,192,256]{2,1,0:T(8,128)(2,1)S(1)}, u32[]{:S(2)}, u32[]{:S(2)}) collective-permute-start(bf16[2,192,256]{2,1,0:T(8,128)(2,1)S(1)} %get-tuple-element.37), channel_id=1, source_target_pairs={{0,48},{16,0},{32,16},{48,32},{1,49},{17,1},{33,17},{49,33},{2,50}... | collective-permute-start | bytes 589832 | tf_op jit(solution)/shard_map/ppermute | solution.py:200
  110.5 0.0 collective-permute-done.9.refs_2_
  110.5 3.4 %collective-permute-done.8.refs_1_ = bf16[2,192,1024]{2,1,0:T(8,128)(2,1)} collective-permute-done((bf16[2,192,1024]{2,1,0:T(8,128)(2,1)S(1)}, bf16[2,192,1024]{2,1,0:T(8,128)(2,1)}, u32[]{:S(2)}, u32[]{:S(2)}) %collective-permute-start.8) | collective-permute-done | bytes 786464 | tf_op jit(solution)/shard_map/ppermute | solution.py:199
  113.9 0.6 collective-permute-done.13.refs_6_
  114.6 3.5 %collective-permute-done.12.refs_5_ = bf16[2,192,256]{2,1,0:T(8,128)(2,1)S(1)} collective-permute-done((bf16[2,192,256]{2,1,0:T(8,128)(2,1)S(1)}, bf16[2,192,256]{2,1,0:T(8,128)(2,1)S(1)}, u32[]{:S(2)}, u32[]{:S(2)}) %collective-permute-start.12) | collective-permute-done | bytes 196640 | tf_op jit(solution)/shard_map/ppermute | solution.py:200
  118.0 3.0 %collective-permute-done.11.refs_4_ = bf16[2,192,256]{2,1,0:T(8,128)(2,1)S(1)} collective-permute-done((bf16[2,192,256]{2,1,0:T(8,128)(2,1)S(1)}, bf16[2,192,256]{2,1,0:T(8,128)(2,1)S(1)}, u32[]{:S(2)}, u32[]{:S(2)}) %collective-permute-start.11) | collective-permute-done | bytes 196640 | tf_op jit(solution)/shard_map/ppermute | solution.py:200
  121.0 4.0 %shard_map.83 = (f32[1024,256]{1,0:T(8,128)}, f32[256,1024]{1,0:T(8,128)}) custom-call(bf16[4,2,192,256]{3,2,1,0:T(8,128)(2,1)S(1)} %bitcast.3, bf16[2,192,1024]{2,1,0:T(8,128)(2,1)S(1)} %shard_map.82.refs_0_, bf16[2,192,1024]{2,1,0:T(8,128)(2,1)} %collective-permute-done.8.refs_1_, bf16[2,192,1024]{2,1,0:T(8,128)(2,1)} %collective-permute-done.9.refs_2_, ...), custom_call_target="tpu_custom_call" | custom-call | flops 12884901888 | bytes 6619136 | tf_op jit(solution)/shard_map/pallas_call | solution.py:28
  125.0 1.9 %all-to-all-done.2.part_ref = bf16[16,24,512]{2,1,0:T(8,128)(2,1)S(1)} async-done(((bf16[16,24,512]{2,1,0:T(8,128)(2,1)}), bf16[16,24,512]{2,1,0:T(8,128)(2,1)S(1)}, u32[]{:S(2)}, u32[]{:S(2)}) %all-to-all-start.2) | async-done | bytes 393248 | tf_op jit(solution)/shard_map/all_to_all | solution.py:22
  126.9 0.7 shard_map.84
  (7 shorter events, 0.1 us)
Async XLA Ops:
  0.6 0.8 copy-start.2
  1.4 0.8 copy-start.3
  3.1 15.3 %copy-start = (bf16[256,1024]{1,0:T(8,128)(2,1)S(1)}, bf16[256,1024]{1,0:T(8,128)(2,1)}, u32[]{:S(2)}) copy-start(bf16[256,1024]{1,0:T(8,128)(2,1)} %own_ref.4) | copy-start | bytes 1572868
  3.1 17.7 %copy-start.1 = (bf16[1024,256]{1,0:T(8,128)(2,1)S(1)}, bf16[1024,256]{1,0:T(8,128)(2,1)}, u32[]{:S(2)}) copy-start(bf16[1024,256]{1,0:T(8,128)(2,1)} %own_ref.5) | copy-start | bytes 1572868
  3.1 38.1 %copy-start.4 = (bf16[96,256]{1,0:T(8,128)(2,1)S(1)}, bf16[96,256]{1,0:T(8,128)(2,1)}, u32[]{:S(2)}) copy-start(bf16[96,256]{1,0:T(8,128)(2,1)} %param.7) | copy-start | bytes 147460
  3.1 54.6 %all-to-all-start = ((bf16[16,48,512]{2,1,0:T(8,128)(2,1)}), bf16[16,48,512]{2,1,0:T(8,128)(2,1)S(1)}, u32[]{:S(2)}, u32[]{:S(2)}) async-start(bf16[16,48,512]{2,1,0:T(8,128)(2,1)} %shard_map.76), calls=%async_computation | async-start | bytes 1572864 | tf_op jit(solution)/shard_map/all_to_all | solution.py:22
  18.4 16.7 %collective-permute-start = (bf16[256,1024]{1,0:T(8,128)(2,1)S(1)}, bf16[256,1024]{1,0:T(8,128)(2,1)S(1)}, u32[]{:S(2)}, u32[]{:S(2)}) collective-permute-start(bf16[256,1024]{1,0:T(8,128)(2,1)S(1)} %copy-done), channel_id=1, source_target_pairs={{0,16},{16,32},{32,48},{48,0},{1,17},{17,33},{33,49},{49,1},{2,18}... | collective-permute-start | bytes 1572872 | tf_op jit(solution)/shard_map/ppermute | solution.py:150
  20.8 18.1 %collective-permute-start.4 = (bf16[1024,256]{1,0:T(8,128)(2,1)S(1)}, bf16[1024,256]{1,0:T(8,128)(2,1)}, u32[]{:S(2)}, u32[]{:S(2)}) collective-permute-start(bf16[1024,256]{1,0:T(8,128)(2,1)S(1)} %copy-done.1), channel_id=1, source_target_pairs={{0,48},{16,0},{32,16},{48,32},{1,49},{17,1},{33,17},{49,33},{2,50}... | collective-permute-start | bytes 1572872 | tf_op jit(solution)/shard_map/ppermute | solution.py:150
  24.3 24.1 %collective-permute-start.3 = (bf16[1024,256]{1,0:T(8,128)(2,1)S(1)}, bf16[1024,256]{1,0:T(8,128)(2,1)}, u32[]{:S(2)}, u32[]{:S(2)}) collective-permute-start(bf16[1024,256]{1,0:T(8,128)(2,1)S(1)} %copy-done.1), channel_id=1, source_target_pairs={{0,16},{16,32},{32,48},{48,0},{1,17},{17,33},{33,49},{49,1},{2,18}... | collective-permute-start | bytes 1572872 | tf_op jit(solution)/shard_map/ppermute | solution.py:150
  27.9 22.1 %collective-permute-start.1 = (bf16[256,1024]{1,0:T(8,128)(2,1)S(1)}, bf16[256,1024]{1,0:T(8,128)(2,1)S(1)}, u32[]{:S(2)}, u32[]{:S(2)}) collective-permute-start(bf16[256,1024]{1,0:T(8,128)(2,1)S(1)} %copy-done), channel_id=1, source_target_pairs={{0,48},{16,0},{32,16},{48,32},{1,49},{17,1},{33,17},{49,33},{2,50}... | collective-permute-start | bytes 1572872 | tf_op jit(solution)/shard_map/ppermute | solution.py:150
  35.2 21.5 %collective-permute-start.2 = (bf16[256,1024]{1,0:T(8,128)(2,1)S(1)}, bf16[256,1024]{1,0:T(8,128)(2,1)S(1)}, u32[]{:S(2)}, u32[]{:S(2)}) collective-permute-start(bf16[256,1024]{1,0:T(8,128)(2,1)S(1)} %collective-permute-done.before_ref), channel_id=1, source_target_pairs={{0,16},{16,32},{32,48},{48,0},{1,17},{17,33},{33,49},{49,1},{2,18}... | collective-permute-start | bytes 1572872 | tf_op jit(solution)/shard_map/ppermute | solution.py:162
  38.9 20.7 %collective-permute-start.6 = (bf16[1024,256]{1,0:T(8,128)(2,1)}, bf16[1024,256]{1,0:T(8,128)(2,1)}, u32[]{:S(2)}, u32[]{:S(2)}) collective-permute-start(bf16[1024,256]{1,0:T(8,128)(2,1)} %collective-permute-done.4.after_ref), channel_id=1, source_target_pairs={{0,48},{16,0},{32,16},{48,32},{1,49},{17,1},{33,17},{49,33},{2,50}... | collective-permute-start | bytes 1572872 | tf_op jit(solution)/shard_map/ppermute | solution.py:164
  41.2 17.5 %collective-permute-start.5 = (bf16[96,256]{1,0:T(8,128)(2,1)S(1)}, bf16[96,256]{1,0:T(8,128)(2,1)S(1)}, u32[]{:S(2)}, u32[]{:S(2)}) collective-permute-start(bf16[96,256]{1,0:T(8,128)(2,1)S(1)} %copy-done.4), channel_id=1, source_target_pairs={{0,0},{16,128},{32,256},{48,384},{128,400},{144,16},{160,144},{176... | collective-permute-start | bytes 147464 | tf_op jit(solution)/shard_map/ppermute | solution.py:160
  59.6 3.6 %collective-permute-start.7 = (f32[4,96,256]{2,1,0:T(8,128)S(1)}, f32[4,96,256]{2,1,0:T(8,128)S(1)}, u32[]{:S(2)}, u32[]{:S(2)}) collective-permute-start(f32[4,96,256]{2,1,0:T(8,128)S(1)} %get-tuple-element.25), channel_id=1, source_target_pairs={{0,64},{64,0},{1,65},{65,1},{2,66},{66,2},{3,67},{67,3},{4,68},{68... | collective-permute-start | bytes 1179656 | tf_op jit(solution)/shard_map/ppermute | solution.py:181
  64.3 21.3 %all-to-all-start.1 = ((bf16[4,5,96,256]{3,2,1,0:T(8,128)(2,1)}), bf16[4,5,96,256]{3,2,1,0:T(8,128)(2,1)S(1)}, u32[]{:S(2)}, u32[]{:S(2)}) async-start(bf16[4,5,96,256]{3,2,1,0:T(8,128)(2,1)} %shard_map.79), calls=%async_computation.1 | async-start | bytes 1966080 | tf_op jit(solution)/shard_map/all_to_all | solution.py:22
  71.1 36.2 %collective-permute-start.10 = (bf16[2,192,1024]{2,1,0:T(8,128)(2,1)S(1)}, bf16[2,192,1024]{2,1,0:T(8,128)(2,1)}, u32[]{:S(2)}, u32[]{:S(2)}) collective-permute-start(bf16[2,192,1024]{2,1,0:T(8,128)(2,1)S(1)} %shard_map.82.refs_0_), channel_id=1, source_target_pairs={{0,16},{16,32},{32,48},{48,0},{1,17},{17,33},{33,49},{49,1},{2,18}... | collective-permute-start | bytes 2359304 | tf_op jit(solution)/shard_map/ppermute | solution.py:199
  73.1 37.5 %collective-permute-start.9 = (bf16[2,192,1024]{2,1,0:T(8,128)(2,1)S(1)}, bf16[2,192,1024]{2,1,0:T(8,128)(2,1)}, u32[]{:S(2)}, u32[]{:S(2)}) collective-permute-start(bf16[2,192,1024]{2,1,0:T(8,128)(2,1)S(1)} %shard_map.82.refs_0_), channel_id=1, source_target_pairs={{0,32},{16,48},{32,0},{48,16},{1,33},{17,49},{33,1},{49,17},{2,34}... | collective-permute-start | bytes 2359304 | tf_op jit(solution)/shard_map/ppermute | solution.py:199
  75.8 38.2 %collective-permute-start.8 = (bf16[2,192,1024]{2,1,0:T(8,128)(2,1)S(1)}, bf16[2,192,1024]{2,1,0:T(8,128)(2,1)}, u32[]{:S(2)}, u32[]{:S(2)}) collective-permute-start(bf16[2,192,1024]{2,1,0:T(8,128)(2,1)S(1)} %shard_map.82.refs_0_), channel_id=1, source_target_pairs={{0,48},{16,0},{32,16},{48,32},{1,49},{17,1},{33,17},{49,33},{2,50}... | collective-permute-start | bytes 2359304 | tf_op jit(solution)/shard_map/ppermute | solution.py:199
  90.9 36.1 %all-to-all-start.2 = ((bf16[16,24,512]{2,1,0:T(8,128)(2,1)}), bf16[16,24,512]{2,1,0:T(8,128)(2,1)S(1)}, u32[]{:S(2)}, u32[]{:S(2)}) async-start(bf16[16,24,512]{2,1,0:T(8,128)(2,1)} %shard_map.81), calls=%async_computation.2 | async-start | bytes 786432 | tf_op jit(solution)/shard_map/all_to_all | solution.py:22
  102.7 11.9 %collective-permute-start.13 = (bf16[2,192,256]{2,1,0:T(8,128)(2,1)S(1)}, bf16[2,192,256]{2,1,0:T(8,128)(2,1)S(1)}, u32[]{:S(2)}, u32[]{:S(2)}) collective-permute-start(bf16[2,192,256]{2,1,0:T(8,128)(2,1)S(1)} %get-tuple-element.35), channel_id=1, source_target_pairs={{0,16},{16,32},{32,48},{48,0},{1,17},{17,33},{33,49},{49,1},{2,18}... | collective-permute-start | bytes 589832 | tf_op jit(solution)/shard_map/ppermute | solution.py:200
  104.6 13.4 %collective-permute-start.12 = (bf16[2,192,256]{2,1,0:T(8,128)(2,1)S(1)}, bf16[2,192,256]{2,1,0:T(8,128)(2,1)S(1)}, u32[]{:S(2)}, u32[]{:S(2)}) collective-permute-start(bf16[2,192,256]{2,1,0:T(8,128)(2,1)S(1)} %get-tuple-element.36), channel_id=1, source_target_pairs={{0,32},{16,48},{32,0},{48,16},{1,33},{17,49},{33,1},{49,17},{2,34}... | collective-permute-start | bytes 589832 | tf_op jit(solution)/shard_map/ppermute | solution.py:200
  107.3 13.7 %collective-permute-start.11 = (bf16[2,192,256]{2,1,0:T(8,128)(2,1)S(1)}, bf16[2,192,256]{2,1,0:T(8,128)(2,1)S(1)}, u32[]{:S(2)}, u32[]{:S(2)}) collective-permute-start(bf16[2,192,256]{2,1,0:T(8,128)(2,1)S(1)} %get-tuple-element.37), channel_id=1, source_target_pairs={{0,48},{16,0},{32,16},{48,32},{1,49},{17,1},{33,17},{49,33},{2,50}... | collective-permute-start | bytes 589832 | tf_op jit(solution)/shard_map/ppermute | solution.py:200
